TPU v7x, 32 devices: a whole 2x2x4 slice. The times are simulated.
32 devices in a mesh: gx: 4 (over z), gy: 4 (over y, core), gz: 2 (over x).
Axes of the slice: x: 2, y: 2, z: 4, core: 2. Of those that a mesh axis runs over, the one named last changes fastest.
Arguments:
- operator: bfloat16 [4, 4, 3072, 3072], P('gx', 'gy', 'gz'), may hold values from -1 to 4
- rhs_parts: float32 [4, 4, 8, 3072], P('gx', 'gy'), may hold values from -6 to 6
- stiffness: float32 [4, 4, 3072], P('gx', 'gy'), may hold values from 1 to 10
- traces: float32 [4, 4, 6, 3072], P('gx', 'gy'), may hold values from -6 to 6
- coarse_inverse: float32 [4, 4, 6, 96], P('gx', 'gy'), may hold values from -1 to 1, as said below
- rigid_loads: float32 [4, 4, 6, 8], P('gx', 'gy'), may hold values from -8192 to 8192
- face_lengths: int32 [4, 4, 4], P('gx', 'gy'), may hold values from 0 to 768, as said below
- face_order: int32 [4, 4, 4, 768], P('gx', 'gy'), may hold values from 0 to 767, as said below
- mode_count: int32 [4, 4], P('gx', 'gy'), may hold values from 0 to 6, as said below
Outputs:
- multipliers: float32 [4, 4, 8, 3072], P('gx', 'gy')
Inputs may be any that keep to these rules, and one draw needn't show every extreme that they name: `coarse_inverse`: symmetric over the coefficient ordering. `face_lengths`: a face on the grid's edge has length 0; the two sides of an interface have the same length. `face_order`: on each face the live slots map one to one onto the neighbour's live slots of the opposite face, and that face maps them back; other slots map to themselves. `mode_count`: subdomains off the grid's edge have 6.
All inputs are finite; a program needn't handle non-finite values.
Results may differ from a plain program's by a relative error of at most 0.0036.
Values may be sent and summed in bfloat16 or wider, within the bound.
No kernel may reach another device: no remote copies, remote signals or barrier semaphores. Data moves between devices by JAX's collectives and lax.ppermute only.
A program may use at most 64 MiB of HBM per device.

v0:
```python
import jax
import jax.numpy as jnp
from jax import lax
from jax.sharding import PartitionSpec as P

ITERS = 2


highest = lax.Precision.HIGHEST


def with_halo(block, sides, width):
    for axis, dim in sides:
        count = lax.axis_size(axis)
        forward = [(i, i + 1) for i in range(count - 1)]
        backward = [(target, source) for source, target in forward]
        low = lax.ppermute(
            lax.slice_in_dim(block, block.shape[dim] - width, None, axis=dim), axis, forward
        )
        high = lax.ppermute(lax.slice_in_dim(block, 0, width, axis=dim), axis, backward)
        block = jnp.concatenate([low, block, high], axis=dim)
    return block


def shards(
    operator,
    rhs_parts,
    stiffness,
    traces,
    coarse_inverse,
    rigid_loads,
    face_lengths,
    face_order,
    mode_count,
):
    local_rows = operator[0, 0]
    right_side = rhs_parts[0, 0]
    stiff_local = stiffness[0, 0]
    modes_local = traces[0, 0]
    inverse_rows = coarse_inverse[0, 0]
    loads_modes = rigid_loads[0, 0]
    lengths = face_lengths[0, 0]
    partner_slots = face_order[0, 0]
    modes_live = mode_count[0, 0]
    mode_total, order_size = modes_local.shape
    face_slots = partner_slots.shape[1]
    load_count = right_side.shape[0]
    position = lax.broadcasted_iota(jnp.int32, (4, face_slots), 1)
    live_mask = (position < lengths[:, None]).astype(jnp.float32).reshape(order_size)
    mode_mask = (lax.broadcasted_iota(jnp.int32, (mode_total, 1), 0) < modes_live).astype(
        jnp.float32
    )
    active_modes = modes_local * mode_mask
    face_start = lax.broadcasted_iota(jnp.int32, (4, face_slots), 0) * face_slots
    flat_slots = (partner_slots + face_start).reshape(order_size)

    def partner(vectors):
        row_count = vectors.shape[0]
        blocks = vectors.reshape(row_count, 4, face_slots)
        x_rim = with_halo(jnp.stack([blocks[:, 0], blocks[:, 1]], axis=0), (("gx", 0),), 1)
        y_rim = with_halo(jnp.stack([blocks[:, 2], blocks[:, 3]], axis=0), (("gy", 0),), 1)
        facing = jnp.stack([x_rim[0], x_rim[3], y_rim[0], y_rim[3]], axis=1).reshape(
            row_count, order_size
        )
        return jnp.take(facing, flat_slots, axis=1)

    def assemble(vectors):
        return live_mask * (vectors + partner(vectors))

    def coarse_step(local_coarse, partial_value):
        pieces, partials = (
            lax.all_gather(local_coarse[None], ("gx", "gy"), axis=0, tiled=True),
            lax.all_gather(partial_value[None], ("gx", "gy"), axis=0, tiled=True),
        )
        stacked = pieces.reshape(-1, load_count)
        own_coeffs = jnp.dot(inverse_rows, stacked, precision=highest)
        return (own_coeffs, None, jnp.sum(partials, axis=0))

    def correction(own_coeffs):
        own_term = jnp.einsum("ml,mi->li", own_coeffs, active_modes, precision=highest)
        return assemble(own_term)

    def product_rows(vectors):
        own_part = jnp.einsum(
            "lj,ij->li",
            vectors.astype(jnp.bfloat16),
            local_rows,
            preferred_element_type=jnp.float32,
        )
        return own_part.astype(jnp.bfloat16)

    def assembled_product(vectors, subtract_from):
        own_rows = product_rows(vectors)
        full_rows = lax.all_gather(own_rows, "gz", axis=1, tiled=True).astype(jnp.float32)
        if subtract_from is None:
            return assemble(full_rows)
        return assemble(subtract_from - full_rows)

    nothing = jnp.zeros((load_count,), jnp.float32)
    start_coeffs, start_grid, discard = coarse_step(mode_mask * loads_modes, nothing)
    start_term = jnp.einsum("ml,mi->li", start_coeffs, active_modes, precision=highest)
    outgoing = [start_term, stiff_local[None]] + []
    received = partner(jnp.concatenate(outgoing, axis=0))
    estimate = live_mask * (start_term + received[:load_count])
    weight = live_mask / (live_mask * (stiff_local + received[load_count]) + 1.0 - live_mask)

    def project(vectors, partial_value, needed):
        local_coarse = jnp.einsum("mi,li->ml", active_modes, vectors, precision=highest)
        own_coeffs, coarse_grid, dot_total = coarse_step(local_coarse, partial_value)
        if needed:
            return (vectors - correction(own_coeffs), dot_total)
        return (vectors, dot_total)

    gap = assembled_product(estimate, right_side)
    residual, discard = project(gap, nothing, True)
    direction = residual
    previous = nothing
    for iteration in range(ITERS):
        scaled = weight * residual
        projected, resid_dot = project(scaled, jnp.sum(residual * scaled, axis=1), True)
        if iteration == 0:
            direction = projected
        else:
            direction = projected + (resid_dot / previous)[:, None] * direction
        image = assembled_product(direction, None)
        corrected, curvature = project(
            image, jnp.sum(direction * image, axis=1), iteration + 1 < ITERS
        )
        step_size = resid_dot / curvature
        estimate = estimate + step_size[:, None] * direction
        if iteration + 1 < ITERS:
            residual = residual - step_size[:, None] * corrected
        previous = resid_dot
    return estimate[None, None]


def solution(mesh):
    in_specs = (
        P("gx", "gy", "gz", None),
        P("gx", "gy", None, None),
        P("gx", "gy", None),
        P("gx", "gy", None, None),
        P("gx", "gy", None, None),
        P("gx", "gy", None, None),
        P("gx", "gy", None),
        P("gx", "gy", None, None),
        P("gx", "gy"),
    )
    out_specs = P("gx", "gy", None, None)
    return jax.shard_map(shards, mesh=mesh, in_specs=in_specs, out_specs=out_specs, check_vma=False)
```

profile of v0, /device:TPU:0, one launch (start us, length us, event | category | flops | bytes accessed | tf_op | source)
XLA Modules:
  0.0 409.1 jit_solution(17842651838134853437)
XLA Ops:
  1.4 23.2 %all_gather.36 = f32[16,6,8]{2,1,0:T(8,128)S(1)} all-gather(f32[1,6,8]{2,1,0:T(8,128)S(1)} %copy.49), channel_id=1, replica_groups=mesh['gx'=4,'gy'=4,'gz'=2] {'gx','gy'}, dimensions={0}, use_global_device_ids=true | all-gather | bytes 3264 | tf_op jit(solution)/shard_map/all_gather | solution.py:72
  25.6 1.2 fusion.25
  27.5 1.3 collective-permute-start.3
  28.8 3.0 collective-permute-start.2
  31.9 1.3 collective-permute-start.1
  33.2 4.5 %collective-permute-start = (f32[1,9,768]{2,1,0:T(8,128)S(1)}, f32[1,9,768]{2,1,0:T(8,128)S(1)}, u32[]{:S(2)}, u32[]{:S(2)}) collective-permute-start(f32[1,9,768]{2,1,0:T(8,128)S(1)} %get-tuple-element.12), channel_id=1, source_target_pairs={{0,8},{8,16},{16,24},{1,9},{9,17},{17,25},{2,10},{10,18},{18,26},{... | collective-permute-start | bytes 82952 | tf_op jit(solution)/shard_map/ppermute | solution.py:17
  39.4 1.3 fusion.64
  41.3 8.1 %gather_fusion = f32[3072,9]{1,0:T(8,128)S(1)} fusion(f32[9,3072]{0,1:T(8,128)S(1)} %bitcast.255, s32[3072]{0:T(1024)S(1)} %broadcast_clamp_fusion.1), kind=kCustom, calls=%fused_computation.7 | custom fusion | bytes 233472 | tf_op jit(solution)/shard_map/jit(_take)/gather | solution.py:65
  50.0 6.3 %fusion.6 = bf16[8,1536]{1,0:T(8,128)(2,1)S(1)} fusion(bf16[1,1,1536,3072]{3,2,1,0:T(8,128)(2,1)} %param.11, f32[8,3072]{1,0:T(8,128)S(1)} %fusion.25, f32[9,3072]{1,0:T(8,128)S(1)} %select_bitcast_fusion, f32[3072]{0:T(1024)S(1)} %reshape.220), kind=kOutput, calls=%fused_computation.14 | convolution fusion | flops 75583488 | bytes 9670656 | tf_op jit(solution)/shard_map/lj,ij->li/dot_general | solution.py:84
  56.3 4.7 %all_gather.37 = bf16[8,3072]{1,0:T(8,128)(2,1)S(1)} all-gather(bf16[8,1536]{1,0:T(8,128)(2,1)S(1)} %fusion.6), channel_id=1, replica_groups=mesh['gx'=4,'gy'=4,'gz'=2] {'gz'}, dimensions={1}, use_global_device_ids=true | all-gather | bytes 73728 | tf_op jit(solution)/shard_map/all_gather | solution.py:94
  61.1 1.3 collective-permute-start.7
  62.4 3.0 collective-permute-start.6
  65.4 1.3 collective-permute-start.5
  66.7 4.5 %collective-permute-start.4 = (f32[1,8,768]{2,1,0:T(8,128)S(1)}, f32[1,8,768]{2,1,0:T(8,128)S(1)}, u32[]{:S(2)}, u32[]{:S(2)}) collective-permute-start(f32[1,8,768]{2,1,0:T(8,128)S(1)} %get-tuple-element.40), channel_id=1, source_target_pairs={{0,8},{8,16},{16,24},{1,9},{9,17},{17,25},{2,10},{10,18},{18,26},{... | collective-permute-start | bytes 73736 | tf_op jit(solution)/shard_map/ppermute | solution.py:17
  73.3 8.1 %gather_fusion.1 = f32[3072,8]{1,0:T(8,128)S(1)} fusion(f32[8,3072]{0,1:T(8,128)S(1)} %bitcast.257, s32[3072]{0:T(1024)S(1)} %broadcast_clamp_fusion), kind=kCustom, calls=%fused_computation.clone | custom fusion | bytes 208896 | tf_op jit(solution)/shard_map/jit(_take)/gather | solution.py:65
  82.2 20.2 %all-gather.8 = f32[16,6,8]{2,1,0:T(8,128)S(1)} all-gather(f32[1,6,8]{2,1,0:T(8,128)S(1)} %convolution_bitcast_fusion.3), channel_id=2, replica_groups=mesh['gx'=4,'gy'=4,'gz'=2] {'gx','gy'}, dimensions={0}, use_global_device_ids=true | all-gather | bytes 3264 | tf_op jit(solution)/shard_map/all_gather | solution.py:72
  103.0 1.3 collective-permute-start.11
  104.3 3.0 collective-permute-start.10
  107.3 1.3 collective-permute-start.9
  108.6 4.5 %collective-permute-start.8 = (f32[1,8,768]{2,1,0:T(8,128)S(1)}, f32[1,8,768]{2,1,0:T(8,128)S(1)}, u32[]{:S(2)}, u32[]{:S(2)}) collective-permute-start(f32[1,8,768]{2,1,0:T(8,128)S(1)} %get-tuple-element.36), channel_id=1, source_target_pairs={{0,8},{8,16},{16,24},{1,9},{9,17},{17,25},{2,10},{10,18},{18,26},{... | collective-permute-start | bytes 73736 | tf_op jit(solution)/shard_map/ppermute | solution.py:17
  113.2 0.9 subtract_divide_fusion
  115.2 8.1 %gather_fusion.2 = f32[3072,8]{1,0:T(8,128)S(1)} fusion(f32[8,3072]{0,1:T(8,128)S(1)} %bitcast.258, s32[3072]{0:T(1024)S(1)} %broadcast_clamp_fusion), kind=kCustom, calls=%fused_computation.1.clone | custom fusion | bytes 208896 | tf_op jit(solution)/shard_map/jit(_take)/gather | solution.py:65
  124.9 1.0 convolution_bitcast_fusion.2
  125.8 18.8 %all-gather.9 = f32[16,6,8]{2,1,0:T(8,128)S(1)} all-gather(f32[1,6,8]{2,1,0:T(8,128)S(1)} %convolution_bitcast_fusion.2), channel_id=4, replica_groups=mesh['gx'=4,'gy'=4,'gz'=2] {'gx','gy'}, dimensions={0}, use_global_device_ids=true | all-gather | bytes 3264 | tf_op jit(solution)/shard_map/all_gather | solution.py:72
  145.2 1.3 collective-permute-start.15
  146.5 3.0 collective-permute-start.14
  149.5 1.3 collective-permute-start.13
  150.8 4.5 %collective-permute-start.12 = (f32[1,8,768]{2,1,0:T(8,128)S(1)}, f32[1,8,768]{2,1,0:T(8,128)S(1)}, u32[]{:S(2)}, u32[]{:S(2)}) collective-permute-start(f32[1,8,768]{2,1,0:T(8,128)S(1)} %get-tuple-element.32), channel_id=1, source_target_pairs={{0,8},{8,16},{16,24},{1,9},{9,17},{17,25},{2,10},{10,18},{18,26},{... | collective-permute-start | bytes 73736 | tf_op jit(solution)/shard_map/ppermute | solution.py:17
  155.4 1.5 collective-permute-done.12
  157.4 8.1 %gather_fusion.3 = f32[3072,8]{1,0:T(8,128)S(1)} fusion(f32[8,3072]{0,1:T(8,128)S(1)} %bitcast.259, s32[3072]{0:T(1024)S(1)} %broadcast_clamp_fusion), kind=kCustom, calls=%fused_computation.2.clone | custom fusion | bytes 208896 | tf_op jit(solution)/shard_map/jit(_take)/gather | solution.py:65
  165.9 0.9 multiply_subtract_fusion.1
  166.9 6.2 %fusion.9 = bf16[8,1536]{1,0:T(8,128)(2,1)S(1)} fusion(bf16[1,1,1536,3072]{3,2,1,0:T(8,128)(2,1)} %param.11, f32[8,3072]{1,0:T(8,128)S(1)} %multiply_subtract_fusion.1), kind=kOutput, calls=%fused_computation.15 | convolution fusion | flops 75534336 | bytes 9560064 | tf_op jit(solution)/shard_map/lj,ij->li/dot_general | solution.py:84
  173.1 4.5 %all_gather.41 = bf16[8,3072]{1,0:T(8,128)(2,1)S(1)} all-gather(bf16[8,1536]{1,0:T(8,128)(2,1)S(1)} %fusion.9), channel_id=1, replica_groups=mesh['gx'=4,'gy'=4,'gz'=2] {'gz'}, dimensions={1}, use_global_device_ids=true | all-gather | bytes 73728 | tf_op jit(solution)/shard_map/all_gather | solution.py:94
  177.7 1.3 collective-permute-start.19
  179.0 3.0 collective-permute-start.18
  182.0 1.3 collective-permute-start.17
  183.3 4.8 %collective-permute-start.16 = (f32[1,8,768]{2,1,0:T(8,128)S(1)}, f32[1,8,768]{2,1,0:T(8,128)S(1)}, u32[]{:S(2)}, u32[]{:S(2)}) collective-permute-start(f32[1,8,768]{2,1,0:T(8,128)S(1)} %get-tuple-element.28), channel_id=1, source_target_pairs={{0,8},{8,16},{16,24},{1,9},{9,17},{17,25},{2,10},{10,18},{18,26},{... | collective-permute-start | bytes 73736 | tf_op jit(solution)/shard_map/ppermute | solution.py:17
  190.7 8.1 %gather_fusion.4 = f32[3072,8]{1,0:T(8,128)S(1)} fusion(f32[8,3072]{0,1:T(8,128)S(1)} %bitcast.260, s32[3072]{0:T(1024)S(1)} %broadcast_clamp_fusion), kind=kCustom, calls=%fused_computation.3.clone | custom fusion | bytes 208896 | tf_op jit(solution)/shard_map/jit(_take)/gather | solution.py:65
  199.9 21.1 %all-gather.10 = f32[16,6,8]{2,1,0:T(8,128)S(1)} all-gather(f32[1,6,8]{2,1,0:T(8,128)S(1)} %convolution_bitcast_fusion.1), channel_id=6, replica_groups=mesh['gx'=4,'gy'=4,'gz'=2] {'gx','gy'}, dimensions={0}, use_global_device_ids=true | all-gather | bytes 3264 | tf_op jit(solution)/shard_map/all_gather | solution.py:72
  221.6 1.3 collective-permute-start.23
  222.9 3.0 collective-permute-start.22
  225.9 1.3 collective-permute-start.21
  227.2 4.5 %collective-permute-start.20 = (f32[1,8,768]{2,1,0:T(8,128)S(1)}, f32[1,8,768]{2,1,0:T(8,128)S(1)}, u32[]{:S(2)}, u32[]{:S(2)}) collective-permute-start(f32[1,8,768]{2,1,0:T(8,128)S(1)} %get-tuple-element.24), channel_id=1, source_target_pairs={{0,8},{8,16},{16,24},{1,9},{9,17},{17,25},{2,10},{10,18},{18,26},{... | collective-permute-start | bytes 73736 | tf_op jit(solution)/shard_map/ppermute | solution.py:17
  232.2 30.5 %all-reduce.4 = (f32[128]{0:T(128)S(1)}, f32[128]{0:T(128)S(1)}) all-reduce(f32[128]{0:T(128)S(1)} %copy-done.37, f32[128]{0:T(128)S(1)} %dynamic-update-slice.1), channel_id=3, replica_groups=mesh['gx'=4,'gy'=4,'gz'=2] {'gx','gy'}, use_global_device_ids=true, to_apply=%add | all-reduce | flops 256 | bytes 2048
  264.0 8.1 %gather_fusion.5 = f32[3072,8]{1,0:T(8,128)S(1)} fusion(f32[8,3072]{0,1:T(8,128)S(1)} %bitcast.261, s32[3072]{0:T(1024)S(1)} %broadcast_clamp_fusion), kind=kCustom, calls=%fused_computation.4.clone | custom fusion | bytes 208896 | tf_op jit(solution)/shard_map/jit(_take)/gather | solution.py:65
  273.1 0.9 fusion.18
  274.0 1.0 convolution_bitcast_fusion
  275.1 17.3 %all-gather.11 = f32[16,6,8]{2,1,0:T(8,128)S(1)} all-gather(f32[1,6,8]{2,1,0:T(8,128)S(1)} %convolution_bitcast_fusion), channel_id=8, replica_groups=mesh['gx'=4,'gy'=4,'gz'=2] {'gx','gy'}, dimensions={0}, use_global_device_ids=true | all-gather | bytes 3264 | tf_op jit(solution)/shard_map/all_gather | solution.py:72
  293.0 1.3 collective-permute-start.27
  294.3 3.0 collective-permute-start.26
  297.3 1.3 collective-permute-start.25
  298.6 4.5 %collective-permute-start.24 = (f32[1,8,768]{2,1,0:T(8,128)S(1)}, f32[1,8,768]{2,1,0:T(8,128)S(1)}, u32[]{:S(2)}, u32[]{:S(2)}) collective-permute-start(f32[1,8,768]{2,1,0:T(8,128)S(1)} %get-tuple-element.20), channel_id=1, source_target_pairs={{0,8},{8,16},{16,24},{1,9},{9,17},{17,25},{2,10},{10,18},{18,26},{... | collective-permute-start | bytes 73736 | tf_op jit(solution)/shard_map/ppermute | solution.py:17
  303.4 30.5 %all-reduce.2 = f32[128]{0:T(128)S(1)} all-reduce(f32[128]{0:T(128)S(1)} %dynamic-update-slice.2), channel_id=7, replica_groups=mesh['gx'=4,'gy'=4,'gz'=2] {'gx','gy'}, use_global_device_ids=true, to_apply=%add.2 | all-reduce | flops 128 | bytes 1024
  334.0 1.1 div.27
  335.7 9.6 %gather_fusion.6 = f32[3072,8]{1,0:T(8,128)S(1)} fusion(f32[8,3072]{0,1:T(8,128)S(1)} %bitcast.262, s32[3072]{0:T(1024)} %copy-done.13), kind=kCustom, calls=%fused_computation.5.clone | custom fusion | bytes 208896 | tf_op jit(solution)/shard_map/jit(_take)/gather | solution.py:65
  346.7 6.2 %fusion.12 = bf16[8,1536]{1,0:T(8,128)(2,1)S(1)} fusion(bf16[1,1,1536,3072]{3,2,1,0:T(8,128)(2,1)} %param.11, f32[8,3072]{1,0:T(8,128)S(1)} %fusion.19), kind=kOutput, calls=%fused_computation.16 | convolution fusion | flops 75534336 | bytes 9560064 | tf_op jit(solution)/shard_map/lj,ij->li/dot_general | solution.py:84
  352.9 4.6 %all_gather.46 = bf16[8,3072]{1,0:T(8,128)(2,1)S(1)} all-gather(bf16[8,1536]{1,0:T(8,128)(2,1)S(1)} %fusion.12), channel_id=1, replica_groups=mesh['gx'=4,'gy'=4,'gz'=2] {'gz'}, dimensions={1}, use_global_device_ids=true | all-gather | bytes 73728 | tf_op jit(solution)/shard_map/all_gather | solution.py:94
  357.6 1.3 collective-permute-start.31
  358.9 3.0 collective-permute-start.30
  361.9 1.3 collective-permute-start.29
  363.2 4.5 %collective-permute-start.28 = (f32[1,8,768]{2,1,0:T(8,128)S(1)}, f32[1,8,768]{2,1,0:T(8,128)S(1)}, u32[]{:S(2)}, u32[]{:S(2)}) collective-permute-start(f32[1,8,768]{2,1,0:T(8,128)S(1)} %get-tuple-element.16), channel_id=1, source_target_pairs={{0,8},{8,16},{16,24},{1,9},{9,17},{17,25},{2,10},{10,18},{18,26},{... | collective-permute-start | bytes 73736 | tf_op jit(solution)/shard_map/ppermute | solution.py:17
  367.8 1.5 collective-permute-done.28
  369.8 8.1 %gather_fusion.7 = f32[3072,8]{1,0:T(8,128)S(1)} fusion(f32[8,3072]{0,1:T(8,128)S(1)} %bitcast.256, s32[3072]{0:T(1024)S(1)} %copy-done.14), kind=kCustom, calls=%fused_computation.6.clone | custom fusion | bytes 208896 | tf_op jit(solution)/shard_map/jit(_take)/gather | solution.py:65
  378.8 29.5 %all-reduce.3 = f32[128]{0:T(128)S(1)} all-reduce(f32[128]{0:T(128)S(1)} %dynamic-update-slice.3), channel_id=9, replica_groups=mesh['gx'=4,'gy'=4,'gz'=2] {'gx','gy'}, use_global_device_ids=true, to_apply=%add.3 | all-reduce | flops 128 | bytes 1024
  (198 shorter events, 23.5 us)
Async XLA Ops:
  0.7 40.1 %copy-start.22 = (f32[6]{0:T(128)}, f32[6]{0:T(128)S(1)}, u32[]{:S(2)}) copy-start(f32[6]{0:T(128)S(1)} %compare_convert_fusion) | copy-start | bytes 76
  27.5 13.2 %collective-permute-start.3 = (f32[1,9,768]{2,1,0:T(8,128)S(1)}, f32[1,9,768]{2,1,0:T(8,128)S(1)}, u32[]{:S(2)}, u32[]{:S(2)}) collective-permute-start(f32[1,9,768]{2,1,0:T(8,128)S(1)} %get-tuple-element.14), channel_id=1, source_target_pairs={{2,0},{4,2},{6,4},{3,1},{5,3},{7,5},{10,8},{12,10},{14,12},{11,9},... | collective-permute-start | bytes 82952 | tf_op jit(solution)/shard_map/ppermute | solution.py:20
  28.8 11.9 %collective-permute-start.2 = (f32[1,9,768]{2,1,0:T(8,128)S(1)}, f32[1,9,768]{2,1,0:T(8,128)S(1)}, u32[]{:S(2)}, u32[]{:S(2)}) collective-permute-start(f32[1,9,768]{2,1,0:T(8,128)S(1)} %get-tuple-element.15), channel_id=1, source_target_pairs={{0,2},{2,4},{4,6},{1,3},{3,5},{5,7},{8,10},{10,12},{12,14},{9,11},... | collective-permute-start | bytes 82952 | tf_op jit(solution)/shard_map/ppermute | solution.py:17
  31.9 8.9 %collective-permute-start.1 = (f32[1,9,768]{2,1,0:T(8,128)S(1)}, f32[1,9,768]{2,1,0:T(8,128)S(1)}, u32[]{:S(2)}, u32[]{:S(2)}) collective-permute-start(f32[1,9,768]{2,1,0:T(8,128)S(1)} %get-tuple-element.13), channel_id=1, source_target_pairs={{8,0},{16,8},{24,16},{9,1},{17,9},{25,17},{10,2},{18,10},{26,18},{... | collective-permute-start | bytes 82952 | tf_op jit(solution)/shard_map/ppermute | solution.py:20
  33.2 7.6 %collective-permute-start = (f32[1,9,768]{2,1,0:T(8,128)S(1)}, f32[1,9,768]{2,1,0:T(8,128)S(1)}, u32[]{:S(2)}, u32[]{:S(2)}) collective-permute-start(f32[1,9,768]{2,1,0:T(8,128)S(1)} %get-tuple-element.12), channel_id=1, source_target_pairs={{0,8},{8,16},{16,24},{1,9},{9,17},{17,25},{2,10},{10,18},{18,26},{... | collective-permute-start | bytes 82952 | tf_op jit(solution)/shard_map/ppermute | solution.py:17
  50.0 6.4 %copy-start.11 = (f32[9,3072]{1,0:T(8,128)}, f32[9,3072]{1,0:T(8,128)S(1)}, u32[]{:S(2)}) copy-start(f32[9,3072]{1,0:T(8,128)S(1)} %select_bitcast_fusion) | copy-start | bytes 331780
  50.0 11.1 %copy-start.21 = (f32[1,1,8,3072]{3,2,1,0:T(8,128)S(1)}, f32[1,1,8,3072]{3,2,1,0:T(8,128)}, u32[]{:S(2)}) copy-start(f32[1,1,8,3072]{3,2,1,0:T(8,128)} %param.12) | copy-start | bytes 294916
  50.0 21.3 %copy-start.29 = (pred[1,1,4,768]{3,2,1,0:T(4,128)(4,1)S(1)}, pred[1,1,4,768]{3,2,1,0:T(4,128)(4,1)}, u32[]{:S(2)}) copy-start(pred[1,1,4,768]{3,2,1,0:T(4,128)(4,1)} %get-tuple-element.45) | copy-start | bytes 9220
  61.1 10.9 %collective-permute-start.7 = (f32[1,8,768]{2,1,0:T(8,128)S(1)}, f32[1,8,768]{2,1,0:T(8,128)S(1)}, u32[]{:S(2)}, u32[]{:S(2)}) collective-permute-start(f32[1,8,768]{2,1,0:T(8,128)S(1)} %get-tuple-element.41), channel_id=1, source_target_pairs={{2,0},{4,2},{6,4},{3,1},{5,3},{7,5},{10,8},{12,10},{14,12},{11,9},... | collective-permute-start | bytes 73736 | tf_op jit(solution)/shard_map/ppermute | solution.py:20
  62.4 9.6 %collective-permute-start.6 = (f32[1,8,768]{2,1,0:T(8,128)S(1)}, f32[1,8,768]{2,1,0:T(8,128)S(1)}, u32[]{:S(2)}, u32[]{:S(2)}) collective-permute-start(f32[1,8,768]{2,1,0:T(8,128)S(1)} %get-tuple-element.42), channel_id=1, source_target_pairs={{0,2},{2,4},{4,6},{1,3},{3,5},{5,7},{8,10},{10,12},{12,14},{9,11},... | collective-permute-start | bytes 73736 | tf_op jit(solution)/shard_map/ppermute | solution.py:17
  65.4 6.5 %collective-permute-start.5 = (f32[1,8,768]{2,1,0:T(8,128)S(1)}, f32[1,8,768]{2,1,0:T(8,128)S(1)}, u32[]{:S(2)}, u32[]{:S(2)}) collective-permute-start(f32[1,8,768]{2,1,0:T(8,128)S(1)} %get-tuple-element.43), channel_id=1, source_target_pairs={{8,0},{16,8},{24,16},{9,1},{17,9},{25,17},{10,2},{18,10},{26,18},{... | collective-permute-start | bytes 73736 | tf_op jit(solution)/shard_map/ppermute | solution.py:20
  66.7 6.1 %collective-permute-start.4 = (f32[1,8,768]{2,1,0:T(8,128)S(1)}, f32[1,8,768]{2,1,0:T(8,128)S(1)}, u32[]{:S(2)}, u32[]{:S(2)}) collective-permute-start(f32[1,8,768]{2,1,0:T(8,128)S(1)} %get-tuple-element.40), channel_id=1, source_target_pairs={{0,8},{8,16},{16,24},{1,9},{9,17},{17,25},{2,10},{10,18},{18,26},{... | collective-permute-start | bytes 73736 | tf_op jit(solution)/shard_map/ppermute | solution.py:17
  71.3 192.7 %copy-start.13 = (s32[3072]{0:T(1024)}, s32[3072]{0:T(1024)S(1)}, u32[]{:S(2)}) copy-start(s32[3072]{0:T(1024)S(1)} %broadcast_clamp_fusion) | copy-start | bytes 36868
  73.3 8.6 %copy-start = (f32[1,1,6,3072]{3,1,2,0:T(1,128)S(1)}, f32[1,1,6,3072]{3,1,2,0:T(1,128)}, u32[]{:S(2)}) copy-start(f32[1,1,6,3072]{3,1,2,0:T(1,128)} %param.14) | copy-start | bytes 221188
  73.3 8.6 %copy-start.23 = (f32[6]{0:T(128)S(1)}, f32[6]{0:T(128)}, u32[]{:S(2)}) copy-start(f32[6]{0:T(128)} %copy-done.22) | copy-start | bytes 76
  73.3 29.2 %copy-start.17 = (f32[1,1,6,96]{3,1,2,0:T(1,128)S(1)}, f32[1,1,6,96]{3,1,2,0:T(1,128)}, u32[]{:S(2)}) copy-start(f32[1,1,6,96]{3,1,2,0:T(1,128)} %param.15) | copy-start | bytes 6916
  81.4 31.8 %copy-start.27 = (f32[1,1,3072]{2,1,0:T(1,128)S(1)}, f32[1,1,3072]{2,1,0:T(1,128)}, u32[]{:S(2)}) copy-start(f32[1,1,3072]{2,1,0:T(1,128)} %param.13) | copy-start | bytes 36868
  81.4 31.8 %copy-start.28 = (pred[1,1,4,768]{3,1,2,0:T(4,128)(4,1)S(1)}, pred[1,1,4,768]{3,1,2,0:T(4,128)(4,1)}, u32[]{:S(2)}) copy-start(pred[1,1,4,768]{3,1,2,0:T(4,128)(4,1)} %copy.81) | copy-start | bytes 9220
  103.0 11.7 %copy-start.6 = (f32[8,3072]{1,0:T(8,128)}, f32[8,3072]{1,0:T(8,128)S(1)}, u32[]{:S(2)}) copy-start(f32[8,3072]{1,0:T(8,128)S(1)} %fusion.24) | copy-start | bytes 294916
  103.0 11.2 %collective-permute-start.11 = (f32[1,8,768]{2,1,0:T(8,128)S(1)}, f32[1,8,768]{2,1,0:T(8,128)S(1)}, u32[]{:S(2)}, u32[]{:S(2)}) collective-permute-start(f32[1,8,768]{2,1,0:T(8,128)S(1)} %get-tuple-element.37), channel_id=1, source_target_pairs={{2,0},{4,2},{6,4},{3,1},{5,3},{7,5},{10,8},{12,10},{14,12},{11,9},... | collective-permute-start | bytes 73736 | tf_op jit(solution)/shard_map/ppermute | solution.py:20
  104.3 9.9 %collective-permute-start.10 = (f32[1,8,768]{2,1,0:T(8,128)S(1)}, f32[1,8,768]{2,1,0:T(8,128)S(1)}, u32[]{:S(2)}, u32[]{:S(2)}) collective-permute-start(f32[1,8,768]{2,1,0:T(8,128)S(1)} %get-tuple-element.38), channel_id=1, source_target_pairs={{0,2},{2,4},{4,6},{1,3},{3,5},{5,7},{8,10},{10,12},{12,14},{9,11},... | collective-permute-start | bytes 73736 | tf_op jit(solution)/shard_map/ppermute | solution.py:17
  107.3 6.8 %collective-permute-start.9 = (f32[1,8,768]{2,1,0:T(8,128)S(1)}, f32[1,8,768]{2,1,0:T(8,128)S(1)}, u32[]{:S(2)}, u32[]{:S(2)}) collective-permute-start(f32[1,8,768]{2,1,0:T(8,128)S(1)} %get-tuple-element.39), channel_id=1, source_target_pairs={{8,0},{16,8},{24,16},{9,1},{17,9},{25,17},{10,2},{18,10},{26,18},{... | collective-permute-start | bytes 73736 | tf_op jit(solution)/shard_map/ppermute | solution.py:20
  108.6 6.1 %collective-permute-start.8 = (f32[1,8,768]{2,1,0:T(8,128)S(1)}, f32[1,8,768]{2,1,0:T(8,128)S(1)}, u32[]{:S(2)}, u32[]{:S(2)}) collective-permute-start(f32[1,8,768]{2,1,0:T(8,128)S(1)} %get-tuple-element.36), channel_id=1, source_target_pairs={{0,8},{8,16},{16,24},{1,9},{9,17},{17,25},{2,10},{10,18},{18,26},{... | collective-permute-start | bytes 73736 | tf_op jit(solution)/shard_map/ppermute | solution.py:17
  114.2 51.8 %copy-start.15 = (f32[1,3072]{1,0:T(1,128)}, f32[1,3072]{1,0:T(1,128)S(1)}, u32[]{:S(2)}) copy-start(f32[1,3072]{1,0:T(1,128)S(1)} %subtract_divide_fusion) | copy-start | bytes 36868
  123.3 21.3 %copy-start.18 = (f32[1,1,6,96]{3,1,2,0:T(1,128)S(1)}, f32[1,1,6,96]{3,1,2,0:T(1,128)}, u32[]{:S(2)}) copy-start(f32[1,1,6,96]{3,1,2,0:T(1,128)} %param.15) | copy-start | bytes 6916
  123.3 21.5 %copy-start.24 = (f32[6]{0:T(128)S(1)}, f32[6]{0:T(128)}, u32[]{:S(2)}) copy-start(f32[6]{0:T(128)} %copy-done.22) | copy-start | bytes 76
  145.2 20.3 %copy-start.8 = (f32[8,3072]{1,0:T(8,128)}, f32[8,3072]{1,0:T(8,128)S(1)}, u32[]{:S(2)}) copy-start(f32[8,3072]{1,0:T(8,128)S(1)} %fusion.23) | copy-start | bytes 294916
  145.2 10.2 %collective-permute-start.15 = (f32[1,8,768]{2,1,0:T(8,128)S(1)}, f32[1,8,768]{2,1,0:T(8,128)S(1)}, u32[]{:S(2)}, u32[]{:S(2)}) collective-permute-start(f32[1,8,768]{2,1,0:T(8,128)S(1)} %get-tuple-element.33), channel_id=1, source_target_pairs={{2,0},{4,2},{6,4},{3,1},{5,3},{7,5},{10,8},{12,10},{14,12},{11,9},... | collective-permute-start | bytes 73736 | tf_op jit(solution)/shard_map/ppermute | solution.py:20
  146.5 8.9 %collective-permute-start.14 = (f32[1,8,768]{2,1,0:T(8,128)S(1)}, f32[1,8,768]{2,1,0:T(8,128)S(1)}, u32[]{:S(2)}, u32[]{:S(2)}) collective-permute-start(f32[1,8,768]{2,1,0:T(8,128)S(1)} %get-tuple-element.34), channel_id=1, source_target_pairs={{0,2},{2,4},{4,6},{1,3},{3,5},{5,7},{8,10},{10,12},{12,14},{9,11},... | collective-permute-start | bytes 73736 | tf_op jit(solution)/shard_map/ppermute | solution.py:17
  149.5 5.9 %collective-permute-start.13 = (f32[1,8,768]{2,1,0:T(8,128)S(1)}, f32[1,8,768]{2,1,0:T(8,128)S(1)}, u32[]{:S(2)}, u32[]{:S(2)}) collective-permute-start(f32[1,8,768]{2,1,0:T(8,128)S(1)} %get-tuple-element.35), channel_id=1, source_target_pairs={{8,0},{16,8},{24,16},{9,1},{17,9},{25,17},{10,2},{18,10},{26,18},{... | collective-permute-start | bytes 73736 | tf_op jit(solution)/shard_map/ppermute | solution.py:20
  150.8 6.1 %collective-permute-start.12 = (f32[1,8,768]{2,1,0:T(8,128)S(1)}, f32[1,8,768]{2,1,0:T(8,128)S(1)}, u32[]{:S(2)}, u32[]{:S(2)}) collective-permute-start(f32[1,8,768]{2,1,0:T(8,128)S(1)} %get-tuple-element.32), channel_id=1, source_target_pairs={{0,8},{8,16},{16,24},{1,9},{9,17},{17,25},{2,10},{10,18},{18,26},{... | collective-permute-start | bytes 73736 | tf_op jit(solution)/shard_map/ppermute | solution.py:17
  166.9 21.3 %copy-start.35 = (u32[32]{0:T(128)S(1)}, u32[32]{0:T(128)}, u32[]{:S(2)}) copy-start(u32[32]{0:T(128)} %constant.44) | copy-start | bytes 388
  166.9 22.5 %copy-start.31 = (f32[8]{0:T(128)S(1)}, f32[8]{0:T(128)}, u32[]{:S(2)}) copy-start(f32[8]{0:T(128)} %get-tuple-element.10) | copy-start | bytes 100
  177.6 12.1 %copy-start.3 = (bf16[8,3072]{1,0:T(8,128)(2,1)}, bf16[8,3072]{1,0:T(8,128)(2,1)S(1)}, u32[]{:S(2)}) copy-start(bf16[8,3072]{1,0:T(8,128)(2,1)S(1)} %all_gather.41) | copy-start | bytes 147460
  177.7 12.0 %collective-permute-start.19 = (f32[1,8,768]{2,1,0:T(8,128)S(1)}, f32[1,8,768]{2,1,0:T(8,128)S(1)}, u32[]{:S(2)}, u32[]{:S(2)}) collective-permute-start(f32[1,8,768]{2,1,0:T(8,128)S(1)} %get-tuple-element.29), channel_id=1, source_target_pairs={{2,0},{4,2},{6,4},{3,1},{5,3},{7,5},{10,8},{12,10},{14,12},{11,9},... | collective-permute-start | bytes 73736 | tf_op jit(solution)/shard_map/ppermute | solution.py:20
  179.0 10.7 %collective-permute-start.18 = (f32[1,8,768]{2,1,0:T(8,128)S(1)}, f32[1,8,768]{2,1,0:T(8,128)S(1)}, u32[]{:S(2)}, u32[]{:S(2)}) collective-permute-start(f32[1,8,768]{2,1,0:T(8,128)S(1)} %get-tuple-element.30), channel_id=1, source_target_pairs={{0,2},{2,4},{4,6},{1,3},{3,5},{5,7},{8,10},{10,12},{12,14},{9,11},... | collective-permute-start | bytes 73736 | tf_op jit(solution)/shard_map/ppermute | solution.py:17
  182.0 7.7 %collective-permute-start.17 = (f32[1,8,768]{2,1,0:T(8,128)S(1)}, f32[1,8,768]{2,1,0:T(8,128)S(1)}, u32[]{:S(2)}, u32[]{:S(2)}) collective-permute-start(f32[1,8,768]{2,1,0:T(8,128)S(1)} %get-tuple-element.31), channel_id=1, source_target_pairs={{8,0},{16,8},{24,16},{9,1},{17,9},{25,17},{10,2},{18,10},{26,18},{... | collective-permute-start | bytes 73736 | tf_op jit(solution)/shard_map/ppermute | solution.py:20
  183.3 6.4 %collective-permute-start.16 = (f32[1,8,768]{2,1,0:T(8,128)S(1)}, f32[1,8,768]{2,1,0:T(8,128)S(1)}, u32[]{:S(2)}, u32[]{:S(2)}) collective-permute-start(f32[1,8,768]{2,1,0:T(8,128)S(1)} %get-tuple-element.28), channel_id=1, source_target_pairs={{0,8},{8,16},{16,24},{1,9},{9,17},{17,25},{2,10},{10,18},{18,26},{... | collective-permute-start | bytes 73736 | tf_op jit(solution)/shard_map/ppermute | solution.py:17
  190.7 8.6 %copy-start.25 = (f32[6]{0:T(128)S(1)}, f32[6]{0:T(128)}, u32[]{:S(2)}) copy-start(f32[6]{0:T(128)} %copy-done.22) | copy-start | bytes 76
  190.7 30.4 %copy-start.19 = (f32[1,1,6,96]{3,1,2,0:T(1,128)S(1)}, f32[1,1,6,96]{3,1,2,0:T(1,128)}, u32[]{:S(2)}) copy-start(f32[1,1,6,96]{3,1,2,0:T(1,128)} %param.15) | copy-start | bytes 6916
  198.8 33.4 %copy-start.37 = (f32[128]{0:T(128)S(1)}, f32[128]{0:T(128)}, u32[]{:S(2)}) copy-start(f32[128]{0:T(128)} %copy-done.36) | copy-start | bytes 1540
  199.6 63.9 %copy-start.1 = (f32[3072,8]{0,1:T(8,128)}, f32[3072,8]{0,1:T(8,128)S(1)}, u32[]{:S(2)}) copy-start(f32[3072,8]{0,1:T(8,128)S(1)} %copy.63) | copy-start | bytes 294916
  221.6 10.4 %copy-start.9 = (f32[8,3072]{1,0:T(8,128)}, f32[8,3072]{1,0:T(8,128)S(1)}, u32[]{:S(2)}) copy-start(f32[8,3072]{1,0:T(8,128)S(1)} %fusion.22) | copy-start | bytes 294916
  221.6 41.9 %collective-permute-start.23 = (f32[1,8,768]{2,1,0:T(8,128)S(1)}, f32[1,8,768]{2,1,0:T(8,128)S(1)}, u32[]{:S(2)}, u32[]{:S(2)}) collective-permute-start(f32[1,8,768]{2,1,0:T(8,128)S(1)} %get-tuple-element.25), channel_id=1, source_target_pairs={{2,0},{4,2},{6,4},{3,1},{5,3},{7,5},{10,8},{12,10},{14,12},{11,9},... | collective-permute-start | bytes 73736 | tf_op jit(solution)/shard_map/ppermute | solution.py:20
  222.9 40.6 %collective-permute-start.22 = (f32[1,8,768]{2,1,0:T(8,128)S(1)}, f32[1,8,768]{2,1,0:T(8,128)S(1)}, u32[]{:S(2)}, u32[]{:S(2)}) collective-permute-start(f32[1,8,768]{2,1,0:T(8,128)S(1)} %get-tuple-element.26), channel_id=1, source_target_pairs={{0,2},{2,4},{4,6},{1,3},{3,5},{5,7},{8,10},{10,12},{12,14},{9,11},... | collective-permute-start | bytes 73736 | tf_op jit(solution)/shard_map/ppermute | solution.py:17
  225.9 37.5 %collective-permute-start.21 = (f32[1,8,768]{2,1,0:T(8,128)S(1)}, f32[1,8,768]{2,1,0:T(8,128)S(1)}, u32[]{:S(2)}, u32[]{:S(2)}) collective-permute-start(f32[1,8,768]{2,1,0:T(8,128)S(1)} %get-tuple-element.27), channel_id=1, source_target_pairs={{8,0},{16,8},{24,16},{9,1},{17,9},{25,17},{10,2},{18,10},{26,18},{... | collective-permute-start | bytes 73736 | tf_op jit(solution)/shard_map/ppermute | solution.py:20
  227.2 36.2 %collective-permute-start.20 = (f32[1,8,768]{2,1,0:T(8,128)S(1)}, f32[1,8,768]{2,1,0:T(8,128)S(1)}, u32[]{:S(2)}, u32[]{:S(2)}) collective-permute-start(f32[1,8,768]{2,1,0:T(8,128)S(1)} %get-tuple-element.24), channel_id=1, source_target_pairs={{0,8},{8,16},{16,24},{1,9},{9,17},{17,25},{2,10},{10,18},{18,26},{... | collective-permute-start | bytes 73736 | tf_op jit(solution)/shard_map/ppermute | solution.py:17
  262.9 9.2 %copy-start.34 = (f32[8]{0:T(128)}, f32[8]{0:T(128)S(1)}, u32[]{:S(2)}) copy-start(f32[8]{0:T(128)S(1)} %reduce_sum.73) | copy-start | bytes 100
  272.1 1.0 copy-start.10
  272.1 20.3 %copy-start.20 = (f32[1,1,6,96]{3,1,2,0:T(1,128)S(1)}, f32[1,1,6,96]{3,1,2,0:T(1,128)}, u32[]{:S(2)}) copy-start(f32[1,1,6,96]{3,1,2,0:T(1,128)} %param.15) | copy-start | bytes 6916
  272.2 20.4 %copy-start.26 = (f32[6]{0:T(128)S(1)}, f32[6]{0:T(128)}, u32[]{:S(2)}) copy-start(f32[6]{0:T(128)} %copy-done.22) | copy-start | bytes 76
  293.0 42.2 %collective-permute-start.27 = (f32[1,8,768]{2,1,0:T(8,128)S(1)}, f32[1,8,768]{2,1,0:T(8,128)S(1)}, u32[]{:S(2)}, u32[]{:S(2)}) collective-permute-start(f32[1,8,768]{2,1,0:T(8,128)S(1)} %get-tuple-element.21), channel_id=1, source_target_pairs={{2,0},{4,2},{6,4},{3,1},{5,3},{7,5},{10,8},{12,10},{14,12},{11,9},... | collective-permute-start | bytes 73736 | tf_op jit(solution)/shard_map/ppermute | solution.py:20
  294.3 40.9 %collective-permute-start.26 = (f32[1,8,768]{2,1,0:T(8,128)S(1)}, f32[1,8,768]{2,1,0:T(8,128)S(1)}, u32[]{:S(2)}, u32[]{:S(2)}) collective-permute-start(f32[1,8,768]{2,1,0:T(8,128)S(1)} %get-tuple-element.22), channel_id=1, source_target_pairs={{0,2},{2,4},{4,6},{1,3},{3,5},{5,7},{8,10},{10,12},{12,14},{9,11},... | collective-permute-start | bytes 73736 | tf_op jit(solution)/shard_map/ppermute | solution.py:17
  297.3 37.9 %collective-permute-start.25 = (f32[1,8,768]{2,1,0:T(8,128)S(1)}, f32[1,8,768]{2,1,0:T(8,128)S(1)}, u32[]{:S(2)}, u32[]{:S(2)}) collective-permute-start(f32[1,8,768]{2,1,0:T(8,128)S(1)} %get-tuple-element.23), channel_id=1, source_target_pairs={{8,0},{16,8},{24,16},{9,1},{17,9},{25,17},{10,2},{18,10},{26,18},{... | collective-permute-start | bytes 73736 | tf_op jit(solution)/shard_map/ppermute | solution.py:20
  298.6 36.6 %collective-permute-start.24 = (f32[1,8,768]{2,1,0:T(8,128)S(1)}, f32[1,8,768]{2,1,0:T(8,128)S(1)}, u32[]{:S(2)}, u32[]{:S(2)}) collective-permute-start(f32[1,8,768]{2,1,0:T(8,128)S(1)} %get-tuple-element.20), channel_id=1, source_target_pairs={{0,8},{8,16},{16,24},{1,9},{9,17},{17,25},{2,10},{10,18},{18,26},{... | collective-permute-start | bytes 73736 | tf_op jit(solution)/shard_map/ppermute | solution.py:17
  334.0 1.6 copy-start.32
  352.9 16.9 %copy-start.14 = (s32[3072]{0:T(1024)S(1)}, s32[3072]{0:T(1024)}, u32[]{:S(2)}) copy-start(s32[3072]{0:T(1024)} %copy-done.13) | copy-start | bytes 36868
  357.6 10.2 %collective-permute-start.31 = (f32[1,8,768]{2,1,0:T(8,128)S(1)}, f32[1,8,768]{2,1,0:T(8,128)S(1)}, u32[]{:S(2)}, u32[]{:S(2)}) collective-permute-start(f32[1,8,768]{2,1,0:T(8,128)S(1)} %get-tuple-element.17), channel_id=1, source_target_pairs={{2,0},{4,2},{6,4},{3,1},{5,3},{7,5},{10,8},{12,10},{14,12},{11,9},... | collective-permute-start | bytes 73736 | tf_op jit(solution)/shard_map/ppermute | solution.py:20
  358.9 8.9 %collective-permute-start.30 = (f32[1,8,768]{2,1,0:T(8,128)S(1)}, f32[1,8,768]{2,1,0:T(8,128)S(1)}, u32[]{:S(2)}, u32[]{:S(2)}) collective-permute-start(f32[1,8,768]{2,1,0:T(8,128)S(1)} %get-tuple-element.18), channel_id=1, source_target_pairs={{0,2},{2,4},{4,6},{1,3},{3,5},{5,7},{8,10},{10,12},{12,14},{9,11},... | collective-permute-start | bytes 73736 | tf_op jit(solution)/shard_map/ppermute | solution.py:17
  361.9 5.9 %collective-permute-start.29 = (f32[1,8,768]{2,1,0:T(8,128)S(1)}, f32[1,8,768]{2,1,0:T(8,128)S(1)}, u32[]{:S(2)}, u32[]{:S(2)}) collective-permute-start(f32[1,8,768]{2,1,0:T(8,128)S(1)} %get-tuple-element.19), channel_id=1, source_target_pairs={{8,0},{16,8},{24,16},{9,1},{17,9},{25,17},{10,2},{18,10},{26,18},{... | collective-permute-start | bytes 73736 | tf_op jit(solution)/shard_map/ppermute | solution.py:20
  363.2 6.1 %collective-permute-start.28 = (f32[1,8,768]{2,1,0:T(8,128)S(1)}, f32[1,8,768]{2,1,0:T(8,128)S(1)}, u32[]{:S(2)}, u32[]{:S(2)}) collective-permute-start(f32[1,8,768]{2,1,0:T(8,128)S(1)} %get-tuple-element.16), channel_id=1, source_target_pairs={{0,8},{8,16},{16,24},{1,9},{9,17},{17,25},{2,10},{10,18},{18,26},{... | collective-permute-start | bytes 73736 | tf_op jit(solution)/shard_map/ppermute | solution.py:17
  369.8 38.6 %copy-start.33 = (f32[8]{0:T(128)S(1)}, f32[8]{0:T(128)}, u32[]{:S(2)}) copy-start(f32[8]{0:T(128)} %copy-done.32) | copy-start | bytes 100
  369.8 38.6 %copy-start.30 = (f32[8]{0:T(128)S(1)}, f32[8]{0:T(128)}, u32[]{:S(2)}) copy-start(f32[8]{0:T(128)} %div.26) | copy-start | bytes 100
  378.0 30.5 %copy-start.12 = (f32[9,3072]{1,0:T(8,128)S(1)}, f32[9,3072]{1,0:T(8,128)}, u32[]{:S(2)}) copy-start(f32[9,3072]{1,0:T(8,128)} %copy-done.11) | copy-start | bytes 331780
  (6 other events, 4.7 us)
where the time goes:
time: 411 us; the launch traced here: 409 us
  blocking collectives  205 us (50%)
  starting transfers between devices  81.6 us (20%)
  local copies, waits for them, and re-layouts  80.1 us (19%)
  matrix products  25.6 us (6%)
  other arithmetic  10 us (2%)
  waiting for transfers between devices  4.35 us (1%)
    all_gather x5, blocking collectives, coarse_step(): lax.all_gather(local_coarse[None], ('gx', 'gy'), axis=0, tiled=True)  101 us
    unnamed x3, blocking collectives  90.5 us
    gather x16, local copies, waits for them, and re-layouts, partner(): return jnp.take(facing, flat_slots, axis=1)  69.9 us
    ppermute x16, starting transfers between devices, with_halo(): lax.ppermute(lax.slice_in_dim(block, block.shape[dim] - width, None, axis...  60.9 us
    ppermute x16, starting transfers between devices, with_halo(): lax.ppermute(lax.slice_in_dim(block, 0, width, axis=dim), axis, backward)  20.7 us
    dot_general x3, matrix products, product_rows(): jnp.einsum('lj,ij->li', vectors.astype(jnp.bfloat16), local_rows, preferr...  18.7 us
    all_gather x3, blocking collectives, assembled_product(): lax.all_gather(own_rows, 'gz', axis=1, tiled=True).astype(jnp.float32)  13.9 us
  transfers between devices with their start and end apart: 32, of which 4 were waited for; matrix products, arithmetic and copies ran while one was open for 2% of the time, Pallas kernels for 0%

commit v1 on v0

v1 whole, which is shorter than its diff:
```python
import functools

import jax
import jax.numpy as jnp
from jax import lax
from jax.experimental import pallas as pl
from jax.experimental.pallas import tpu as pltpu
from jax.sharding import PartitionSpec as P

ROW_CHUNK = 256
IN_FLIGHT = 2
TILE = 128
SLOT = 8
MODE_SPAN = 5 * SLOT
SCALARS = 3 * MODE_SPAN
MIB = 1024 * 1024


class Sizes:
    def __init__(self, mesh_shape, operator, traces, loads):
        self.sx, self.sy, self.gz = mesh_shape
        self.rows = operator.shape[2]
        self.order = operator.shape[3]
        self.modes = traces.shape[2]
        self.cap = self.order // 4
        self.loads = loads
        self.subs = self.sx * self.sy
        self.devices = self.subs * self.gz
        self.coarse = self.subs * SLOT
        self.coarse_pad = -(-self.coarse // TILE) * TILE
        self.own_faces = self.rows // self.cap
        assert self.rows % self.cap == 0 and self.cap % TILE == 0
        assert self.modes <= SLOT - 2 and self.loads == 8


def f32(*shape):
    return jax.ShapeDtypeStruct(shape, jnp.float32)


def lanes(shape=(8, TILE)):
    return lax.broadcasted_iota(jnp.int32, shape, 1)


def exact_dot(a, b):
    return jnp.dot(a, b, precision=lax.Precision.HIGHEST, preferred_element_type=jnp.float32)


def clamp(index, count):
    return jnp.minimum(jnp.maximum(index, 0), count - 1)


def neighbour(sz, face):
    gx, gy = lax.axis_index("gx"), lax.axis_index("gy")
    x = gx + jnp.where(face == 0, -1, jnp.where(face == 1, 1, 0))
    y = gy + jnp.where(face == 2, -1, jnp.where(face == 3, 1, 0))
    return clamp(x, sz.sx) * sz.sy + clamp(y, sz.sy)


def grid_neighbour(sz, sub, face):
    x, y = divmod(sub, sz.sy)
    x, y = [(x - 1, y), (x + 1, y), (x, y - 1), (x, y + 1)][face]
    return x * sz.sy + y if 0 <= x < sz.sx and 0 <= y < sz.sy else None


def face_pairs(sz, local):
    pairs = []
    for sub in range(sz.subs):
        for part in range(sz.gz):
            face = part * sz.own_faces + local
            other = grid_neighbour(sz, sub, face)
            if other is not None:
                pairs.append((sub * sz.gz + part, other * sz.gz + (face ^ 1) // sz.own_faces))
    return pairs


def own_face(sz, j):
    return slice(j * sz.cap, (j + 1) * sz.cap)


def facing(sz, j):
    return j ^ 1 if sz.own_faces > 1 else j


def permuted(sz, block, slots):
    count = sz.cap // TILE
    pieces = [block[:, k * TILE : (k + 1) * TILE] for k in range(count)]
    result = []
    for j in range(count):
        index = slots[:, j * TILE : (j + 1) * TILE].astype(jnp.int32)
        low = index & (TILE - 1)
        high = index >> (TILE.bit_length() - 1)
        total = jnp.zeros((8, TILE), jnp.float32)
        for k in range(count):
            picked = jnp.take_along_axis(pieces[k], low, axis=1, mode="promise_in_bounds")
            total = jnp.where(high == k, picked, total)
        result.append(total)
    return jnp.concatenate(result, axis=1)


def coefficients(sz, coarse_ref):
    gz = lax.axis_index("gz")
    subs = [lax.axis_index("gx") * sz.sy + lax.axis_index("gy")]
    subs += [neighbour(sz, gz * sz.own_faces + j) for j in range(sz.own_faces)]
    result = []
    for sub in subs:
        start = sub * SLOT
        base = pl.multiple_of((start // TILE) * TILE, TILE)
        tile = coarse_ref[:, pl.ds(base, TILE)]
        shift = lax.rem(TILE - lax.rem(start, TILE), TILE)
        result.append(pltpu.roll(tile, shift, 1))
    return result


def mode_sum(sz, coeffs, modes_ref, j):
    total = None
    for tile, base in ((coeffs[0], 0), (coeffs[1 + j], SLOT)):
        for m in range(sz.modes):
            term = tile[:, m : m + 1] * modes_ref[base + m : base + m + 1, own_face(sz, j)]
            total = term if total is None else total + term
    return total


def mode_products(sz, tile, blocks, modes_ref, first_lane):
    lane = lanes()
    gz = lax.axis_index("gz")
    for m in range(sz.modes):
        total = None
        for j, block in enumerate(blocks):
            term = jnp.sum(block * modes_ref[m : m + 1, own_face(sz, j)], axis=1, keepdims=True)
            total = term if total is None else total + term
        tile = jnp.where(lane == first_lane + m, total, tile)
    for j, block in enumerate(blocks):
        face_lane = first_lane + SLOT * (1 + gz * sz.own_faces + j)
        for m in range(sz.modes):
            row = modes_ref[SLOT + m : SLOT + m + 1, own_face(sz, j)]
            total = jnp.sum(block * row, axis=1, keepdims=True)
            tile = jnp.where(lane == face_lane + m, total, tile)
    return tile


def weights_of(sz, modes_ref):
    return [modes_ref[6:7, own_face(sz, j)] for j in range(sz.own_faces)]


def sub_tile(sz, tiles, sub):
    total = tiles[sub * sz.gz]
    for part in range(1, sz.gz):
        total = total + tiles[sub * sz.gz + part]
    return total


def gathered_coarse(sz, tiles, held_ref, group):
    lane = lanes()
    held_ref[...] = jnp.zeros((8, sz.coarse_pad), jnp.float32)
    for sub in range(sz.subs):
        total = tiles[sub]
        for face in range(4):
            other = grid_neighbour(sz, sub, face)
            if other is not None:
                total = total + pltpu.roll(tiles[other], TILE - SLOT * (1 + (face ^ 1)), 1)
        start = sub * SLOT
        base, offset = start // TILE * TILE, start % TILE
        moved = pltpu.roll(total, (offset - group * MODE_SPAN) % TILE, 1)
        moved = jnp.where((lane >= offset) & (lane < offset + sz.modes), moved, 0.0)
        held_ref[:, base : base + TILE] += moved


def fill_coupling(sz, tiles, coupling_ref):
    lane = lanes()
    coupling_ref[...] = jnp.zeros((sz.coarse_pad, sz.coarse_pad), jnp.float32)
    for sub in range(sz.subs):
        for k in range(5):
            other = sub if k == 0 else grid_neighbour(sz, sub, k - 1)
            if other is None:
                continue
            base, offset = other * SLOT // TILE * TILE, other * SLOT % TILE
            moved = pltpu.roll(tiles[sub], (offset - 2 * MODE_SPAN - SLOT * k) % TILE, 1)
            moved = jnp.where((lane >= offset) & (lane < offset + sz.modes), moved, 0.0)
            coupling_ref[sub * SLOT : (sub + 1) * SLOT, base : base + TILE] += moved


def fill_inverse(sz, shared, inverse_ref):
    if sz.coarse_pad > sz.coarse:
        inverse_ref[sz.coarse :, :] = jnp.zeros((sz.coarse_pad - sz.coarse, sz.coarse_pad), jnp.float32)
    for sub in range(sz.subs):
        inverse_ref[sub * SLOT : (sub + 1) * SLOT, :] = shared[sub, :, 0 : sz.coarse_pad]


def solve_pair(sz, tiles, inverse_ref, coupling_ref, coarse_a, coarse_b):
    gathered_coarse(sz, tiles, coarse_a, 0)
    gathered_coarse(sz, tiles, coarse_b, 1)
    first = exact_dot(coarse_a[...], inverse_ref[...])
    coarse_a[...] = first
    coarse_b[...] = exact_dot(coarse_b[...] - exact_dot(first, coupling_ref[...]), inverse_ref[...])
    return coefficients(sz, coarse_a), coefficients(sz, coarse_b)


def spread(out, tile):
    out[...] = jnp.broadcast_to(tile[None], out.shape)


def part_slots(sz, part):
    return pl.ds(pl.multiple_of(part * sz.rows, TILE), sz.rows)


def put_parts(sz, parts, vector):
    if len(parts) == 1:
        for z in range(sz.gz):
            vector[:, z * sz.rows : (z + 1) * sz.rows] = parts[0][z].astype(vector.dtype)
    else:
        gz = lax.axis_index("gz")
        vector[:, part_slots(sz, gz)] = parts[0][...].astype(vector.dtype)
        vector[:, part_slots(sz, 1 - gz)] = parts[1][...].astype(vector.dtype)


def start_kernel(sz, traces, loads, inverse, stiffness, orders, rhs, lengths, count, *refs):
    outs, scratch = refs[: sz.own_faces + 2], refs[sz.own_faces + 2 :]
    faces, (pay, base) = outs[: sz.own_faces], outs[sz.own_faces :]
    traces_in, loads_in, inverse_in, stiffness_in, slots, lengths_in, count_in, sems = scratch
    gz = lax.axis_index("gz")
    here = pl.ds(pl.multiple_of(gz * sz.rows, TILE), sz.rows)
    copies = [
        pltpu.make_async_copy(inverse, inverse_in, sems.at[0]),
        pltpu.make_async_copy(loads, loads_in, sems.at[1]),
        pltpu.make_async_copy(traces.at[:, :, here], traces_in, sems.at[2]),
        pltpu.make_async_copy(stiffness.at[0, :, here], stiffness_in, sems.at[3]),
        pltpu.make_async_copy(orders.at[0, 0], slots, sems.at[4]),
        pltpu.make_async_copy(rhs.at[0, 0, :, here], base.at[pl.ds(8, 8), :], sems.at[5]),
        pltpu.make_async_copy(lengths, lengths_in, sems.at[6]),
        pltpu.make_async_copy(count, count_in, sems.at[7]),
    ]
    for copy in copies:
        copy.start()
    pay[...] = jnp.zeros(pay.shape, jnp.float32)
    for face in faces:
        face[sz.modes :, :] = jnp.zeros((8 - sz.modes, sz.cap), jnp.float32)
    for copy in copies:
        copy.wait()
    for m in range(sz.modes):
        mask = (m < count_in[0, 0]).astype(jnp.float32)
        for t in range(sz.subs):
            pay[0, m : m + 1, t * SLOT : t * SLOT + sz.modes] = inverse_in[
                m, :, t * sz.modes : (t + 1) * sz.modes
            ]
        pay[0, m : m + 1, sz.coarse_pad : sz.coarse_pad + sz.loads] = loads_in[m] * mask
        for j, face in enumerate(faces):
            face[m : m + 1, :] = traces_in[m, :, own_face(sz, j)] * mask
    position = lax.broadcasted_iota(jnp.int32, (1, sz.cap), 1)
    for j, face in enumerate(faces):
        face[6:7, :] = stiffness_in[:, own_face(sz, j)]
        index = gz * sz.own_faces + j
        face[7:8, :] = (position < lengths_in[0, 0, index]).astype(jnp.float32)
        base[0:8, own_face(sz, j)] = face[...]
        chosen = jnp.broadcast_to(slots[pl.ds(index, 1), :], (8, sz.cap))
        base[16:24, own_face(sz, j)] = chosen.astype(jnp.float32)
    chunk = pay[0]
    for k in range(1, pay.shape[0]):
        pay[k] = chunk


def first_kernel(sz, shared, base, *refs):
    arrived, refs = refs[: sz.own_faces], refs[sz.own_faces :]
    estimate_ref, modes_ref, inverse_ref, loads_ref, coarse_ref = refs
    fill_inverse(sz, shared, inverse_ref)
    if sz.coarse_pad > sz.coarse:
        loads_ref[sz.coarse :, :] = jnp.zeros((sz.coarse_pad - sz.coarse, TILE), jnp.float32)
    for sub in range(sz.subs):
        loads_ref[sub * SLOT : (sub + 1) * SLOT, :] = shared[sub, :, sz.coarse_pad :]
    turned = jnp.concatenate(
        [
            jnp.transpose(loads_ref[k * TILE : (k + 1) * TILE, :])[0:8, :]
            for k in range(sz.coarse_pad // TILE)
        ],
        axis=1,
    )
    coarse_ref[...] = exact_dot(turned, inverse_ref[...])
    row = lax.broadcasted_iota(jnp.int32, (8, 1), 0)
    for j in range(sz.own_faces):
        here = own_face(sz, j)
        other = permuted(sz, arrived[facing(sz, j)][...], base[16:24, here])
        mine = base[0:8, here]
        live = mine[7:8, :]
        total = live * (mine[6:7, :] + other[6:7, :])
        weight = live / (total + 1.0 - live)
        modes_ref[0:8, here] = jnp.where(row == 6, weight, jnp.where(row == 7, live, mine * live))
        modes_ref[8:16, here] = jnp.where(row < sz.modes, other * live, 0.0)
    coeffs = coefficients(sz, coarse_ref)
    for j in range(sz.own_faces):
        estimate_ref[:, own_face(sz, j)] = mode_sum(sz, coeffs, modes_ref, j)


def apply_rows(sz, vector, held, outs, arrive=None):
    for k in range(sz.rows // ROW_CHUNK):
        if arrive is not None:
            arrive(k)
        part = lax.dot_general(
            vector[...], held[k], (((1,), (1,)), ((), ())), preferred_element_type=jnp.float32
        )
        j, start = divmod(k * ROW_CHUNK, sz.cap)
        outs[j][:, start : start + ROW_CHUNK] = part.astype(jnp.bfloat16).astype(jnp.float32)


def first_apply_kernel(sz, operator, modes_ref, base, *refs):
    parts, refs = refs[: -sz.own_faces - 4], refs[-sz.own_faces - 4 :]
    outs, (pay, held, vector, sems) = refs[: sz.own_faces], refs[sz.own_faces :]
    copies = [
        pltpu.make_async_copy(
            operator.at[0, 0, pl.ds(k * ROW_CHUNK, ROW_CHUNK), :], held.at[k], sems.at[k]
        )
        for k in range(sz.rows // ROW_CHUNK)
    ]
    for copy in copies[:IN_FLIGHT]:
        copy.start()

    def arrive(k):
        copies[k].wait()
        if k + IN_FLIGHT < len(copies):
            copies[k + IN_FLIGHT].start()

    put_parts(sz, parts, vector)
    weights = weights_of(sz, modes_ref)
    row = lax.broadcasted_iota(jnp.int32, (8, 1), 0)
    coarse_rows = [
        jnp.where(row < sz.modes, modes_ref[0:8, own_face(sz, j)] * weights[j], 0.0)
        for j in range(sz.own_faces)
    ]
    tile = jnp.zeros((8, TILE), jnp.float32)
    tile = mode_products(sz, tile, coarse_rows, modes_ref, 2 * MODE_SPAN)
    apply_rows(sz, vector, held, outs, arrive)
    vectors = []
    for j, out in enumerate(outs):
        vectors.append(base[8:16, own_face(sz, j)] - out[...])
        out[...] = vectors[-1]
    tile = mode_products(sz, tile, vectors, modes_ref, 0)
    scaled = [v * w for v, w in zip(vectors, weights)]
    spread(pay, mode_products(sz, tile, scaled, modes_ref, MODE_SPAN))


def assembled(sz, own, arrived, base, modes_ref, j):
    other = permuted(sz, arrived[facing(sz, j)][...], base[16:24, own_face(sz, j)])
    return modes_ref[7:8, own_face(sz, j)] * (own[j][...] + other)


def second_kernel(sz, pieces, shared, base, modes_ref, *refs):
    own, refs = refs[: sz.own_faces], refs[sz.own_faces :]
    arrived, refs = refs[: sz.own_faces], refs[sz.own_faces :]
    residual_ref, direction_ref, inverse_ref, coupling_ref, coarse_a, coarse_b = refs
    fill_inverse(sz, shared, inverse_ref)
    tiles = [sub_tile(sz, pieces, sub) for sub in range(sz.subs)]
    fill_coupling(sz, tiles, coupling_ref)
    first, second = solve_pair(sz, tiles, inverse_ref, coupling_ref, coarse_a, coarse_b)
    for j in range(sz.own_faces):
        here = own_face(sz, j)
        gap = assembled(sz, own, arrived, base, modes_ref, j)
        residual = gap - mode_sum(sz, first, modes_ref, j)
        residual_ref[:, here] = residual
        direction_ref[:, here] = modes_ref[6:7, here] * residual - mode_sum(sz, second, modes_ref, j)


def second_apply_kernel(sz, held, modes_ref, direction, residual, *refs):
    parts, refs = refs[: -sz.own_faces - 2], refs[-sz.own_faces - 2 :]
    outs, (pay, vector) = refs[: sz.own_faces], refs[sz.own_faces :]
    put_parts(sz, parts, vector)
    weights = weights_of(sz, modes_ref)
    lane = lanes()
    curvature = jnp.zeros((8, 1), jnp.float32)
    resid_dot = jnp.zeros((8, 1), jnp.float32)
    for j in range(sz.own_faces):
        own = residual[:, own_face(sz, j)]
        resid_dot += jnp.sum(own * (weights[j] * own), axis=1, keepdims=True)
    apply_rows(sz, vector, held, outs)
    pieces = [out[...] for out in outs]
    for j, piece in enumerate(pieces):
        curvature += jnp.sum(direction[:, own_face(sz, j)] * piece, axis=1, keepdims=True)
    tile = jnp.where(lane == SCALARS, curvature, jnp.zeros((8, TILE), jnp.float32))
    tile = jnp.where(lane == SCALARS + 1, resid_dot, tile)
    tile = mode_products(sz, tile, pieces, modes_ref, 0)
    scaled = [v * w for v, w in zip(pieces, weights)]
    spread(pay, mode_products(sz, tile, scaled, modes_ref, MODE_SPAN))


def third_kernel(sz, pieces, shared, before, base, modes_ref, residual_ref, direction_ref, *refs):
    own, refs = refs[: sz.own_faces], refs[sz.own_faces :]
    arrived, refs = refs[: sz.own_faces], refs[sz.own_faces :]
    later_ref, scalars_ref, inverse_ref, coupling_ref, coarse_a, coarse_b = refs
    lane = lanes()
    fill_inverse(sz, shared, inverse_ref)
    fill_coupling(sz, [sub_tile(sz, before, sub) for sub in range(sz.subs)], coupling_ref)
    tiles = [sub_tile(sz, pieces, sub) for sub in range(sz.subs)]
    totals = tiles[0]
    for tile in tiles[1:]:
        totals = totals + tile
    curvature = 2.0 * totals[:, SCALARS : SCALARS + 1]
    resid_dot = totals[:, SCALARS + 1 : SCALARS + 2]
    step = resid_dot / curvature
    first, second = solve_pair(sz, tiles, inverse_ref, coupling_ref, coarse_a, coarse_b)
    dot_part = jnp.zeros((8, 1), jnp.float32)
    for j in range(sz.own_faces):
        here = own_face(sz, j)
        image = assembled(sz, own, arrived, base, modes_ref, j)
        corrected = image - mode_sum(sz, first, modes_ref, j)
        weight = modes_ref[6:7, here]
        scaled = weight * corrected - mode_sum(sz, second, modes_ref, j)
        residual = residual_ref[:, here] - step * corrected
        dot_part += jnp.sum(residual * (weight * residual), axis=1, keepdims=True)
        later_ref[:, here] = direction_ref[:, here] - step * scaled
    scalars_ref[...] = jnp.where(lane == 0, curvature, jnp.where(lane == 1, resid_dot, dot_part))


def third_apply_kernel(sz, held, later, direction, scalars, *refs):
    before, refs = refs[: sz.own_faces], refs[sz.own_faces :]
    parts, refs = refs[: -sz.own_faces - 2], refs[-sz.own_faces - 2 :]
    pay, vector, outs = *refs[:2], refs[2:]
    put_parts(sz, parts, vector)
    apply_rows(sz, vector, held, outs)
    lane = lanes()
    later_part = jnp.zeros((8, 1), jnp.float32)
    cross_part = jnp.zeros((8, 1), jnp.float32)
    for j, out in enumerate(outs):
        piece = out[...]
        mine = later[:, own_face(sz, j)]
        earlier = direction[:, own_face(sz, j)]
        later_part += jnp.sum(mine * piece, axis=1, keepdims=True)
        cross_part += jnp.sum(mine * before[j][...] + earlier * piece, axis=1, keepdims=True)
    load = lax.broadcasted_iota(jnp.int32, (8, TILE), 0)
    line = jnp.where(lane == load, later_part, 0.0)
    line = jnp.where(lane == load + 8, cross_part, line)
    line = jnp.where(lane == load + 16, scalars[:, 2:3], line)
    spread(pay, jnp.sum(line, axis=0, keepdims=True))


def last_kernel(sz, pieces, scalars, *refs):
    out = refs[-1]
    count = (len(refs) - 1) // 3
    estimate, direction, later = refs[:count], refs[count : 2 * count], refs[2 * count : 3 * count]
    totals = pieces[0]
    for k in range(1, pieces.shape[0]):
        totals = totals + pieces[k]
    curvature, previous = scalars[:, 0:1], scalars[:, 1:2]
    load = lax.broadcasted_iota(jnp.int32, (8, TILE), 0)
    later_part, cross_part, dot = [
        jnp.sum(jnp.where(lanes() == load + 8 * k, totals, 0.0), axis=1, keepdims=True)
        for k in range(3)
    ]
    ratio = dot / previous
    final = 2.0 * (later_part + ratio * cross_part) + ratio * ratio * curvature
    first, second = previous / curvature, dot / final
    gz = lax.axis_index("gz")
    for z in range(sz.gz):
        if count == 1:
            here, parts = part_slots(sz, z), [x[0][z] for x in (estimate, direction, later)]
        else:
            here = part_slots(sz, 1 - gz if z else gz)
            parts = [x[z][...] for x in (estimate, direction, later)]
        moved = parts[0] + first * parts[1]
        out[0, 0, :, here] = moved + second * (parts[2] + ratio * parts[1])


def shards(mesh_shape, operator, rhs_parts, stiffness, traces, coarse_inverse, rigid_loads,
           face_lengths, face_order, mode_count):
    sz = Sizes(mesh_shape, operator, traces, rhs_parts.shape[2])
    vmem = pl.BlockSpec(memory_space=pltpu.VMEM)
    smem = pl.BlockSpec(memory_space=pltpu.SMEM)
    hbm = pl.BlockSpec(memory_space=pltpu.HBM)
    everywhere = ("gx", "gy", "gz")
    small = sz.coarse_pad <= 256

    def call(kernel, out_shape, in_specs, scratch, *operands, limit=None):
        return pl.pallas_call(
            functools.partial(kernel, sz),
            out_shape=out_shape,
            in_specs=in_specs,
            out_specs=jax.tree.map(lambda _: vmem, out_shape),
            scratch_shapes=scratch,
            compiler_params=pltpu.CompilerParams(
                vmem_limit_bytes=(limit or (16 if small else 56)) * MIB
            ),
        )(*operands)

    faces = sz.own_faces
    chunks = sz.rows // ROW_CHUNK
    coarse = pltpu.VMEM((8, sz.coarse_pad), jnp.float32)
    square = pltpu.VMEM((sz.coarse_pad, sz.coarse_pad), jnp.float32)
    half = f32(8, sz.rows)
    face = f32(8, sz.cap)
    one_step = sz.devices <= 64
    spread_tile = f32(sz.devices if one_step else 1, 8, TILE)
    vector = pltpu.VMEM((8, sz.order), jnp.bfloat16)

    def swap(own):
        return [lax.ppermute(own[j], everywhere, face_pairs(sz, j)) for j in range(faces)]

    def share(chunk, axes):
        if chunk.shape[0] == 1:
            return lax.all_gather(chunk, axes, axis=0, tiled=True)
        return lax.all_to_all(chunk, axes, split_axis=0, concat_axis=0, tiled=True)

    def whole(part):
        if sz.gz == 2:
            return [part, lax.ppermute(part, "gz", [(0, 1), (1, 0)])]
        return [lax.all_gather(part, "gz", axis=0, tiled=False)]

    *own, pay, base = call(
        start_kernel,
        [face] * faces + [
            f32(sz.subs if one_step else 1, 8, sz.coarse_pad + TILE),
            f32(24, sz.rows),
        ],
        [hbm] * 8,
        [
            pltpu.VMEM((sz.modes, 1, sz.rows), jnp.float32),
            pltpu.VMEM((sz.modes, 1, sz.loads), jnp.float32),
            pltpu.VMEM((sz.modes, 1, sz.subs * sz.modes), jnp.float32),
            pltpu.VMEM((1, sz.rows), jnp.float32),
            pltpu.VMEM((4, sz.cap), jnp.int32),
            pltpu.SMEM((1, 1, 4), jnp.int32),
            pltpu.SMEM((1, 1), jnp.int32),
            pltpu.SemaphoreType.DMA((8,)),
        ],
        traces.reshape(sz.modes, 1, sz.order), rigid_loads.reshape(sz.modes, 1, sz.loads),
        coarse_inverse.reshape(sz.modes, 1, -1), stiffness, face_order, rhs_parts,
        face_lengths, mode_count, limit=60,
    )
    arrived = swap(own)
    shared = share(pay, ("gx", "gy"))
    estimate, modes = call(
        first_kernel, [half, f32(16, sz.rows)], [vmem] * (2 + faces),
        [square, pltpu.VMEM((sz.coarse_pad, TILE), jnp.float32), coarse],
        shared, base, *arrived,
    )
    estimates = whole(estimate)
    *own, pay, held = call(
        first_apply_kernel,
        [face] * faces + [
            spread_tile,
            jax.ShapeDtypeStruct((chunks, ROW_CHUNK, sz.order), jnp.bfloat16),
        ],
        [hbm] + [vmem] * (2 + len(estimates)),
        [vector, pltpu.SemaphoreType.DMA((chunks,))],
        operator, modes, base, *estimates, limit=42,
    )
    arrived = swap(own)
    before = share(pay, everywhere)
    residual, direction = call(
        second_kernel, [half, half], [vmem] * (4 + 2 * faces), [square, square, coarse, coarse],
        before, shared, base, modes, *own, *arrived,
    )
    directions = whole(direction)
    *own, pay = call(
        second_apply_kernel, [face] * faces + [spread_tile], [vmem] * (4 + len(directions)),
        [vector], held, modes, direction, residual, *directions,
    )
    arrived = swap(own)
    pieces = share(pay, everywhere)
    later, scalars = call(
        third_kernel, [half, f32(8, TILE)], [vmem] * (7 + 2 * faces),
        [square, square, coarse, coarse],
        pieces, shared, before, base, modes, residual, direction, *own, *arrived,
    )
    laters = whole(later)
    pay = call(
        third_apply_kernel, f32(sz.devices if one_step else 1, 1, TILE),
        [vmem] * (4 + faces + len(laters)),
        [vector] + [pltpu.VMEM((8, sz.cap), jnp.float32)] * faces,
        held, later, direction, scalars, *own, *laters,
    )
    return call(
        last_kernel, f32(1, 1, 8, sz.order), [vmem] * (2 + 3 * len(laters)), [],
        share(pay, everywhere), scalars, *estimates, *directions, *laters,
    )


def solution(mesh):
    in_specs = (
        P("gx", "gy", "gz", None),
        P("gx", "gy", None, None),
        P("gx", "gy", None),
        P("gx", "gy", None, None),
        P("gx", "gy", None, None),
        P("gx", "gy", None, None),
        P("gx", "gy", None),
        P("gx", "gy", None, None),
        P("gx", "gy"),
    )
    out_specs = P("gx", "gy", None, None)
    mesh_shape = tuple(mesh.shape[axis] for axis in ("gx", "gy", "gz"))
    return jax.shard_map(
        functools.partial(shards, mesh_shape),
        mesh=mesh, in_specs=in_specs, out_specs=out_specs, check_vma=False,
    )
```

time: 411 us -> 100 us (0.24)
  blocking collectives: 205 us -> 11.6 us
  local copies, waits for them, and re-layouts: 80.1 us -> 12.9 us
  starting transfers between devices: 81.6 us -> 37.5 us
  matrix products: 25.6 us -> 0 us
  Pallas kernels: 0 us -> 18.9 us
  waiting for transfers between devices: 4.35 us -> 17.7 us
  other arithmetic: 10 us -> 0 us
    all_gather x8 -> x0, blocking collectives: 115 us -> none  [the longest x5 101 us: coarse_step(): lax.all_gather(local_coarse[None], ('gx', 'gy'), axis=0, tiled=True)]
    unnamed x3 -> x0, blocking collectives: 90.5 us -> none
    gather x16 -> x0, local copies, waits for them, and re-layouts: 69.9 us -> none  [partner(): return jnp.take(facing, flat_slots, axis=1)]
    ppermute x32 -> x9, starting transfers between devices: 81.6 us -> 19.9 us  [the longest x6 17.5 us: swap(): lax.ppermute(own[j], everywhere, face_pairs(sz, j))]
    dot_general x17 -> x0, matrix products: 25.6 us -> none  [the longest x3 18.7 us: product_rows(): jnp.einsum('lj,ij->li', vectors.astype(jnp.bfloat16), local_rows, preferr...]
    pallas_call x0 -> x8, Pallas kernels: none -> 18.9 us  [call(): pl.pallas_call(functools.partial(kernel, sz), out_shape=out_shape, in_spe...]
    all_to_all x0 -> x3, starting transfers between devices: none -> 17.6 us  [share(): return lax.all_to_all(chunk, axes, split_axis=0, concat_axis=0, tiled=True)]
    all_to_all x0 -> x1, blocking collectives: none -> 11.6 us  [share(): return lax.all_to_all(chunk, axes, split_axis=0, concat_axis=0, tiled=True)]
  transfers between devices with their start and end apart: 32 -> 12, of which waited for: 4 -> 12; matrix products, arithmetic and copies ran while one was open for 2% -> 0% of each run, Pallas kernels for 0% -> 0%
where the time goes in v1:
time: 100 us; the launch traced here: 99.4 us
  starting transfers between devices  37.5 us (38%)
  Pallas kernels  18.9 us (19%)
  waiting for transfers between devices  17.7 us (18%)
  local copies, waits for them, and re-layouts  12.9 us (13%)
  blocking collectives  11.6 us (12%)
    pallas_call x8, Pallas kernels, call(): pl.pallas_call(functools.partial(kernel, sz), out_shape=out_shape, in_spe...  18.9 us
    all_to_all x3, starting transfers between devices, share(): return lax.all_to_all(chunk, axes, split_axis=0, concat_axis=0, tiled=True)  17.6 us
    ppermute x6, starting transfers between devices, swap(): lax.ppermute(own[j], everywhere, face_pairs(sz, j))  17.5 us
    unnamed x12, local copies, waits for them, and re-layouts  12.9 us
    all_to_all x1, blocking collectives, share(): return lax.all_to_all(chunk, axes, split_axis=0, concat_axis=0, tiled=True)  11.6 us
    ppermute x3, waiting for transfers between devices, whole(): return [part, lax.ppermute(part, 'gz', [(0, 1), (1, 0)])]  10.1 us
    ppermute x6, waiting for transfers between devices, swap(): lax.ppermute(own[j], everywhere, face_pairs(sz, j))  4.71 us
    all_to_all x3, waiting for transfers between devices, share(): return lax.all_to_all(chunk, axes, split_axis=0, concat_axis=0, tiled=True)  2.91 us
  transfers between devices with their start and end apart: 12, of which 12 were waited for; matrix products, arithmetic and copies ran while one was open for 0% of the time, Pallas kernels for 0%

profile of v1, /device:TPU:0, one launch (start us, length us, event | category | flops | bytes accessed | tf_op | source)
XLA Modules:
  0.0 99.4 jit_solution(4705964941377368510)
XLA Ops:
  0.7 1.8 %shard_map.91 = (f32[8,768]{1,0:T(8,128)}, f32[8,768]{1,0:T(8,128)}, f32[16,8,256]{2,1,0:T(8,128)}, f32[24,1536]{1,0:T(8,128)}) custom-call(f32[6,1,3072]{2,1,0:T(1,128)} %bitcast.3, f32[6,1,8]{2,1,0:T(1,128)} %bitcast.4, f32[6,1,96]{2,1,0:T(1,128)} %bitcast.5, f32[1,1,3072]{2,1,0:T(1,128)} %stiffness.1, s32[1,1,4,768]{3,2,1,0:T(4,128)} %orders.1, ...), custom_call_target="tpu_custom_call" | custom-call | tf_op jit(solution)/shard_map/pallas_call | solution.py:469
  2.5 0.0 copy-start.5
  2.5 7.5 %all-to-all-start = ((f32[16,8,256]{2,1,0:T(8,128)}), f32[16,8,256]{2,1,0:T(8,128)S(1)}, u32[]{:S(2)}, u32[]{:S(2)}) async-start(f32[16,8,256]{2,1,0:T(8,128)} %get-tuple-element.22), calls=%async_computation | async-start | bytes 262144 | tf_op jit(solution)/shard_map/all_to_all | solution.py:496
  10.0 1.3 %collective-permute-start = (f32[8,768]{1,0:T(8,128)}, f32[8,768]{1,0:T(8,128)S(1)}, u32[]{:S(2)}, u32[]{:S(2)}) collective-permute-start(f32[8,768]{1,0:T(8,128)} %get-tuple-element.24), channel_id=1, source_target_pairs={{3,1},{5,3},{7,5},{8,0},{10,2},{11,9},{12,4},{13,11},{14,6},{15,13... | collective-permute-start | bytes 73736 | tf_op jit(solution)/shard_map/ppermute | solution.py:491
  11.3 4.5 %collective-permute-start.1 = (f32[8,768]{1,0:T(8,128)}, f32[8,768]{1,0:T(8,128)S(1)}, u32[]{:S(2)}, u32[]{:S(2)}) collective-permute-start(f32[8,768]{1,0:T(8,128)} %get-tuple-element.25), channel_id=1, source_target_pairs={{0,8},{1,3},{2,10},{3,5},{4,12},{5,7},{6,14},{8,16},{9,11},{10,18}... | collective-permute-start | bytes 73736 | tf_op jit(solution)/shard_map/ppermute | solution.py:491
  15.9 0.3 collective-permute-done.refs_0_
  16.1 1.5 %collective-permute-done.1.refs_1_ = f32[8,768]{1,0:T(8,128)S(1)} collective-permute-done((f32[8,768]{1,0:T(8,128)}, f32[8,768]{1,0:T(8,128)S(1)}, u32[]{:S(2)}, u32[]{:S(2)}) %collective-permute-start.1) | collective-permute-done | bytes 24608 | tf_op jit(solution)/shard_map/ppermute | solution.py:491
  17.6 0.4 all-to-all-done.shared
  18.0 0.0 copy-start.3
  18.0 0.9 copy-done.3
  18.9 0.4 shard_map.92
  19.3 1.5 %collective-permute-start.2 = (f32[8,1536]{1,0:T(8,128)S(1)}, f32[8,1536]{1,0:T(8,128)S(1)}, u32[]{:S(2)}, u32[]{:S(2)}) collective-permute-start(f32[8,1536]{1,0:T(8,128)S(1)} %get-tuple-element.27.refs_0_), channel_id=1, source_target_pairs={{0,1},{1,0},{2,3},{3,2},{4,5},{5,4},{6,7},{7,6},{8,9},{9,8},{10,11... | collective-permute-start | bytes 147464 | tf_op jit(solution)/shard_map/ppermute | solution.py:500
  20.8 2.6 %collective-permute-done.2.refs_1_ = f32[8,1536]{1,0:T(8,128)S(1)} collective-permute-done((f32[8,1536]{1,0:T(8,128)S(1)}, f32[8,1536]{1,0:T(8,128)S(1)}, u32[]{:S(2)}, u32[]{:S(2)}) %collective-permute-start.2) | collective-permute-done | bytes 49184 | tf_op jit(solution)/shard_map/ppermute | solution.py:500
  23.4 0.0 copy-start.4
  23.4 0.9 copy-done.4
  24.4 7.8 %shard_map.93 = (f32[8,768]{1,0:T(8,128)S(1)}, f32[8,768]{1,0:T(8,128)S(1)}, f32[32,8,128]{2,1,0:T(8,128)}, bf16[6,256,3072]{2,1,0:T(8,128)(2,1)S(1)}) custom-call(bf16[1,1,1536,3072]{3,2,1,0:T(8,128)(2,1)} %operator.1, f32[16,1536]{1,0:T(8,128)S(1)} %get-tuple-element.26.modes_ref, f32[24,1536]{1,0:T(8,128)S(1)} %copy-done.4, ...), custom_call_target="tpu_custom_call" | custom-call | tf_op jit(solution)/shard_map/pallas_call | solution.py:469
  32.2 0.0 copy-start
  32.2 3.7 %copy-done = bf16[6,256,3072]{2,1,0:T(8,128)(2,1)} copy-done((bf16[6,256,3072]{2,1,0:T(8,128)(2,1)}, bf16[6,256,3072]{2,1,0:T(8,128)(2,1)S(1)}, u32[]{:S(2)}) %copy-start) | copy-done | bytes 9437208
  35.9 5.6 %all-to-all-start.1 = ((f32[32,8,128]{2,1,0:T(8,128)}), f32[32,8,128]{2,1,0:T(8,128)S(1)}, u32[]{:S(2)}, u32[]{:S(2)}) async-start(f32[32,8,128]{2,1,0:T(8,128)} %get-tuple-element.29), calls=%async_computation.1 | async-start | bytes 262144 | tf_op jit(solution)/shard_map/all_to_all | solution.py:496
  41.4 1.3 %collective-permute-start.3 = (f32[8,768]{1,0:T(8,128)S(1)}, f32[8,768]{1,0:T(8,128)S(1)}, u32[]{:S(2)}, u32[]{:S(2)}) collective-permute-start(f32[8,768]{1,0:T(8,128)S(1)} %get-tuple-element.30.refs_0_), channel_id=1, source_target_pairs={{3,1},{5,3},{7,5},{8,0},{10,2},{11,9},{12,4},{13,11},{14,6},{15,13... | collective-permute-start | bytes 73736 | tf_op jit(solution)/shard_map/ppermute | solution.py:491
  42.7 4.5 %collective-permute-start.4 = (f32[8,768]{1,0:T(8,128)S(1)}, f32[8,768]{1,0:T(8,128)S(1)}, u32[]{:S(2)}, u32[]{:S(2)}) collective-permute-start(f32[8,768]{1,0:T(8,128)S(1)} %get-tuple-element.31.refs_1_), channel_id=1, source_target_pairs={{0,8},{1,3},{2,10},{3,5},{4,12},{5,7},{6,14},{8,16},{9,11},{10,18}... | collective-permute-start | bytes 73736 | tf_op jit(solution)/shard_map/ppermute | solution.py:491
  47.3 0.1 collective-permute-done.3.refs_2_
  47.4 1.4 %collective-permute-done.4.refs_3_ = f32[8,768]{1,0:T(8,128)S(1)} collective-permute-done((f32[8,768]{1,0:T(8,128)S(1)}, f32[8,768]{1,0:T(8,128)S(1)}, u32[]{:S(2)}, u32[]{:S(2)}) %collective-permute-start.4) | collective-permute-done | bytes 24608 | tf_op jit(solution)/shard_map/ppermute | solution.py:491
  48.8 1.3 %all-to-all-done.1.pieces.before = f32[32,8,128]{2,1,0:T(8,128)S(1)} async-done(((f32[32,8,128]{2,1,0:T(8,128)}), f32[32,8,128]{2,1,0:T(8,128)S(1)}, u32[]{:S(2)}, u32[]{:S(2)}) %all-to-all-start.1) | async-done | bytes 131104 | tf_op jit(solution)/shard_map/all_to_all | solution.py:496
  50.1 0.0 copy-done.5
  50.1 1.0 %shard_map.94 = (f32[8,1536]{1,0:T(8,128)S(1)}, f32[8,1536]{1,0:T(8,128)S(1)}) custom-call(f32[32,8,128]{2,1,0:T(8,128)S(1)} %all-to-all-done.1.pieces.before, f32[16,8,256]{2,1,0:T(8,128)S(1)} %all-to-all-done.shared, f32[24,1536]{1,0:T(8,128)S(1)} %copy-done.5, f32[16,1536]{1,0:T(8,128)S(1)} %get-tuple-element.26.modes_ref, ...), custom_call_target="tpu_custom_call" | custom-call | tf_op jit(solution)/shard_map/pallas_call | solution.py:469
  51.1 0.4 collective-permute-start.5
  51.5 3.8 %collective-permute-done.5.refs_1_.refs_3_ = f32[8,1536]{1,0:T(8,128)S(1)} collective-permute-done((f32[8,1536]{1,0:T(8,128)S(1)}, f32[8,1536]{1,0:T(8,128)S(1)}, u32[]{:S(2)}, u32[]{:S(2)}) %collective-permute-start.5) | collective-permute-done | bytes 49184 | tf_op jit(solution)/shard_map/ppermute | solution.py:500
  55.3 0.0 copy-start.1
  55.3 3.7 %copy-done.1 = bf16[6,256,3072]{2,1,0:T(8,128)(2,1)S(1)} copy-done((bf16[6,256,3072]{2,1,0:T(8,128)(2,1)S(1)}, bf16[6,256,3072]{2,1,0:T(8,128)(2,1)}, u32[]{:S(2)}) %copy-start.1) | copy-done | bytes 9437208
  58.9 3.3 %shard_map.95 = (f32[8,768]{1,0:T(8,128)S(1)}, f32[8,768]{1,0:T(8,128)S(1)}, f32[32,8,128]{2,1,0:T(8,128)}) custom-call(bf16[6,256,3072]{2,1,0:T(8,128)(2,1)S(1)} %copy-done.1, f32[16,1536]{1,0:T(8,128)S(1)} %get-tuple-element.26.modes_ref, f32[8,1536]{1,0:T(8,128)S(1)} %get-tuple-element.32.direction.refs_0_.direction_ref.refs_2_, ...), custom_call_target="tpu_custom_call" | custom-call | tf_op jit(solution)/shard_map/pallas_call | solution.py:469
  62.3 4.6 %all-to-all-start.2 = ((f32[32,8,128]{2,1,0:T(8,128)}), f32[32,8,128]{2,1,0:T(8,128)S(1)}, u32[]{:S(2)}, u32[]{:S(2)}) async-start(f32[32,8,128]{2,1,0:T(8,128)} %get-tuple-element.34), calls=%async_computation.2 | async-start | bytes 262144 | tf_op jit(solution)/shard_map/all_to_all | solution.py:496
  66.8 1.3 %collective-permute-start.6 = (f32[8,768]{1,0:T(8,128)S(1)}, f32[8,768]{1,0:T(8,128)S(1)}, u32[]{:S(2)}, u32[]{:S(2)}) collective-permute-start(f32[8,768]{1,0:T(8,128)S(1)} %get-tuple-element.35.refs_0_), channel_id=1, source_target_pairs={{3,1},{5,3},{7,5},{8,0},{10,2},{11,9},{12,4},{13,11},{14,6},{15,13... | collective-permute-start | bytes 73736 | tf_op jit(solution)/shard_map/ppermute | solution.py:491
  68.1 4.5 %collective-permute-start.7 = (f32[8,768]{1,0:T(8,128)S(1)}, f32[8,768]{1,0:T(8,128)S(1)}, u32[]{:S(2)}, u32[]{:S(2)}) collective-permute-start(f32[8,768]{1,0:T(8,128)S(1)} %get-tuple-element.36.refs_1_), channel_id=1, source_target_pairs={{0,8},{1,3},{2,10},{3,5},{4,12},{5,7},{6,14},{8,16},{9,11},{10,18}... | collective-permute-start | bytes 73736 | tf_op jit(solution)/shard_map/ppermute | solution.py:491
  72.7 0.1 collective-permute-done.6.refs_2_
  72.8 1.4 %collective-permute-done.7.refs_3_ = f32[8,768]{1,0:T(8,128)S(1)} collective-permute-done((f32[8,768]{1,0:T(8,128)S(1)}, f32[8,768]{1,0:T(8,128)S(1)}, u32[]{:S(2)}, u32[]{:S(2)}) %collective-permute-start.7) | collective-permute-done | bytes 24608 | tf_op jit(solution)/shard_map/ppermute | solution.py:491
  74.2 1.3 %all-to-all-done.2.pieces = f32[32,8,128]{2,1,0:T(8,128)S(1)} async-done(((f32[32,8,128]{2,1,0:T(8,128)}), f32[32,8,128]{2,1,0:T(8,128)S(1)}, u32[]{:S(2)}, u32[]{:S(2)}) %all-to-all-start.2) | async-done | bytes 131104 | tf_op jit(solution)/shard_map/all_to_all | solution.py:496
  75.5 1.0 %shard_map.96 = (f32[8,1536]{1,0:T(8,128)S(1)}, f32[8,128]{1,0:T(8,128)S(1)}) custom-call(f32[32,8,128]{2,1,0:T(8,128)S(1)} %all-to-all-done.2.pieces, f32[16,8,256]{2,1,0:T(8,128)S(1)} %all-to-all-done.shared, f32[32,8,128]{2,1,0:T(8,128)S(1)} %all-to-all-done.1.pieces.before, f32[24,1536]{1,0:T(8,128)S(1)} %copy-done.5, ...), custom_call_target="tpu_custom_call" | custom-call | tf_op jit(solution)/shard_map/pallas_call | solution.py:469
  76.5 0.4 collective-permute-start.8
  76.9 3.8 %collective-permute-done.8.refs_3_.refs_5_ = f32[8,1536]{1,0:T(8,128)S(1)} collective-permute-done((f32[8,1536]{1,0:T(8,128)S(1)}, f32[8,1536]{1,0:T(8,128)S(1)}, u32[]{:S(2)}, u32[]{:S(2)}) %collective-permute-start.8) | collective-permute-done | bytes 49184 | tf_op jit(solution)/shard_map/ppermute | solution.py:500
  80.7 0.0 copy-start.2
  80.7 3.7 %copy-done.2 = bf16[6,256,3072]{2,1,0:T(8,128)(2,1)S(1)} copy-done((bf16[6,256,3072]{2,1,0:T(8,128)(2,1)S(1)}, bf16[6,256,3072]{2,1,0:T(8,128)(2,1)}, u32[]{:S(2)}) %copy-start.2) | copy-done | bytes 9437208
  84.4 2.6 %shard_map.97 = f32[32,1,128]{2,1,0:T(1,128)S(1)} custom-call(bf16[6,256,3072]{2,1,0:T(8,128)(2,1)S(1)} %copy-done.2, f32[8,1536]{1,0:T(8,128)S(1)} %get-tuple-element.37.later.refs_2_.refs_4_, f32[8,1536]{1,0:T(8,128)S(1)} %get-tuple-element.32.direction.refs_0_.direction_ref.refs_2_, f32[8,128]{1,0:T(8,128)S(1)} %get-tuple-element.38.scalars, ...), custom_call_target="tpu_custom_call" | custom-call | tf_op jit(solution)/shard_map/pallas_call | solution.py:469
  87.0 11.6 %all_to_all.20.pieces = f32[32,1,128]{2,1,0:T(1,128)S(1)} all-to-all(f32[32,1,128]{2,1,0:T(1,128)S(1)} %shard_map.97), channel_id=1, replica_groups=mesh['gx'=4,'gy'=4,'gz'=2] {'gx','gy','gz'}, dimensions={0} | all-to-all | bytes 32768 | tf_op jit(solution)/shard_map/all_to_all | solution.py:496
  98.6 0.8 shard_map.98
Async XLA Ops:
  2.5 47.6 %copy-start.5 = (f32[24,1536]{1,0:T(8,128)S(1)}, f32[24,1536]{1,0:T(8,128)}, u32[]{:S(2)}) copy-start(f32[24,1536]{1,0:T(8,128)} %get-tuple-element.23.base) | copy-start | bytes 442372
  2.5 15.5 %all-to-all-start = ((f32[16,8,256]{2,1,0:T(8,128)}), f32[16,8,256]{2,1,0:T(8,128)S(1)}, u32[]{:S(2)}, u32[]{:S(2)}) async-start(f32[16,8,256]{2,1,0:T(8,128)} %get-tuple-element.22), calls=%async_computation | async-start | bytes 262144 | tf_op jit(solution)/shard_map/all_to_all | solution.py:496
  10.0 6.1 %collective-permute-start = (f32[8,768]{1,0:T(8,128)}, f32[8,768]{1,0:T(8,128)S(1)}, u32[]{:S(2)}, u32[]{:S(2)}) collective-permute-start(f32[8,768]{1,0:T(8,128)} %get-tuple-element.24), channel_id=1, source_target_pairs={{3,1},{5,3},{7,5},{8,0},{10,2},{11,9},{12,4},{13,11},{14,6},{15,13... | collective-permute-start | bytes 73736 | tf_op jit(solution)/shard_map/ppermute | solution.py:491
  11.3 6.3 %collective-permute-start.1 = (f32[8,768]{1,0:T(8,128)}, f32[8,768]{1,0:T(8,128)S(1)}, u32[]{:S(2)}, u32[]{:S(2)}) collective-permute-start(f32[8,768]{1,0:T(8,128)} %get-tuple-element.25), channel_id=1, source_target_pairs={{0,8},{1,3},{2,10},{3,5},{4,12},{5,7},{6,14},{8,16},{9,11},{10,18}... | collective-permute-start | bytes 73736 | tf_op jit(solution)/shard_map/ppermute | solution.py:491
  18.0 0.9 copy-start.3
  19.3 4.2 %collective-permute-start.2 = (f32[8,1536]{1,0:T(8,128)S(1)}, f32[8,1536]{1,0:T(8,128)S(1)}, u32[]{:S(2)}, u32[]{:S(2)}) collective-permute-start(f32[8,1536]{1,0:T(8,128)S(1)} %get-tuple-element.27.refs_0_), channel_id=1, source_target_pairs={{0,1},{1,0},{2,3},{3,2},{4,5},{5,4},{6,7},{7,6},{8,9},{9,8},{10,11... | collective-permute-start | bytes 147464 | tf_op jit(solution)/shard_map/ppermute | solution.py:500
  23.4 0.9 copy-start.4
  32.2 3.7 %copy-start = (bf16[6,256,3072]{2,1,0:T(8,128)(2,1)}, bf16[6,256,3072]{2,1,0:T(8,128)(2,1)S(1)}, u32[]{:S(2)}) copy-start(bf16[6,256,3072]{2,1,0:T(8,128)(2,1)S(1)} %get-tuple-element.28.held) | copy-start | bytes 28311556
  35.9 14.2 %all-to-all-start.1 = ((f32[32,8,128]{2,1,0:T(8,128)}), f32[32,8,128]{2,1,0:T(8,128)S(1)}, u32[]{:S(2)}, u32[]{:S(2)}) async-start(f32[32,8,128]{2,1,0:T(8,128)} %get-tuple-element.29), calls=%async_computation.1 | async-start | bytes 262144 | tf_op jit(solution)/shard_map/all_to_all | solution.py:496
  41.4 5.9 %collective-permute-start.3 = (f32[8,768]{1,0:T(8,128)S(1)}, f32[8,768]{1,0:T(8,128)S(1)}, u32[]{:S(2)}, u32[]{:S(2)}) collective-permute-start(f32[8,768]{1,0:T(8,128)S(1)} %get-tuple-element.30.refs_0_), channel_id=1, source_target_pairs={{3,1},{5,3},{7,5},{8,0},{10,2},{11,9},{12,4},{13,11},{14,6},{15,13... | collective-permute-start | bytes 73736 | tf_op jit(solution)/shard_map/ppermute | solution.py:491
  42.7 6.1 %collective-permute-start.4 = (f32[8,768]{1,0:T(8,128)S(1)}, f32[8,768]{1,0:T(8,128)S(1)}, u32[]{:S(2)}, u32[]{:S(2)}) collective-permute-start(f32[8,768]{1,0:T(8,128)S(1)} %get-tuple-element.31.refs_1_), channel_id=1, source_target_pairs={{0,8},{1,3},{2,10},{3,5},{4,12},{5,7},{6,14},{8,16},{9,11},{10,18}... | collective-permute-start | bytes 73736 | tf_op jit(solution)/shard_map/ppermute | solution.py:491
  51.1 4.2 %collective-permute-start.5 = (f32[8,1536]{1,0:T(8,128)S(1)}, f32[8,1536]{1,0:T(8,128)S(1)}, u32[]{:S(2)}, u32[]{:S(2)}) collective-permute-start(f32[8,1536]{1,0:T(8,128)S(1)} %get-tuple-element.32.direction.refs_0_.direction_ref.refs_2_), channel_id=1, source_target_pairs={{0,1},{1,0},{2,3},{3,2},{4,5},{5,4},{6,7},{7,6},{8,9},{9,8},{10,11... | collective-permute-start | bytes 147464 | tf_op jit(solution)/shard_map/ppermute | solution.py:500
  55.3 3.7 %copy-start.1 = (bf16[6,256,3072]{2,1,0:T(8,128)(2,1)S(1)}, bf16[6,256,3072]{2,1,0:T(8,128)(2,1)}, u32[]{:S(2)}) copy-start(bf16[6,256,3072]{2,1,0:T(8,128)(2,1)} %copy-done) | copy-start | bytes 28311556
  62.3 13.2 %all-to-all-start.2 = ((f32[32,8,128]{2,1,0:T(8,128)}), f32[32,8,128]{2,1,0:T(8,128)S(1)}, u32[]{:S(2)}, u32[]{:S(2)}) async-start(f32[32,8,128]{2,1,0:T(8,128)} %get-tuple-element.34), calls=%async_computation.2 | async-start | bytes 262144 | tf_op jit(solution)/shard_map/all_to_all | solution.py:496
  66.8 5.9 %collective-permute-start.6 = (f32[8,768]{1,0:T(8,128)S(1)}, f32[8,768]{1,0:T(8,128)S(1)}, u32[]{:S(2)}, u32[]{:S(2)}) collective-permute-start(f32[8,768]{1,0:T(8,128)S(1)} %get-tuple-element.35.refs_0_), channel_id=1, source_target_pairs={{3,1},{5,3},{7,5},{8,0},{10,2},{11,9},{12,4},{13,11},{14,6},{15,13... | collective-permute-start | bytes 73736 | tf_op jit(solution)/shard_map/ppermute | solution.py:491
  68.1 6.1 %collective-permute-start.7 = (f32[8,768]{1,0:T(8,128)S(1)}, f32[8,768]{1,0:T(8,128)S(1)}, u32[]{:S(2)}, u32[]{:S(2)}) collective-permute-start(f32[8,768]{1,0:T(8,128)S(1)} %get-tuple-element.36.refs_1_), channel_id=1, source_target_pairs={{0,8},{1,3},{2,10},{3,5},{4,12},{5,7},{6,14},{8,16},{9,11},{10,18}... | collective-permute-start | bytes 73736 | tf_op jit(solution)/shard_map/ppermute | solution.py:491
  76.5 4.2 %collective-permute-start.8 = (f32[8,1536]{1,0:T(8,128)S(1)}, f32[8,1536]{1,0:T(8,128)S(1)}, u32[]{:S(2)}, u32[]{:S(2)}) collective-permute-start(f32[8,1536]{1,0:T(8,128)S(1)} %get-tuple-element.37.later.refs_2_.refs_4_), channel_id=1, source_target_pairs={{0,1},{1,0},{2,3},{3,2},{4,5},{5,4},{6,7},{7,6},{8,9},{9,8},{10,11... | collective-permute-start | bytes 147464 | tf_op jit(solution)/shard_map/ppermute | solution.py:500
  80.7 3.7 %copy-start.2 = (bf16[6,256,3072]{2,1,0:T(8,128)(2,1)S(1)}, bf16[6,256,3072]{2,1,0:T(8,128)(2,1)}, u32[]{:S(2)}) copy-start(bf16[6,256,3072]{2,1,0:T(8,128)(2,1)} %copy-done) | copy-start | bytes 28311556

commit v2 on v1

--- a/solution.py
+++ b/solution.py
@@ -8,7 +8,6 @@
 from jax.sharding import PartitionSpec as P
 
 ROW_CHUNK = 256
-IN_FLIGHT = 2
 TILE = 128
 SLOT = 8
 MODE_SPAN = 5 * SLOT
@@ -62,10 +61,15 @@
     return x * sz.sy + y if 0 <= x < sz.sx and 0 <= y < sz.sy else None
 
 
-def face_pairs(sz, local):
+def face_pairs(sz, slot):
     pairs = []
     for sub in range(sz.subs):
         for part in range(sz.gz):
+            local = slot
+            if sz.own_faces > 1:
+                first = part * sz.own_faces + slot // 2 * 2
+                index = divmod(sub, sz.sy)[first // 2]
+                local = slot ^ 1 ^ index & 1
             face = part * sz.own_faces + local
             other = grid_neighbour(sz, sub, face)
             if other is not None:
@@ -73,12 +77,30 @@
     return pairs
 
 
+def by_slot(sz, values):
+    if sz.own_faces == 1:
+        return values
+    result = []
+    for j in range(0, sz.own_faces, 2):
+        first = lax.axis_index("gz") * sz.own_faces + j
+        index = jnp.where(first < 2, lax.axis_index("gx"), lax.axis_index("gy"))
+        odd = lax.rem(index, 2) == 1
+        low, high = values[j], values[j + 1]
+        result += [jnp.where(odd, low, high), jnp.where(odd, high, low)]
+    return result
+
+
 def own_face(sz, j):
     return slice(j * sz.cap, (j + 1) * sz.cap)
 
 
-def facing(sz, j):
-    return j ^ 1 if sz.own_faces > 1 else j
+def put_slots(sz, outs, values):
+    for out, value in zip(outs, by_slot(sz, values)):
+        out[...] = value
+
+
+def get_slots(sz, refs):
+    return by_slot(sz, [ref[...] for ref in refs])
 
 
 def permuted(sz, block, slots):
@@ -86,7 +108,7 @@
     pieces = [block[:, k * TILE : (k + 1) * TILE] for k in range(count)]
     result = []
     for j in range(count):
-        index = slots[:, j * TILE : (j + 1) * TILE].astype(jnp.int32)
+        index = jnp.broadcast_to(slots[:, j * TILE : (j + 1) * TILE], (8, TILE)).astype(jnp.int32)
         low = index & (TILE - 1)
         high = index >> (TILE.bit_length() - 1)
         total = jnp.zeros((8, TILE), jnp.float32)
@@ -232,8 +254,7 @@
     for copy in copies:
         copy.start()
     pay[...] = jnp.zeros(pay.shape, jnp.float32)
-    for face in faces:
-        face[sz.modes :, :] = jnp.zeros((8 - sz.modes, sz.cap), jnp.float32)
+    base[sz.modes : 8, :] = jnp.zeros((8 - sz.modes, sz.rows), jnp.float32)
     for copy in copies:
         copy.wait()
     for m in range(sz.modes):
@@ -243,16 +264,15 @@
                 m, :, t * sz.modes : (t + 1) * sz.modes
             ]
         pay[0, m : m + 1, sz.coarse_pad : sz.coarse_pad + sz.loads] = loads_in[m] * mask
-        for j, face in enumerate(faces):
-            face[m : m + 1, :] = traces_in[m, :, own_face(sz, j)] * mask
+        base[m : m + 1, :] = traces_in[m] * mask
     position = lax.broadcasted_iota(jnp.int32, (1, sz.cap), 1)
-    for j, face in enumerate(faces):
-        face[6:7, :] = stiffness_in[:, own_face(sz, j)]
+    base[6:7, :] = stiffness_in[...]
+    for j in range(sz.own_faces):
         index = gz * sz.own_faces + j
-        face[7:8, :] = (position < lengths_in[0, 0, index]).astype(jnp.float32)
-        base[0:8, own_face(sz, j)] = face[...]
+        base[7:8, own_face(sz, j)] = (position < lengths_in[0, 0, index]).astype(jnp.float32)
         chosen = jnp.broadcast_to(slots[pl.ds(index, 1), :], (8, sz.cap))
         base[16:24, own_face(sz, j)] = chosen.astype(jnp.float32)
+    put_slots(sz, faces, [base[0:8, own_face(sz, j)] for j in range(sz.own_faces)])
     chunk = pay[0]
     for k in range(1, pay.shape[0]):
         pay[k] = chunk
@@ -260,7 +280,8 @@
 
 def first_kernel(sz, shared, base, *refs):
     arrived, refs = refs[: sz.own_faces], refs[sz.own_faces :]
-    estimate_ref, modes_ref, inverse_ref, loads_ref, coarse_ref = refs
+    estimate_ref, modes_ref, right, inverse_ref, loads_ref, coarse_ref = refs
+    right[...] = base[8:16, :]
     fill_inverse(sz, shared, inverse_ref)
     if sz.coarse_pad > sz.coarse:
         loads_ref[sz.coarse :, :] = jnp.zeros((sz.coarse_pad - sz.coarse, TILE), jnp.float32)
@@ -275,48 +296,53 @@
     )
     coarse_ref[...] = exact_dot(turned, inverse_ref[...])
     row = lax.broadcasted_iota(jnp.int32, (8, 1), 0)
+    arrived = get_slots(sz, arrived)
     for j in range(sz.own_faces):
         here = own_face(sz, j)
-        other = permuted(sz, arrived[facing(sz, j)][...], base[16:24, here])
+        other = permuted(sz, arrived[j], base[16:24, here])
         mine = base[0:8, here]
         live = mine[7:8, :]
         total = live * (mine[6:7, :] + other[6:7, :])
         weight = live / (total + 1.0 - live)
         modes_ref[0:8, here] = jnp.where(row == 6, weight, jnp.where(row == 7, live, mine * live))
-        modes_ref[8:16, here] = jnp.where(row < sz.modes, other * live, 0.0)
+        shared_rows = jnp.where(row == 6, base[16:24, here], 0.0)
+        modes_ref[8:16, here] = jnp.where(row < sz.modes, other * live, shared_rows)
     coeffs = coefficients(sz, coarse_ref)
     for j in range(sz.own_faces):
         estimate_ref[:, own_face(sz, j)] = mode_sum(sz, coeffs, modes_ref, j)
 
 
-def apply_rows(sz, vector, held, outs, arrive=None):
-    for k in range(sz.rows // ROW_CHUNK):
-        if arrive is not None:
-            arrive(k)
-        part = lax.dot_general(
-            vector[...], held[k], (((1,), (1,)), ((), ())), preferred_element_type=jnp.float32
-        )
-        j, start = divmod(k * ROW_CHUNK, sz.cap)
-        outs[j][:, start : start + ROW_CHUNK] = part.astype(jnp.bfloat16).astype(jnp.float32)
-
-
-def first_apply_kernel(sz, operator, modes_ref, base, *refs):
-    parts, refs = refs[: -sz.own_faces - 4], refs[-sz.own_faces - 4 :]
-    outs, (pay, held, vector, sems) = refs[: sz.own_faces], refs[sz.own_faces :]
+def hold_kernel(sz, operator, after, held, sems):
+    del after
     copies = [
         pltpu.make_async_copy(
             operator.at[0, 0, pl.ds(k * ROW_CHUNK, ROW_CHUNK), :], held.at[k], sems.at[k]
         )
         for k in range(sz.rows // ROW_CHUNK)
     ]
-    for copy in copies[:IN_FLIGHT]:
+    for copy in copies:
         copy.start()
-
-    def arrive(k):
-        copies[k].wait()
-        if k + IN_FLIGHT < len(copies):
-            copies[k + IN_FLIGHT].start()
-
+    for copy in copies:
+        copy.wait()
+
+
+def apply_rows(sz, vector, held):
+    parts = []
+    for k in range(sz.rows // ROW_CHUNK):
+        part = lax.dot_general(
+            vector[...], held[k], (((1,), (1,)), ((), ())), preferred_element_type=jnp.float32
+        )
+        parts.append(part.astype(jnp.bfloat16).astype(jnp.float32))
+    per_face = sz.cap // ROW_CHUNK
+    return [
+        jnp.concatenate(parts[j * per_face : (j + 1) * per_face], axis=1)
+        for j in range(sz.own_faces)
+    ]
+
+
+def first_apply_kernel(sz, held, modes_ref, right, *refs):
+    parts, refs = refs[: -sz.own_faces - 2], refs[-sz.own_faces - 2 :]
+    outs, (pay, vector) = refs[: sz.own_faces], refs[sz.own_faces :]
     put_parts(sz, parts, vector)
     weights = weights_of(sz, modes_ref)
     row = lax.broadcasted_iota(jnp.int32, (8, 1), 0)
@@ -326,22 +352,20 @@
     ]
     tile = jnp.zeros((8, TILE), jnp.float32)
     tile = mode_products(sz, tile, coarse_rows, modes_ref, 2 * MODE_SPAN)
-    apply_rows(sz, vector, held, outs, arrive)
-    vectors = []
-    for j, out in enumerate(outs):
-        vectors.append(base[8:16, own_face(sz, j)] - out[...])
-        out[...] = vectors[-1]
+    pieces = apply_rows(sz, vector, held)
+    vectors = [right[:, own_face(sz, j)] - piece for j, piece in enumerate(pieces)]
+    put_slots(sz, outs, vectors)
     tile = mode_products(sz, tile, vectors, modes_ref, 0)
     scaled = [v * w for v, w in zip(vectors, weights)]
     spread(pay, mode_products(sz, tile, scaled, modes_ref, MODE_SPAN))
 
 
-def assembled(sz, own, arrived, base, modes_ref, j):
-    other = permuted(sz, arrived[facing(sz, j)][...], base[16:24, own_face(sz, j)])
-    return modes_ref[7:8, own_face(sz, j)] * (own[j][...] + other)
-
-
-def second_kernel(sz, pieces, shared, base, modes_ref, *refs):
+def assembled(sz, own, arrived, modes_ref, j):
+    other = permuted(sz, arrived[j], modes_ref[14:15, own_face(sz, j)])
+    return modes_ref[7:8, own_face(sz, j)] * (own[j] + other)
+
+
+def second_kernel(sz, pieces, shared, modes_ref, *refs):
     own, refs = refs[: sz.own_faces], refs[sz.own_faces :]
     arrived, refs = refs[: sz.own_faces], refs[sz.own_faces :]
     residual_ref, direction_ref, inverse_ref, coupling_ref, coarse_a, coarse_b = refs
@@ -349,9 +373,10 @@
     tiles = [sub_tile(sz, pieces, sub) for sub in range(sz.subs)]
     fill_coupling(sz, tiles, coupling_ref)
     first, second = solve_pair(sz, tiles, inverse_ref, coupling_ref, coarse_a, coarse_b)
+    own, arrived = get_slots(sz, own), get_slots(sz, arrived)
     for j in range(sz.own_faces):
         here = own_face(sz, j)
-        gap = assembled(sz, own, arrived, base, modes_ref, j)
+        gap = assembled(sz, own, arrived, modes_ref, j)
         residual = gap - mode_sum(sz, first, modes_ref, j)
         residual_ref[:, here] = residual
         direction_ref[:, here] = modes_ref[6:7, here] * residual - mode_sum(sz, second, modes_ref, j)
@@ -368,8 +393,8 @@
     for j in range(sz.own_faces):
         own = residual[:, own_face(sz, j)]
         resid_dot += jnp.sum(own * (weights[j] * own), axis=1, keepdims=True)
-    apply_rows(sz, vector, held, outs)
-    pieces = [out[...] for out in outs]
+    pieces = apply_rows(sz, vector, held)
+    put_slots(sz, outs, pieces)
     for j, piece in enumerate(pieces):
         curvature += jnp.sum(direction[:, own_face(sz, j)] * piece, axis=1, keepdims=True)
     tile = jnp.where(lane == SCALARS, curvature, jnp.zeros((8, TILE), jnp.float32))
@@ -379,7 +404,7 @@
     spread(pay, mode_products(sz, tile, scaled, modes_ref, MODE_SPAN))
 
 
-def third_kernel(sz, pieces, shared, before, base, modes_ref, residual_ref, direction_ref, *refs):
+def third_kernel(sz, pieces, shared, before, modes_ref, residual_ref, direction_ref, *refs):
     own, refs = refs[: sz.own_faces], refs[sz.own_faces :]
     arrived, refs = refs[: sz.own_faces], refs[sz.own_faces :]
     later_ref, scalars_ref, inverse_ref, coupling_ref, coarse_a, coarse_b = refs
@@ -395,9 +420,10 @@
     step = resid_dot / curvature
     first, second = solve_pair(sz, tiles, inverse_ref, coupling_ref, coarse_a, coarse_b)
     dot_part = jnp.zeros((8, 1), jnp.float32)
+    own, arrived = get_slots(sz, own), get_slots(sz, arrived)
     for j in range(sz.own_faces):
         here = own_face(sz, j)
-        image = assembled(sz, own, arrived, base, modes_ref, j)
+        image = assembled(sz, own, arrived, modes_ref, j)
         corrected = image - mode_sum(sz, first, modes_ref, j)
         weight = modes_ref[6:7, here]
         scaled = weight * corrected - mode_sum(sz, second, modes_ref, j)
@@ -408,20 +434,18 @@
 
 
 def third_apply_kernel(sz, held, later, direction, scalars, *refs):
-    before, refs = refs[: sz.own_faces], refs[sz.own_faces :]
-    parts, refs = refs[: -sz.own_faces - 2], refs[-sz.own_faces - 2 :]
-    pay, vector, outs = *refs[:2], refs[2:]
+    before, refs = get_slots(sz, refs[: sz.own_faces]), refs[sz.own_faces :]
+    parts, (pay, vector) = refs[:-2], refs[-2:]
     put_parts(sz, parts, vector)
-    apply_rows(sz, vector, held, outs)
+    pieces = apply_rows(sz, vector, held)
     lane = lanes()
     later_part = jnp.zeros((8, 1), jnp.float32)
     cross_part = jnp.zeros((8, 1), jnp.float32)
-    for j, out in enumerate(outs):
-        piece = out[...]
+    for j, piece in enumerate(pieces):
         mine = later[:, own_face(sz, j)]
         earlier = direction[:, own_face(sz, j)]
         later_part += jnp.sum(mine * piece, axis=1, keepdims=True)
-        cross_part += jnp.sum(mine * before[j][...] + earlier * piece, axis=1, keepdims=True)
+        cross_part += jnp.sum(mine * before[j] + earlier * piece, axis=1, keepdims=True)
     load = lax.broadcasted_iota(jnp.int32, (8, TILE), 0)
     line = jnp.where(lane == load, later_part, 0.0)
     line = jnp.where(lane == load + 8, cross_part, line)
@@ -465,27 +489,35 @@
     everywhere = ("gx", "gy", "gz")
     small = sz.coarse_pad <= 256
 
-    def call(kernel, out_shape, in_specs, scratch, *operands, limit=None):
+    def call(kernel, out_shape, in_specs, scratch, *operands, limit=None, cost=None):
         return pl.pallas_call(
             functools.partial(kernel, sz),
             out_shape=out_shape,
             in_specs=in_specs,
             out_specs=jax.tree.map(lambda _: vmem, out_shape),
             scratch_shapes=scratch,
+            cost_estimate=cost,
             compiler_params=pltpu.CompilerParams(
                 vmem_limit_bytes=(limit or (16 if small else 56)) * MIB
             ),
         )(*operands)
 
     faces = sz.own_faces
-    chunks = sz.rows // ROW_CHUNK
     coarse = pltpu.VMEM((8, sz.coarse_pad), jnp.float32)
     square = pltpu.VMEM((sz.coarse_pad, sz.coarse_pad), jnp.float32)
     half = f32(8, sz.rows)
     face = f32(8, sz.cap)
     one_step = sz.devices <= 64
     spread_tile = f32(sz.devices if one_step else 1, 8, TILE)
-    vector = pltpu.VMEM((8, sz.order), jnp.bfloat16)
+    chunks = sz.rows // ROW_CHUNK
+    vector = [pltpu.VMEM((8, sz.order), jnp.bfloat16)]
+
+    def hold(after):
+        return call(
+            hold_kernel, jax.ShapeDtypeStruct((chunks, ROW_CHUNK, sz.order), jnp.bfloat16),
+            [hbm, vmem], [pltpu.SemaphoreType.DMA((chunks,))], operator, after, limit=42,
+            cost=pl.CostEstimate(flops=0, bytes_accessed=4 * sz.rows * sz.order, transcendentals=0),
+        )
 
     def swap(own):
         return [lax.ppermute(own[j], everywhere, face_pairs(sz, j)) for j in range(faces)]
@@ -523,46 +555,39 @@
     )
     arrived = swap(own)
     shared = share(pay, ("gx", "gy"))
-    estimate, modes = call(
-        first_kernel, [half, f32(16, sz.rows)], [vmem] * (2 + faces),
+    estimate, modes, right = call(
+        first_kernel, [half, f32(16, sz.rows), half], [vmem] * (2 + faces),
         [square, pltpu.VMEM((sz.coarse_pad, TILE), jnp.float32), coarse],
         shared, base, *arrived,
     )
     estimates = whole(estimate)
-    *own, pay, held = call(
-        first_apply_kernel,
-        [face] * faces + [
-            spread_tile,
-            jax.ShapeDtypeStruct((chunks, ROW_CHUNK, sz.order), jnp.bfloat16),
-        ],
-        [hbm] + [vmem] * (2 + len(estimates)),
-        [vector, pltpu.SemaphoreType.DMA((chunks,))],
-        operator, modes, base, *estimates, limit=42,
+    *own, pay = call(
+        first_apply_kernel, [face] * faces + [spread_tile], [vmem] * (3 + len(estimates)),
+        vector, hold(estimate), modes, right, *estimates,
     )
     arrived = swap(own)
     before = share(pay, everywhere)
     residual, direction = call(
-        second_kernel, [half, half], [vmem] * (4 + 2 * faces), [square, square, coarse, coarse],
-        before, shared, base, modes, *own, *arrived,
+        second_kernel, [half, half], [vmem] * (3 + 2 * faces), [square, square, coarse, coarse],
+        before, shared, modes, *own, *arrived,
     )
     directions = whole(direction)
     *own, pay = call(
         second_apply_kernel, [face] * faces + [spread_tile], [vmem] * (4 + len(directions)),
-        [vector], held, modes, direction, residual, *directions,
+        vector, hold(direction), modes, direction, residual, *directions,
     )
     arrived = swap(own)
     pieces = share(pay, everywhere)
     later, scalars = call(
-        third_kernel, [half, f32(8, TILE)], [vmem] * (7 + 2 * faces),
+        third_kernel, [half, f32(8, TILE)], [vmem] * (6 + 2 * faces),
         [square, square, coarse, coarse],
-        pieces, shared, before, base, modes, residual, direction, *own, *arrived,
+        pieces, shared, before, modes, residual, direction, *own, *arrived,
     )
     laters = whole(later)
     pay = call(
         third_apply_kernel, f32(sz.devices if one_step else 1, 1, TILE),
         [vmem] * (4 + faces + len(laters)),
-        [vector] + [pltpu.VMEM((8, sz.cap), jnp.float32)] * faces,
-        held, later, direction, scalars, *own, *laters,
+        vector, hold(later), later, direction, scalars, *own, *laters,
     )
     return call(
         last_kernel, f32(1, 1, 8, sz.order), [vmem] * (2 + 3 * len(laters)), [],

time: 100 us -> 80.9 us (0.81)
  starting transfers between devices: 37.5 us -> 24.5 us
  local copies, waits for them, and re-layouts: 12.9 us -> 0.91 us
  Pallas kernels: 18.9 us -> 25.8 us
  blocking collectives: 11.6 us -> 10.6 us
    unnamed x12 -> x2, local copies, waits for them, and re-layouts: 12.9 us -> 0.91 us
    ppermute x3, waiting for transfers between devices: 10.1 us -> 0.01 us  [whole(): return [part, lax.ppermute(part, 'gz', [(0, 1), (1, 0)])]]
    ppermute x6, starting transfers between devices: 17.5 us -> 7.55 us  [swap(): lax.ppermute(own[j], everywhere, face_pairs(sz, j))]
    all_to_all x3, waiting for transfers between devices: 2.91 us -> 11.9 us  [share(): return lax.all_to_all(chunk, axes, split_axis=0, concat_axis=0, tiled=True)]
    pallas_call x8 -> x11, Pallas kernels: 18.9 us -> 25.8 us  [call(): pl.pallas_call(functools.partial(kernel, sz), out_shape=out_shape, in_spe...]
    all_to_all x3, starting transfers between devices: 17.6 us -> 14.5 us  [share(): return lax.all_to_all(chunk, axes, split_axis=0, concat_axis=0, tiled=True)]
    ppermute x6, waiting for transfers between devices: 4.71 us -> 5.97 us  [swap(): lax.ppermute(own[j], everywhere, face_pairs(sz, j))]
  transfers between devices with their start and end apart: 12 -> 12, of which waited for: 12 -> 6; matrix products, arithmetic and copies ran while one was open for 0% -> 0% of each run, Pallas kernels for 0% -> 14%
where the time goes in v2:
time: 80.9 us; the launch traced here: 80.5 us
  Pallas kernels  25.8 us (32%)
  starting transfers between devices  24.5 us (30%)
  waiting for transfers between devices  17.9 us (22%)
  blocking collectives  10.6 us (13%)
  local copies, waits for them, and re-layouts  0.91 us (1%)
    pallas_call x11, Pallas kernels, call(): pl.pallas_call(functools.partial(kernel, sz), out_shape=out_shape, in_spe...  25.8 us
    all_to_all x3, starting transfers between devices, share(): return lax.all_to_all(chunk, axes, split_axis=0, concat_axis=0, tiled=True)  14.5 us
    all_to_all x3, waiting for transfers between devices, share(): return lax.all_to_all(chunk, axes, split_axis=0, concat_axis=0, tiled=True)  11.9 us
    all_to_all x1, blocking collectives, share(): return lax.all_to_all(chunk, axes, split_axis=0, concat_axis=0, tiled=True)  10.6 us
    ppermute x6, starting transfers between devices, swap(): lax.ppermute(own[j], everywhere, face_pairs(sz, j))  7.55 us
    ppermute x6, waiting for transfers between devices, swap(): lax.ppermute(own[j], everywhere, face_pairs(sz, j))  5.97 us
    ppermute x3, starting transfers between devices, whole(): return [part, lax.ppermute(part, 'gz', [(0, 1), (1, 0)])]  2.49 us
  transfers between devices with their start and end apart: 12, of which 6 were waited for; matrix products, arithmetic and copies ran while one was open for 0% of the time, Pallas kernels for 14%

profile of v2, /device:TPU:0, one launch (start us, length us, event | category | flops | bytes accessed | tf_op | source)
XLA Modules:
  0.0 80.5 jit_solution(12005728568208961437)
XLA Ops:
  0.7 1.8 %shard_map.91 = (f32[8,768]{1,0:T(8,128)}, f32[8,768]{1,0:T(8,128)}, f32[16,8,256]{2,1,0:T(8,128)}, f32[24,1536]{1,0:T(8,128)}) custom-call(f32[6,1,3072]{2,1,0:T(1,128)} %bitcast.3, f32[6,1,8]{2,1,0:T(1,128)} %bitcast.4, f32[6,1,96]{2,1,0:T(1,128)} %bitcast.5, f32[1,1,3072]{2,1,0:T(1,128)} %stiffness.1, s32[1,1,4,768]{3,2,1,0:T(4,128)} %orders.1, ...), custom_call_target="tpu_custom_call" | custom-call | tf_op jit(solution)/shard_map/pallas_call | solution.py:493
  2.5 7.4 %all-to-all-start = ((f32[16,8,256]{2,1,0:T(8,128)}), f32[16,8,256]{2,1,0:T(8,128)S(1)}, u32[]{:S(2)}, u32[]{:S(2)}) async-start(f32[16,8,256]{2,1,0:T(8,128)} %get-tuple-element.22), calls=%async_computation | async-start | bytes 262144 | tf_op jit(solution)/shard_map/all_to_all | solution.py:528
  9.9 1.9 %collective-permute-start = (f32[8,768]{1,0:T(8,128)}, f32[8,768]{1,0:T(8,128)S(1)}, u32[]{:S(2)}, u32[]{:S(2)}) collective-permute-start(f32[8,768]{1,0:T(8,128)} %get-tuple-element.24), channel_id=1, source_target_pairs={{0,8},{1,3},{2,10},{3,1},{4,12},{5,7},{6,14},{7,5},{8,0},{9,11},{1... | collective-permute-start | bytes 73736 | tf_op jit(solution)/shard_map/ppermute | solution.py:523
  11.8 0.7 collective-permute-start.1
  12.4 2.3 %collective-permute-done.refs_0_ = f32[8,768]{1,0:T(8,128)S(1)} collective-permute-done((f32[8,768]{1,0:T(8,128)}, f32[8,768]{1,0:T(8,128)S(1)}, u32[]{:S(2)}, u32[]{:S(2)}) %collective-permute-start) | collective-permute-done | bytes 24608 | tf_op jit(solution)/shard_map/ppermute | solution.py:523
  14.7 0.0 collective-permute-done.1.refs_1_
  14.8 3.3 %all-to-all-done.shared = f32[16,8,256]{2,1,0:T(8,128)S(1)} async-done(((f32[16,8,256]{2,1,0:T(8,128)}), f32[16,8,256]{2,1,0:T(8,128)S(1)}, u32[]{:S(2)}, u32[]{:S(2)}) %all-to-all-start) | async-done | bytes 131104 | tf_op jit(solution)/shard_map/all_to_all | solution.py:528
  18.1 0.0 copy-start
  18.1 0.9 %copy-done = f32[24,1536]{1,0:T(8,128)S(1)} copy-done((f32[24,1536]{1,0:T(8,128)S(1)}, f32[24,1536]{1,0:T(8,128)}, u32[]{:S(2)}) %copy-start) | copy-done | bytes 147480
  19.0 0.4 shard_map.92
  19.4 1.3 %collective-permute-start.2 = (f32[8,1536]{1,0:T(8,128)S(1)}, f32[8,1536]{1,0:T(8,128)S(1)}, u32[]{:S(2)}, u32[]{:S(2)}) collective-permute-start(f32[8,1536]{1,0:T(8,128)S(1)} %get-tuple-element.26.after.refs_0_), channel_id=1, source_target_pairs={{0,1},{1,0},{2,3},{3,2},{4,5},{5,4},{6,7},{7,6},{8,9},{9,8},{10,11... | collective-permute-start | bytes 147464 | tf_op jit(solution)/shard_map/ppermute | solution.py:532
  20.7 3.8 %shard_map.93.held = bf16[6,256,3072]{2,1,0:T(8,128)(2,1)S(1)} custom-call(bf16[1,1,1536,3072]{3,2,1,0:T(8,128)(2,1)} %operator.5, f32[8,1536]{1,0:T(8,128)S(1)} %get-tuple-element.26.after.refs_0_), custom_call_target="tpu_custom_call" | custom-call | bytes 18874368 | tf_op jit(solution)/shard_map/pallas_call | solution.py:493
  24.5 0.0 collective-permute-done.2.refs_1_
  24.5 3.3 %shard_map.94 = (f32[8,768]{1,0:T(8,128)S(1)}, f32[8,768]{1,0:T(8,128)S(1)}, f32[32,8,128]{2,1,0:T(8,128)}) custom-call(bf16[6,256,3072]{2,1,0:T(8,128)(2,1)S(1)} %shard_map.93.held, f32[16,1536]{1,0:T(8,128)S(1)} %get-tuple-element.27.modes_ref, f32[8,1536]{1,0:T(8,128)S(1)} %get-tuple-element.28.right, f32[8,1536]{1,0:T(8,128)S(1)} %get-tuple-element.26.after.refs_0_, ...), custom_call_target="tpu_custom_call" | custom-call | tf_op jit(solution)/shard_map/pallas_call | solution.py:493
  27.8 3.5 %all-to-all-start.1 = ((f32[32,8,128]{2,1,0:T(8,128)}), f32[32,8,128]{2,1,0:T(8,128)S(1)}, u32[]{:S(2)}, u32[]{:S(2)}) async-start(f32[32,8,128]{2,1,0:T(8,128)} %get-tuple-element.29), calls=%async_computation.1 | async-start | bytes 262144 | tf_op jit(solution)/shard_map/all_to_all | solution.py:528
  31.4 1.8 %collective-permute-start.3 = (f32[8,768]{1,0:T(8,128)S(1)}, f32[8,768]{1,0:T(8,128)S(1)}, u32[]{:S(2)}, u32[]{:S(2)}) collective-permute-start(f32[8,768]{1,0:T(8,128)S(1)} %get-tuple-element.30.refs_0_), channel_id=1, source_target_pairs={{0,8},{1,3},{2,10},{3,1},{4,12},{5,7},{6,14},{7,5},{8,0},{9,11},{1... | collective-permute-start | bytes 73736 | tf_op jit(solution)/shard_map/ppermute | solution.py:523
  33.2 0.7 collective-permute-start.4
  33.9 1.8 %collective-permute-done.3.refs_2_ = f32[8,768]{1,0:T(8,128)S(1)} collective-permute-done((f32[8,768]{1,0:T(8,128)S(1)}, f32[8,768]{1,0:T(8,128)S(1)}, u32[]{:S(2)}, u32[]{:S(2)}) %collective-permute-start.3) | collective-permute-done | bytes 24608 | tf_op jit(solution)/shard_map/ppermute | solution.py:523
  35.7 0.0 collective-permute-done.4.refs_3_
  35.7 4.3 %all-to-all-done.1.pieces.before = f32[32,8,128]{2,1,0:T(8,128)S(1)} async-done(((f32[32,8,128]{2,1,0:T(8,128)}), f32[32,8,128]{2,1,0:T(8,128)S(1)}, u32[]{:S(2)}, u32[]{:S(2)}) %all-to-all-start.1) | async-done | bytes 131104 | tf_op jit(solution)/shard_map/all_to_all | solution.py:528
  40.0 1.0 %shard_map.95 = (f32[8,1536]{1,0:T(8,128)S(1)}, f32[8,1536]{1,0:T(8,128)S(1)}) custom-call(f32[32,8,128]{2,1,0:T(8,128)S(1)} %all-to-all-done.1.pieces.before, f32[16,8,256]{2,1,0:T(8,128)S(1)} %all-to-all-done.shared, f32[16,1536]{1,0:T(8,128)S(1)} %get-tuple-element.27.modes_ref, f32[8,768]{1,0:T(8,128)S(1)} %get-tuple-element.30.refs_0_, ...), custom_call_target="tpu_custom_call" | custom-call | tf_op jit(solution)/shard_map/pallas_call | solution.py:493
  41.0 0.6 collective-permute-start.5
  41.6 3.8 %shard_map.96.held = bf16[6,256,3072]{2,1,0:T(8,128)(2,1)S(1)} custom-call(bf16[1,1,1536,3072]{3,2,1,0:T(8,128)(2,1)} %operator.5, f32[8,1536]{1,0:T(8,128)S(1)} %get-tuple-element.32.after.direction.refs_0_.direction_ref.refs_2_), custom_call_target="tpu_custom_call" | custom-call | bytes 18874368 | tf_op jit(solution)/shard_map/pallas_call | solution.py:493
  45.4 0.0 collective-permute-done.5.refs_1_.refs_3_
  45.4 3.3 %shard_map.97 = (f32[8,768]{1,0:T(8,128)S(1)}, f32[8,768]{1,0:T(8,128)S(1)}, f32[32,8,128]{2,1,0:T(8,128)}) custom-call(bf16[6,256,3072]{2,1,0:T(8,128)(2,1)S(1)} %shard_map.96.held, f32[16,1536]{1,0:T(8,128)S(1)} %get-tuple-element.27.modes_ref, f32[8,1536]{1,0:T(8,128)S(1)} %get-tuple-element.32.after.direction.refs_0_.direction_ref.refs_2_, ...), custom_call_target="tpu_custom_call" | custom-call | tf_op jit(solution)/shard_map/pallas_call | solution.py:493
  48.8 3.6 %all-to-all-start.2 = ((f32[32,8,128]{2,1,0:T(8,128)}), f32[32,8,128]{2,1,0:T(8,128)S(1)}, u32[]{:S(2)}, u32[]{:S(2)}) async-start(f32[32,8,128]{2,1,0:T(8,128)} %get-tuple-element.34), calls=%async_computation.2 | async-start | bytes 262144 | tf_op jit(solution)/shard_map/all_to_all | solution.py:528
  52.4 1.8 %collective-permute-start.6 = (f32[8,768]{1,0:T(8,128)S(1)}, f32[8,768]{1,0:T(8,128)S(1)}, u32[]{:S(2)}, u32[]{:S(2)}) collective-permute-start(f32[8,768]{1,0:T(8,128)S(1)} %get-tuple-element.35.refs_0_), channel_id=1, source_target_pairs={{0,8},{1,3},{2,10},{3,1},{4,12},{5,7},{6,14},{7,5},{8,0},{9,11},{1... | collective-permute-start | bytes 73736 | tf_op jit(solution)/shard_map/ppermute | solution.py:523
  54.2 0.7 collective-permute-start.7
  54.8 1.8 %collective-permute-done.6.refs_2_ = f32[8,768]{1,0:T(8,128)S(1)} collective-permute-done((f32[8,768]{1,0:T(8,128)S(1)}, f32[8,768]{1,0:T(8,128)S(1)}, u32[]{:S(2)}, u32[]{:S(2)}) %collective-permute-start.6) | collective-permute-done | bytes 24608 | tf_op jit(solution)/shard_map/ppermute | solution.py:523
  56.7 0.0 collective-permute-done.7.refs_3_
  56.7 4.3 %all-to-all-done.2.pieces = f32[32,8,128]{2,1,0:T(8,128)S(1)} async-done(((f32[32,8,128]{2,1,0:T(8,128)}), f32[32,8,128]{2,1,0:T(8,128)S(1)}, u32[]{:S(2)}, u32[]{:S(2)}) %all-to-all-start.2) | async-done | bytes 131104 | tf_op jit(solution)/shard_map/all_to_all | solution.py:528
  61.0 1.0 %shard_map.98 = (f32[8,1536]{1,0:T(8,128)S(1)}, f32[8,128]{1,0:T(8,128)S(1)}) custom-call(f32[32,8,128]{2,1,0:T(8,128)S(1)} %all-to-all-done.2.pieces, f32[16,8,256]{2,1,0:T(8,128)S(1)} %all-to-all-done.shared, f32[32,8,128]{2,1,0:T(8,128)S(1)} %all-to-all-done.1.pieces.before, f32[16,1536]{1,0:T(8,128)S(1)} %get-tuple-element.27.modes_ref, ...), custom_call_target="tpu_custom_call" | custom-call | tf_op jit(solution)/shard_map/pallas_call | solution.py:493
  62.0 0.6 collective-permute-start.8
  62.6 3.8 %shard_map.99.held = bf16[6,256,3072]{2,1,0:T(8,128)(2,1)S(1)} custom-call(bf16[1,1,1536,3072]{3,2,1,0:T(8,128)(2,1)} %operator.5, f32[8,1536]{1,0:T(8,128)S(1)} %get-tuple-element.37.after.later.refs_2_.refs_4_), custom_call_target="tpu_custom_call" | custom-call | bytes 18874368 | tf_op jit(solution)/shard_map/pallas_call | solution.py:493
  66.4 0.0 collective-permute-done.8.refs_3_.refs_5_
  66.4 2.6 %shard_map.100 = f32[32,1,128]{2,1,0:T(1,128)S(1)} custom-call(bf16[6,256,3072]{2,1,0:T(8,128)(2,1)S(1)} %shard_map.99.held, f32[8,1536]{1,0:T(8,128)S(1)} %get-tuple-element.37.after.later.refs_2_.refs_4_, f32[8,1536]{1,0:T(8,128)S(1)} %get-tuple-element.32.after.direction.refs_0_.direction_ref.refs_2_, f32[8,128]{1,0:T(8,128)S(1)} %get-tuple-element.38.scalars, ...), custom_call_target="tpu_custom_call" | custom-call | tf_op jit(solution)/shard_map/pallas_call | solution.py:493
  69.1 10.6 %all_to_all.20.pieces = f32[32,1,128]{2,1,0:T(1,128)S(1)} all-to-all(f32[32,1,128]{2,1,0:T(1,128)S(1)} %shard_map.100), channel_id=1, replica_groups=mesh['gx'=4,'gy'=4,'gz'=2] {'gx','gy','gz'}, dimensions={0} | all-to-all | bytes 32768 | tf_op jit(solution)/shard_map/all_to_all | solution.py:528
  79.7 0.8 %shard_map.101 = f32[1,1,8,3072]{3,2,1,0:T(8,128)} custom-call(f32[32,1,128]{2,1,0:T(1,128)S(1)} %all_to_all.20.pieces, f32[8,128]{1,0:T(8,128)S(1)} %get-tuple-element.38.scalars, f32[8,1536]{1,0:T(8,128)S(1)} %get-tuple-element.26.after.refs_0_, f32[8,1536]{1,0:T(8,128)S(1)} %collective-permute-done.2.refs_1_, ...), custom_call_target="tpu_custom_call" | custom-call | tf_op jit(solution)/shard_map/pallas_call | solution.py:493
Async XLA Ops:
  2.5 15.6 %all-to-all-start = ((f32[16,8,256]{2,1,0:T(8,128)}), f32[16,8,256]{2,1,0:T(8,128)S(1)}, u32[]{:S(2)}, u32[]{:S(2)}) async-start(f32[16,8,256]{2,1,0:T(8,128)} %get-tuple-element.22), calls=%async_computation | async-start | bytes 262144 | tf_op jit(solution)/shard_map/all_to_all | solution.py:528
  9.9 4.9 %collective-permute-start = (f32[8,768]{1,0:T(8,128)}, f32[8,768]{1,0:T(8,128)S(1)}, u32[]{:S(2)}, u32[]{:S(2)}) collective-permute-start(f32[8,768]{1,0:T(8,128)} %get-tuple-element.24), channel_id=1, source_target_pairs={{0,8},{1,3},{2,10},{3,1},{4,12},{5,7},{6,14},{7,5},{8,0},{9,11},{1... | collective-permute-start | bytes 73736 | tf_op jit(solution)/shard_map/ppermute | solution.py:523
  11.8 3.0 %collective-permute-start.1 = (f32[8,768]{1,0:T(8,128)}, f32[8,768]{1,0:T(8,128)S(1)}, u32[]{:S(2)}, u32[]{:S(2)}) collective-permute-start(f32[8,768]{1,0:T(8,128)} %get-tuple-element.25), channel_id=1, source_target_pairs={{3,5},{5,3},{8,16},{10,18},{11,13},{12,20},{13,11},{14,22},{16,8},... | collective-permute-start | bytes 73736 | tf_op jit(solution)/shard_map/ppermute | solution.py:523
  18.1 0.9 %copy-start = (f32[24,1536]{1,0:T(8,128)S(1)}, f32[24,1536]{1,0:T(8,128)}, u32[]{:S(2)}) copy-start(f32[24,1536]{1,0:T(8,128)} %get-tuple-element.23.base) | copy-start | bytes 442372
  19.4 5.1 %collective-permute-start.2 = (f32[8,1536]{1,0:T(8,128)S(1)}, f32[8,1536]{1,0:T(8,128)S(1)}, u32[]{:S(2)}, u32[]{:S(2)}) collective-permute-start(f32[8,1536]{1,0:T(8,128)S(1)} %get-tuple-element.26.after.refs_0_), channel_id=1, source_target_pairs={{0,1},{1,0},{2,3},{3,2},{4,5},{5,4},{6,7},{7,6},{8,9},{9,8},{10,11... | collective-permute-start | bytes 147464 | tf_op jit(solution)/shard_map/ppermute | solution.py:532
  27.8 12.2 %all-to-all-start.1 = ((f32[32,8,128]{2,1,0:T(8,128)}), f32[32,8,128]{2,1,0:T(8,128)S(1)}, u32[]{:S(2)}, u32[]{:S(2)}) async-start(f32[32,8,128]{2,1,0:T(8,128)} %get-tuple-element.29), calls=%async_computation.1 | async-start | bytes 262144 | tf_op jit(solution)/shard_map/all_to_all | solution.py:528
  31.4 4.3 %collective-permute-start.3 = (f32[8,768]{1,0:T(8,128)S(1)}, f32[8,768]{1,0:T(8,128)S(1)}, u32[]{:S(2)}, u32[]{:S(2)}) collective-permute-start(f32[8,768]{1,0:T(8,128)S(1)} %get-tuple-element.30.refs_0_), channel_id=1, source_target_pairs={{0,8},{1,3},{2,10},{3,1},{4,12},{5,7},{6,14},{7,5},{8,0},{9,11},{1... | collective-permute-start | bytes 73736 | tf_op jit(solution)/shard_map/ppermute | solution.py:523
  33.2 2.5 %collective-permute-start.4 = (f32[8,768]{1,0:T(8,128)S(1)}, f32[8,768]{1,0:T(8,128)S(1)}, u32[]{:S(2)}, u32[]{:S(2)}) collective-permute-start(f32[8,768]{1,0:T(8,128)S(1)} %get-tuple-element.31.refs_1_), channel_id=1, source_target_pairs={{3,5},{5,3},{8,16},{10,18},{11,13},{12,20},{13,11},{14,22},{16,8},... | collective-permute-start | bytes 73736 | tf_op jit(solution)/shard_map/ppermute | solution.py:523
  41.0 4.4 %collective-permute-start.5 = (f32[8,1536]{1,0:T(8,128)S(1)}, f32[8,1536]{1,0:T(8,128)S(1)}, u32[]{:S(2)}, u32[]{:S(2)}) collective-permute-start(f32[8,1536]{1,0:T(8,128)S(1)} %get-tuple-element.32.after.direction.refs_0_.direction_ref.refs_2_), channel_id=1, source_target_pairs={{0,1},{1,0},{2,3},{3,2},{4,5},{5,4},{6,7},{7,6},{8,9},{9,8},{10,11... | collective-permute-start | bytes 147464 | tf_op jit(solution)/shard_map/ppermute | solution.py:532
  48.8 12.2 %all-to-all-start.2 = ((f32[32,8,128]{2,1,0:T(8,128)}), f32[32,8,128]{2,1,0:T(8,128)S(1)}, u32[]{:S(2)}, u32[]{:S(2)}) async-start(f32[32,8,128]{2,1,0:T(8,128)} %get-tuple-element.34), calls=%async_computation.2 | async-start | bytes 262144 | tf_op jit(solution)/shard_map/all_to_all | solution.py:528
  52.4 4.3 %collective-permute-start.6 = (f32[8,768]{1,0:T(8,128)S(1)}, f32[8,768]{1,0:T(8,128)S(1)}, u32[]{:S(2)}, u32[]{:S(2)}) collective-permute-start(f32[8,768]{1,0:T(8,128)S(1)} %get-tuple-element.35.refs_0_), channel_id=1, source_target_pairs={{0,8},{1,3},{2,10},{3,1},{4,12},{5,7},{6,14},{7,5},{8,0},{9,11},{1... | collective-permute-start | bytes 73736 | tf_op jit(solution)/shard_map/ppermute | solution.py:523
  54.2 2.5 %collective-permute-start.7 = (f32[8,768]{1,0:T(8,128)S(1)}, f32[8,768]{1,0:T(8,128)S(1)}, u32[]{:S(2)}, u32[]{:S(2)}) collective-permute-start(f32[8,768]{1,0:T(8,128)S(1)} %get-tuple-element.36.refs_1_), channel_id=1, source_target_pairs={{3,5},{5,3},{8,16},{10,18},{11,13},{12,20},{13,11},{14,22},{16,8},... | collective-permute-start | bytes 73736 | tf_op jit(solution)/shard_map/ppermute | solution.py:523
  62.0 4.4 %collective-permute-start.8 = (f32[8,1536]{1,0:T(8,128)S(1)}, f32[8,1536]{1,0:T(8,128)S(1)}, u32[]{:S(2)}, u32[]{:S(2)}) collective-permute-start(f32[8,1536]{1,0:T(8,128)S(1)} %get-tuple-element.37.after.later.refs_2_.refs_4_), channel_id=1, source_target_pairs={{0,1},{1,0},{2,3},{3,2},{4,5},{5,4},{6,7},{7,6},{8,9},{9,8},{10,11... | collective-permute-start | bytes 147464 | tf_op jit(solution)/shard_map/ppermute | solution.py:532

commit v3 on v2

--- a/solution.py
+++ b/solution.py
@@ -8,6 +8,9 @@
 from jax.sharding import PartitionSpec as P
 
 ROW_CHUNK = 256
+PIECE = 128
+IN_FLIGHT = 4
+LOAD_LANE = 6
 TILE = 128
 SLOT = 8
 MODE_SPAN = 5 * SLOT
@@ -119,27 +122,36 @@
     return jnp.concatenate(result, axis=1)
 
 
-def coefficients(sz, coarse_ref):
-    gz = lax.axis_index("gz")
-    subs = [lax.axis_index("gx") * sz.sy + lax.axis_index("gy")]
-    subs += [neighbour(sz, gz * sz.own_faces + j) for j in range(sz.own_faces)]
-    result = []
-    for sub in subs:
-        start = sub * SLOT
-        base = pl.multiple_of((start // TILE) * TILE, TILE)
-        tile = coarse_ref[:, pl.ds(base, TILE)]
-        shift = lax.rem(TILE - lax.rem(start, TILE), TILE)
-        result.append(pltpu.roll(tile, shift, 1))
-    return result
-
-
-def mode_sum(sz, coeffs, modes_ref, j):
+def coefficients(sz, coarse_ref, sub):
+    start = sub * SLOT
+    base = pl.multiple_of((start // TILE) * TILE, TILE)
+    tile = coarse_ref[:, pl.ds(base, TILE)]
+    return pltpu.roll(tile, lax.rem(TILE - lax.rem(start, TILE), TILE), 1)
+
+
+def views(sz, own, rest):
+    if sz.gz == 2:
+        gz = lax.axis_index("gz")
+        return [(gz, own), (1 - gz, rest)]
+    return [(z, rest.at[z]) for z in range(sz.gz)]
+
+
+def mode_sum(sz, coarse_ref, mine, modes_ref, part, j):
+    other = coefficients(sz, coarse_ref, neighbour(sz, part * sz.own_faces + j))
     total = None
-    for tile, base in ((coeffs[0], 0), (coeffs[1 + j], SLOT)):
+    for tile, base in ((mine, 0), (other, SLOT)):
         for m in range(sz.modes):
             term = tile[:, m : m + 1] * modes_ref[base + m : base + m + 1, own_face(sz, j)]
             total = term if total is None else total + term
     return total
+
+
+def own_coefficients(sz, coarse_ref):
+    return coefficients(sz, coarse_ref, lax.axis_index("gx") * sz.sy + lax.axis_index("gy"))
+
+
+def face_slots(sz, part, j):
+    return pl.ds(pl.multiple_of(part * sz.rows + j * sz.cap, TILE), sz.cap)
 
 
 def mode_products(sz, tile, blocks, modes_ref, first_lane):
@@ -205,7 +217,7 @@
     if sz.coarse_pad > sz.coarse:
         inverse_ref[sz.coarse :, :] = jnp.zeros((sz.coarse_pad - sz.coarse, sz.coarse_pad), jnp.float32)
     for sub in range(sz.subs):
-        inverse_ref[sub * SLOT : (sub + 1) * SLOT, :] = shared[sub, :, 0 : sz.coarse_pad]
+        inverse_ref[sub * SLOT : (sub + 1) * SLOT, :] = shared[sub]
 
 
 def solve_pair(sz, tiles, inverse_ref, coupling_ref, coarse_a, coarse_b):
@@ -214,25 +226,43 @@
     first = exact_dot(coarse_a[...], inverse_ref[...])
     coarse_a[...] = first
     coarse_b[...] = exact_dot(coarse_b[...] - exact_dot(first, coupling_ref[...]), inverse_ref[...])
-    return coefficients(sz, coarse_a), coefficients(sz, coarse_b)
 
 
 def spread(out, tile):
     out[...] = jnp.broadcast_to(tile[None], out.shape)
 
 
-def part_slots(sz, part):
-    return pl.ds(pl.multiple_of(part * sz.rows, TILE), sz.rows)
-
-
-def put_parts(sz, parts, vector):
-    if len(parts) == 1:
-        for z in range(sz.gz):
-            vector[:, z * sz.rows : (z + 1) * sz.rows] = parts[0][z].astype(vector.dtype)
-    else:
-        gz = lax.axis_index("gz")
-        vector[:, part_slots(sz, gz)] = parts[0][...].astype(vector.dtype)
-        vector[:, part_slots(sz, 1 - gz)] = parts[1][...].astype(vector.dtype)
+class Stream:
+    def __init__(self, sz, operator, held, sems):
+        self.sz, self.held = sz, held
+        blocks = PIECE // 8
+        self.copies = [
+            pltpu.make_async_copy(
+                operator.at[pl.ds(k * blocks, blocks)], held.at[pl.ds(k * blocks, blocks)], sems.at[k]
+            )
+            for k in range(sz.rows // PIECE)
+        ]
+        for copy in self.copies[:IN_FLIGHT]:
+            copy.start()
+
+    def apply(self, vector):
+        sz, step, blocks = self.sz, ROW_CHUNK // PIECE, ROW_CHUNK // 8
+        parts = []
+        for k in range(sz.rows // ROW_CHUNK):
+            for p in range(k * step, (k + 1) * step):
+                self.copies[p].wait()
+                if p + IN_FLIGHT < len(self.copies):
+                    self.copies[p + IN_FLIGHT].start()
+            rows = self.held[k * blocks : (k + 1) * blocks].reshape(ROW_CHUNK, sz.order)
+            part = lax.dot_general(
+                vector[...], rows, (((1,), (1,)), ((), ())), preferred_element_type=jnp.float32
+            )
+            parts.append(part.astype(jnp.bfloat16).astype(jnp.float32))
+        per_face = sz.cap // ROW_CHUNK
+        return [
+            jnp.concatenate(parts[j * per_face : (j + 1) * per_face], axis=1)
+            for j in range(sz.own_faces)
+        ]
 
 
 def start_kernel(sz, traces, loads, inverse, stiffness, orders, rhs, lengths, count, *refs):
@@ -263,7 +293,11 @@
             pay[0, m : m + 1, t * SLOT : t * SLOT + sz.modes] = inverse_in[
                 m, :, t * sz.modes : (t + 1) * sz.modes
             ]
-        pay[0, m : m + 1, sz.coarse_pad : sz.coarse_pad + sz.loads] = loads_in[m] * mask
+        loads_row = loads_in[m] * mask
+        row = pay[0, m : m + 1, 0:TILE]
+        for load in range(sz.loads):
+            row = jnp.where(lanes((1, TILE)) == SLOT * load + LOAD_LANE, loads_row[:, load : load + 1], row)
+        pay[0, m : m + 1, 0:TILE] = row
         base[m : m + 1, :] = traces_in[m] * mask
     position = lax.broadcasted_iota(jnp.int32, (1, sz.cap), 1)
     base[6:7, :] = stiffness_in[...]
@@ -278,23 +312,9 @@
         pay[k] = chunk
 
 
-def first_kernel(sz, shared, base, *refs):
-    arrived, refs = refs[: sz.own_faces], refs[sz.own_faces :]
-    estimate_ref, modes_ref, right, inverse_ref, loads_ref, coarse_ref = refs
+def modes_kernel(sz, base, *refs):
+    arrived, (modes_ref, right) = refs[: sz.own_faces], refs[sz.own_faces :]
     right[...] = base[8:16, :]
-    fill_inverse(sz, shared, inverse_ref)
-    if sz.coarse_pad > sz.coarse:
-        loads_ref[sz.coarse :, :] = jnp.zeros((sz.coarse_pad - sz.coarse, TILE), jnp.float32)
-    for sub in range(sz.subs):
-        loads_ref[sub * SLOT : (sub + 1) * SLOT, :] = shared[sub, :, sz.coarse_pad :]
-    turned = jnp.concatenate(
-        [
-            jnp.transpose(loads_ref[k * TILE : (k + 1) * TILE, :])[0:8, :]
-            for k in range(sz.coarse_pad // TILE)
-        ],
-        axis=1,
-    )
-    coarse_ref[...] = exact_dot(turned, inverse_ref[...])
     row = lax.broadcasted_iota(jnp.int32, (8, 1), 0)
     arrived = get_slots(sz, arrived)
     for j in range(sz.own_faces):
@@ -305,45 +325,37 @@
         total = live * (mine[6:7, :] + other[6:7, :])
         weight = live / (total + 1.0 - live)
         modes_ref[0:8, here] = jnp.where(row == 6, weight, jnp.where(row == 7, live, mine * live))
-        shared_rows = jnp.where(row == 6, base[16:24, here], 0.0)
-        modes_ref[8:16, here] = jnp.where(row < sz.modes, other * live, shared_rows)
-    coeffs = coefficients(sz, coarse_ref)
+        slots_row = jnp.where(row == 6, base[16:24, here], 0.0)
+        modes_ref[8:16, here] = jnp.where(row < sz.modes, other * live, slots_row)
+
+
+def assemble_kernel(sz, modes_ref, *refs):
+    own, arrived = get_slots(sz, refs[: sz.own_faces]), get_slots(sz, refs[sz.own_faces : -1])
+    out = refs[-1]
     for j in range(sz.own_faces):
-        estimate_ref[:, own_face(sz, j)] = mode_sum(sz, coeffs, modes_ref, j)
-
-
-def hold_kernel(sz, operator, after, held, sems):
-    del after
-    copies = [
-        pltpu.make_async_copy(
-            operator.at[0, 0, pl.ds(k * ROW_CHUNK, ROW_CHUNK), :], held.at[k], sems.at[k]
-        )
-        for k in range(sz.rows // ROW_CHUNK)
-    ]
-    for copy in copies:
-        copy.start()
-    for copy in copies:
-        copy.wait()
-
-
-def apply_rows(sz, vector, held):
-    parts = []
-    for k in range(sz.rows // ROW_CHUNK):
-        part = lax.dot_general(
-            vector[...], held[k], (((1,), (1,)), ((), ())), preferred_element_type=jnp.float32
-        )
-        parts.append(part.astype(jnp.bfloat16).astype(jnp.float32))
-    per_face = sz.cap // ROW_CHUNK
-    return [
-        jnp.concatenate(parts[j * per_face : (j + 1) * per_face], axis=1)
-        for j in range(sz.own_faces)
-    ]
-
-
-def first_apply_kernel(sz, held, modes_ref, right, *refs):
-    parts, refs = refs[: -sz.own_faces - 2], refs[-sz.own_faces - 2 :]
-    outs, (pay, vector) = refs[: sz.own_faces], refs[sz.own_faces :]
-    put_parts(sz, parts, vector)
+        here = own_face(sz, j)
+        other = permuted(sz, arrived[j], modes_ref[14:15, here])
+        out[:, here] = modes_ref[7:8, here] * (own[j] + other)
+
+
+def first_kernel(sz, operator, shared, right, modes_ref, modes_rest, *refs):
+    outs, refs = refs[: sz.own_faces], refs[sz.own_faces :]
+    pay, estimate_ref, inverse_ref, coarse_ref, held, vector, sems = refs
+    stream = Stream(sz, operator, held, sems)
+    fill_inverse(sz, shared, inverse_ref)
+    turned = []
+    for k in range(sz.coarse_pad // TILE):
+        block = jnp.transpose(inverse_ref[k * TILE : (k + 1) * TILE, 0:TILE])
+        rows = [SLOT * load + LOAD_LANE for load in range(sz.loads)]
+        turned.append(jnp.concatenate([block[r : r + 1] for r in rows], axis=0))
+    coarse_ref[...] = exact_dot(jnp.concatenate(turned, axis=1), inverse_ref[...])
+    mine = own_coefficients(sz, coarse_ref)
+    for part, modes in views(sz, modes_ref, modes_rest):
+        for j in range(sz.own_faces):
+            here = face_slots(sz, part, j)
+            estimate = mode_sum(sz, coarse_ref, mine, modes, part, j)
+            estimate_ref[:, here] = estimate
+            vector[:, here] = estimate.astype(jnp.bfloat16)
     weights = weights_of(sz, modes_ref)
     row = lax.broadcasted_iota(jnp.int32, (8, 1), 0)
     coarse_rows = [
@@ -352,7 +364,7 @@
     ]
     tile = jnp.zeros((8, TILE), jnp.float32)
     tile = mode_products(sz, tile, coarse_rows, modes_ref, 2 * MODE_SPAN)
-    pieces = apply_rows(sz, vector, held)
+    pieces = stream.apply(vector)
     vectors = [right[:, own_face(sz, j)] - piece for j, piece in enumerate(pieces)]
     put_slots(sz, outs, vectors)
     tile = mode_products(sz, tile, vectors, modes_ref, 0)
@@ -360,43 +372,39 @@
     spread(pay, mode_products(sz, tile, scaled, modes_ref, MODE_SPAN))
 
 
-def assembled(sz, own, arrived, modes_ref, j):
-    other = permuted(sz, arrived[j], modes_ref[14:15, own_face(sz, j)])
-    return modes_ref[7:8, own_face(sz, j)] * (own[j] + other)
-
-
-def second_kernel(sz, pieces, shared, modes_ref, *refs):
-    own, refs = refs[: sz.own_faces], refs[sz.own_faces :]
-    arrived, refs = refs[: sz.own_faces], refs[sz.own_faces :]
-    residual_ref, direction_ref, inverse_ref, coupling_ref, coarse_a, coarse_b = refs
+def second_kernel(sz, operator, pieces, shared, modes_ref, modes_rest, gap, gap_rest, *refs):
+    outs, refs = refs[: sz.own_faces], refs[sz.own_faces :]
+    pay, residual_ref, direction_ref = refs[:3]
+    inverse_ref, coupling_ref, coarse_a, coarse_b, held, vector, sems = refs[3:]
+    stream = Stream(sz, operator, held, sems)
     fill_inverse(sz, shared, inverse_ref)
     tiles = [sub_tile(sz, pieces, sub) for sub in range(sz.subs)]
     fill_coupling(sz, tiles, coupling_ref)
-    first, second = solve_pair(sz, tiles, inverse_ref, coupling_ref, coarse_a, coarse_b)
-    own, arrived = get_slots(sz, own), get_slots(sz, arrived)
-    for j in range(sz.own_faces):
-        here = own_face(sz, j)
-        gap = assembled(sz, own, arrived, modes_ref, j)
-        residual = gap - mode_sum(sz, first, modes_ref, j)
-        residual_ref[:, here] = residual
-        direction_ref[:, here] = modes_ref[6:7, here] * residual - mode_sum(sz, second, modes_ref, j)
-
-
-def second_apply_kernel(sz, held, modes_ref, direction, residual, *refs):
-    parts, refs = refs[: -sz.own_faces - 2], refs[-sz.own_faces - 2 :]
-    outs, (pay, vector) = refs[: sz.own_faces], refs[sz.own_faces :]
-    put_parts(sz, parts, vector)
+    solve_pair(sz, tiles, inverse_ref, coupling_ref, coarse_a, coarse_b)
+    first, second = own_coefficients(sz, coarse_a), own_coefficients(sz, coarse_b)
+    both = zip(views(sz, gap, gap_rest), views(sz, modes_ref, modes_rest))
+    for (part, vector_part), (_, modes) in both:
+        for j in range(sz.own_faces):
+            here = face_slots(sz, part, j)
+            residual = vector_part[:, own_face(sz, j)] - mode_sum(sz, coarse_a, first, modes, part, j)
+            weight = modes[6:7, own_face(sz, j)]
+            direction = weight * residual - mode_sum(sz, coarse_b, second, modes, part, j)
+            residual_ref[:, here] = residual
+            direction_ref[:, here] = direction
+            vector[:, here] = direction.astype(jnp.bfloat16)
     weights = weights_of(sz, modes_ref)
+    gz = lax.axis_index("gz")
     lane = lanes()
     curvature = jnp.zeros((8, 1), jnp.float32)
     resid_dot = jnp.zeros((8, 1), jnp.float32)
     for j in range(sz.own_faces):
-        own = residual[:, own_face(sz, j)]
+        own = residual_ref[:, face_slots(sz, gz, j)]
         resid_dot += jnp.sum(own * (weights[j] * own), axis=1, keepdims=True)
-    pieces = apply_rows(sz, vector, held)
+    pieces = stream.apply(vector)
     put_slots(sz, outs, pieces)
     for j, piece in enumerate(pieces):
-        curvature += jnp.sum(direction[:, own_face(sz, j)] * piece, axis=1, keepdims=True)
+        direction = direction_ref[:, face_slots(sz, gz, j)]
+        curvature += jnp.sum(direction * piece, axis=1, keepdims=True)
     tile = jnp.where(lane == SCALARS, curvature, jnp.zeros((8, TILE), jnp.float32))
     tile = jnp.where(lane == SCALARS + 1, resid_dot, tile)
     tile = mode_products(sz, tile, pieces, modes_ref, 0)
@@ -404,10 +412,14 @@
     spread(pay, mode_products(sz, tile, scaled, modes_ref, MODE_SPAN))
 
 
-def third_kernel(sz, pieces, shared, before, modes_ref, residual_ref, direction_ref, *refs):
-    own, refs = refs[: sz.own_faces], refs[sz.own_faces :]
-    arrived, refs = refs[: sz.own_faces], refs[sz.own_faces :]
-    later_ref, scalars_ref, inverse_ref, coupling_ref, coarse_a, coarse_b = refs
+def third_kernel(
+    sz, operator, pieces, shared, before, residual_ref, direction_ref,
+    modes_ref, modes_rest, image, image_rest, *refs,
+):
+    earlier, refs = get_slots(sz, refs[: sz.own_faces]), refs[sz.own_faces :]
+    pay, later_ref, scalars_ref = refs[:3]
+    inverse_ref, coupling_ref, coarse_a, coarse_b, dots, held, vector, sems = refs[3:]
+    stream = Stream(sz, operator, held, sems)
     lane = lanes()
     fill_inverse(sz, shared, inverse_ref)
     fill_coupling(sz, [sub_tile(sz, before, sub) for sub in range(sz.subs)], coupling_ref)
@@ -418,45 +430,41 @@
     curvature = 2.0 * totals[:, SCALARS : SCALARS + 1]
     resid_dot = totals[:, SCALARS + 1 : SCALARS + 2]
     step = resid_dot / curvature
-    first, second = solve_pair(sz, tiles, inverse_ref, coupling_ref, coarse_a, coarse_b)
+    scalars_ref[...] = jnp.where(lane == 0, curvature, resid_dot)
+    solve_pair(sz, tiles, inverse_ref, coupling_ref, coarse_a, coarse_b)
+    first, second = own_coefficients(sz, coarse_a), own_coefficients(sz, coarse_b)
+    both = zip(views(sz, image, image_rest), views(sz, modes_ref, modes_rest))
+    for (part, vector_part), (_, modes) in both:
+        for j in range(sz.own_faces):
+            here = face_slots(sz, part, j)
+            corrected = vector_part[:, own_face(sz, j)] - mode_sum(sz, coarse_a, first, modes, part, j)
+            weight = modes[6:7, own_face(sz, j)]
+            scaled = weight * corrected - mode_sum(sz, coarse_b, second, modes, part, j)
+            residual = residual_ref[:, here] - step * corrected
+            dots[:, here] = residual * (weight * residual)
+            later = direction_ref[:, here] - step * scaled
+            later_ref[:, here] = later
+            vector[:, here] = later.astype(jnp.bfloat16)
+    gz = lax.axis_index("gz")
     dot_part = jnp.zeros((8, 1), jnp.float32)
-    own, arrived = get_slots(sz, own), get_slots(sz, arrived)
     for j in range(sz.own_faces):
-        here = own_face(sz, j)
-        image = assembled(sz, own, arrived, modes_ref, j)
-        corrected = image - mode_sum(sz, first, modes_ref, j)
-        weight = modes_ref[6:7, here]
-        scaled = weight * corrected - mode_sum(sz, second, modes_ref, j)
-        residual = residual_ref[:, here] - step * corrected
-        dot_part += jnp.sum(residual * (weight * residual), axis=1, keepdims=True)
-        later_ref[:, here] = direction_ref[:, here] - step * scaled
-    scalars_ref[...] = jnp.where(lane == 0, curvature, jnp.where(lane == 1, resid_dot, dot_part))
-
-
-def third_apply_kernel(sz, held, later, direction, scalars, *refs):
-    before, refs = get_slots(sz, refs[: sz.own_faces]), refs[sz.own_faces :]
-    parts, (pay, vector) = refs[:-2], refs[-2:]
-    put_parts(sz, parts, vector)
-    pieces = apply_rows(sz, vector, held)
-    lane = lanes()
+        dot_part += jnp.sum(dots[:, face_slots(sz, gz, j)], axis=1, keepdims=True)
+    pieces = stream.apply(vector)
     later_part = jnp.zeros((8, 1), jnp.float32)
     cross_part = jnp.zeros((8, 1), jnp.float32)
     for j, piece in enumerate(pieces):
-        mine = later[:, own_face(sz, j)]
-        earlier = direction[:, own_face(sz, j)]
+        mine = later_ref[:, face_slots(sz, gz, j)]
+        direction = direction_ref[:, face_slots(sz, gz, j)]
         later_part += jnp.sum(mine * piece, axis=1, keepdims=True)
-        cross_part += jnp.sum(mine * before[j] + earlier * piece, axis=1, keepdims=True)
+        cross_part += jnp.sum(mine * earlier[j] + direction * piece, axis=1, keepdims=True)
     load = lax.broadcasted_iota(jnp.int32, (8, TILE), 0)
     line = jnp.where(lane == load, later_part, 0.0)
     line = jnp.where(lane == load + 8, cross_part, line)
-    line = jnp.where(lane == load + 16, scalars[:, 2:3], line)
+    line = jnp.where(lane == load + 16, dot_part, line)
     spread(pay, jnp.sum(line, axis=0, keepdims=True))
 
 
-def last_kernel(sz, pieces, scalars, *refs):
-    out = refs[-1]
-    count = (len(refs) - 1) // 3
-    estimate, direction, later = refs[:count], refs[count : 2 * count], refs[2 * count : 3 * count]
+def last_kernel(sz, pieces, scalars, estimate, direction, later, out):
     totals = pieces[0]
     for k in range(1, pieces.shape[0]):
         totals = totals + pieces[k]
@@ -469,15 +477,8 @@
     ratio = dot / previous
     final = 2.0 * (later_part + ratio * cross_part) + ratio * ratio * curvature
     first, second = previous / curvature, dot / final
-    gz = lax.axis_index("gz")
-    for z in range(sz.gz):
-        if count == 1:
-            here, parts = part_slots(sz, z), [x[0][z] for x in (estimate, direction, later)]
-        else:
-            here = part_slots(sz, 1 - gz if z else gz)
-            parts = [x[z][...] for x in (estimate, direction, later)]
-        moved = parts[0] + first * parts[1]
-        out[0, 0, :, here] = moved + second * (parts[2] + ratio * parts[1])
+    moved = estimate[...] + first * direction[...]
+    out[0, 0] = moved + second * (later[...] + ratio * direction[...])
 
 
 def shards(mesh_shape, operator, rhs_parts, stiffness, traces, coarse_inverse, rigid_loads,
@@ -503,21 +504,19 @@
         )(*operands)
 
     faces = sz.own_faces
+    pieces = sz.rows // PIECE
     coarse = pltpu.VMEM((8, sz.coarse_pad), jnp.float32)
     square = pltpu.VMEM((sz.coarse_pad, sz.coarse_pad), jnp.float32)
-    half = f32(8, sz.rows)
-    face = f32(8, sz.cap)
+    half, full, face = f32(8, sz.rows), f32(8, sz.order), f32(8, sz.cap)
+    blocks = operator.reshape(sz.rows // 8, 8, sz.order)
     one_step = sz.devices <= 64
     spread_tile = f32(sz.devices if one_step else 1, 8, TILE)
-    chunks = sz.rows // ROW_CHUNK
-    vector = [pltpu.VMEM((8, sz.order), jnp.bfloat16)]
-
-    def hold(after):
-        return call(
-            hold_kernel, jax.ShapeDtypeStruct((chunks, ROW_CHUNK, sz.order), jnp.bfloat16),
-            [hbm, vmem], [pltpu.SemaphoreType.DMA((chunks,))], operator, after, limit=42,
-            cost=pl.CostEstimate(flops=0, bytes_accessed=4 * sz.rows * sz.order, transcendentals=0),
-        )
+    apply_scratch = [
+        pltpu.VMEM((sz.rows // 8, 8, sz.order), jnp.bfloat16),
+        pltpu.VMEM((8, sz.order), jnp.bfloat16),
+        pltpu.SemaphoreType.DMA((pieces,)),
+    ]
+    large = 50 if small else 56
 
     def swap(own):
         return [lax.ppermute(own[j], everywhere, face_pairs(sz, j)) for j in range(faces)]
@@ -527,17 +526,20 @@
             return lax.all_gather(chunk, axes, axis=0, tiled=True)
         return lax.all_to_all(chunk, axes, split_axis=0, concat_axis=0, tiled=True)
 
-    def whole(part):
+    def rest(part):
         if sz.gz == 2:
-            return [part, lax.ppermute(part, "gz", [(0, 1), (1, 0)])]
-        return [lax.all_gather(part, "gz", axis=0, tiled=False)]
+            return lax.ppermute(part, "gz", [(0, 1), (1, 0)])
+        return lax.all_gather(part, "gz", axis=0, tiled=False)
+
+    def assemble(own):
+        part = call(
+            assemble_kernel, half, [vmem] * (1 + 2 * faces), [], modes, *own, *swap(own)
+        )
+        return part, rest(part)
 
     *own, pay, base = call(
         start_kernel,
-        [face] * faces + [
-            f32(sz.subs if one_step else 1, 8, sz.coarse_pad + TILE),
-            f32(24, sz.rows),
-        ],
+        [face] * faces + [f32(sz.subs if one_step else 1, 8, sz.coarse_pad), f32(24, sz.rows)],
         [hbm] * 8,
         [
             pltpu.VMEM((sz.modes, 1, sz.rows), jnp.float32),
@@ -553,45 +555,36 @@
         coarse_inverse.reshape(sz.modes, 1, -1), stiffness, face_order, rhs_parts,
         face_lengths, mode_count, limit=60,
     )
-    arrived = swap(own)
     shared = share(pay, ("gx", "gy"))
-    estimate, modes, right = call(
-        first_kernel, [half, f32(16, sz.rows), half], [vmem] * (2 + faces),
-        [square, pltpu.VMEM((sz.coarse_pad, TILE), jnp.float32), coarse],
-        shared, base, *arrived,
-    )
-    estimates = whole(estimate)
-    *own, pay = call(
-        first_apply_kernel, [face] * faces + [spread_tile], [vmem] * (3 + len(estimates)),
-        vector, hold(estimate), modes, right, *estimates,
-    )
-    arrived = swap(own)
+    modes, right = call(
+        modes_kernel, [f32(16, sz.rows), half], [vmem] * (1 + faces), [], base, *swap(own)
+    )
+    modes_rest = rest(modes)
+    *own, pay, estimate = call(
+        first_kernel, [face] * faces + [spread_tile, full], [hbm] + [vmem] * 4,
+        [square, coarse] + apply_scratch,
+        blocks, shared, right, modes, modes_rest, limit=large,
+    )
     before = share(pay, everywhere)
-    residual, direction = call(
-        second_kernel, [half, half], [vmem] * (3 + 2 * faces), [square, square, coarse, coarse],
-        before, shared, modes, *own, *arrived,
-    )
-    directions = whole(direction)
-    *own, pay = call(
-        second_apply_kernel, [face] * faces + [spread_tile], [vmem] * (4 + len(directions)),
-        vector, hold(direction), modes, direction, residual, *directions,
-    )
-    arrived = swap(own)
-    pieces = share(pay, everywhere)
-    later, scalars = call(
-        third_kernel, [half, f32(8, TILE)], [vmem] * (6 + 2 * faces),
-        [square, square, coarse, coarse],
-        pieces, shared, before, modes, residual, direction, *own, *arrived,
-    )
-    laters = whole(later)
-    pay = call(
-        third_apply_kernel, f32(sz.devices if one_step else 1, 1, TILE),
-        [vmem] * (4 + faces + len(laters)),
-        vector, hold(later), later, direction, scalars, *own, *laters,
+    gap, gap_rest = assemble(own)
+    *own, pay, residual, direction = call(
+        second_kernel, [face] * faces + [spread_tile, full, full], [hbm] + [vmem] * 6,
+        [square, square, coarse, coarse] + apply_scratch,
+        blocks, before, shared, modes, modes_rest, gap, gap_rest, limit=large,
+    )
+    after = share(pay, everywhere)
+    image, image_rest = assemble(own)
+    pay, later, scalars = call(
+        third_kernel,
+        [f32(sz.devices if one_step else 1, 1, TILE), full, f32(8, TILE)],
+        [hbm] + [vmem] * (9 + faces),
+        [square, square, coarse, coarse, pltpu.VMEM((8, sz.order), jnp.float32)] + apply_scratch,
+        blocks, after, shared, before, residual, direction, modes, modes_rest,
+        image, image_rest, *own, limit=large,
     )
     return call(
-        last_kernel, f32(1, 1, 8, sz.order), [vmem] * (2 + 3 * len(laters)), [],
-        share(pay, everywhere), scalars, *estimates, *directions, *laters,
+        last_kernel, f32(1, 1, 8, sz.order), [vmem] * 5, [],
+        share(pay, everywhere), scalars, estimate, direction, later,
     )
 
 

time: 80.9 us -> 88.5 us (1.094)
  starting transfers between devices: 24.5 us -> 28.2 us
  blocking collectives: 10.6 us -> 13.9 us
  Pallas kernels: 25.8 us -> 27.8 us
  waiting for transfers between devices: 17.9 us -> 16.5 us
    ppermute x3, waiting for transfers between devices: 0.01 us -> 8.16 us  [rest(): return lax.ppermute(part, 'gz', [(0, 1), (1, 0)])]
    all_to_all x3, waiting for transfers between devices: 11.9 us -> 4.68 us  [share(): return lax.all_to_all(chunk, axes, split_axis=0, concat_axis=0, tiled=True)]
    all_to_all x3, starting transfers between devices: 14.5 us -> 18.3 us  [share(): return lax.all_to_all(chunk, axes, split_axis=0, concat_axis=0, tiled=True)]
    all_to_all x1, blocking collectives: 10.6 us -> 13.9 us  [share(): return lax.all_to_all(chunk, axes, split_axis=0, concat_axis=0, tiled=True)]
    ppermute x6, waiting for transfers between devices: 5.97 us -> 3.68 us  [swap(): lax.ppermute(own[j], everywhere, face_pairs(sz, j))]
    pallas_call x11 -> x8, Pallas kernels: 25.8 us -> 27.8 us  [call(): pl.pallas_call(functools.partial(kernel, sz), out_shape=out_shape, in_spe...]
    ppermute x3, starting transfers between devices: 2.49 us -> 1.19 us  [rest(): return lax.ppermute(part, 'gz', [(0, 1), (1, 0)])]
    ppermute x6, starting transfers between devices: 7.55 us -> 8.71 us  [swap(): lax.ppermute(own[j], everywhere, face_pairs(sz, j))]
  transfers between devices with their start and end apart: 12 -> 12, of which waited for: 6 -> 5; matrix products, arithmetic and copies ran while one was open for 0% -> 0% of each run, Pallas kernels for 14% -> 1%
where the time goes in v3:
time: 88.5 us; the launch traced here: 88.1 us
  starting transfers between devices  28.2 us (32%)
  Pallas kernels  27.8 us (31%)
  waiting for transfers between devices  16.5 us (19%)
  blocking collectives  13.9 us (16%)
  local copies, waits for them, and re-layouts  0.9 us (1%)
    pallas_call x8, Pallas kernels, call(): pl.pallas_call(functools.partial(kernel, sz), out_shape=out_shape, in_spe...  27.8 us
    all_to_all x3, starting transfers between devices, share(): return lax.all_to_all(chunk, axes, split_axis=0, concat_axis=0, tiled=True)  18.3 us
    all_to_all x1, blocking collectives, share(): return lax.all_to_all(chunk, axes, split_axis=0, concat_axis=0, tiled=True)  13.9 us
    ppermute x6, starting transfers between devices, swap(): lax.ppermute(own[j], everywhere, face_pairs(sz, j))  8.71 us
    ppermute x3, waiting for transfers between devices, rest(): return lax.ppermute(part, 'gz', [(0, 1), (1, 0)])  8.16 us
    all_to_all x3, waiting for transfers between devices, share(): return lax.all_to_all(chunk, axes, split_axis=0, concat_axis=0, tiled=True)  4.68 us
    ppermute x6, waiting for transfers between devices, swap(): lax.ppermute(own[j], everywhere, face_pairs(sz, j))  3.68 us
  transfers between devices with their start and end apart: 12, of which 5 were waited for; matrix products, arithmetic and copies ran while one was open for 0% of the time, Pallas kernels for 1%

profile of v3, /device:TPU:0, one launch (start us, length us, event | category | flops | bytes accessed | tf_op | source)
XLA Modules:
  0.0 88.1 jit_solution(7490310462126954301)
XLA Ops:
  0.7 1.9 %shard_map.91 = (f32[8,768]{1,0:T(8,128)}, f32[8,768]{1,0:T(8,128)}, f32[16,8,128]{2,1,0:T(8,128)}, f32[24,1536]{1,0:T(8,128)}) custom-call(f32[6,1,3072]{2,1,0:T(1,128)} %bitcast.7, f32[6,1,8]{2,1,0:T(1,128)} %bitcast.8, f32[6,1,96]{2,1,0:T(1,128)} %bitcast.9, f32[1,1,3072]{2,1,0:T(1,128)} %stiffness.1, s32[1,1,4,768]{3,2,1,0:T(4,128)} %orders.1, ...), custom_call_target="tpu_custom_call" | custom-call | tf_op jit(solution)/shard_map/pallas_call | solution.py:494
  2.5 3.1 %collective-permute-start = (f32[8,768]{1,0:T(8,128)}, f32[8,768]{1,0:T(8,128)S(1)}, u32[]{:S(2)}, u32[]{:S(2)}) collective-permute-start(f32[8,768]{1,0:T(8,128)} %get-tuple-element.25), channel_id=1, source_target_pairs={{0,8},{1,3},{2,10},{3,1},{4,12},{5,7},{6,14},{7,5},{8,0},{9,11},{1... | collective-permute-start | bytes 73736 | tf_op jit(solution)/shard_map/ppermute | solution.py:522
  5.6 0.7 collective-permute-start.1
  6.3 6.7 %all-to-all-start = ((f32[16,8,128]{2,1,0:T(8,128)}), f32[16,8,128]{2,1,0:T(8,128)S(1)}, u32[]{:S(2)}, u32[]{:S(2)}) async-start(f32[16,8,128]{2,1,0:T(8,128)} %get-tuple-element.23), calls=%async_computation | async-start | bytes 131072 | tf_op jit(solution)/shard_map/all_to_all | solution.py:527
  13.0 0.0 collective-permute-done.refs_0_
  13.0 0.0 collective-permute-done.1.refs_1_
  13.0 0.0 copy-start
  13.1 0.9 %copy-done = f32[24,1536]{1,0:T(8,128)S(1)} copy-done((f32[24,1536]{1,0:T(8,128)S(1)}, f32[24,1536]{1,0:T(8,128)}, u32[]{:S(2)}) %copy-start) | copy-done | bytes 147480
  14.0 0.2 shard_map.92
  14.2 1.1 %collective-permute-start.2 = (f32[16,1536]{1,0:T(8,128)S(1)}, f32[16,1536]{1,0:T(8,128)S(1)}, u32[]{:S(2)}, u32[]{:S(2)}) collective-permute-start(f32[16,1536]{1,0:T(8,128)S(1)} %get-tuple-element.28.modes_ref), channel_id=1, source_target_pairs={{0,1},{1,0},{2,3},{3,2},{4,5},{5,4},{6,7},{7,6},{8,9},{9,8},{10,11... | collective-permute-start | bytes 294920 | tf_op jit(solution)/shard_map/ppermute | solution.py:531
  15.2 4.7 %all-to-all-done.shared = f32[16,8,128]{2,1,0:T(8,128)S(1)} async-done(((f32[16,8,128]{2,1,0:T(8,128)}), f32[16,8,128]{2,1,0:T(8,128)S(1)}, u32[]{:S(2)}, u32[]{:S(2)}) %all-to-all-start) | async-done | bytes 65568 | tf_op jit(solution)/shard_map/all_to_all | solution.py:527
  19.9 0.0 collective-permute-done.2.modes_rest
  19.9 8.1 %shard_map.93 = (f32[8,768]{1,0:T(8,128)S(1)}, f32[8,768]{1,0:T(8,128)S(1)}, f32[32,8,128]{2,1,0:T(8,128)}, f32[8,3072]{1,0:T(8,128)S(1)}) custom-call(bf16[192,8,3072]{2,1,0:T(8,128)(2,1)} %bitcast.4, f32[16,8,128]{2,1,0:T(8,128)S(1)} %all-to-all-done.shared, f32[8,1536]{1,0:T(8,128)S(1)} %get-tuple-element.27.right, ...), custom_call_target="tpu_custom_call" | custom-call | tf_op jit(solution)/shard_map/pallas_call | solution.py:494
  28.0 4.6 %all-to-all-start.1 = ((f32[32,8,128]{2,1,0:T(8,128)}), f32[32,8,128]{2,1,0:T(8,128)S(1)}, u32[]{:S(2)}, u32[]{:S(2)}) async-start(f32[32,8,128]{2,1,0:T(8,128)} %get-tuple-element.29), calls=%async_computation.1 | async-start | bytes 262144 | tf_op jit(solution)/shard_map/all_to_all | solution.py:527
  32.6 1.8 %collective-permute-start.3 = (f32[8,768]{1,0:T(8,128)S(1)}, f32[8,768]{1,0:T(8,128)S(1)}, u32[]{:S(2)}, u32[]{:S(2)}) collective-permute-start(f32[8,768]{1,0:T(8,128)S(1)} %get-tuple-element.30.refs_0_), channel_id=1, source_target_pairs={{0,8},{1,3},{2,10},{3,1},{4,12},{5,7},{6,14},{7,5},{8,0},{9,11},{1... | collective-permute-start | bytes 73736 | tf_op jit(solution)/shard_map/ppermute | solution.py:522
  34.4 0.7 collective-permute-start.4
  35.1 1.8 %collective-permute-done.3.refs_2_ = f32[8,768]{1,0:T(8,128)S(1)} collective-permute-done((f32[8,768]{1,0:T(8,128)S(1)}, f32[8,768]{1,0:T(8,128)S(1)}, u32[]{:S(2)}, u32[]{:S(2)}) %collective-permute-start.3) | collective-permute-done | bytes 24608 | tf_op jit(solution)/shard_map/ppermute | solution.py:522
  36.9 0.0 collective-permute-done.4.refs_3_
  36.9 0.2 shard_map.94.gap
  37.1 0.1 collective-permute-start.5
  37.2 4.1 %collective-permute-done.5.gap_rest = f32[8,1536]{1,0:T(8,128)S(1)} collective-permute-done((f32[8,1536]{1,0:T(8,128)S(1)}, f32[8,1536]{1,0:T(8,128)S(1)}, u32[]{:S(2)}, u32[]{:S(2)}) %collective-permute-start.5) | collective-permute-done | bytes 49184 | tf_op jit(solution)/shard_map/ppermute | solution.py:531
  41.3 0.0 all-to-all-done.1.pieces.before
  41.3 8.7 %shard_map.95 = (f32[8,768]{1,0:T(8,128)S(1)}, f32[8,768]{1,0:T(8,128)S(1)}, f32[32,8,128]{2,1,0:T(8,128)}, f32[8,3072]{1,0:T(8,128)S(1)}, f32[8,3072]{1,0:T(8,128)S(1)}) custom-call(bf16[192,8,3072]{2,1,0:T(8,128)(2,1)} %bitcast.5, f32[32,8,128]{2,1,0:T(8,128)S(1)} %all-to-all-done.1.pieces.before, f32[16,8,128]{2,1,0:T(8,128)S(1)} %all-to-all-done.shared, ...), custom_call_target="tpu_custom_call" | custom-call | tf_op jit(solution)/shard_map/pallas_call | solution.py:494
  50.0 6.9 %all-to-all-start.2 = ((f32[32,8,128]{2,1,0:T(8,128)}), f32[32,8,128]{2,1,0:T(8,128)S(1)}, u32[]{:S(2)}, u32[]{:S(2)}) async-start(f32[32,8,128]{2,1,0:T(8,128)} %get-tuple-element.32), calls=%async_computation.2 | async-start | bytes 262144 | tf_op jit(solution)/shard_map/all_to_all | solution.py:527
  57.0 1.8 %collective-permute-start.6 = (f32[8,768]{1,0:T(8,128)S(1)}, f32[8,768]{1,0:T(8,128)S(1)}, u32[]{:S(2)}, u32[]{:S(2)}) collective-permute-start(f32[8,768]{1,0:T(8,128)S(1)} %get-tuple-element.35.refs_0_), channel_id=1, source_target_pairs={{0,8},{1,3},{2,10},{3,1},{4,12},{5,7},{6,14},{7,5},{8,0},{9,11},{1... | collective-permute-start | bytes 73736 | tf_op jit(solution)/shard_map/ppermute | solution.py:522
  58.8 0.7 collective-permute-start.7
  59.4 1.8 %collective-permute-done.6.refs_2_ = f32[8,768]{1,0:T(8,128)S(1)} collective-permute-done((f32[8,768]{1,0:T(8,128)S(1)}, f32[8,768]{1,0:T(8,128)S(1)}, u32[]{:S(2)}, u32[]{:S(2)}) %collective-permute-start.6) | collective-permute-done | bytes 24608 | tf_op jit(solution)/shard_map/ppermute | solution.py:522
  61.3 0.0 collective-permute-done.7.refs_3_
  61.3 0.2 shard_map.96.image
  61.5 0.1 collective-permute-start.8
  61.6 4.1 %collective-permute-done.8.image_rest = f32[8,1536]{1,0:T(8,128)S(1)} collective-permute-done((f32[8,1536]{1,0:T(8,128)S(1)}, f32[8,1536]{1,0:T(8,128)S(1)}, u32[]{:S(2)}, u32[]{:S(2)}) %collective-permute-start.8) | collective-permute-done | bytes 49184 | tf_op jit(solution)/shard_map/ppermute | solution.py:531
  65.6 0.0 all-to-all-done.2.pieces
  65.7 7.7 %shard_map.97 = (f32[32,1,128]{2,1,0:T(1,128)S(1)}, f32[8,3072]{1,0:T(8,128)S(1)}, f32[8,128]{1,0:T(8,128)S(1)}) custom-call(bf16[192,8,3072]{2,1,0:T(8,128)(2,1)} %bitcast.6, f32[32,8,128]{2,1,0:T(8,128)S(1)} %all-to-all-done.2.pieces, f32[16,8,128]{2,1,0:T(8,128)S(1)} %all-to-all-done.shared, f32[32,8,128]{2,1,0:T(8,128)S(1)} %all-to-all-done.1.pieces.before, ...), custom_call_target="tpu_custom_call" | custom-call | tf_op jit(solution)/shard_map/pallas_call | solution.py:494
  73.3 13.9 %all_to_all.20.pieces = f32[32,1,128]{2,1,0:T(1,128)S(1)} all-to-all(f32[32,1,128]{2,1,0:T(1,128)S(1)} %get-tuple-element.37), channel_id=1, replica_groups=mesh['gx'=4,'gy'=4,'gz'=2] {'gx','gy','gz'}, dimensions={0} | all-to-all | bytes 32768 | tf_op jit(solution)/shard_map/all_to_all | solution.py:527
  87.3 0.8 shard_map.98
Async XLA Ops:
  2.5 10.5 %collective-permute-start = (f32[8,768]{1,0:T(8,128)}, f32[8,768]{1,0:T(8,128)S(1)}, u32[]{:S(2)}, u32[]{:S(2)}) collective-permute-start(f32[8,768]{1,0:T(8,128)} %get-tuple-element.25), channel_id=1, source_target_pairs={{0,8},{1,3},{2,10},{3,1},{4,12},{5,7},{6,14},{7,5},{8,0},{9,11},{1... | collective-permute-start | bytes 73736 | tf_op jit(solution)/shard_map/ppermute | solution.py:522
  5.6 7.4 %collective-permute-start.1 = (f32[8,768]{1,0:T(8,128)}, f32[8,768]{1,0:T(8,128)S(1)}, u32[]{:S(2)}, u32[]{:S(2)}) collective-permute-start(f32[8,768]{1,0:T(8,128)} %get-tuple-element.26), channel_id=1, source_target_pairs={{3,5},{5,3},{8,16},{10,18},{11,13},{12,20},{13,11},{14,22},{16,8},... | collective-permute-start | bytes 73736 | tf_op jit(solution)/shard_map/ppermute | solution.py:522
  6.3 13.7 %all-to-all-start = ((f32[16,8,128]{2,1,0:T(8,128)}), f32[16,8,128]{2,1,0:T(8,128)S(1)}, u32[]{:S(2)}, u32[]{:S(2)}) async-start(f32[16,8,128]{2,1,0:T(8,128)} %get-tuple-element.23), calls=%async_computation | async-start | bytes 131072 | tf_op jit(solution)/shard_map/all_to_all | solution.py:527
  13.0 0.9 %copy-start = (f32[24,1536]{1,0:T(8,128)S(1)}, f32[24,1536]{1,0:T(8,128)}, u32[]{:S(2)}) copy-start(f32[24,1536]{1,0:T(8,128)} %get-tuple-element.24.base) | copy-start | bytes 442372
  14.2 5.7 %collective-permute-start.2 = (f32[16,1536]{1,0:T(8,128)S(1)}, f32[16,1536]{1,0:T(8,128)S(1)}, u32[]{:S(2)}, u32[]{:S(2)}) collective-permute-start(f32[16,1536]{1,0:T(8,128)S(1)} %get-tuple-element.28.modes_ref), channel_id=1, source_target_pairs={{0,1},{1,0},{2,3},{3,2},{4,5},{5,4},{6,7},{7,6},{8,9},{9,8},{10,11... | collective-permute-start | bytes 294920 | tf_op jit(solution)/shard_map/ppermute | solution.py:531
  28.0 13.3 %all-to-all-start.1 = ((f32[32,8,128]{2,1,0:T(8,128)}), f32[32,8,128]{2,1,0:T(8,128)S(1)}, u32[]{:S(2)}, u32[]{:S(2)}) async-start(f32[32,8,128]{2,1,0:T(8,128)} %get-tuple-element.29), calls=%async_computation.1 | async-start | bytes 262144 | tf_op jit(solution)/shard_map/all_to_all | solution.py:527
  32.6 4.3 %collective-permute-start.3 = (f32[8,768]{1,0:T(8,128)S(1)}, f32[8,768]{1,0:T(8,128)S(1)}, u32[]{:S(2)}, u32[]{:S(2)}) collective-permute-start(f32[8,768]{1,0:T(8,128)S(1)} %get-tuple-element.30.refs_0_), channel_id=1, source_target_pairs={{0,8},{1,3},{2,10},{3,1},{4,12},{5,7},{6,14},{7,5},{8,0},{9,11},{1... | collective-permute-start | bytes 73736 | tf_op jit(solution)/shard_map/ppermute | solution.py:522
  34.4 2.5 %collective-permute-start.4 = (f32[8,768]{1,0:T(8,128)S(1)}, f32[8,768]{1,0:T(8,128)S(1)}, u32[]{:S(2)}, u32[]{:S(2)}) collective-permute-start(f32[8,768]{1,0:T(8,128)S(1)} %get-tuple-element.31.refs_1_), channel_id=1, source_target_pairs={{3,5},{5,3},{8,16},{10,18},{11,13},{12,20},{13,11},{14,22},{16,8},... | collective-permute-start | bytes 73736 | tf_op jit(solution)/shard_map/ppermute | solution.py:522
  37.1 4.2 %collective-permute-start.5 = (f32[8,1536]{1,0:T(8,128)S(1)}, f32[8,1536]{1,0:T(8,128)S(1)}, u32[]{:S(2)}, u32[]{:S(2)}) collective-permute-start(f32[8,1536]{1,0:T(8,128)S(1)} %shard_map.94.gap), channel_id=1, source_target_pairs={{0,1},{1,0},{2,3},{3,2},{4,5},{5,4},{6,7},{7,6},{8,9},{9,8},{10,11... | collective-permute-start | bytes 147464 | tf_op jit(solution)/shard_map/ppermute | solution.py:531
  50.0 15.6 %all-to-all-start.2 = ((f32[32,8,128]{2,1,0:T(8,128)}), f32[32,8,128]{2,1,0:T(8,128)S(1)}, u32[]{:S(2)}, u32[]{:S(2)}) async-start(f32[32,8,128]{2,1,0:T(8,128)} %get-tuple-element.32), calls=%async_computation.2 | async-start | bytes 262144 | tf_op jit(solution)/shard_map/all_to_all | solution.py:527
  57.0 4.3 %collective-permute-start.6 = (f32[8,768]{1,0:T(8,128)S(1)}, f32[8,768]{1,0:T(8,128)S(1)}, u32[]{:S(2)}, u32[]{:S(2)}) collective-permute-start(f32[8,768]{1,0:T(8,128)S(1)} %get-tuple-element.35.refs_0_), channel_id=1, source_target_pairs={{0,8},{1,3},{2,10},{3,1},{4,12},{5,7},{6,14},{7,5},{8,0},{9,11},{1... | collective-permute-start | bytes 73736 | tf_op jit(solution)/shard_map/ppermute | solution.py:522
  58.8 2.5 %collective-permute-start.7 = (f32[8,768]{1,0:T(8,128)S(1)}, f32[8,768]{1,0:T(8,128)S(1)}, u32[]{:S(2)}, u32[]{:S(2)}) collective-permute-start(f32[8,768]{1,0:T(8,128)S(1)} %get-tuple-element.36.refs_1_), channel_id=1, source_target_pairs={{3,5},{5,3},{8,16},{10,18},{11,13},{12,20},{13,11},{14,22},{16,8},... | collective-permute-start | bytes 73736 | tf_op jit(solution)/shard_map/ppermute | solution.py:522
  61.5 4.2 %collective-permute-start.8 = (f32[8,1536]{1,0:T(8,128)S(1)}, f32[8,1536]{1,0:T(8,128)S(1)}, u32[]{:S(2)}, u32[]{:S(2)}) collective-permute-start(f32[8,1536]{1,0:T(8,128)S(1)} %shard_map.96.image), channel_id=1, source_target_pairs={{0,1},{1,0},{2,3},{3,2},{4,5},{5,4},{6,7},{7,6},{8,9},{9,8},{10,11... | collective-permute-start | bytes 147464 | tf_op jit(solution)/shard_map/ppermute | solution.py:531

commit v4 on v3

--- a/solution.py
+++ b/solution.py
@@ -9,7 +9,6 @@
 
 ROW_CHUNK = 256
 PIECE = 128
-IN_FLIGHT = 4
 LOAD_LANE = 6
 TILE = 128
 SLOT = 8
@@ -233,36 +232,31 @@
 
 
 class Stream:
-    def __init__(self, sz, operator, held, sems):
-        self.sz, self.held = sz, held
-        blocks = PIECE // 8
-        self.copies = [
-            pltpu.make_async_copy(
-                operator.at[pl.ds(k * blocks, blocks)], held.at[pl.ds(k * blocks, blocks)], sems.at[k]
-            )
-            for k in range(sz.rows // PIECE)
-        ]
-        for copy in self.copies[:IN_FLIGHT]:
-            copy.start()
+    def __init__(self, sz, operator, held, product, sems):
+        self.sz, self.operator, self.held, self.product, self.sems = sz, operator, held, product, sems
+        for p in range(sz.rows // PIECE):
+            self.copy(p).start()
+
+    def copy(self, p):
+        here = pl.ds(p * (PIECE // 8), PIECE // 8)
+        return pltpu.make_async_copy(self.operator.at[here], self.held.at[here], self.sems.at[p])
 
     def apply(self, vector):
         sz, step, blocks = self.sz, ROW_CHUNK // PIECE, ROW_CHUNK // 8
-        parts = []
-        for k in range(sz.rows // ROW_CHUNK):
-            for p in range(k * step, (k + 1) * step):
-                self.copies[p].wait()
-                if p + IN_FLIGHT < len(self.copies):
-                    self.copies[p + IN_FLIGHT].start()
-            rows = self.held[k * blocks : (k + 1) * blocks].reshape(ROW_CHUNK, sz.order)
+
+        def chunk(k, carry):
+            for p in range(step):
+                self.copy(k * step + p).wait()
+            rows = self.held[pl.ds(k * blocks, blocks)].reshape(ROW_CHUNK, sz.order)
             part = lax.dot_general(
                 vector[...], rows, (((1,), (1,)), ((), ())), preferred_element_type=jnp.float32
             )
-            parts.append(part.astype(jnp.bfloat16).astype(jnp.float32))
-        per_face = sz.cap // ROW_CHUNK
-        return [
-            jnp.concatenate(parts[j * per_face : (j + 1) * per_face], axis=1)
-            for j in range(sz.own_faces)
-        ]
+            here = pl.ds(pl.multiple_of(k * ROW_CHUNK, TILE), ROW_CHUNK)
+            self.product[:, here] = part.astype(jnp.bfloat16).astype(jnp.float32)
+            return carry
+
+        lax.fori_loop(0, sz.rows // ROW_CHUNK, chunk, 0)
+        return [self.product[:, own_face(sz, j)] for j in range(sz.own_faces)]
 
 
 def start_kernel(sz, traces, loads, inverse, stiffness, orders, rhs, lengths, count, *refs):
@@ -340,8 +334,8 @@
 
 def first_kernel(sz, operator, shared, right, modes_ref, modes_rest, *refs):
     outs, refs = refs[: sz.own_faces], refs[sz.own_faces :]
-    pay, estimate_ref, inverse_ref, coarse_ref, held, vector, sems = refs
-    stream = Stream(sz, operator, held, sems)
+    pay, estimate_ref, inverse_ref, coarse_ref, held, product, vector, sems = refs
+    stream = Stream(sz, operator, held, product, sems)
     fill_inverse(sz, shared, inverse_ref)
     turned = []
     for k in range(sz.coarse_pad // TILE):
@@ -375,8 +369,8 @@
 def second_kernel(sz, operator, pieces, shared, modes_ref, modes_rest, gap, gap_rest, *refs):
     outs, refs = refs[: sz.own_faces], refs[sz.own_faces :]
     pay, residual_ref, direction_ref = refs[:3]
-    inverse_ref, coupling_ref, coarse_a, coarse_b, held, vector, sems = refs[3:]
-    stream = Stream(sz, operator, held, sems)
+    inverse_ref, coupling_ref, coarse_a, coarse_b, held, product, vector, sems = refs[3:]
+    stream = Stream(sz, operator, held, product, sems)
     fill_inverse(sz, shared, inverse_ref)
     tiles = [sub_tile(sz, pieces, sub) for sub in range(sz.subs)]
     fill_coupling(sz, tiles, coupling_ref)
@@ -418,8 +412,8 @@
 ):
     earlier, refs = get_slots(sz, refs[: sz.own_faces]), refs[sz.own_faces :]
     pay, later_ref, scalars_ref = refs[:3]
-    inverse_ref, coupling_ref, coarse_a, coarse_b, dots, held, vector, sems = refs[3:]
-    stream = Stream(sz, operator, held, sems)
+    inverse_ref, coupling_ref, coarse_a, coarse_b, dots, held, product, vector, sems = refs[3:]
+    stream = Stream(sz, operator, held, product, sems)
     lane = lanes()
     fill_inverse(sz, shared, inverse_ref)
     fill_coupling(sz, [sub_tile(sz, before, sub) for sub in range(sz.subs)], coupling_ref)
@@ -513,6 +507,7 @@
     spread_tile = f32(sz.devices if one_step else 1, 8, TILE)
     apply_scratch = [
         pltpu.VMEM((sz.rows // 8, 8, sz.order), jnp.bfloat16),
+        pltpu.VMEM((8, sz.rows), jnp.float32),
         pltpu.VMEM((8, sz.order), jnp.bfloat16),
         pltpu.SemaphoreType.DMA((pieces,)),
     ]

time: 88.5 us -> 81.5 us (0.921)
  Pallas kernels: 27.8 us -> 20.8 us
    pallas_call x8, Pallas kernels: 27.8 us -> 20.8 us  [call(): pl.pallas_call(functools.partial(kernel, sz), out_shape=out_shape, in_spe...]
where the time goes in v4:
time: 81.5 us; the launch traced here: 81.1 us
  starting transfers between devices  28.2 us (35%)
  Pallas kernels  20.8 us (26%)
  waiting for transfers between devices  16.5 us (20%)
  blocking collectives  13.9 us (17%)
  local copies, waits for them, and re-layouts  0.9 us (1%)
    pallas_call x8, Pallas kernels, call(): pl.pallas_call(functools.partial(kernel, sz), out_shape=out_shape, in_spe...  20.8 us
    all_to_all x3, starting transfers between devices, share(): return lax.all_to_all(chunk, axes, split_axis=0, concat_axis=0, tiled=True)  18.3 us
    all_to_all x1, blocking collectives, share(): return lax.all_to_all(chunk, axes, split_axis=0, concat_axis=0, tiled=True)  13.9 us
    ppermute x6, starting transfers between devices, swap(): lax.ppermute(own[j], everywhere, face_pairs(sz, j))  8.71 us
    ppermute x3, waiting for transfers between devices, rest(): return lax.ppermute(part, 'gz', [(0, 1), (1, 0)])  8.16 us
    all_to_all x3, waiting for transfers between devices, share(): return lax.all_to_all(chunk, axes, split_axis=0, concat_axis=0, tiled=True)  4.68 us
    ppermute x6, waiting for transfers between devices, swap(): lax.ppermute(own[j], everywhere, face_pairs(sz, j))  3.68 us
  transfers between devices with their start and end apart: 12, of which 5 were waited for; matrix products, arithmetic and copies ran while one was open for 0% of the time, Pallas kernels for 1%

profile of v4, /device:TPU:0, one launch (start us, length us, event | category | flops | bytes accessed | tf_op | source)
XLA Modules:
  0.0 81.1 jit_solution(6027542123795431887)
XLA Ops:
  0.7 1.9 %shard_map.91 = (f32[8,768]{1,0:T(8,128)}, f32[8,768]{1,0:T(8,128)}, f32[16,8,128]{2,1,0:T(8,128)}, f32[24,1536]{1,0:T(8,128)}) custom-call(f32[6,1,3072]{2,1,0:T(1,128)} %bitcast.7, f32[6,1,8]{2,1,0:T(1,128)} %bitcast.8, f32[6,1,96]{2,1,0:T(1,128)} %bitcast.9, f32[1,1,3072]{2,1,0:T(1,128)} %stiffness.1, s32[1,1,4,768]{3,2,1,0:T(4,128)} %orders.1, ...), custom_call_target="tpu_custom_call" | custom-call | tf_op jit(solution)/shard_map/pallas_call | solution.py:488
  2.5 3.1 %collective-permute-start = (f32[8,768]{1,0:T(8,128)}, f32[8,768]{1,0:T(8,128)S(1)}, u32[]{:S(2)}, u32[]{:S(2)}) collective-permute-start(f32[8,768]{1,0:T(8,128)} %get-tuple-element.25), channel_id=1, source_target_pairs={{0,8},{1,3},{2,10},{3,1},{4,12},{5,7},{6,14},{7,5},{8,0},{9,11},{1... | collective-permute-start | bytes 73736 | tf_op jit(solution)/shard_map/ppermute | solution.py:517
  5.6 0.7 collective-permute-start.1
  6.3 6.7 %all-to-all-start = ((f32[16,8,128]{2,1,0:T(8,128)}), f32[16,8,128]{2,1,0:T(8,128)S(1)}, u32[]{:S(2)}, u32[]{:S(2)}) async-start(f32[16,8,128]{2,1,0:T(8,128)} %get-tuple-element.23), calls=%async_computation | async-start | bytes 131072 | tf_op jit(solution)/shard_map/all_to_all | solution.py:522
  13.0 0.0 collective-permute-done.refs_0_
  13.0 0.0 collective-permute-done.1.refs_1_
  13.0 0.0 copy-start
  13.1 0.9 %copy-done = f32[24,1536]{1,0:T(8,128)S(1)} copy-done((f32[24,1536]{1,0:T(8,128)S(1)}, f32[24,1536]{1,0:T(8,128)}, u32[]{:S(2)}) %copy-start) | copy-done | bytes 147480
  14.0 0.2 shard_map.92
  14.2 1.1 %collective-permute-start.2 = (f32[16,1536]{1,0:T(8,128)S(1)}, f32[16,1536]{1,0:T(8,128)S(1)}, u32[]{:S(2)}, u32[]{:S(2)}) collective-permute-start(f32[16,1536]{1,0:T(8,128)S(1)} %get-tuple-element.28.modes_ref), channel_id=1, source_target_pairs={{0,1},{1,0},{2,3},{3,2},{4,5},{5,4},{6,7},{7,6},{8,9},{9,8},{10,11... | collective-permute-start | bytes 294920 | tf_op jit(solution)/shard_map/ppermute | solution.py:526
  15.2 4.7 %all-to-all-done.shared = f32[16,8,128]{2,1,0:T(8,128)S(1)} async-done(((f32[16,8,128]{2,1,0:T(8,128)}), f32[16,8,128]{2,1,0:T(8,128)S(1)}, u32[]{:S(2)}, u32[]{:S(2)}) %all-to-all-start) | async-done | bytes 65568 | tf_op jit(solution)/shard_map/all_to_all | solution.py:522
  19.9 0.0 collective-permute-done.2.modes_rest
  19.9 5.7 %shard_map.93 = (f32[8,768]{1,0:T(8,128)S(1)}, f32[8,768]{1,0:T(8,128)S(1)}, f32[32,8,128]{2,1,0:T(8,128)}, f32[8,3072]{1,0:T(8,128)S(1)}) custom-call(bf16[192,8,3072]{2,1,0:T(8,128)(2,1)} %bitcast.4, f32[16,8,128]{2,1,0:T(8,128)S(1)} %all-to-all-done.shared, f32[8,1536]{1,0:T(8,128)S(1)} %get-tuple-element.27.right, ...), custom_call_target="tpu_custom_call" | custom-call | tf_op jit(solution)/shard_map/pallas_call | solution.py:488
  25.6 4.6 %all-to-all-start.1 = ((f32[32,8,128]{2,1,0:T(8,128)}), f32[32,8,128]{2,1,0:T(8,128)S(1)}, u32[]{:S(2)}, u32[]{:S(2)}) async-start(f32[32,8,128]{2,1,0:T(8,128)} %get-tuple-element.29), calls=%async_computation.1 | async-start | bytes 262144 | tf_op jit(solution)/shard_map/all_to_all | solution.py:522
  30.2 1.8 %collective-permute-start.3 = (f32[8,768]{1,0:T(8,128)S(1)}, f32[8,768]{1,0:T(8,128)S(1)}, u32[]{:S(2)}, u32[]{:S(2)}) collective-permute-start(f32[8,768]{1,0:T(8,128)S(1)} %get-tuple-element.30.refs_0_), channel_id=1, source_target_pairs={{0,8},{1,3},{2,10},{3,1},{4,12},{5,7},{6,14},{7,5},{8,0},{9,11},{1... | collective-permute-start | bytes 73736 | tf_op jit(solution)/shard_map/ppermute | solution.py:517
  32.0 0.7 collective-permute-start.4
  32.7 1.8 %collective-permute-done.3.refs_2_ = f32[8,768]{1,0:T(8,128)S(1)} collective-permute-done((f32[8,768]{1,0:T(8,128)S(1)}, f32[8,768]{1,0:T(8,128)S(1)}, u32[]{:S(2)}, u32[]{:S(2)}) %collective-permute-start.3) | collective-permute-done | bytes 24608 | tf_op jit(solution)/shard_map/ppermute | solution.py:517
  34.5 0.0 collective-permute-done.4.refs_3_
  34.5 0.2 shard_map.94.gap
  34.8 0.1 collective-permute-start.5
  34.8 4.1 %collective-permute-done.5.gap_rest = f32[8,1536]{1,0:T(8,128)S(1)} collective-permute-done((f32[8,1536]{1,0:T(8,128)S(1)}, f32[8,1536]{1,0:T(8,128)S(1)}, u32[]{:S(2)}, u32[]{:S(2)}) %collective-permute-start.5) | collective-permute-done | bytes 49184 | tf_op jit(solution)/shard_map/ppermute | solution.py:526
  38.9 0.0 all-to-all-done.1.pieces.before
  38.9 6.2 %shard_map.95 = (f32[8,768]{1,0:T(8,128)S(1)}, f32[8,768]{1,0:T(8,128)S(1)}, f32[32,8,128]{2,1,0:T(8,128)}, f32[8,3072]{1,0:T(8,128)S(1)}, f32[8,3072]{1,0:T(8,128)S(1)}) custom-call(bf16[192,8,3072]{2,1,0:T(8,128)(2,1)} %bitcast.5, f32[32,8,128]{2,1,0:T(8,128)S(1)} %all-to-all-done.1.pieces.before, f32[16,8,128]{2,1,0:T(8,128)S(1)} %all-to-all-done.shared, ...), custom_call_target="tpu_custom_call" | custom-call | tf_op jit(solution)/shard_map/pallas_call | solution.py:488
  45.1 6.9 %all-to-all-start.2 = ((f32[32,8,128]{2,1,0:T(8,128)}), f32[32,8,128]{2,1,0:T(8,128)S(1)}, u32[]{:S(2)}, u32[]{:S(2)}) async-start(f32[32,8,128]{2,1,0:T(8,128)} %get-tuple-element.32), calls=%async_computation.2 | async-start | bytes 262144 | tf_op jit(solution)/shard_map/all_to_all | solution.py:522
  52.1 1.8 %collective-permute-start.6 = (f32[8,768]{1,0:T(8,128)S(1)}, f32[8,768]{1,0:T(8,128)S(1)}, u32[]{:S(2)}, u32[]{:S(2)}) collective-permute-start(f32[8,768]{1,0:T(8,128)S(1)} %get-tuple-element.35.refs_0_), channel_id=1, source_target_pairs={{0,8},{1,3},{2,10},{3,1},{4,12},{5,7},{6,14},{7,5},{8,0},{9,11},{1... | collective-permute-start | bytes 73736 | tf_op jit(solution)/shard_map/ppermute | solution.py:517
  53.9 0.7 collective-permute-start.7
  54.6 1.8 %collective-permute-done.6.refs_2_ = f32[8,768]{1,0:T(8,128)S(1)} collective-permute-done((f32[8,768]{1,0:T(8,128)S(1)}, f32[8,768]{1,0:T(8,128)S(1)}, u32[]{:S(2)}, u32[]{:S(2)}) %collective-permute-start.6) | collective-permute-done | bytes 24608 | tf_op jit(solution)/shard_map/ppermute | solution.py:517
  56.4 0.0 collective-permute-done.7.refs_3_
  56.4 0.2 shard_map.96.image
  56.6 0.1 collective-permute-start.8
  56.7 4.1 %collective-permute-done.8.image_rest = f32[8,1536]{1,0:T(8,128)S(1)} collective-permute-done((f32[8,1536]{1,0:T(8,128)S(1)}, f32[8,1536]{1,0:T(8,128)S(1)}, u32[]{:S(2)}, u32[]{:S(2)}) %collective-permute-start.8) | collective-permute-done | bytes 49184 | tf_op jit(solution)/shard_map/ppermute | solution.py:526
  60.8 0.0 all-to-all-done.2.pieces
  60.8 5.6 %shard_map.97 = (f32[32,1,128]{2,1,0:T(1,128)S(1)}, f32[8,3072]{1,0:T(8,128)S(1)}, f32[8,128]{1,0:T(8,128)S(1)}) custom-call(bf16[192,8,3072]{2,1,0:T(8,128)(2,1)} %bitcast.6, f32[32,8,128]{2,1,0:T(8,128)S(1)} %all-to-all-done.2.pieces, f32[16,8,128]{2,1,0:T(8,128)S(1)} %all-to-all-done.shared, f32[32,8,128]{2,1,0:T(8,128)S(1)} %all-to-all-done.1.pieces.before, ...), custom_call_target="tpu_custom_call" | custom-call | tf_op jit(solution)/shard_map/pallas_call | solution.py:488
  66.3 13.9 %all_to_all.20.pieces = f32[32,1,128]{2,1,0:T(1,128)S(1)} all-to-all(f32[32,1,128]{2,1,0:T(1,128)S(1)} %get-tuple-element.37), channel_id=1, replica_groups=mesh['gx'=4,'gy'=4,'gz'=2] {'gx','gy','gz'}, dimensions={0} | all-to-all | bytes 32768 | tf_op jit(solution)/shard_map/all_to_all | solution.py:522
  80.3 0.8 %shard_map.98 = f32[1,1,8,3072]{3,2,1,0:T(8,128)} custom-call(f32[32,1,128]{2,1,0:T(1,128)S(1)} %all_to_all.20.pieces, f32[8,128]{1,0:T(8,128)S(1)} %get-tuple-element.38.scalars, f32[8,3072]{1,0:T(8,128)S(1)} %get-tuple-element.39.estimate, f32[8,3072]{1,0:T(8,128)S(1)} %get-tuple-element.34.direction_ref.direction, f32[8,3072]{1,0:T(8,128)S(1)} %get-tuple-element.40.later), custom_call_target="tpu_custom_call" | custom-call | tf_op jit(solution)/shard_map/pallas_call | solution.py:488
Async XLA Ops:
  2.5 10.5 %collective-permute-start = (f32[8,768]{1,0:T(8,128)}, f32[8,768]{1,0:T(8,128)S(1)}, u32[]{:S(2)}, u32[]{:S(2)}) collective-permute-start(f32[8,768]{1,0:T(8,128)} %get-tuple-element.25), channel_id=1, source_target_pairs={{0,8},{1,3},{2,10},{3,1},{4,12},{5,7},{6,14},{7,5},{8,0},{9,11},{1... | collective-permute-start | bytes 73736 | tf_op jit(solution)/shard_map/ppermute | solution.py:517
  5.6 7.4 %collective-permute-start.1 = (f32[8,768]{1,0:T(8,128)}, f32[8,768]{1,0:T(8,128)S(1)}, u32[]{:S(2)}, u32[]{:S(2)}) collective-permute-start(f32[8,768]{1,0:T(8,128)} %get-tuple-element.26), channel_id=1, source_target_pairs={{3,5},{5,3},{8,16},{10,18},{11,13},{12,20},{13,11},{14,22},{16,8},... | collective-permute-start | bytes 73736 | tf_op jit(solution)/shard_map/ppermute | solution.py:517
  6.3 13.7 %all-to-all-start = ((f32[16,8,128]{2,1,0:T(8,128)}), f32[16,8,128]{2,1,0:T(8,128)S(1)}, u32[]{:S(2)}, u32[]{:S(2)}) async-start(f32[16,8,128]{2,1,0:T(8,128)} %get-tuple-element.23), calls=%async_computation | async-start | bytes 131072 | tf_op jit(solution)/shard_map/all_to_all | solution.py:522
  13.0 0.9 %copy-start = (f32[24,1536]{1,0:T(8,128)S(1)}, f32[24,1536]{1,0:T(8,128)}, u32[]{:S(2)}) copy-start(f32[24,1536]{1,0:T(8,128)} %get-tuple-element.24.base) | copy-start | bytes 442372
  14.2 5.7 %collective-permute-start.2 = (f32[16,1536]{1,0:T(8,128)S(1)}, f32[16,1536]{1,0:T(8,128)S(1)}, u32[]{:S(2)}, u32[]{:S(2)}) collective-permute-start(f32[16,1536]{1,0:T(8,128)S(1)} %get-tuple-element.28.modes_ref), channel_id=1, source_target_pairs={{0,1},{1,0},{2,3},{3,2},{4,5},{5,4},{6,7},{7,6},{8,9},{9,8},{10,11... | collective-permute-start | bytes 294920 | tf_op jit(solution)/shard_map/ppermute | solution.py:526
  25.6 13.3 %all-to-all-start.1 = ((f32[32,8,128]{2,1,0:T(8,128)}), f32[32,8,128]{2,1,0:T(8,128)S(1)}, u32[]{:S(2)}, u32[]{:S(2)}) async-start(f32[32,8,128]{2,1,0:T(8,128)} %get-tuple-element.29), calls=%async_computation.1 | async-start | bytes 262144 | tf_op jit(solution)/shard_map/all_to_all | solution.py:522
  30.2 4.3 %collective-permute-start.3 = (f32[8,768]{1,0:T(8,128)S(1)}, f32[8,768]{1,0:T(8,128)S(1)}, u32[]{:S(2)}, u32[]{:S(2)}) collective-permute-start(f32[8,768]{1,0:T(8,128)S(1)} %get-tuple-element.30.refs_0_), channel_id=1, source_target_pairs={{0,8},{1,3},{2,10},{3,1},{4,12},{5,7},{6,14},{7,5},{8,0},{9,11},{1... | collective-permute-start | bytes 73736 | tf_op jit(solution)/shard_map/ppermute | solution.py:517
  32.0 2.5 %collective-permute-start.4 = (f32[8,768]{1,0:T(8,128)S(1)}, f32[8,768]{1,0:T(8,128)S(1)}, u32[]{:S(2)}, u32[]{:S(2)}) collective-permute-start(f32[8,768]{1,0:T(8,128)S(1)} %get-tuple-element.31.refs_1_), channel_id=1, source_target_pairs={{3,5},{5,3},{8,16},{10,18},{11,13},{12,20},{13,11},{14,22},{16,8},... | collective-permute-start | bytes 73736 | tf_op jit(solution)/shard_map/ppermute | solution.py:517
  34.8 4.2 %collective-permute-start.5 = (f32[8,1536]{1,0:T(8,128)S(1)}, f32[8,1536]{1,0:T(8,128)S(1)}, u32[]{:S(2)}, u32[]{:S(2)}) collective-permute-start(f32[8,1536]{1,0:T(8,128)S(1)} %shard_map.94.gap), channel_id=1, source_target_pairs={{0,1},{1,0},{2,3},{3,2},{4,5},{5,4},{6,7},{7,6},{8,9},{9,8},{10,11... | collective-permute-start | bytes 147464 | tf_op jit(solution)/shard_map/ppermute | solution.py:526
  45.1 15.6 %all-to-all-start.2 = ((f32[32,8,128]{2,1,0:T(8,128)}), f32[32,8,128]{2,1,0:T(8,128)S(1)}, u32[]{:S(2)}, u32[]{:S(2)}) async-start(f32[32,8,128]{2,1,0:T(8,128)} %get-tuple-element.32), calls=%async_computation.2 | async-start | bytes 262144 | tf_op jit(solution)/shard_map/all_to_all | solution.py:522
  52.1 4.3 %collective-permute-start.6 = (f32[8,768]{1,0:T(8,128)S(1)}, f32[8,768]{1,0:T(8,128)S(1)}, u32[]{:S(2)}, u32[]{:S(2)}) collective-permute-start(f32[8,768]{1,0:T(8,128)S(1)} %get-tuple-element.35.refs_0_), channel_id=1, source_target_pairs={{0,8},{1,3},{2,10},{3,1},{4,12},{5,7},{6,14},{7,5},{8,0},{9,11},{1... | collective-permute-start | bytes 73736 | tf_op jit(solution)/shard_map/ppermute | solution.py:517
  53.9 2.5 %collective-permute-start.7 = (f32[8,768]{1,0:T(8,128)S(1)}, f32[8,768]{1,0:T(8,128)S(1)}, u32[]{:S(2)}, u32[]{:S(2)}) collective-permute-start(f32[8,768]{1,0:T(8,128)S(1)} %get-tuple-element.36.refs_1_), channel_id=1, source_target_pairs={{3,5},{5,3},{8,16},{10,18},{11,13},{12,20},{13,11},{14,22},{16,8},... | collective-permute-start | bytes 73736 | tf_op jit(solution)/shard_map/ppermute | solution.py:517
  56.6 4.2 %collective-permute-start.8 = (f32[8,1536]{1,0:T(8,128)S(1)}, f32[8,1536]{1,0:T(8,128)S(1)}, u32[]{:S(2)}, u32[]{:S(2)}) collective-permute-start(f32[8,1536]{1,0:T(8,128)S(1)} %shard_map.96.image), channel_id=1, source_target_pairs={{0,1},{1,0},{2,3},{3,2},{4,5},{5,4},{6,7},{7,6},{8,9},{9,8},{10,11... | collective-permute-start | bytes 147464 | tf_op jit(solution)/shard_map/ppermute | solution.py:526

commit v5 on v4

--- a/solution.py
+++ b/solution.py
@@ -307,7 +307,7 @@
 
 
 def modes_kernel(sz, base, *refs):
-    arrived, (modes_ref, right) = refs[: sz.own_faces], refs[sz.own_faces :]
+    arrived, (modes_ref, right, coupling) = refs[: sz.own_faces], refs[sz.own_faces :]
     right[...] = base[8:16, :]
     row = lax.broadcasted_iota(jnp.int32, (8, 1), 0)
     arrived = get_slots(sz, arrived)
@@ -321,20 +321,53 @@
         modes_ref[0:8, here] = jnp.where(row == 6, weight, jnp.where(row == 7, live, mine * live))
         slots_row = jnp.where(row == 6, base[16:24, here], 0.0)
         modes_ref[8:16, here] = jnp.where(row < sz.modes, other * live, slots_row)
-
-
-def assemble_kernel(sz, modes_ref, *refs):
+    weights = weights_of(sz, modes_ref)
+    coarse_rows = [
+        jnp.where(row < sz.modes, modes_ref[0:8, own_face(sz, j)] * weights[j], 0.0)
+        for j in range(sz.own_faces)
+    ]
+    tile = jnp.zeros((8, TILE), jnp.float32)
+    coupling[...] = mode_products(sz, tile, coarse_rows, modes_ref, 2 * MODE_SPAN)
+
+
+def assemble(sz, modes_ref, refs):
     own, arrived = get_slots(sz, refs[: sz.own_faces]), get_slots(sz, refs[sz.own_faces : -1])
-    out = refs[-1]
     for j in range(sz.own_faces):
         here = own_face(sz, j)
         other = permuted(sz, arrived[j], modes_ref[14:15, here])
-        out[:, here] = modes_ref[7:8, here] * (own[j] + other)
+        refs[-1][:, here] = modes_ref[7:8, here] * (own[j] + other)
+    return own
+
+
+def first_tile_kernel(sz, modes_ref, coupling, *refs):
+    vectors, pay = assemble(sz, modes_ref, refs[:-1]), refs[-1]
+    tile = mode_products(sz, coupling[...], vectors, modes_ref, 0)
+    scaled = [v * w for v, w in zip(vectors, weights_of(sz, modes_ref))]
+    spread(pay, mode_products(sz, tile, scaled, modes_ref, MODE_SPAN))
+
+
+def second_tile_kernel(sz, modes_ref, residual_ref, direction_ref, *refs):
+    pieces, pay = assemble(sz, modes_ref, refs[:-1]), refs[-1]
+    weights = weights_of(sz, modes_ref)
+    gz = lax.axis_index("gz")
+    lane = lanes()
+    curvature = jnp.zeros((8, 1), jnp.float32)
+    resid_dot = jnp.zeros((8, 1), jnp.float32)
+    for j, piece in enumerate(pieces):
+        own = residual_ref[:, face_slots(sz, gz, j)]
+        resid_dot += jnp.sum(own * (weights[j] * own), axis=1, keepdims=True)
+        direction = direction_ref[:, face_slots(sz, gz, j)]
+        curvature += jnp.sum(direction * piece, axis=1, keepdims=True)
+    tile = jnp.where(lane == SCALARS, curvature, jnp.zeros((8, TILE), jnp.float32))
+    tile = jnp.where(lane == SCALARS + 1, resid_dot, tile)
+    tile = mode_products(sz, tile, pieces, modes_ref, 0)
+    scaled = [v * w for v, w in zip(pieces, weights)]
+    spread(pay, mode_products(sz, tile, scaled, modes_ref, MODE_SPAN))
 
 
 def first_kernel(sz, operator, shared, right, modes_ref, modes_rest, *refs):
     outs, refs = refs[: sz.own_faces], refs[sz.own_faces :]
-    pay, estimate_ref, inverse_ref, coarse_ref, held, product, vector, sems = refs
+    estimate_ref, inverse_ref, coarse_ref, held, product, vector, sems = refs
     stream = Stream(sz, operator, held, product, sems)
     fill_inverse(sz, shared, inverse_ref)
     turned = []
@@ -350,26 +383,14 @@
             estimate = mode_sum(sz, coarse_ref, mine, modes, part, j)
             estimate_ref[:, here] = estimate
             vector[:, here] = estimate.astype(jnp.bfloat16)
-    weights = weights_of(sz, modes_ref)
-    row = lax.broadcasted_iota(jnp.int32, (8, 1), 0)
-    coarse_rows = [
-        jnp.where(row < sz.modes, modes_ref[0:8, own_face(sz, j)] * weights[j], 0.0)
-        for j in range(sz.own_faces)
-    ]
-    tile = jnp.zeros((8, TILE), jnp.float32)
-    tile = mode_products(sz, tile, coarse_rows, modes_ref, 2 * MODE_SPAN)
     pieces = stream.apply(vector)
-    vectors = [right[:, own_face(sz, j)] - piece for j, piece in enumerate(pieces)]
-    put_slots(sz, outs, vectors)
-    tile = mode_products(sz, tile, vectors, modes_ref, 0)
-    scaled = [v * w for v, w in zip(vectors, weights)]
-    spread(pay, mode_products(sz, tile, scaled, modes_ref, MODE_SPAN))
+    put_slots(sz, outs, [right[:, own_face(sz, j)] - piece for j, piece in enumerate(pieces)])
 
 
 def second_kernel(sz, operator, pieces, shared, modes_ref, modes_rest, gap, gap_rest, *refs):
     outs, refs = refs[: sz.own_faces], refs[sz.own_faces :]
-    pay, residual_ref, direction_ref = refs[:3]
-    inverse_ref, coupling_ref, coarse_a, coarse_b, held, product, vector, sems = refs[3:]
+    residual_ref, direction_ref, inverse_ref, coupling_ref, *refs = refs
+    coarse_a, coarse_b, held, product, vector, sems = refs
     stream = Stream(sz, operator, held, product, sems)
     fill_inverse(sz, shared, inverse_ref)
     tiles = [sub_tile(sz, pieces, sub) for sub in range(sz.subs)]
@@ -386,24 +407,7 @@
             residual_ref[:, here] = residual
             direction_ref[:, here] = direction
             vector[:, here] = direction.astype(jnp.bfloat16)
-    weights = weights_of(sz, modes_ref)
-    gz = lax.axis_index("gz")
-    lane = lanes()
-    curvature = jnp.zeros((8, 1), jnp.float32)
-    resid_dot = jnp.zeros((8, 1), jnp.float32)
-    for j in range(sz.own_faces):
-        own = residual_ref[:, face_slots(sz, gz, j)]
-        resid_dot += jnp.sum(own * (weights[j] * own), axis=1, keepdims=True)
-    pieces = stream.apply(vector)
-    put_slots(sz, outs, pieces)
-    for j, piece in enumerate(pieces):
-        direction = direction_ref[:, face_slots(sz, gz, j)]
-        curvature += jnp.sum(direction * piece, axis=1, keepdims=True)
-    tile = jnp.where(lane == SCALARS, curvature, jnp.zeros((8, TILE), jnp.float32))
-    tile = jnp.where(lane == SCALARS + 1, resid_dot, tile)
-    tile = mode_products(sz, tile, pieces, modes_ref, 0)
-    scaled = [v * w for v, w in zip(pieces, weights)]
-    spread(pay, mode_products(sz, tile, scaled, modes_ref, MODE_SPAN))
+    put_slots(sz, outs, stream.apply(vector))
 
 
 def third_kernel(
@@ -526,11 +530,10 @@
             return lax.ppermute(part, "gz", [(0, 1), (1, 0)])
         return lax.all_gather(part, "gz", axis=0, tiled=False)
 
-    def assemble(own):
-        part = call(
-            assemble_kernel, half, [vmem] * (1 + 2 * faces), [], modes, *own, *swap(own)
-        )
-        return part, rest(part)
+    def tile(kernel, own, *operands):
+        operands = operands + tuple(own) + tuple(swap(own))
+        part, pay = call(kernel, [half, spread_tile], [vmem] * len(operands), [], *operands)
+        return share(pay, everywhere), part, rest(part)
 
     *own, pay, base = call(
         start_kernel,
@@ -551,24 +554,22 @@
         face_lengths, mode_count, limit=60,
     )
     shared = share(pay, ("gx", "gy"))
-    modes, right = call(
-        modes_kernel, [f32(16, sz.rows), half], [vmem] * (1 + faces), [], base, *swap(own)
+    modes, right, coupling = call(
+        modes_kernel, [f32(16, sz.rows), half, f32(8, TILE)], [vmem] * (1 + faces), [], base, *swap(own)
     )
     modes_rest = rest(modes)
-    *own, pay, estimate = call(
-        first_kernel, [face] * faces + [spread_tile, full], [hbm] + [vmem] * 4,
+    *own, estimate = call(
+        first_kernel, [face] * faces + [full], [hbm] + [vmem] * 4,
         [square, coarse] + apply_scratch,
         blocks, shared, right, modes, modes_rest, limit=large,
     )
-    before = share(pay, everywhere)
-    gap, gap_rest = assemble(own)
-    *own, pay, residual, direction = call(
-        second_kernel, [face] * faces + [spread_tile, full, full], [hbm] + [vmem] * 6,
+    before, gap, gap_rest = tile(first_tile_kernel, own, modes, coupling)
+    *own, residual, direction = call(
+        second_kernel, [face] * faces + [full, full], [hbm] + [vmem] * 6,
         [square, square, coarse, coarse] + apply_scratch,
         blocks, before, shared, modes, modes_rest, gap, gap_rest, limit=large,
     )
-    after = share(pay, everywhere)
-    image, image_rest = assemble(own)
+    after, image, image_rest = tile(second_tile_kernel, own, modes, residual, direction)
     pay, later, scalars = call(
         third_kernel,
         [f32(sz.devices if one_step else 1, 1, TILE), full, f32(8, TILE)],

time: 81.5 us -> 84.2 us (1.033)
  waiting for transfers between devices: 16.5 us -> 23.2 us
  blocking collectives: 13.9 us -> 8.89 us
    all_to_all x3, waiting for transfers between devices: 4.68 us -> 12.6 us  [share(): return lax.all_to_all(chunk, axes, split_axis=0, concat_axis=0, tiled=True)]
    all_to_all x1, blocking collectives: 13.9 us -> 8.89 us  [share(): return lax.all_to_all(chunk, axes, split_axis=0, concat_axis=0, tiled=True)]
    ppermute x3, starting transfers between devices: 1.19 us -> 4.72 us  [rest(): return lax.ppermute(part, 'gz', [(0, 1), (1, 0)])]
    ppermute x3, waiting for transfers between devices: 8.16 us -> 5.48 us  [rest(): return lax.ppermute(part, 'gz', [(0, 1), (1, 0)])]
    ppermute x6, starting transfers between devices: 8.71 us -> 6.43 us  [swap(): lax.ppermute(own[j], everywhere, face_pairs(sz, j))]
    ppermute x6, waiting for transfers between devices: 3.68 us -> 5.08 us  [swap(): lax.ppermute(own[j], everywhere, face_pairs(sz, j))]
  transfers between devices with their start and end apart: 12 -> 12, of which waited for: 5 -> 7; matrix products, arithmetic and copies ran while one was open for 0% -> 0% of each run, Pallas kernels for 1% -> 0%
where the time goes in v5:
time: 84.2 us; the launch traced here: 83.8 us
  starting transfers between devices  28.9 us (34%)
  waiting for transfers between devices  23.2 us (28%)
  Pallas kernels  21.1 us (25%)
  blocking collectives  8.89 us (11%)
  local copies, waits for them, and re-layouts  0.9 us (1%)
    pallas_call x8, Pallas kernels, call(): pl.pallas_call(functools.partial(kernel, sz), out_shape=out_shape, in_spe...  21.1 us
    all_to_all x3, starting transfers between devices, share(): return lax.all_to_all(chunk, axes, split_axis=0, concat_axis=0, tiled=True)  17.8 us
    all_to_all x3, waiting for transfers between devices, share(): return lax.all_to_all(chunk, axes, split_axis=0, concat_axis=0, tiled=True)  12.6 us
    all_to_all x1, blocking collectives, share(): return lax.all_to_all(chunk, axes, split_axis=0, concat_axis=0, tiled=True)  8.89 us
    ppermute x6, starting transfers between devices, swap(): lax.ppermute(own[j], everywhere, face_pairs(sz, j))  6.43 us
    ppermute x3, waiting for transfers between devices, rest(): return lax.ppermute(part, 'gz', [(0, 1), (1, 0)])  5.48 us
    ppermute x6, waiting for transfers between devices, swap(): lax.ppermute(own[j], everywhere, face_pairs(sz, j))  5.08 us
    ppermute x3, starting transfers between devices, rest(): return lax.ppermute(part, 'gz', [(0, 1), (1, 0)])  4.72 us
  transfers between devices with their start and end apart: 12, of which 7 were waited for; matrix products, arithmetic and copies ran while one was open for 0% of the time, Pallas kernels for 0%

profile of v5, /device:TPU:0, one launch (start us, length us, event | category | flops | bytes accessed | tf_op | source)
XLA Modules:
  0.0 83.8 jit_solution(18095046354177089977)
XLA Ops:
  0.7 1.9 %shard_map.91 = (f32[8,768]{1,0:T(8,128)}, f32[8,768]{1,0:T(8,128)}, f32[16,8,128]{2,1,0:T(8,128)}, f32[24,1536]{1,0:T(8,128)}) custom-call(f32[6,1,3072]{2,1,0:T(1,128)} %bitcast.7, f32[6,1,8]{2,1,0:T(1,128)} %bitcast.8, f32[6,1,96]{2,1,0:T(1,128)} %bitcast.9, f32[1,1,3072]{2,1,0:T(1,128)} %stiffness.1, s32[1,1,4,768]{3,2,1,0:T(4,128)} %orders.1, ...), custom_call_target="tpu_custom_call" | custom-call | tf_op jit(solution)/shard_map/pallas_call | solution.py:492
  2.5 3.1 %collective-permute-start = (f32[8,768]{1,0:T(8,128)}, f32[8,768]{1,0:T(8,128)S(1)}, u32[]{:S(2)}, u32[]{:S(2)}) collective-permute-start(f32[8,768]{1,0:T(8,128)} %get-tuple-element.27), channel_id=1, source_target_pairs={{0,8},{1,3},{2,10},{3,1},{4,12},{5,7},{6,14},{7,5},{8,0},{9,11},{1... | collective-permute-start | bytes 73736 | tf_op jit(solution)/shard_map/ppermute | solution.py:521
  5.6 0.7 collective-permute-start.1
  6.3 6.7 %all-to-all-start = ((f32[16,8,128]{2,1,0:T(8,128)}), f32[16,8,128]{2,1,0:T(8,128)S(1)}, u32[]{:S(2)}, u32[]{:S(2)}) async-start(f32[16,8,128]{2,1,0:T(8,128)} %get-tuple-element.31), calls=%async_computation | async-start | bytes 131072 | tf_op jit(solution)/shard_map/all_to_all | solution.py:526
  13.0 0.0 collective-permute-done.refs_0_
  13.0 0.0 collective-permute-done.1.refs_1_
  13.0 0.0 copy-start
  13.1 0.9 %copy-done = f32[24,1536]{1,0:T(8,128)S(1)} copy-done((f32[24,1536]{1,0:T(8,128)S(1)}, f32[24,1536]{1,0:T(8,128)}, u32[]{:S(2)}) %copy-start) | copy-done | bytes 147480
  14.0 0.4 shard_map.92
  14.3 1.1 %collective-permute-start.2 = (f32[16,1536]{1,0:T(8,128)S(1)}, f32[16,1536]{1,0:T(8,128)S(1)}, u32[]{:S(2)}, u32[]{:S(2)}) collective-permute-start(f32[16,1536]{1,0:T(8,128)S(1)} %get-tuple-element.29.modes_ref), channel_id=1, source_target_pairs={{0,1},{1,0},{2,3},{3,2},{4,5},{5,4},{6,7},{7,6},{8,9},{9,8},{10,11... | collective-permute-start | bytes 294920 | tf_op jit(solution)/shard_map/ppermute | solution.py:530
  15.4 4.5 %all-to-all-done.shared = f32[16,8,128]{2,1,0:T(8,128)S(1)} async-done(((f32[16,8,128]{2,1,0:T(8,128)}), f32[16,8,128]{2,1,0:T(8,128)S(1)}, u32[]{:S(2)}, u32[]{:S(2)}) %all-to-all-start) | async-done | bytes 65568 | tf_op jit(solution)/shard_map/all_to_all | solution.py:526
  19.9 0.0 collective-permute-done.2.modes_rest
  19.9 4.9 %shard_map.93 = (f32[8,768]{1,0:T(8,128)S(1)}, f32[8,768]{1,0:T(8,128)S(1)}, f32[8,3072]{1,0:T(8,128)S(1)}) custom-call(bf16[192,8,3072]{2,1,0:T(8,128)(2,1)} %bitcast.4, f32[16,8,128]{2,1,0:T(8,128)S(1)} %all-to-all-done.shared, f32[8,1536]{1,0:T(8,128)S(1)} %get-tuple-element.32.right, f32[16,1536]{1,0:T(8,128)S(1)} %get-tuple-element.29.modes_ref, ...), custom_call_target="tpu_custom_call" | custom-call | tf_op jit(solution)/shard_map/pallas_call | solution.py:492
  24.8 1.3 %collective-permute-start.3 = (f32[8,768]{1,0:T(8,128)S(1)}, f32[8,768]{1,0:T(8,128)S(1)}, u32[]{:S(2)}, u32[]{:S(2)}) collective-permute-start(f32[8,768]{1,0:T(8,128)S(1)} %get-tuple-element.33.refs_0_), channel_id=1, source_target_pairs={{0,8},{1,3},{2,10},{3,1},{4,12},{5,7},{6,14},{7,5},{8,0},{9,11},{1... | collective-permute-start | bytes 73736 | tf_op jit(solution)/shard_map/ppermute | solution.py:521
  26.1 0.7 collective-permute-start.4
  26.8 1.9 %collective-permute-done.3.refs_2_ = f32[8,768]{1,0:T(8,128)S(1)} collective-permute-done((f32[8,768]{1,0:T(8,128)S(1)}, f32[8,768]{1,0:T(8,128)S(1)}, u32[]{:S(2)}, u32[]{:S(2)}) %collective-permute-start.3) | collective-permute-done | bytes 24608 | tf_op jit(solution)/shard_map/ppermute | solution.py:521
  28.7 0.0 collective-permute-done.4.refs_3_
  28.7 0.9 %shard_map.94 = (f32[8,1536]{1,0:T(8,128)S(1)}, f32[32,8,128]{2,1,0:T(8,128)}) custom-call(f32[16,1536]{1,0:T(8,128)S(1)} %get-tuple-element.29.modes_ref, f32[8,128]{1,0:T(8,128)S(1)} %get-tuple-element.30.coupling, f32[8,768]{1,0:T(8,128)S(1)} %get-tuple-element.33.refs_0_, f32[8,768]{1,0:T(8,128)S(1)} %get-tuple-element.34.refs_1_, ...), custom_call_target="tpu_custom_call" | custom-call | tf_op jit(solution)/shard_map/pallas_call | solution.py:492
  29.7 6.8 %all-to-all-start.1 = ((f32[32,8,128]{2,1,0:T(8,128)}), f32[32,8,128]{2,1,0:T(8,128)S(1)}, u32[]{:S(2)}, u32[]{:S(2)}) async-start(f32[32,8,128]{2,1,0:T(8,128)} %get-tuple-element.35), calls=%async_computation.1 | async-start | bytes 262144 | tf_op jit(solution)/shard_map/all_to_all | solution.py:526
  36.4 1.8 %collective-permute-start.5 = (f32[8,1536]{1,0:T(8,128)S(1)}, f32[8,1536]{1,0:T(8,128)S(1)}, u32[]{:S(2)}, u32[]{:S(2)}) collective-permute-start(f32[8,1536]{1,0:T(8,128)S(1)} %get-tuple-element.36.gap), channel_id=1, source_target_pairs={{0,1},{1,0},{2,3},{3,2},{4,5},{5,4},{6,7},{7,6},{8,9},{9,8},{10,11... | collective-permute-start | bytes 147464 | tf_op jit(solution)/shard_map/ppermute | solution.py:530
  38.3 2.7 %collective-permute-done.5.gap_rest = f32[8,1536]{1,0:T(8,128)S(1)} collective-permute-done((f32[8,1536]{1,0:T(8,128)S(1)}, f32[8,1536]{1,0:T(8,128)S(1)}, u32[]{:S(2)}, u32[]{:S(2)}) %collective-permute-start.5) | collective-permute-done | bytes 49184 | tf_op jit(solution)/shard_map/ppermute | solution.py:530
  41.0 4.1 %all-to-all-done.1.pieces.before = f32[32,8,128]{2,1,0:T(8,128)S(1)} async-done(((f32[32,8,128]{2,1,0:T(8,128)}), f32[32,8,128]{2,1,0:T(8,128)S(1)}, u32[]{:S(2)}, u32[]{:S(2)}) %all-to-all-start.1) | async-done | bytes 131104 | tf_op jit(solution)/shard_map/all_to_all | solution.py:526
  45.1 5.6 %shard_map.95 = (f32[8,768]{1,0:T(8,128)S(1)}, f32[8,768]{1,0:T(8,128)S(1)}, f32[8,3072]{1,0:T(8,128)S(1)}, f32[8,3072]{1,0:T(8,128)S(1)}) custom-call(bf16[192,8,3072]{2,1,0:T(8,128)(2,1)} %bitcast.5, f32[32,8,128]{2,1,0:T(8,128)S(1)} %all-to-all-done.1.pieces.before, f32[16,8,128]{2,1,0:T(8,128)S(1)} %all-to-all-done.shared, ...), custom_call_target="tpu_custom_call" | custom-call | tf_op jit(solution)/shard_map/pallas_call | solution.py:492
  50.7 0.1 collective-permute-start.6
  50.8 0.7 collective-permute-start.7
  51.5 3.1 %collective-permute-done.6.refs_2_ = f32[8,768]{1,0:T(8,128)S(1)} collective-permute-done((f32[8,768]{1,0:T(8,128)S(1)}, f32[8,768]{1,0:T(8,128)S(1)}, u32[]{:S(2)}, u32[]{:S(2)}) %collective-permute-start.6) | collective-permute-done | bytes 24608 | tf_op jit(solution)/shard_map/ppermute | solution.py:521
  54.6 0.0 collective-permute-done.7.refs_3_
  54.6 1.0 %shard_map.96 = (f32[8,1536]{1,0:T(8,128)S(1)}, f32[32,8,128]{2,1,0:T(8,128)}) custom-call(f32[16,1536]{1,0:T(8,128)S(1)} %get-tuple-element.29.modes_ref, f32[8,3072]{1,0:T(8,128)S(1)} %get-tuple-element.37.residual_ref, f32[8,3072]{1,0:T(8,128)S(1)} %get-tuple-element.38.direction_ref.direction, f32[8,768]{1,0:T(8,128)S(1)} %get-tuple-element.39.refs_0_, ...), custom_call_target="tpu_custom_call" | custom-call | tf_op jit(solution)/shard_map/pallas_call | solution.py:492
  55.6 4.3 %all-to-all-start.2 = ((f32[32,8,128]{2,1,0:T(8,128)}), f32[32,8,128]{2,1,0:T(8,128)S(1)}, u32[]{:S(2)}, u32[]{:S(2)}) async-start(f32[32,8,128]{2,1,0:T(8,128)} %get-tuple-element.41), calls=%async_computation.2 | async-start | bytes 262144 | tf_op jit(solution)/shard_map/all_to_all | solution.py:526
  59.8 1.8 %collective-permute-start.8 = (f32[8,1536]{1,0:T(8,128)S(1)}, f32[8,1536]{1,0:T(8,128)S(1)}, u32[]{:S(2)}, u32[]{:S(2)}) collective-permute-start(f32[8,1536]{1,0:T(8,128)S(1)} %get-tuple-element.42.image), channel_id=1, source_target_pairs={{0,1},{1,0},{2,3},{3,2},{4,5},{5,4},{6,7},{7,6},{8,9},{9,8},{10,11... | collective-permute-start | bytes 147464 | tf_op jit(solution)/shard_map/ppermute | solution.py:530
  61.7 2.7 %collective-permute-done.8.image_rest = f32[8,1536]{1,0:T(8,128)S(1)} collective-permute-done((f32[8,1536]{1,0:T(8,128)S(1)}, f32[8,1536]{1,0:T(8,128)S(1)}, u32[]{:S(2)}, u32[]{:S(2)}) %collective-permute-start.8) | collective-permute-done | bytes 49184 | tf_op jit(solution)/shard_map/ppermute | solution.py:530
  64.4 4.1 %all-to-all-done.2.pieces = f32[32,8,128]{2,1,0:T(8,128)S(1)} async-done(((f32[32,8,128]{2,1,0:T(8,128)}), f32[32,8,128]{2,1,0:T(8,128)S(1)}, u32[]{:S(2)}, u32[]{:S(2)}) %all-to-all-start.2) | async-done | bytes 131104 | tf_op jit(solution)/shard_map/all_to_all | solution.py:526
  68.5 5.6 %shard_map.97 = (f32[32,1,128]{2,1,0:T(1,128)S(1)}, f32[8,3072]{1,0:T(8,128)S(1)}, f32[8,128]{1,0:T(8,128)S(1)}) custom-call(bf16[192,8,3072]{2,1,0:T(8,128)(2,1)} %bitcast.6, f32[32,8,128]{2,1,0:T(8,128)S(1)} %all-to-all-done.2.pieces, f32[16,8,128]{2,1,0:T(8,128)S(1)} %all-to-all-done.shared, f32[32,8,128]{2,1,0:T(8,128)S(1)} %all-to-all-done.1.pieces.before, ...), custom_call_target="tpu_custom_call" | custom-call | tf_op jit(solution)/shard_map/pallas_call | solution.py:492
  74.0 8.9 %all_to_all.20.pieces = f32[32,1,128]{2,1,0:T(1,128)S(1)} all-to-all(f32[32,1,128]{2,1,0:T(1,128)S(1)} %get-tuple-element.43), channel_id=1, replica_groups=mesh['gx'=4,'gy'=4,'gz'=2] {'gx','gy','gz'}, dimensions={0} | all-to-all | bytes 32768 | tf_op jit(solution)/shard_map/all_to_all | solution.py:526
  82.9 0.8 %shard_map.98 = f32[1,1,8,3072]{3,2,1,0:T(8,128)} custom-call(f32[32,1,128]{2,1,0:T(1,128)S(1)} %all_to_all.20.pieces, f32[8,128]{1,0:T(8,128)S(1)} %get-tuple-element.44.scalars, f32[8,3072]{1,0:T(8,128)S(1)} %get-tuple-element.45.estimate, f32[8,3072]{1,0:T(8,128)S(1)} %get-tuple-element.38.direction_ref.direction, f32[8,3072]{1,0:T(8,128)S(1)} %get-tuple-element.46.later), custom_call_target="tpu_custom_call" | custom-call | tf_op jit(solution)/shard_map/pallas_call | solution.py:492
Async XLA Ops:
  2.5 10.5 %collective-permute-start = (f32[8,768]{1,0:T(8,128)}, f32[8,768]{1,0:T(8,128)S(1)}, u32[]{:S(2)}, u32[]{:S(2)}) collective-permute-start(f32[8,768]{1,0:T(8,128)} %get-tuple-element.27), channel_id=1, source_target_pairs={{0,8},{1,3},{2,10},{3,1},{4,12},{5,7},{6,14},{7,5},{8,0},{9,11},{1... | collective-permute-start | bytes 73736 | tf_op jit(solution)/shard_map/ppermute | solution.py:521
  5.6 7.4 %collective-permute-start.1 = (f32[8,768]{1,0:T(8,128)}, f32[8,768]{1,0:T(8,128)S(1)}, u32[]{:S(2)}, u32[]{:S(2)}) collective-permute-start(f32[8,768]{1,0:T(8,128)} %get-tuple-element.28), channel_id=1, source_target_pairs={{3,5},{5,3},{8,16},{10,18},{11,13},{12,20},{13,11},{14,22},{16,8},... | collective-permute-start | bytes 73736 | tf_op jit(solution)/shard_map/ppermute | solution.py:521
  6.3 13.7 %all-to-all-start = ((f32[16,8,128]{2,1,0:T(8,128)}), f32[16,8,128]{2,1,0:T(8,128)S(1)}, u32[]{:S(2)}, u32[]{:S(2)}) async-start(f32[16,8,128]{2,1,0:T(8,128)} %get-tuple-element.31), calls=%async_computation | async-start | bytes 131072 | tf_op jit(solution)/shard_map/all_to_all | solution.py:526
  13.0 0.9 %copy-start = (f32[24,1536]{1,0:T(8,128)S(1)}, f32[24,1536]{1,0:T(8,128)}, u32[]{:S(2)}) copy-start(f32[24,1536]{1,0:T(8,128)} %get-tuple-element.26.base) | copy-start | bytes 442372
  14.3 5.6 %collective-permute-start.2 = (f32[16,1536]{1,0:T(8,128)S(1)}, f32[16,1536]{1,0:T(8,128)S(1)}, u32[]{:S(2)}, u32[]{:S(2)}) collective-permute-start(f32[16,1536]{1,0:T(8,128)S(1)} %get-tuple-element.29.modes_ref), channel_id=1, source_target_pairs={{0,1},{1,0},{2,3},{3,2},{4,5},{5,4},{6,7},{7,6},{8,9},{9,8},{10,11... | collective-permute-start | bytes 294920 | tf_op jit(solution)/shard_map/ppermute | solution.py:530
  24.8 3.9 %collective-permute-start.3 = (f32[8,768]{1,0:T(8,128)S(1)}, f32[8,768]{1,0:T(8,128)S(1)}, u32[]{:S(2)}, u32[]{:S(2)}) collective-permute-start(f32[8,768]{1,0:T(8,128)S(1)} %get-tuple-element.33.refs_0_), channel_id=1, source_target_pairs={{0,8},{1,3},{2,10},{3,1},{4,12},{5,7},{6,14},{7,5},{8,0},{9,11},{1... | collective-permute-start | bytes 73736 | tf_op jit(solution)/shard_map/ppermute | solution.py:521
  26.1 2.6 %collective-permute-start.4 = (f32[8,768]{1,0:T(8,128)S(1)}, f32[8,768]{1,0:T(8,128)S(1)}, u32[]{:S(2)}, u32[]{:S(2)}) collective-permute-start(f32[8,768]{1,0:T(8,128)S(1)} %get-tuple-element.34.refs_1_), channel_id=1, source_target_pairs={{3,5},{5,3},{8,16},{10,18},{11,13},{12,20},{13,11},{14,22},{16,8},... | collective-permute-start | bytes 73736 | tf_op jit(solution)/shard_map/ppermute | solution.py:521
  29.7 15.4 %all-to-all-start.1 = ((f32[32,8,128]{2,1,0:T(8,128)}), f32[32,8,128]{2,1,0:T(8,128)S(1)}, u32[]{:S(2)}, u32[]{:S(2)}) async-start(f32[32,8,128]{2,1,0:T(8,128)} %get-tuple-element.35), calls=%async_computation.1 | async-start | bytes 262144 | tf_op jit(solution)/shard_map/all_to_all | solution.py:526
  36.4 4.6 %collective-permute-start.5 = (f32[8,1536]{1,0:T(8,128)S(1)}, f32[8,1536]{1,0:T(8,128)S(1)}, u32[]{:S(2)}, u32[]{:S(2)}) collective-permute-start(f32[8,1536]{1,0:T(8,128)S(1)} %get-tuple-element.36.gap), channel_id=1, source_target_pairs={{0,1},{1,0},{2,3},{3,2},{4,5},{5,4},{6,7},{7,6},{8,9},{9,8},{10,11... | collective-permute-start | bytes 147464 | tf_op jit(solution)/shard_map/ppermute | solution.py:530
  50.7 3.9 %collective-permute-start.6 = (f32[8,768]{1,0:T(8,128)S(1)}, f32[8,768]{1,0:T(8,128)S(1)}, u32[]{:S(2)}, u32[]{:S(2)}) collective-permute-start(f32[8,768]{1,0:T(8,128)S(1)} %get-tuple-element.39.refs_0_), channel_id=1, source_target_pairs={{0,8},{1,3},{2,10},{3,1},{4,12},{5,7},{6,14},{7,5},{8,0},{9,11},{1... | collective-permute-start | bytes 73736 | tf_op jit(solution)/shard_map/ppermute | solution.py:521
  50.8 3.8 %collective-permute-start.7 = (f32[8,768]{1,0:T(8,128)S(1)}, f32[8,768]{1,0:T(8,128)S(1)}, u32[]{:S(2)}, u32[]{:S(2)}) collective-permute-start(f32[8,768]{1,0:T(8,128)S(1)} %get-tuple-element.40.refs_1_), channel_id=1, source_target_pairs={{3,5},{5,3},{8,16},{10,18},{11,13},{12,20},{13,11},{14,22},{16,8},... | collective-permute-start | bytes 73736 | tf_op jit(solution)/shard_map/ppermute | solution.py:521
  55.6 12.9 %all-to-all-start.2 = ((f32[32,8,128]{2,1,0:T(8,128)}), f32[32,8,128]{2,1,0:T(8,128)S(1)}, u32[]{:S(2)}, u32[]{:S(2)}) async-start(f32[32,8,128]{2,1,0:T(8,128)} %get-tuple-element.41), calls=%async_computation.2 | async-start | bytes 262144 | tf_op jit(solution)/shard_map/all_to_all | solution.py:526
  59.8 4.6 %collective-permute-start.8 = (f32[8,1536]{1,0:T(8,128)S(1)}, f32[8,1536]{1,0:T(8,128)S(1)}, u32[]{:S(2)}, u32[]{:S(2)}) collective-permute-start(f32[8,1536]{1,0:T(8,128)S(1)} %get-tuple-element.42.image), channel_id=1, source_target_pairs={{0,1},{1,0},{2,3},{3,2},{4,5},{5,4},{6,7},{7,6},{8,9},{9,8},{10,11... | collective-permute-start | bytes 147464 | tf_op jit(solution)/shard_map/ppermute | solution.py:530

commit v6 on v4

--- a/solution.py
+++ b/solution.py
@@ -231,32 +231,65 @@
     out[...] = jnp.broadcast_to(tile[None], out.shape)
 
 
+def front_chunks(sz):
+    return sz.rows // ROW_CHUNK * 2 // 3
+
+
 class Stream:
-    def __init__(self, sz, operator, held, product, sems):
+    def __init__(self, sz, operator, held, product, sems, front=None):
         self.sz, self.operator, self.held, self.product, self.sems = sz, operator, held, product, sems
-        for p in range(sz.rows // PIECE):
+        self.front, self.first = front, front_chunks(sz) if front is not None else 0
+        for p in range((sz.rows // ROW_CHUNK - self.first) * (ROW_CHUNK // PIECE)):
             self.copy(p).start()
 
     def copy(self, p):
-        here = pl.ds(p * (PIECE // 8), PIECE // 8)
-        return pltpu.make_async_copy(self.operator.at[here], self.held.at[here], self.sems.at[p])
+        blocks = PIECE // 8
+        source = pl.ds(self.first * (ROW_CHUNK // 8) + p * blocks, blocks)
+        target = self.held.at[pl.ds(p * blocks, blocks)]
+        return pltpu.make_async_copy(self.operator.at[source], target, self.sems.at[p])
+
+    def multiply(self, vector, rows, k):
+        part = lax.dot_general(
+            vector[...], rows.reshape(ROW_CHUNK, self.sz.order), (((1,), (1,)), ((), ())),
+            preferred_element_type=jnp.float32,
+        )
+        here = pl.ds(pl.multiple_of(k * ROW_CHUNK, TILE), ROW_CHUNK)
+        self.product[:, here] = part.astype(jnp.bfloat16).astype(jnp.float32)
 
     def apply(self, vector):
         sz, step, blocks = self.sz, ROW_CHUNK // PIECE, ROW_CHUNK // 8
+        for k in range(self.first):
+            self.multiply(vector, self.front[k * blocks : (k + 1) * blocks], k)
 
         def chunk(k, carry):
             for p in range(step):
                 self.copy(k * step + p).wait()
-            rows = self.held[pl.ds(k * blocks, blocks)].reshape(ROW_CHUNK, sz.order)
-            part = lax.dot_general(
-                vector[...], rows, (((1,), (1,)), ((), ())), preferred_element_type=jnp.float32
-            )
-            here = pl.ds(pl.multiple_of(k * ROW_CHUNK, TILE), ROW_CHUNK)
-            self.product[:, here] = part.astype(jnp.bfloat16).astype(jnp.float32)
+            self.multiply(vector, self.held[pl.ds(k * blocks, blocks)], self.first + k)
             return carry
 
-        lax.fori_loop(0, sz.rows // ROW_CHUNK, chunk, 0)
+        lax.fori_loop(0, sz.rows // ROW_CHUNK - self.first, chunk, 0)
         return [self.product[:, own_face(sz, j)] for j in range(sz.own_faces)]
+
+
+def hold_kernel(sz, operator, after, front, sems):
+    del after
+    blocks = ROW_CHUNK // 8
+    copies = []
+    for k in range(front_chunks(sz)):
+        here = pl.ds(k * blocks, blocks)
+        copies.append(pltpu.make_async_copy(operator.at[here], front.at[here], sems.at[k]))
+        copies[-1].start()
+    for copy in copies:
+        copy.wait()
+
+
+def part_slots(sz, part):
+    return pl.ds(pl.multiple_of(part * sz.rows, TILE), sz.rows)
+
+
+def put_parts(sz, own, rest, vector):
+    for part, ref in views(sz, own, rest):
+        vector[:, part_slots(sz, part)] = ref[...].astype(vector.dtype)
 
 
 def start_kernel(sz, traces, loads, inverse, stiffness, orders, rhs, lengths, count, *refs):
@@ -307,7 +340,7 @@
 
 
 def modes_kernel(sz, base, *refs):
-    arrived, (modes_ref, right) = refs[: sz.own_faces], refs[sz.own_faces :]
+    arrived, (modes_ref, right, coupling) = refs[: sz.own_faces], refs[sz.own_faces :]
     right[...] = base[8:16, :]
     row = lax.broadcasted_iota(jnp.int32, (8, 1), 0)
     arrived = get_slots(sz, arrived)
@@ -321,18 +354,27 @@
         modes_ref[0:8, here] = jnp.where(row == 6, weight, jnp.where(row == 7, live, mine * live))
         slots_row = jnp.where(row == 6, base[16:24, here], 0.0)
         modes_ref[8:16, here] = jnp.where(row < sz.modes, other * live, slots_row)
-
-
-def assemble_kernel(sz, modes_ref, *refs):
-    own, arrived = get_slots(sz, refs[: sz.own_faces]), get_slots(sz, refs[sz.own_faces : -1])
-    out = refs[-1]
-    for j in range(sz.own_faces):
-        here = own_face(sz, j)
-        other = permuted(sz, arrived[j], modes_ref[14:15, here])
-        out[:, here] = modes_ref[7:8, here] * (own[j] + other)
-
-
-def first_kernel(sz, operator, shared, right, modes_ref, modes_rest, *refs):
+    weights = weights_of(sz, modes_ref)
+    coarse_rows = [
+        jnp.where(row < sz.modes, modes_ref[0:8, own_face(sz, j)] * weights[j], 0.0)
+        for j in range(sz.own_faces)
+    ]
+    tile = jnp.zeros((8, TILE), jnp.float32)
+    coupling[...] = mode_products(sz, tile, coarse_rows, modes_ref, 2 * MODE_SPAN)
+
+
+def assembled(sz, own, arrived, modes_ref, j):
+    here = own_face(sz, j)
+    return modes_ref[7:8, here] * (own[j] + permuted(sz, arrived[j], modes_ref[14:15, here]))
+
+
+def tile_products(sz, tile, vectors, modes_ref):
+    tile = mode_products(sz, tile, vectors, modes_ref, 0)
+    scaled = [v * w for v, w in zip(vectors, weights_of(sz, modes_ref))]
+    return mode_products(sz, tile, scaled, modes_ref, MODE_SPAN)
+
+
+def first_kernel(sz, operator, shared, right, coupling, modes_ref, modes_rest, *refs):
     outs, refs = refs[: sz.own_faces], refs[sz.own_faces :]
     pay, estimate_ref, inverse_ref, coarse_ref, held, product, vector, sems = refs
     stream = Stream(sz, operator, held, product, sems)
@@ -350,70 +392,57 @@
             estimate = mode_sum(sz, coarse_ref, mine, modes, part, j)
             estimate_ref[:, here] = estimate
             vector[:, here] = estimate.astype(jnp.bfloat16)
-    weights = weights_of(sz, modes_ref)
-    row = lax.broadcasted_iota(jnp.int32, (8, 1), 0)
-    coarse_rows = [
-        jnp.where(row < sz.modes, modes_ref[0:8, own_face(sz, j)] * weights[j], 0.0)
-        for j in range(sz.own_faces)
-    ]
-    tile = jnp.zeros((8, TILE), jnp.float32)
-    tile = mode_products(sz, tile, coarse_rows, modes_ref, 2 * MODE_SPAN)
     pieces = stream.apply(vector)
     vectors = [right[:, own_face(sz, j)] - piece for j, piece in enumerate(pieces)]
     put_slots(sz, outs, vectors)
-    tile = mode_products(sz, tile, vectors, modes_ref, 0)
-    scaled = [v * w for v, w in zip(vectors, weights)]
-    spread(pay, mode_products(sz, tile, scaled, modes_ref, MODE_SPAN))
-
-
-def second_kernel(sz, operator, pieces, shared, modes_ref, modes_rest, gap, gap_rest, *refs):
-    outs, refs = refs[: sz.own_faces], refs[sz.own_faces :]
-    pay, residual_ref, direction_ref = refs[:3]
-    inverse_ref, coupling_ref, coarse_a, coarse_b, held, product, vector, sems = refs[3:]
-    stream = Stream(sz, operator, held, product, sems)
+    spread(pay, tile_products(sz, coupling[...], vectors, modes_ref))
+
+
+def second_kernel(sz, pieces, shared, modes_ref, *refs):
+    own, refs = get_slots(sz, refs[: sz.own_faces]), refs[sz.own_faces :]
+    arrived, refs = get_slots(sz, refs[: sz.own_faces]), refs[sz.own_faces :]
+    residual_ref, direction_ref, inverse_ref, coupling_ref, coarse_a, coarse_b = refs
+    gz = lax.axis_index("gz")
     fill_inverse(sz, shared, inverse_ref)
     tiles = [sub_tile(sz, pieces, sub) for sub in range(sz.subs)]
     fill_coupling(sz, tiles, coupling_ref)
     solve_pair(sz, tiles, inverse_ref, coupling_ref, coarse_a, coarse_b)
     first, second = own_coefficients(sz, coarse_a), own_coefficients(sz, coarse_b)
-    both = zip(views(sz, gap, gap_rest), views(sz, modes_ref, modes_rest))
-    for (part, vector_part), (_, modes) in both:
-        for j in range(sz.own_faces):
-            here = face_slots(sz, part, j)
-            residual = vector_part[:, own_face(sz, j)] - mode_sum(sz, coarse_a, first, modes, part, j)
-            weight = modes[6:7, own_face(sz, j)]
-            direction = weight * residual - mode_sum(sz, coarse_b, second, modes, part, j)
-            residual_ref[:, here] = residual
-            direction_ref[:, here] = direction
-            vector[:, here] = direction.astype(jnp.bfloat16)
+    for j in range(sz.own_faces):
+        here = own_face(sz, j)
+        gap = assembled(sz, own, arrived, modes_ref, j)
+        residual = gap - mode_sum(sz, coarse_a, first, modes_ref, gz, j)
+        residual_ref[:, here] = residual
+        correction = mode_sum(sz, coarse_b, second, modes_ref, gz, j)
+        direction_ref[:, here] = modes_ref[6:7, here] * residual - correction
+
+
+def second_apply_kernel(sz, operator, front, modes_ref, residual, direction, rest, *refs):
+    outs, refs = refs[: sz.own_faces], refs[sz.own_faces :]
+    pay, held, product, vector, sems = refs
+    stream = Stream(sz, operator, held, product, sems, front)
+    put_parts(sz, direction, rest, vector)
     weights = weights_of(sz, modes_ref)
-    gz = lax.axis_index("gz")
     lane = lanes()
     curvature = jnp.zeros((8, 1), jnp.float32)
     resid_dot = jnp.zeros((8, 1), jnp.float32)
-    for j in range(sz.own_faces):
-        own = residual_ref[:, face_slots(sz, gz, j)]
-        resid_dot += jnp.sum(own * (weights[j] * own), axis=1, keepdims=True)
     pieces = stream.apply(vector)
     put_slots(sz, outs, pieces)
     for j, piece in enumerate(pieces):
-        direction = direction_ref[:, face_slots(sz, gz, j)]
-        curvature += jnp.sum(direction * piece, axis=1, keepdims=True)
+        here = own_face(sz, j)
+        own = residual[:, here]
+        resid_dot += jnp.sum(own * (weights[j] * own), axis=1, keepdims=True)
+        curvature += jnp.sum(direction[:, here] * piece, axis=1, keepdims=True)
     tile = jnp.where(lane == SCALARS, curvature, jnp.zeros((8, TILE), jnp.float32))
     tile = jnp.where(lane == SCALARS + 1, resid_dot, tile)
-    tile = mode_products(sz, tile, pieces, modes_ref, 0)
-    scaled = [v * w for v, w in zip(pieces, weights)]
-    spread(pay, mode_products(sz, tile, scaled, modes_ref, MODE_SPAN))
-
-
-def third_kernel(
-    sz, operator, pieces, shared, before, residual_ref, direction_ref,
-    modes_ref, modes_rest, image, image_rest, *refs,
-):
-    earlier, refs = get_slots(sz, refs[: sz.own_faces]), refs[sz.own_faces :]
-    pay, later_ref, scalars_ref = refs[:3]
-    inverse_ref, coupling_ref, coarse_a, coarse_b, dots, held, product, vector, sems = refs[3:]
-    stream = Stream(sz, operator, held, product, sems)
+    spread(pay, tile_products(sz, tile, pieces, modes_ref))
+
+
+def third_kernel(sz, pieces, shared, before, modes_ref, residual_ref, direction_ref, *refs):
+    own, refs = get_slots(sz, refs[: sz.own_faces]), refs[sz.own_faces :]
+    arrived, refs = get_slots(sz, refs[: sz.own_faces]), refs[sz.own_faces :]
+    later_ref, scalars_ref, inverse_ref, coupling_ref, coarse_a, coarse_b = refs
+    gz = lax.axis_index("gz")
     lane = lanes()
     fill_inverse(sz, shared, inverse_ref)
     fill_coupling(sz, [sub_tile(sz, before, sub) for sub in range(sz.subs)], coupling_ref)
@@ -424,41 +453,43 @@
     curvature = 2.0 * totals[:, SCALARS : SCALARS + 1]
     resid_dot = totals[:, SCALARS + 1 : SCALARS + 2]
     step = resid_dot / curvature
-    scalars_ref[...] = jnp.where(lane == 0, curvature, resid_dot)
     solve_pair(sz, tiles, inverse_ref, coupling_ref, coarse_a, coarse_b)
     first, second = own_coefficients(sz, coarse_a), own_coefficients(sz, coarse_b)
-    both = zip(views(sz, image, image_rest), views(sz, modes_ref, modes_rest))
-    for (part, vector_part), (_, modes) in both:
-        for j in range(sz.own_faces):
-            here = face_slots(sz, part, j)
-            corrected = vector_part[:, own_face(sz, j)] - mode_sum(sz, coarse_a, first, modes, part, j)
-            weight = modes[6:7, own_face(sz, j)]
-            scaled = weight * corrected - mode_sum(sz, coarse_b, second, modes, part, j)
-            residual = residual_ref[:, here] - step * corrected
-            dots[:, here] = residual * (weight * residual)
-            later = direction_ref[:, here] - step * scaled
-            later_ref[:, here] = later
-            vector[:, here] = later.astype(jnp.bfloat16)
-    gz = lax.axis_index("gz")
     dot_part = jnp.zeros((8, 1), jnp.float32)
     for j in range(sz.own_faces):
-        dot_part += jnp.sum(dots[:, face_slots(sz, gz, j)], axis=1, keepdims=True)
+        here = own_face(sz, j)
+        image = assembled(sz, own, arrived, modes_ref, j)
+        corrected = image - mode_sum(sz, coarse_a, first, modes_ref, gz, j)
+        weight = modes_ref[6:7, here]
+        scaled = weight * corrected - mode_sum(sz, coarse_b, second, modes_ref, gz, j)
+        residual = residual_ref[:, here] - step * corrected
+        dot_part += jnp.sum(residual * (weight * residual), axis=1, keepdims=True)
+        later_ref[:, here] = direction_ref[:, here] - step * scaled
+    scalars_ref[...] = jnp.where(lane == 0, curvature, jnp.where(lane == 1, resid_dot, dot_part))
+
+
+def third_apply_kernel(sz, operator, front, direction, scalars, later, rest, *refs):
+    before, refs = get_slots(sz, refs[: sz.own_faces]), refs[sz.own_faces :]
+    pay, held, product, vector, sems = refs
+    stream = Stream(sz, operator, held, product, sems, front)
+    put_parts(sz, later, rest, vector)
     pieces = stream.apply(vector)
+    lane = lanes()
     later_part = jnp.zeros((8, 1), jnp.float32)
     cross_part = jnp.zeros((8, 1), jnp.float32)
     for j, piece in enumerate(pieces):
-        mine = later_ref[:, face_slots(sz, gz, j)]
-        direction = direction_ref[:, face_slots(sz, gz, j)]
+        mine = later[:, own_face(sz, j)]
+        earlier = direction[:, own_face(sz, j)]
         later_part += jnp.sum(mine * piece, axis=1, keepdims=True)
-        cross_part += jnp.sum(mine * earlier[j] + direction * piece, axis=1, keepdims=True)
+        cross_part += jnp.sum(mine * before[j] + earlier * piece, axis=1, keepdims=True)
     load = lax.broadcasted_iota(jnp.int32, (8, TILE), 0)
     line = jnp.where(lane == load, later_part, 0.0)
     line = jnp.where(lane == load + 8, cross_part, line)
-    line = jnp.where(lane == load + 16, dot_part, line)
+    line = jnp.where(lane == load + 16, scalars[:, 2:3], line)
     spread(pay, jnp.sum(line, axis=0, keepdims=True))
 
 
-def last_kernel(sz, pieces, scalars, estimate, direction, later, out):
+def last_kernel(sz, pieces, scalars, estimate, direction, direction_rest, later, later_rest, out):
     totals = pieces[0]
     for k in range(1, pieces.shape[0]):
         totals = totals + pieces[k]
@@ -471,8 +502,11 @@
     ratio = dot / previous
     final = 2.0 * (later_part + ratio * cross_part) + ratio * ratio * curvature
     first, second = previous / curvature, dot / final
-    moved = estimate[...] + first * direction[...]
-    out[0, 0] = moved + second * (later[...] + ratio * direction[...])
+    both = zip(views(sz, direction, direction_rest), views(sz, later, later_rest))
+    for (part, earlier), (_, mine) in both:
+        here = part_slots(sz, part)
+        moved = estimate[:, here] + first * earlier[...]
+        out[0, 0, :, here] = moved + second * (mine[...] + ratio * earlier[...])
 
 
 def shards(mesh_shape, operator, rhs_parts, stiffness, traces, coarse_inverse, rigid_loads,
@@ -498,20 +532,28 @@
         )(*operands)
 
     faces = sz.own_faces
-    pieces = sz.rows // PIECE
     coarse = pltpu.VMEM((8, sz.coarse_pad), jnp.float32)
     square = pltpu.VMEM((sz.coarse_pad, sz.coarse_pad), jnp.float32)
     half, full, face = f32(8, sz.rows), f32(8, sz.order), f32(8, sz.cap)
     blocks = operator.reshape(sz.rows // 8, 8, sz.order)
     one_step = sz.devices <= 64
     spread_tile = f32(sz.devices if one_step else 1, 8, TILE)
-    apply_scratch = [
-        pltpu.VMEM((sz.rows // 8, 8, sz.order), jnp.bfloat16),
-        pltpu.VMEM((8, sz.rows), jnp.float32),
-        pltpu.VMEM((8, sz.order), jnp.bfloat16),
-        pltpu.SemaphoreType.DMA((pieces,)),
-    ]
-    large = 50 if small else 56
+    front_rows = front_chunks(sz) * ROW_CHUNK
+
+    def apply_scratch(rows):
+        return [
+            pltpu.VMEM((rows // 8, 8, sz.order), jnp.bfloat16),
+            pltpu.VMEM((8, sz.rows), jnp.float32),
+            pltpu.VMEM((8, sz.order), jnp.bfloat16),
+            pltpu.SemaphoreType.DMA((rows // PIECE,)),
+        ]
+
+    def hold(after):
+        return call(
+            hold_kernel, jax.ShapeDtypeStruct((front_rows // 8, 8, sz.order), jnp.bfloat16),
+            [hbm, vmem], [pltpu.SemaphoreType.DMA((front_chunks(sz),))], blocks, after, limit=42,
+            cost=pl.CostEstimate(flops=0, bytes_accessed=4 * sz.rows * sz.order, transcendentals=0),
+        )
 
     def swap(own):
         return [lax.ppermute(own[j], everywhere, face_pairs(sz, j)) for j in range(faces)]
@@ -525,12 +567,6 @@
         if sz.gz == 2:
             return lax.ppermute(part, "gz", [(0, 1), (1, 0)])
         return lax.all_gather(part, "gz", axis=0, tiled=False)
-
-    def assemble(own):
-        part = call(
-            assemble_kernel, half, [vmem] * (1 + 2 * faces), [], modes, *own, *swap(own)
-        )
-        return part, rest(part)
 
     *own, pay, base = call(
         start_kernel,
@@ -551,35 +587,41 @@
         face_lengths, mode_count, limit=60,
     )
     shared = share(pay, ("gx", "gy"))
-    modes, right = call(
-        modes_kernel, [f32(16, sz.rows), half], [vmem] * (1 + faces), [], base, *swap(own)
+    modes, right, coupling = call(
+        modes_kernel, [f32(16, sz.rows), half, f32(8, TILE)], [vmem] * (1 + faces), [], base, *swap(own)
     )
     modes_rest = rest(modes)
     *own, pay, estimate = call(
-        first_kernel, [face] * faces + [spread_tile, full], [hbm] + [vmem] * 4,
-        [square, coarse] + apply_scratch,
-        blocks, shared, right, modes, modes_rest, limit=large,
+        first_kernel, [face] * faces + [spread_tile, full], [hbm] + [vmem] * 5,
+        [square, coarse] + apply_scratch(sz.rows),
+        blocks, shared, right, coupling, modes, modes_rest, limit=50 if small else 56,
     )
     before = share(pay, everywhere)
-    gap, gap_rest = assemble(own)
-    *own, pay, residual, direction = call(
-        second_kernel, [face] * faces + [spread_tile, full, full], [hbm] + [vmem] * 6,
-        [square, square, coarse, coarse] + apply_scratch,
-        blocks, before, shared, modes, modes_rest, gap, gap_rest, limit=large,
+    residual, direction = call(
+        second_kernel, [half, half], [vmem] * (3 + 2 * faces), [square, square, coarse, coarse],
+        before, shared, modes, *own, *swap(own),
+    )
+    direction_rest = rest(direction)
+    *own, pay = call(
+        second_apply_kernel, [face] * faces + [spread_tile], [hbm] + [vmem] * 5,
+        apply_scratch(sz.rows - front_rows),
+        blocks, hold(direction), modes, residual, direction, direction_rest, limit=42,
     )
     after = share(pay, everywhere)
-    image, image_rest = assemble(own)
-    pay, later, scalars = call(
-        third_kernel,
-        [f32(sz.devices if one_step else 1, 1, TILE), full, f32(8, TILE)],
-        [hbm] + [vmem] * (9 + faces),
-        [square, square, coarse, coarse, pltpu.VMEM((8, sz.order), jnp.float32)] + apply_scratch,
-        blocks, after, shared, before, residual, direction, modes, modes_rest,
-        image, image_rest, *own, limit=large,
+    later, scalars = call(
+        third_kernel, [half, f32(8, TILE)], [vmem] * (6 + 2 * faces),
+        [square, square, coarse, coarse],
+        after, shared, before, modes, residual, direction, *own, *swap(own),
+    )
+    later_rest = rest(later)
+    pay = call(
+        third_apply_kernel, f32(sz.devices if one_step else 1, 1, TILE),
+        [hbm] + [vmem] * (5 + faces), apply_scratch(sz.rows - front_rows),
+        blocks, hold(later), direction, scalars, later, later_rest, *own, limit=42,
     )
     return call(
-        last_kernel, f32(1, 1, 8, sz.order), [vmem] * 5, [],
-        share(pay, everywhere), scalars, estimate, direction, later,
+        last_kernel, f32(1, 1, 8, sz.order), [vmem] * 7, [],
+        share(pay, everywhere), scalars, estimate, direction, direction_rest, later, later_rest,
     )
 
 

time: 81.5 us -> 78.8 us (0.967)
  blocking collectives: 13.9 us -> 9.91 us
  starting transfers between devices: 28.2 us -> 25.3 us
  Pallas kernels: 20.8 us -> 23.3 us
  waiting for transfers between devices: 16.5 us -> 18.2 us
    all_to_all x3, waiting for transfers between devices: 4.68 us -> 13.1 us  [share(): return lax.all_to_all(chunk, axes, split_axis=0, concat_axis=0, tiled=True)]
    ppermute x3, waiting for transfers between devices: 8.16 us -> 1.36 us  [rest(): return lax.ppermute(part, 'gz', [(0, 1), (1, 0)])]
    all_to_all x1, blocking collectives: 13.9 us -> 9.91 us  [share(): return lax.all_to_all(chunk, axes, split_axis=0, concat_axis=0, tiled=True)]
    all_to_all x3, starting transfers between devices: 18.3 us -> 14.4 us  [share(): return lax.all_to_all(chunk, axes, split_axis=0, concat_axis=0, tiled=True)]
    pallas_call x8 -> x10, Pallas kernels: 20.8 us -> 23.3 us  [call(): pl.pallas_call(functools.partial(kernel, sz), out_shape=out_shape, in_spe...]
    ppermute x3, starting transfers between devices: 1.19 us -> 2.25 us  [rest(): return lax.ppermute(part, 'gz', [(0, 1), (1, 0)])]
  transfers between devices with their start and end apart: 12 -> 12, of which waited for: 5 -> 7; matrix products, arithmetic and copies ran while one was open for 0% -> 0% of each run, Pallas kernels for 1% -> 8%
where the time goes in v6:
time: 78.8 us; the launch traced here: 78.4 us
  starting transfers between devices  25.3 us (32%)
  Pallas kernels  23.3 us (30%)
  waiting for transfers between devices  18.2 us (23%)
  blocking collectives  9.91 us (13%)
  local copies, waits for them, and re-layouts  0.9 us (1%)
  between operations  0.8 us (1%)
    pallas_call x10, Pallas kernels, call(): pl.pallas_call(functools.partial(kernel, sz), out_shape=out_shape, in_spe...  23.3 us
    all_to_all x3, starting transfers between devices, share(): return lax.all_to_all(chunk, axes, split_axis=0, concat_axis=0, tiled=True)  14.4 us
    all_to_all x3, waiting for transfers between devices, share(): return lax.all_to_all(chunk, axes, split_axis=0, concat_axis=0, tiled=True)  13.1 us
    all_to_all x1, blocking collectives, share(): return lax.all_to_all(chunk, axes, split_axis=0, concat_axis=0, tiled=True)  9.91 us
    ppermute x6, starting transfers between devices, swap(): lax.ppermute(own[j], everywhere, face_pairs(sz, j))  8.71 us
    ppermute x6, waiting for transfers between devices, swap(): lax.ppermute(own[j], everywhere, face_pairs(sz, j))  3.68 us
    ppermute x3, starting transfers between devices, rest(): return lax.ppermute(part, 'gz', [(0, 1), (1, 0)])  2.25 us
  transfers between devices with their start and end apart: 12, of which 7 were waited for; matrix products, arithmetic and copies ran while one was open for 0% of the time, Pallas kernels for 8%

profile of v6, /device:TPU:0, one launch (start us, length us, event | category | flops | bytes accessed | tf_op | source)
XLA Modules:
  0.0 78.4 jit_solution(9502600799746503348)
XLA Ops:
  0.7 1.9 %shard_map.91 = (f32[8,768]{1,0:T(8,128)}, f32[8,768]{1,0:T(8,128)}, f32[16,8,128]{2,1,0:T(8,128)}, f32[24,1536]{1,0:T(8,128)}) custom-call(f32[6,1,3072]{2,1,0:T(1,128)} %bitcast.9, f32[6,1,8]{2,1,0:T(1,128)} %bitcast.10, f32[6,1,96]{2,1,0:T(1,128)} %bitcast.11, f32[1,1,3072]{2,1,0:T(1,128)} %stiffness.1, s32[1,1,4,768]{3,2,1,0:T(4,128)} %orders.1, ...), custom_call_target="tpu_custom_call" | custom-call | tf_op jit(solution)/shard_map/pallas_call | solution.py:522
  2.5 3.1 %collective-permute-start = (f32[8,768]{1,0:T(8,128)}, f32[8,768]{1,0:T(8,128)S(1)}, u32[]{:S(2)}, u32[]{:S(2)}) collective-permute-start(f32[8,768]{1,0:T(8,128)} %get-tuple-element.25), channel_id=1, source_target_pairs={{0,8},{1,3},{2,10},{3,1},{4,12},{5,7},{6,14},{7,5},{8,0},{9,11},{1... | collective-permute-start | bytes 73736 | tf_op jit(solution)/shard_map/ppermute | solution.py:559
  5.6 0.7 collective-permute-start.1
  6.3 6.7 %all-to-all-start = ((f32[16,8,128]{2,1,0:T(8,128)}), f32[16,8,128]{2,1,0:T(8,128)S(1)}, u32[]{:S(2)}, u32[]{:S(2)}) async-start(f32[16,8,128]{2,1,0:T(8,128)} %get-tuple-element.23), calls=%async_computation | async-start | bytes 131072 | tf_op jit(solution)/shard_map/all_to_all | solution.py:564
  13.0 0.0 collective-permute-done.refs_0_
  13.0 0.0 collective-permute-done.1.refs_1_
  13.0 0.0 copy-start
  13.1 0.9 %copy-done = f32[24,1536]{1,0:T(8,128)S(1)} copy-done((f32[24,1536]{1,0:T(8,128)S(1)}, f32[24,1536]{1,0:T(8,128)}, u32[]{:S(2)}) %copy-start) | copy-done | bytes 147480
  14.0 0.4 shard_map.92
  14.3 1.1 %collective-permute-start.2 = (f32[16,1536]{1,0:T(8,128)S(1)}, f32[16,1536]{1,0:T(8,128)S(1)}, u32[]{:S(2)}, u32[]{:S(2)}) collective-permute-start(f32[16,1536]{1,0:T(8,128)S(1)} %get-tuple-element.29.modes_ref), channel_id=1, source_target_pairs={{0,1},{1,0},{2,3},{3,2},{4,5},{5,4},{6,7},{7,6},{8,9},{9,8},{10,11... | collective-permute-start | bytes 294920 | tf_op jit(solution)/shard_map/ppermute | solution.py:568
  15.4 4.5 %all-to-all-done.shared = f32[16,8,128]{2,1,0:T(8,128)S(1)} async-done(((f32[16,8,128]{2,1,0:T(8,128)}), f32[16,8,128]{2,1,0:T(8,128)S(1)}, u32[]{:S(2)}, u32[]{:S(2)}) %all-to-all-start) | async-done | bytes 65568 | tf_op jit(solution)/shard_map/all_to_all | solution.py:564
  19.9 0.0 collective-permute-done.2.modes_rest
  19.9 5.7 %shard_map.93 = (f32[8,768]{1,0:T(8,128)S(1)}, f32[8,768]{1,0:T(8,128)S(1)}, f32[32,8,128]{2,1,0:T(8,128)}, f32[8,3072]{1,0:T(8,128)S(1)}) custom-call(bf16[192,8,3072]{2,1,0:T(8,128)(2,1)} %bitcast.4, f32[16,8,128]{2,1,0:T(8,128)S(1)} %all-to-all-done.shared, f32[8,1536]{1,0:T(8,128)S(1)} %get-tuple-element.27.right, ...), custom_call_target="tpu_custom_call" | custom-call | tf_op jit(solution)/shard_map/pallas_call | solution.py:522
  25.7 4.7 %all-to-all-start.1 = ((f32[32,8,128]{2,1,0:T(8,128)}), f32[32,8,128]{2,1,0:T(8,128)S(1)}, u32[]{:S(2)}, u32[]{:S(2)}) async-start(f32[32,8,128]{2,1,0:T(8,128)} %get-tuple-element.30), calls=%async_computation.1 | async-start | bytes 262144 | tf_op jit(solution)/shard_map/all_to_all | solution.py:564
  30.4 1.8 %collective-permute-start.3 = (f32[8,768]{1,0:T(8,128)S(1)}, f32[8,768]{1,0:T(8,128)S(1)}, u32[]{:S(2)}, u32[]{:S(2)}) collective-permute-start(f32[8,768]{1,0:T(8,128)S(1)} %get-tuple-element.31.refs_0_), channel_id=1, source_target_pairs={{0,8},{1,3},{2,10},{3,1},{4,12},{5,7},{6,14},{7,5},{8,0},{9,11},{1... | collective-permute-start | bytes 73736 | tf_op jit(solution)/shard_map/ppermute | solution.py:559
  32.3 0.7 collective-permute-start.4
  32.9 1.8 %collective-permute-done.3.refs_2_ = f32[8,768]{1,0:T(8,128)S(1)} collective-permute-done((f32[8,768]{1,0:T(8,128)S(1)}, f32[8,768]{1,0:T(8,128)S(1)}, u32[]{:S(2)}, u32[]{:S(2)}) %collective-permute-start.3) | collective-permute-done | bytes 24608 | tf_op jit(solution)/shard_map/ppermute | solution.py:559
  34.7 0.0 collective-permute-done.4.refs_3_
  34.7 4.3 %all-to-all-done.1.pieces.before = f32[32,8,128]{2,1,0:T(8,128)S(1)} async-done(((f32[32,8,128]{2,1,0:T(8,128)}), f32[32,8,128]{2,1,0:T(8,128)S(1)}, u32[]{:S(2)}, u32[]{:S(2)}) %all-to-all-start.1) | async-done | bytes 131104 | tf_op jit(solution)/shard_map/all_to_all | solution.py:564
  39.0 1.0 %shard_map.94 = (f32[8,1536]{1,0:T(8,128)S(1)}, f32[8,1536]{1,0:T(8,128)S(1)}) custom-call(f32[32,8,128]{2,1,0:T(8,128)S(1)} %all-to-all-done.1.pieces.before, f32[16,8,128]{2,1,0:T(8,128)S(1)} %all-to-all-done.shared, f32[16,1536]{1,0:T(8,128)S(1)} %get-tuple-element.29.modes_ref, f32[8,768]{1,0:T(8,128)S(1)} %get-tuple-element.31.refs_0_, ...), custom_call_target="tpu_custom_call" | custom-call | tf_op jit(solution)/shard_map/pallas_call | solution.py:522
  40.1 0.6 collective-permute-start.5
  40.7 2.9 %shard_map.95.front = bf16[128,8,3072]{2,1,0:T(8,128)(2,1)S(1)} custom-call(bf16[192,8,3072]{2,1,0:T(8,128)(2,1)} %bitcast.5, f32[8,1536]{1,0:T(8,128)S(1)} %get-tuple-element.33.after.direction.direction_ref), custom_call_target="tpu_custom_call" | custom-call | bytes 18874368 | tf_op jit(solution)/shard_map/pallas_call | solution.py:522
  43.6 0.7 collective-permute-done.5.rest.direction_rest
  44.2 3.7 %shard_map.96 = (f32[8,768]{1,0:T(8,128)S(1)}, f32[8,768]{1,0:T(8,128)S(1)}, f32[32,8,128]{2,1,0:T(8,128)}) custom-call(bf16[192,8,3072]{2,1,0:T(8,128)(2,1)} %bitcast.6, bf16[128,8,3072]{2,1,0:T(8,128)(2,1)S(1)} %shard_map.95.front, f32[16,1536]{1,0:T(8,128)S(1)} %get-tuple-element.29.modes_ref, f32[8,1536]{1,0:T(8,128)S(1)} %get-tuple-element.34.residual.residual_ref, ...), custom_call_target="tpu_custom_call" | custom-call | tf_op jit(solution)/shard_map/pallas_call | solution.py:522
  47.9 2.9 %all-to-all-start.2 = ((f32[32,8,128]{2,1,0:T(8,128)}), f32[32,8,128]{2,1,0:T(8,128)S(1)}, u32[]{:S(2)}, u32[]{:S(2)}) async-start(f32[32,8,128]{2,1,0:T(8,128)} %get-tuple-element.35), calls=%async_computation.2 | async-start | bytes 262144 | tf_op jit(solution)/shard_map/all_to_all | solution.py:564
  50.8 1.8 %collective-permute-start.6 = (f32[8,768]{1,0:T(8,128)S(1)}, f32[8,768]{1,0:T(8,128)S(1)}, u32[]{:S(2)}, u32[]{:S(2)}) collective-permute-start(f32[8,768]{1,0:T(8,128)S(1)} %get-tuple-element.36.refs_0_), channel_id=1, source_target_pairs={{0,8},{1,3},{2,10},{3,1},{4,12},{5,7},{6,14},{7,5},{8,0},{9,11},{1... | collective-permute-start | bytes 73736 | tf_op jit(solution)/shard_map/ppermute | solution.py:559
  52.7 0.7 collective-permute-start.7
  53.3 1.8 %collective-permute-done.6.refs_2_ = f32[8,768]{1,0:T(8,128)S(1)} collective-permute-done((f32[8,768]{1,0:T(8,128)S(1)}, f32[8,768]{1,0:T(8,128)S(1)}, u32[]{:S(2)}, u32[]{:S(2)}) %collective-permute-start.6) | collective-permute-done | bytes 24608 | tf_op jit(solution)/shard_map/ppermute | solution.py:559
  55.2 0.0 collective-permute-done.7.refs_3_
  55.2 4.3 %all-to-all-done.2.pieces = f32[32,8,128]{2,1,0:T(8,128)S(1)} async-done(((f32[32,8,128]{2,1,0:T(8,128)}), f32[32,8,128]{2,1,0:T(8,128)S(1)}, u32[]{:S(2)}, u32[]{:S(2)}) %all-to-all-start.2) | async-done | bytes 131104 | tf_op jit(solution)/shard_map/all_to_all | solution.py:564
  59.5 1.0 %shard_map.97 = (f32[8,1536]{1,0:T(8,128)S(1)}, f32[8,128]{1,0:T(8,128)S(1)}) custom-call(f32[32,8,128]{2,1,0:T(8,128)S(1)} %all-to-all-done.2.pieces, f32[16,8,128]{2,1,0:T(8,128)S(1)} %all-to-all-done.shared, f32[32,8,128]{2,1,0:T(8,128)S(1)} %all-to-all-done.1.pieces.before, f32[16,1536]{1,0:T(8,128)S(1)} %get-tuple-element.29.modes_ref, ...), custom_call_target="tpu_custom_call" | custom-call | tf_op jit(solution)/shard_map/pallas_call | solution.py:522
  60.5 0.6 collective-permute-start.8
  61.1 2.9 %shard_map.98.front = bf16[128,8,3072]{2,1,0:T(8,128)(2,1)S(1)} custom-call(bf16[192,8,3072]{2,1,0:T(8,128)(2,1)} %bitcast.7, f32[8,1536]{1,0:T(8,128)S(1)} %get-tuple-element.38.after.later), custom_call_target="tpu_custom_call" | custom-call | bytes 18874368 | tf_op jit(solution)/shard_map/pallas_call | solution.py:522
  64.0 0.7 collective-permute-done.8.rest.later_rest
  64.7 2.9 %shard_map.99 = f32[32,1,128]{2,1,0:T(1,128)S(1)} custom-call(bf16[192,8,3072]{2,1,0:T(8,128)(2,1)} %bitcast.8, bf16[128,8,3072]{2,1,0:T(8,128)(2,1)S(1)} %shard_map.98.front, f32[8,1536]{1,0:T(8,128)S(1)} %get-tuple-element.33.after.direction.direction_ref, f32[8,128]{1,0:T(8,128)S(1)} %get-tuple-element.39.scalars, ...), custom_call_target="tpu_custom_call" | custom-call | tf_op jit(solution)/shard_map/pallas_call | solution.py:522
  67.6 9.9 %all_to_all.20.pieces = f32[32,1,128]{2,1,0:T(1,128)S(1)} all-to-all(f32[32,1,128]{2,1,0:T(1,128)S(1)} %shard_map.99), channel_id=1, replica_groups=mesh['gx'=4,'gy'=4,'gz'=2] {'gx','gy','gz'}, dimensions={0} | all-to-all | bytes 32768 | tf_op jit(solution)/shard_map/all_to_all | solution.py:564
  77.5 0.8 %shard_map.100 = f32[1,1,8,3072]{3,2,1,0:T(8,128)} custom-call(f32[32,1,128]{2,1,0:T(1,128)S(1)} %all_to_all.20.pieces, f32[8,128]{1,0:T(8,128)S(1)} %get-tuple-element.39.scalars, f32[8,3072]{1,0:T(8,128)S(1)} %get-tuple-element.40.estimate, f32[8,1536]{1,0:T(8,128)S(1)} %get-tuple-element.33.after.direction.direction_ref, ...), custom_call_target="tpu_custom_call" | custom-call | tf_op jit(solution)/shard_map/pallas_call | solution.py:522
Async XLA Ops:
  2.5 10.5 %collective-permute-start = (f32[8,768]{1,0:T(8,128)}, f32[8,768]{1,0:T(8,128)S(1)}, u32[]{:S(2)}, u32[]{:S(2)}) collective-permute-start(f32[8,768]{1,0:T(8,128)} %get-tuple-element.25), channel_id=1, source_target_pairs={{0,8},{1,3},{2,10},{3,1},{4,12},{5,7},{6,14},{7,5},{8,0},{9,11},{1... | collective-permute-start | bytes 73736 | tf_op jit(solution)/shard_map/ppermute | solution.py:559
  5.6 7.4 %collective-permute-start.1 = (f32[8,768]{1,0:T(8,128)}, f32[8,768]{1,0:T(8,128)S(1)}, u32[]{:S(2)}, u32[]{:S(2)}) collective-permute-start(f32[8,768]{1,0:T(8,128)} %get-tuple-element.26), channel_id=1, source_target_pairs={{3,5},{5,3},{8,16},{10,18},{11,13},{12,20},{13,11},{14,22},{16,8},... | collective-permute-start | bytes 73736 | tf_op jit(solution)/shard_map/ppermute | solution.py:559
  6.3 13.7 %all-to-all-start = ((f32[16,8,128]{2,1,0:T(8,128)}), f32[16,8,128]{2,1,0:T(8,128)S(1)}, u32[]{:S(2)}, u32[]{:S(2)}) async-start(f32[16,8,128]{2,1,0:T(8,128)} %get-tuple-element.23), calls=%async_computation | async-start | bytes 131072 | tf_op jit(solution)/shard_map/all_to_all | solution.py:564
  13.0 0.9 %copy-start = (f32[24,1536]{1,0:T(8,128)S(1)}, f32[24,1536]{1,0:T(8,128)}, u32[]{:S(2)}) copy-start(f32[24,1536]{1,0:T(8,128)} %get-tuple-element.24.base) | copy-start | bytes 442372
  14.3 5.6 %collective-permute-start.2 = (f32[16,1536]{1,0:T(8,128)S(1)}, f32[16,1536]{1,0:T(8,128)S(1)}, u32[]{:S(2)}, u32[]{:S(2)}) collective-permute-start(f32[16,1536]{1,0:T(8,128)S(1)} %get-tuple-element.29.modes_ref), channel_id=1, source_target_pairs={{0,1},{1,0},{2,3},{3,2},{4,5},{5,4},{6,7},{7,6},{8,9},{9,8},{10,11... | collective-permute-start | bytes 294920 | tf_op jit(solution)/shard_map/ppermute | solution.py:568
  25.7 13.4 %all-to-all-start.1 = ((f32[32,8,128]{2,1,0:T(8,128)}), f32[32,8,128]{2,1,0:T(8,128)S(1)}, u32[]{:S(2)}, u32[]{:S(2)}) async-start(f32[32,8,128]{2,1,0:T(8,128)} %get-tuple-element.30), calls=%async_computation.1 | async-start | bytes 262144 | tf_op jit(solution)/shard_map/all_to_all | solution.py:564
  30.4 4.3 %collective-permute-start.3 = (f32[8,768]{1,0:T(8,128)S(1)}, f32[8,768]{1,0:T(8,128)S(1)}, u32[]{:S(2)}, u32[]{:S(2)}) collective-permute-start(f32[8,768]{1,0:T(8,128)S(1)} %get-tuple-element.31.refs_0_), channel_id=1, source_target_pairs={{0,8},{1,3},{2,10},{3,1},{4,12},{5,7},{6,14},{7,5},{8,0},{9,11},{1... | collective-permute-start | bytes 73736 | tf_op jit(solution)/shard_map/ppermute | solution.py:559
  32.3 2.5 %collective-permute-start.4 = (f32[8,768]{1,0:T(8,128)S(1)}, f32[8,768]{1,0:T(8,128)S(1)}, u32[]{:S(2)}, u32[]{:S(2)}) collective-permute-start(f32[8,768]{1,0:T(8,128)S(1)} %get-tuple-element.32.refs_1_), channel_id=1, source_target_pairs={{3,5},{5,3},{8,16},{10,18},{11,13},{12,20},{13,11},{14,22},{16,8},... | collective-permute-start | bytes 73736 | tf_op jit(solution)/shard_map/ppermute | solution.py:559
  40.1 4.2 %collective-permute-start.5 = (f32[8,1536]{1,0:T(8,128)S(1)}, f32[8,1536]{1,0:T(8,128)S(1)}, u32[]{:S(2)}, u32[]{:S(2)}) collective-permute-start(f32[8,1536]{1,0:T(8,128)S(1)} %get-tuple-element.33.after.direction.direction_ref), channel_id=1, source_target_pairs={{0,1},{1,0},{2,3},{3,2},{4,5},{5,4},{6,7},{7,6},{8,9},{9,8},{10,11... | collective-permute-start | bytes 147464 | tf_op jit(solution)/shard_map/ppermute | solution.py:568
  47.9 11.5 %all-to-all-start.2 = ((f32[32,8,128]{2,1,0:T(8,128)}), f32[32,8,128]{2,1,0:T(8,128)S(1)}, u32[]{:S(2)}, u32[]{:S(2)}) async-start(f32[32,8,128]{2,1,0:T(8,128)} %get-tuple-element.35), calls=%async_computation.2 | async-start | bytes 262144 | tf_op jit(solution)/shard_map/all_to_all | solution.py:564
  50.8 4.3 %collective-permute-start.6 = (f32[8,768]{1,0:T(8,128)S(1)}, f32[8,768]{1,0:T(8,128)S(1)}, u32[]{:S(2)}, u32[]{:S(2)}) collective-permute-start(f32[8,768]{1,0:T(8,128)S(1)} %get-tuple-element.36.refs_0_), channel_id=1, source_target_pairs={{0,8},{1,3},{2,10},{3,1},{4,12},{5,7},{6,14},{7,5},{8,0},{9,11},{1... | collective-permute-start | bytes 73736 | tf_op jit(solution)/shard_map/ppermute | solution.py:559
  52.7 2.5 %collective-permute-start.7 = (f32[8,768]{1,0:T(8,128)S(1)}, f32[8,768]{1,0:T(8,128)S(1)}, u32[]{:S(2)}, u32[]{:S(2)}) collective-permute-start(f32[8,768]{1,0:T(8,128)S(1)} %get-tuple-element.37.refs_1_), channel_id=1, source_target_pairs={{3,5},{5,3},{8,16},{10,18},{11,13},{12,20},{13,11},{14,22},{16,8},... | collective-permute-start | bytes 73736 | tf_op jit(solution)/shard_map/ppermute | solution.py:559
  60.5 4.2 %collective-permute-start.8 = (f32[8,1536]{1,0:T(8,128)S(1)}, f32[8,1536]{1,0:T(8,128)S(1)}, u32[]{:S(2)}, u32[]{:S(2)}) collective-permute-start(f32[8,1536]{1,0:T(8,128)S(1)} %get-tuple-element.38.after.later), channel_id=1, source_target_pairs={{0,1},{1,0},{2,3},{3,2},{4,5},{5,4},{6,7},{7,6},{8,9},{9,8},{10,11... | collective-permute-start | bytes 147464 | tf_op jit(solution)/shard_map/ppermute | solution.py:568

commit v7 on v6

--- a/solution.py
+++ b/solution.py
@@ -12,8 +12,7 @@
 LOAD_LANE = 6
 TILE = 128
 SLOT = 8
-MODE_SPAN = 5 * SLOT
-SCALARS = 3 * MODE_SPAN
+FOLD = TILE // 2
 MIB = 1024 * 1024
 
 
@@ -30,8 +29,10 @@
         self.coarse = self.subs * SLOT
         self.coarse_pad = -(-self.coarse // TILE) * TILE
         self.own_faces = self.rows // self.cap
+        self.group = self.modes * (1 + self.own_faces)
+        self.sums = 3 * self.group
         assert self.rows % self.cap == 0 and self.cap % TILE == 0
-        assert self.modes <= SLOT - 2 and self.loads == 8
+        assert self.modes <= SLOT - 2 and self.loads == 8 and self.sums + 2 <= FOLD
 
 
 def f32(*shape):
@@ -71,7 +72,7 @@
             if sz.own_faces > 1:
                 first = part * sz.own_faces + slot // 2 * 2
                 index = divmod(sub, sz.sy)[first // 2]
-                local = slot ^ 1 ^ index & 1
+                local = slot ^ index & 1
             face = part * sz.own_faces + local
             other = grid_neighbour(sz, sub, face)
             if other is not None:
@@ -86,9 +87,9 @@
     for j in range(0, sz.own_faces, 2):
         first = lax.axis_index("gz") * sz.own_faces + j
         index = jnp.where(first < 2, lax.axis_index("gx"), lax.axis_index("gy"))
-        odd = lax.rem(index, 2) == 1
+        even = lax.rem(index, 2) == 0
         low, high = values[j], values[j + 1]
-        result += [jnp.where(odd, low, high), jnp.where(odd, high, low)]
+        result += [jnp.where(even, low, high), jnp.where(even, high, low)]
     return result
 
 
@@ -155,7 +156,6 @@
 
 def mode_products(sz, tile, blocks, modes_ref, first_lane):
     lane = lanes()
-    gz = lax.axis_index("gz")
     for m in range(sz.modes):
         total = None
         for j, block in enumerate(blocks):
@@ -163,7 +163,7 @@
             total = term if total is None else total + term
         tile = jnp.where(lane == first_lane + m, total, tile)
     for j, block in enumerate(blocks):
-        face_lane = first_lane + SLOT * (1 + gz * sz.own_faces + j)
+        face_lane = first_lane + sz.modes * (1 + j)
         for m in range(sz.modes):
             row = modes_ref[SLOT + m : SLOT + m + 1, own_face(sz, j)]
             total = jnp.sum(block * row, axis=1, keepdims=True)
@@ -175,41 +175,33 @@
     return [modes_ref[6:7, own_face(sz, j)] for j in range(sz.own_faces)]
 
 
-def sub_tile(sz, tiles, sub):
-    total = tiles[sub * sz.gz]
-    for part in range(1, sz.gz):
-        total = total + tiles[sub * sz.gz + part]
-    return total
-
-
-def gathered_coarse(sz, tiles, held_ref, group):
-    lane = lanes()
-    held_ref[...] = jnp.zeros((8, sz.coarse_pad), jnp.float32)
+def unfolded(tile):
+    return jnp.concatenate([tile, pltpu.roll(tile, FOLD, 1)], axis=0)
+
+
+def put_modes(sz, target, rows, tile, lane, sub):
+    start = sub * SLOT
+    base, offset = start // TILE * TILE, start % TILE
+    moved = pltpu.roll(tile, (offset - lane) % TILE, 1)
+    wanted = (lanes() >= offset) & (lanes() < offset + sz.modes)
+    target[rows, base : base + TILE] += jnp.where(wanted, moved, 0.0)
+
+
+def fill_coupling(sz, pieces, coupling_ref):
+    coupling_ref[...] = jnp.zeros((sz.coarse_pad, sz.coarse_pad), jnp.float32)
     for sub in range(sz.subs):
-        total = tiles[sub]
+        rows = slice(sub * SLOT, (sub + 1) * SLOT)
+        parts = [unfolded(pieces[sub * sz.gz + z]) for z in range(sz.gz)]
+        own = parts[0]
+        for part in parts[1:]:
+            own = own + part
+        put_modes(sz, coupling_ref, rows, own, 2 * sz.group, sub)
         for face in range(4):
             other = grid_neighbour(sz, sub, face)
             if other is not None:
-                total = total + pltpu.roll(tiles[other], TILE - SLOT * (1 + (face ^ 1)), 1)
-        start = sub * SLOT
-        base, offset = start // TILE * TILE, start % TILE
-        moved = pltpu.roll(total, (offset - group * MODE_SPAN) % TILE, 1)
-        moved = jnp.where((lane >= offset) & (lane < offset + sz.modes), moved, 0.0)
-        held_ref[:, base : base + TILE] += moved
-
-
-def fill_coupling(sz, tiles, coupling_ref):
-    lane = lanes()
-    coupling_ref[...] = jnp.zeros((sz.coarse_pad, sz.coarse_pad), jnp.float32)
-    for sub in range(sz.subs):
-        for k in range(5):
-            other = sub if k == 0 else grid_neighbour(sz, sub, k - 1)
-            if other is None:
-                continue
-            base, offset = other * SLOT // TILE * TILE, other * SLOT % TILE
-            moved = pltpu.roll(tiles[sub], (offset - 2 * MODE_SPAN - SLOT * k) % TILE, 1)
-            moved = jnp.where((lane >= offset) & (lane < offset + sz.modes), moved, 0.0)
-            coupling_ref[sub * SLOT : (sub + 1) * SLOT, base : base + TILE] += moved
+                part, j = divmod(face, sz.own_faces)
+                lane = 2 * sz.group + sz.modes * (1 + j)
+                put_modes(sz, coupling_ref, rows, parts[part], lane, other)
 
 
 def fill_inverse(sz, shared, inverse_ref):
@@ -219,9 +211,22 @@
         inverse_ref[sub * SLOT : (sub + 1) * SLOT, :] = shared[sub]
 
 
-def solve_pair(sz, tiles, inverse_ref, coupling_ref, coarse_a, coarse_b):
-    gathered_coarse(sz, tiles, coarse_a, 0)
-    gathered_coarse(sz, tiles, coarse_b, 1)
+def solve_pair(sz, pieces, inverse_ref, coupling_ref, coarse_a, coarse_b):
+    coarse_a[...] = jnp.zeros((8, sz.coarse_pad), jnp.float32)
+    coarse_b[...] = jnp.zeros((8, sz.coarse_pad), jnp.float32)
+    for sub in range(sz.subs):
+        total = pieces[sub * sz.gz]
+        for part in range(1, sz.gz):
+            total = total + pieces[sub * sz.gz + part]
+        for face in range(4):
+            other = grid_neighbour(sz, sub, face)
+            if other is not None:
+                part, j = divmod(face ^ 1, sz.own_faces)
+                moved = pltpu.roll(pieces[other * sz.gz + part], TILE - sz.modes * (1 + j), 1)
+                total = total + moved
+        total = unfolded(total)
+        put_modes(sz, coarse_a, slice(0, 8), total, 0, sub)
+        put_modes(sz, coarse_b, slice(0, 8), total, sz.group, sub)
     first = exact_dot(coarse_a[...], inverse_ref[...])
     coarse_a[...] = first
     coarse_b[...] = exact_dot(coarse_b[...] - exact_dot(first, coupling_ref[...]), inverse_ref[...])
@@ -231,53 +236,56 @@
     out[...] = jnp.broadcast_to(tile[None], out.shape)
 
 
-def front_chunks(sz):
-    return sz.rows // ROW_CHUNK * 2 // 3
+def spread_folded(out, tile):
+    spread(out, tile[0:4] + pltpu.roll(tile[4:8], FOLD, 1))
+
+
+def multiply(sz, vector, rows, product, k):
+    part = lax.dot_general(
+        vector[...], rows.reshape(ROW_CHUNK, sz.order), (((1,), (1,)), ((), ())),
+        preferred_element_type=jnp.float32,
+    )
+    here = pl.ds(pl.multiple_of(k * ROW_CHUNK, TILE), ROW_CHUNK)
+    product[:, here] = part.astype(jnp.bfloat16).astype(jnp.float32)
 
 
 class Stream:
-    def __init__(self, sz, operator, held, product, sems, front=None):
+    def __init__(self, sz, operator, held, product, sems):
         self.sz, self.operator, self.held, self.product, self.sems = sz, operator, held, product, sems
-        self.front, self.first = front, front_chunks(sz) if front is not None else 0
-        for p in range((sz.rows // ROW_CHUNK - self.first) * (ROW_CHUNK // PIECE)):
+        for p in range(sz.rows // PIECE):
             self.copy(p).start()
 
     def copy(self, p):
-        blocks = PIECE // 8
-        source = pl.ds(self.first * (ROW_CHUNK // 8) + p * blocks, blocks)
-        target = self.held.at[pl.ds(p * blocks, blocks)]
-        return pltpu.make_async_copy(self.operator.at[source], target, self.sems.at[p])
-
-    def multiply(self, vector, rows, k):
-        part = lax.dot_general(
-            vector[...], rows.reshape(ROW_CHUNK, self.sz.order), (((1,), (1,)), ((), ())),
-            preferred_element_type=jnp.float32,
-        )
-        here = pl.ds(pl.multiple_of(k * ROW_CHUNK, TILE), ROW_CHUNK)
-        self.product[:, here] = part.astype(jnp.bfloat16).astype(jnp.float32)
+        here = pl.ds(p * (PIECE // 8), PIECE // 8)
+        return pltpu.make_async_copy(self.operator.at[here], self.held.at[here], self.sems.at[p])
 
     def apply(self, vector):
         sz, step, blocks = self.sz, ROW_CHUNK // PIECE, ROW_CHUNK // 8
-        for k in range(self.first):
-            self.multiply(vector, self.front[k * blocks : (k + 1) * blocks], k)
 
         def chunk(k, carry):
             for p in range(step):
                 self.copy(k * step + p).wait()
-            self.multiply(vector, self.held[pl.ds(k * blocks, blocks)], self.first + k)
+            multiply(sz, vector, self.held[pl.ds(k * blocks, blocks)], self.product, k)
             return carry
 
-        lax.fori_loop(0, sz.rows // ROW_CHUNK - self.first, chunk, 0)
+        lax.fori_loop(0, sz.rows // ROW_CHUNK, chunk, 0)
         return [self.product[:, own_face(sz, j)] for j in range(sz.own_faces)]
 
 
-def hold_kernel(sz, operator, after, front, sems):
+def apply_held(sz, vector, held, product):
+    blocks = ROW_CHUNK // 8
+    for k in range(sz.rows // ROW_CHUNK):
+        multiply(sz, vector, held[k * blocks : (k + 1) * blocks], product, k)
+    return [product[:, own_face(sz, j)] for j in range(sz.own_faces)]
+
+
+def hold_kernel(sz, operator, after, held, sems):
     del after
     blocks = ROW_CHUNK // 8
     copies = []
-    for k in range(front_chunks(sz)):
+    for k in range(sz.rows // ROW_CHUNK):
         here = pl.ds(k * blocks, blocks)
-        copies.append(pltpu.make_async_copy(operator.at[here], front.at[here], sems.at[k]))
+        copies.append(pltpu.make_async_copy(operator.at[here], held.at[here], sems.at[k]))
         copies[-1].start()
     for copy in copies:
         copy.wait()
@@ -360,7 +368,7 @@
         for j in range(sz.own_faces)
     ]
     tile = jnp.zeros((8, TILE), jnp.float32)
-    coupling[...] = mode_products(sz, tile, coarse_rows, modes_ref, 2 * MODE_SPAN)
+    coupling[...] = mode_products(sz, tile, coarse_rows, modes_ref, 2 * sz.group)
 
 
 def assembled(sz, own, arrived, modes_ref, j):
@@ -371,7 +379,7 @@
 def tile_products(sz, tile, vectors, modes_ref):
     tile = mode_products(sz, tile, vectors, modes_ref, 0)
     scaled = [v * w for v, w in zip(vectors, weights_of(sz, modes_ref))]
-    return mode_products(sz, tile, scaled, modes_ref, MODE_SPAN)
+    return mode_products(sz, tile, scaled, modes_ref, sz.group)
 
 
 def first_kernel(sz, operator, shared, right, coupling, modes_ref, modes_rest, *refs):
@@ -395,7 +403,7 @@
     pieces = stream.apply(vector)
     vectors = [right[:, own_face(sz, j)] - piece for j, piece in enumerate(pieces)]
     put_slots(sz, outs, vectors)
-    spread(pay, tile_products(sz, coupling[...], vectors, modes_ref))
+    spread_folded(pay, tile_products(sz, coupling[...], vectors, modes_ref))
 
 
 def second_kernel(sz, pieces, shared, modes_ref, *refs):
@@ -404,9 +412,8 @@
     residual_ref, direction_ref, inverse_ref, coupling_ref, coarse_a, coarse_b = refs
     gz = lax.axis_index("gz")
     fill_inverse(sz, shared, inverse_ref)
-    tiles = [sub_tile(sz, pieces, sub) for sub in range(sz.subs)]
-    fill_coupling(sz, tiles, coupling_ref)
-    solve_pair(sz, tiles, inverse_ref, coupling_ref, coarse_a, coarse_b)
+    fill_coupling(sz, pieces, coupling_ref)
+    solve_pair(sz, pieces, inverse_ref, coupling_ref, coarse_a, coarse_b)
     first, second = own_coefficients(sz, coarse_a), own_coefficients(sz, coarse_b)
     for j in range(sz.own_faces):
         here = own_face(sz, j)
@@ -417,25 +424,24 @@
         direction_ref[:, here] = modes_ref[6:7, here] * residual - correction
 
 
-def second_apply_kernel(sz, operator, front, modes_ref, residual, direction, rest, *refs):
+def second_apply_kernel(sz, held, modes_ref, residual, direction, rest, *refs):
     outs, refs = refs[: sz.own_faces], refs[sz.own_faces :]
-    pay, held, product, vector, sems = refs
-    stream = Stream(sz, operator, held, product, sems, front)
+    pay, product, vector = refs
     put_parts(sz, direction, rest, vector)
     weights = weights_of(sz, modes_ref)
     lane = lanes()
     curvature = jnp.zeros((8, 1), jnp.float32)
     resid_dot = jnp.zeros((8, 1), jnp.float32)
-    pieces = stream.apply(vector)
+    pieces = apply_held(sz, vector, held, product)
     put_slots(sz, outs, pieces)
     for j, piece in enumerate(pieces):
         here = own_face(sz, j)
         own = residual[:, here]
         resid_dot += jnp.sum(own * (weights[j] * own), axis=1, keepdims=True)
         curvature += jnp.sum(direction[:, here] * piece, axis=1, keepdims=True)
-    tile = jnp.where(lane == SCALARS, curvature, jnp.zeros((8, TILE), jnp.float32))
-    tile = jnp.where(lane == SCALARS + 1, resid_dot, tile)
-    spread(pay, tile_products(sz, tile, pieces, modes_ref))
+    tile = jnp.where(lane == sz.sums, curvature, jnp.zeros((8, TILE), jnp.float32))
+    tile = jnp.where(lane == sz.sums + 1, resid_dot, tile)
+    spread_folded(pay, tile_products(sz, tile, pieces, modes_ref))
 
 
 def third_kernel(sz, pieces, shared, before, modes_ref, residual_ref, direction_ref, *refs):
@@ -445,15 +451,15 @@
     gz = lax.axis_index("gz")
     lane = lanes()
     fill_inverse(sz, shared, inverse_ref)
-    fill_coupling(sz, [sub_tile(sz, before, sub) for sub in range(sz.subs)], coupling_ref)
-    tiles = [sub_tile(sz, pieces, sub) for sub in range(sz.subs)]
-    totals = tiles[0]
-    for tile in tiles[1:]:
-        totals = totals + tile
-    curvature = 2.0 * totals[:, SCALARS : SCALARS + 1]
-    resid_dot = totals[:, SCALARS + 1 : SCALARS + 2]
+    fill_coupling(sz, before, coupling_ref)
+    totals = pieces[0]
+    for k in range(1, sz.devices):
+        totals = totals + pieces[k]
+    totals = unfolded(totals)
+    curvature = 2.0 * totals[:, sz.sums : sz.sums + 1]
+    resid_dot = totals[:, sz.sums + 1 : sz.sums + 2]
     step = resid_dot / curvature
-    solve_pair(sz, tiles, inverse_ref, coupling_ref, coarse_a, coarse_b)
+    solve_pair(sz, pieces, inverse_ref, coupling_ref, coarse_a, coarse_b)
     first, second = own_coefficients(sz, coarse_a), own_coefficients(sz, coarse_b)
     dot_part = jnp.zeros((8, 1), jnp.float32)
     for j in range(sz.own_faces):
@@ -468,12 +474,11 @@
     scalars_ref[...] = jnp.where(lane == 0, curvature, jnp.where(lane == 1, resid_dot, dot_part))
 
 
-def third_apply_kernel(sz, operator, front, direction, scalars, later, rest, *refs):
+def third_apply_kernel(sz, held, direction, scalars, later, rest, *refs):
     before, refs = get_slots(sz, refs[: sz.own_faces]), refs[sz.own_faces :]
-    pay, held, product, vector, sems = refs
-    stream = Stream(sz, operator, held, product, sems, front)
+    pay, product, vector = refs
     put_parts(sz, later, rest, vector)
-    pieces = stream.apply(vector)
+    pieces = apply_held(sz, vector, held, product)
     lane = lanes()
     later_part = jnp.zeros((8, 1), jnp.float32)
     cross_part = jnp.zeros((8, 1), jnp.float32)
@@ -537,21 +542,19 @@
     half, full, face = f32(8, sz.rows), f32(8, sz.order), f32(8, sz.cap)
     blocks = operator.reshape(sz.rows // 8, 8, sz.order)
     one_step = sz.devices <= 64
-    spread_tile = f32(sz.devices if one_step else 1, 8, TILE)
-    front_rows = front_chunks(sz) * ROW_CHUNK
-
-    def apply_scratch(rows):
-        return [
-            pltpu.VMEM((rows // 8, 8, sz.order), jnp.bfloat16),
-            pltpu.VMEM((8, sz.rows), jnp.float32),
-            pltpu.VMEM((8, sz.order), jnp.bfloat16),
-            pltpu.SemaphoreType.DMA((rows // PIECE,)),
-        ]
+    spread_tile = f32(sz.devices if one_step else 1, 4, TILE)
+    apply_scratch = [
+        pltpu.VMEM((8, sz.rows), jnp.float32),
+        pltpu.VMEM((8, sz.order), jnp.bfloat16),
+    ]
+    copies = sz.rows // PIECE
+    stream_scratch = [pltpu.VMEM((sz.rows // 8, 8, sz.order), jnp.bfloat16)] + apply_scratch
+    stream_scratch += [pltpu.SemaphoreType.DMA((copies,))]
 
     def hold(after):
         return call(
-            hold_kernel, jax.ShapeDtypeStruct((front_rows // 8, 8, sz.order), jnp.bfloat16),
-            [hbm, vmem], [pltpu.SemaphoreType.DMA((front_chunks(sz),))], blocks, after, limit=42,
+            hold_kernel, jax.ShapeDtypeStruct((sz.rows // 8, 8, sz.order), jnp.bfloat16),
+            [hbm, vmem], [pltpu.SemaphoreType.DMA((copies,))], blocks, after, limit=42,
             cost=pl.CostEstimate(flops=0, bytes_accessed=4 * sz.rows * sz.order, transcendentals=0),
         )
 
@@ -593,7 +596,7 @@
     modes_rest = rest(modes)
     *own, pay, estimate = call(
         first_kernel, [face] * faces + [spread_tile, full], [hbm] + [vmem] * 5,
-        [square, coarse] + apply_scratch(sz.rows),
+        [square, coarse] + stream_scratch,
         blocks, shared, right, coupling, modes, modes_rest, limit=50 if small else 56,
     )
     before = share(pay, everywhere)
@@ -603,9 +606,8 @@
     )
     direction_rest = rest(direction)
     *own, pay = call(
-        second_apply_kernel, [face] * faces + [spread_tile], [hbm] + [vmem] * 5,
-        apply_scratch(sz.rows - front_rows),
-        blocks, hold(direction), modes, residual, direction, direction_rest, limit=42,
+        second_apply_kernel, [face] * faces + [spread_tile], [vmem] * 5,
+        apply_scratch, hold(direction), modes, residual, direction, direction_rest,
     )
     after = share(pay, everywhere)
     later, scalars = call(
@@ -616,8 +618,8 @@
     later_rest = rest(later)
     pay = call(
         third_apply_kernel, f32(sz.devices if one_step else 1, 1, TILE),
-        [hbm] + [vmem] * (5 + faces), apply_scratch(sz.rows - front_rows),
-        blocks, hold(later), direction, scalars, later, later_rest, *own, limit=42,
+        [vmem] * (5 + faces), apply_scratch,
+        hold(later), direction, scalars, later, later_rest, *own,
     )
     return call(
         last_kernel, f32(1, 1, 8, sz.order), [vmem] * 7, [],

time: 78.8 us -> 78.5 us (level)
  waiting for transfers between devices: 18.2 us -> 9.04 us
  starting transfers between devices: 25.3 us -> 31.8 us
  Pallas kernels: 23.3 us -> 24.8 us
  blocking collectives: 9.91 us -> 10.8 us
    ppermute x6, starting transfers between devices: 8.71 us -> 17 us  [swap(): lax.ppermute(own[j], everywhere, face_pairs(sz, j))]
    all_to_all x3, waiting for transfers between devices: 13.1 us -> 5.41 us  [share(): return lax.all_to_all(chunk, axes, split_axis=0, concat_axis=0, tiled=True)]
    all_to_all x3, starting transfers between devices: 14.4 us -> 12.5 us  [share(): return lax.all_to_all(chunk, axes, split_axis=0, concat_axis=0, tiled=True)]
    pallas_call x10, Pallas kernels: 23.3 us -> 24.8 us  [call(): pl.pallas_call(functools.partial(kernel, sz), out_shape=out_shape, in_spe...]
    ppermute x3, waiting for transfers between devices: 1.36 us -> 0.01 us  [rest(): return lax.ppermute(part, 'gz', [(0, 1), (1, 0)])]
    all_to_all x1, blocking collectives: 9.91 us -> 10.8 us  [share(): return lax.all_to_all(chunk, axes, split_axis=0, concat_axis=0, tiled=True)]
  transfers between devices with their start and end apart: 12 -> 12, of which waited for: 7 -> 5; matrix products, arithmetic and copies ran while one was open for 0% -> 0% of each run, Pallas kernels for 8% -> 10%
where the time goes in v7:
time: 78.5 us; the launch traced here: 78.1 us
  starting transfers between devices  31.8 us (41%)
  Pallas kernels  24.8 us (32%)
  blocking collectives  10.8 us (14%)
  waiting for transfers between devices  9.04 us (12%)
  local copies, waits for them, and re-layouts  0.9 us (1%)
  between operations  0.81 us (1%)
    pallas_call x10, Pallas kernels, call(): pl.pallas_call(functools.partial(kernel, sz), out_shape=out_shape, in_spe...  24.8 us
    ppermute x6, starting transfers between devices, swap(): lax.ppermute(own[j], everywhere, face_pairs(sz, j))  17 us
    all_to_all x3, starting transfers between devices, share(): return lax.all_to_all(chunk, axes, split_axis=0, concat_axis=0, tiled=True)  12.5 us
    all_to_all x1, blocking collectives, share(): return lax.all_to_all(chunk, axes, split_axis=0, concat_axis=0, tiled=True)  10.8 us
    all_to_all x3, waiting for transfers between devices, share(): return lax.all_to_all(chunk, axes, split_axis=0, concat_axis=0, tiled=True)  5.41 us
    ppermute x6, waiting for transfers between devices, swap(): lax.ppermute(own[j], everywhere, face_pairs(sz, j))  3.62 us
    ppermute x3, starting transfers between devices, rest(): return lax.ppermute(part, 'gz', [(0, 1), (1, 0)])  2.34 us
  transfers between devices with their start and end apart: 12, of which 5 were waited for; matrix products, arithmetic and copies ran while one was open for 0% of the time, Pallas kernels for 10%

profile of v7, /device:TPU:0, one launch (start us, length us, event | category | flops | bytes accessed | tf_op | source)
XLA Modules:
  0.0 78.1 jit_solution(18328421245405966617)
XLA Ops:
  0.7 1.9 %shard_map.91 = (f32[8,768]{1,0:T(8,128)}, f32[8,768]{1,0:T(8,128)}, f32[16,8,128]{2,1,0:T(8,128)}, f32[24,1536]{1,0:T(8,128)}) custom-call(f32[6,1,3072]{2,1,0:T(1,128)} %bitcast.7, f32[6,1,8]{2,1,0:T(1,128)} %bitcast.8, f32[6,1,96]{2,1,0:T(1,128)} %bitcast.9, f32[1,1,3072]{2,1,0:T(1,128)} %stiffness.1, s32[1,1,4,768]{3,2,1,0:T(4,128)} %orders.1, ...), custom_call_target="tpu_custom_call" | custom-call | tf_op jit(solution)/shard_map/pallas_call | solution.py:527
  2.5 0.7 collective-permute-start
  3.2 5.9 %collective-permute-start.1 = (f32[8,768]{1,0:T(8,128)}, f32[8,768]{1,0:T(8,128)S(1)}, u32[]{:S(2)}, u32[]{:S(2)}) collective-permute-start(f32[8,768]{1,0:T(8,128)} %get-tuple-element.26), channel_id=1, source_target_pairs={{0,8},{1,3},{2,10},{3,1},{4,12},{5,7},{6,14},{7,5},{8,0},{9,11},{1... | collective-permute-start | bytes 73736 | tf_op jit(solution)/shard_map/ppermute | solution.py:562
  9.1 3.7 %all-to-all-start = ((f32[16,8,128]{2,1,0:T(8,128)}), f32[16,8,128]{2,1,0:T(8,128)S(1)}, u32[]{:S(2)}, u32[]{:S(2)}) async-start(f32[16,8,128]{2,1,0:T(8,128)} %get-tuple-element.23), calls=%async_computation | async-start | bytes 131072 | tf_op jit(solution)/shard_map/all_to_all | solution.py:567
  12.8 0.0 collective-permute-done.refs_0_
  12.8 0.0 collective-permute-done.1.refs_1_
  12.8 0.0 copy-start
  12.8 0.9 %copy-done = f32[24,1536]{1,0:T(8,128)S(1)} copy-done((f32[24,1536]{1,0:T(8,128)S(1)}, f32[24,1536]{1,0:T(8,128)}, u32[]{:S(2)}) %copy-start) | copy-done | bytes 147480
  13.7 0.4 shard_map.92
  14.1 1.3 %collective-permute-start.2 = (f32[16,1536]{1,0:T(8,128)S(1)}, f32[16,1536]{1,0:T(8,128)S(1)}, u32[]{:S(2)}, u32[]{:S(2)}) collective-permute-start(f32[16,1536]{1,0:T(8,128)S(1)} %get-tuple-element.29.modes_ref), channel_id=1, source_target_pairs={{0,1},{1,0},{2,3},{3,2},{4,5},{5,4},{6,7},{7,6},{8,9},{9,8},{10,11... | collective-permute-start | bytes 294920 | tf_op jit(solution)/shard_map/ppermute | solution.py:571
  15.4 4.2 %all-to-all-done.shared = f32[16,8,128]{2,1,0:T(8,128)S(1)} async-done(((f32[16,8,128]{2,1,0:T(8,128)}), f32[16,8,128]{2,1,0:T(8,128)S(1)}, u32[]{:S(2)}, u32[]{:S(2)}) %all-to-all-start) | async-done | bytes 65568 | tf_op jit(solution)/shard_map/all_to_all | solution.py:567
  19.7 0.0 collective-permute-done.2.modes_rest
  19.7 5.8 %shard_map.93 = (f32[8,768]{1,0:T(8,128)S(1)}, f32[8,768]{1,0:T(8,128)S(1)}, f32[32,4,128]{2,1,0:T(4,128)}, f32[8,3072]{1,0:T(8,128)S(1)}) custom-call(bf16[192,8,3072]{2,1,0:T(8,128)(2,1)} %bitcast.4, f32[16,8,128]{2,1,0:T(8,128)S(1)} %all-to-all-done.shared, f32[8,1536]{1,0:T(8,128)S(1)} %get-tuple-element.27.right, ...), custom_call_target="tpu_custom_call" | custom-call | tf_op jit(solution)/shard_map/pallas_call | solution.py:527
  25.5 5.0 %all-to-all-start.1 = ((f32[32,4,128]{2,1,0:T(4,128)}), f32[32,4,128]{2,1,0:T(4,128)S(1)}, u32[]{:S(2)}, u32[]{:S(2)}) async-start(f32[32,4,128]{2,1,0:T(4,128)} %get-tuple-element.30), calls=%async_computation.1 | async-start | bytes 131072 | tf_op jit(solution)/shard_map/all_to_all | solution.py:567
  30.5 0.7 collective-permute-start.3
  31.2 4.5 %collective-permute-start.4 = (f32[8,768]{1,0:T(8,128)S(1)}, f32[8,768]{1,0:T(8,128)S(1)}, u32[]{:S(2)}, u32[]{:S(2)}) collective-permute-start(f32[8,768]{1,0:T(8,128)S(1)} %get-tuple-element.32.refs_1_), channel_id=1, source_target_pairs={{0,8},{1,3},{2,10},{3,1},{4,12},{5,7},{6,14},{7,5},{8,0},{9,11},{1... | collective-permute-start | bytes 73736 | tf_op jit(solution)/shard_map/ppermute | solution.py:562
  35.7 0.0 collective-permute-done.3.refs_2_
  35.8 1.8 %collective-permute-done.4.refs_3_ = f32[8,768]{1,0:T(8,128)S(1)} collective-permute-done((f32[8,768]{1,0:T(8,128)S(1)}, f32[8,768]{1,0:T(8,128)S(1)}, u32[]{:S(2)}, u32[]{:S(2)}) %collective-permute-start.4) | collective-permute-done | bytes 24608 | tf_op jit(solution)/shard_map/ppermute | solution.py:562
  37.6 0.6 all-to-all-done.1.pieces.before
  38.1 1.1 %shard_map.94 = (f32[8,1536]{1,0:T(8,128)S(1)}, f32[8,1536]{1,0:T(8,128)S(1)}) custom-call(f32[32,4,128]{2,1,0:T(4,128)S(1)} %all-to-all-done.1.pieces.before, f32[16,8,128]{2,1,0:T(8,128)S(1)} %all-to-all-done.shared, f32[16,1536]{1,0:T(8,128)S(1)} %get-tuple-element.29.modes_ref, f32[8,768]{1,0:T(8,128)S(1)} %get-tuple-element.31.refs_0_, ...), custom_call_target="tpu_custom_call" | custom-call | tf_op jit(solution)/shard_map/pallas_call | solution.py:527
  39.3 0.5 collective-permute-start.5
  39.8 3.8 %shard_map.95.held = bf16[192,8,3072]{2,1,0:T(8,128)(2,1)S(1)} custom-call(bf16[192,8,3072]{2,1,0:T(8,128)(2,1)} %bitcast.5, f32[8,1536]{1,0:T(8,128)S(1)} %get-tuple-element.33.after.direction.direction_ref), custom_call_target="tpu_custom_call" | custom-call | bytes 18874368 | tf_op jit(solution)/shard_map/pallas_call | solution.py:527
  43.6 0.0 collective-permute-done.5.rest.direction_rest
  43.6 3.4 %shard_map.96 = (f32[8,768]{1,0:T(8,128)S(1)}, f32[8,768]{1,0:T(8,128)S(1)}, f32[32,4,128]{2,1,0:T(4,128)}) custom-call(bf16[192,8,3072]{2,1,0:T(8,128)(2,1)S(1)} %shard_map.95.held, f32[16,1536]{1,0:T(8,128)S(1)} %get-tuple-element.29.modes_ref, f32[8,1536]{1,0:T(8,128)S(1)} %get-tuple-element.34.residual.residual_ref, ...), custom_call_target="tpu_custom_call" | custom-call | tf_op jit(solution)/shard_map/pallas_call | solution.py:527
  47.0 3.7 %all-to-all-start.2 = ((f32[32,4,128]{2,1,0:T(4,128)}), f32[32,4,128]{2,1,0:T(4,128)S(1)}, u32[]{:S(2)}, u32[]{:S(2)}) async-start(f32[32,4,128]{2,1,0:T(4,128)} %get-tuple-element.35), calls=%async_computation.2 | async-start | bytes 131072 | tf_op jit(solution)/shard_map/all_to_all | solution.py:567
  50.8 0.7 collective-permute-start.6
  51.4 4.5 %collective-permute-start.7 = (f32[8,768]{1,0:T(8,128)S(1)}, f32[8,768]{1,0:T(8,128)S(1)}, u32[]{:S(2)}, u32[]{:S(2)}) collective-permute-start(f32[8,768]{1,0:T(8,128)S(1)} %get-tuple-element.37.refs_1_), channel_id=1, source_target_pairs={{0,8},{1,3},{2,10},{3,1},{4,12},{5,7},{6,14},{7,5},{8,0},{9,11},{1... | collective-permute-start | bytes 73736 | tf_op jit(solution)/shard_map/ppermute | solution.py:562
  56.0 0.0 collective-permute-done.6.refs_2_
  56.0 1.8 %collective-permute-done.7.refs_3_ = f32[8,768]{1,0:T(8,128)S(1)} collective-permute-done((f32[8,768]{1,0:T(8,128)S(1)}, f32[8,768]{1,0:T(8,128)S(1)}, u32[]{:S(2)}, u32[]{:S(2)}) %collective-permute-start.7) | collective-permute-done | bytes 24608 | tf_op jit(solution)/shard_map/ppermute | solution.py:562
  57.8 0.6 all-to-all-done.2.pieces
  58.4 1.1 %shard_map.97 = (f32[8,1536]{1,0:T(8,128)S(1)}, f32[8,128]{1,0:T(8,128)S(1)}) custom-call(f32[32,4,128]{2,1,0:T(4,128)S(1)} %all-to-all-done.2.pieces, f32[16,8,128]{2,1,0:T(8,128)S(1)} %all-to-all-done.shared, f32[32,4,128]{2,1,0:T(4,128)S(1)} %all-to-all-done.1.pieces.before, f32[16,1536]{1,0:T(8,128)S(1)} %get-tuple-element.29.modes_ref, ...), custom_call_target="tpu_custom_call" | custom-call | tf_op jit(solution)/shard_map/pallas_call | solution.py:527
  59.5 0.5 collective-permute-start.8
  60.0 3.8 %shard_map.98.held = bf16[192,8,3072]{2,1,0:T(8,128)(2,1)S(1)} custom-call(bf16[192,8,3072]{2,1,0:T(8,128)(2,1)} %bitcast.6, f32[8,1536]{1,0:T(8,128)S(1)} %get-tuple-element.38.after.later), custom_call_target="tpu_custom_call" | custom-call | bytes 18874368 | tf_op jit(solution)/shard_map/pallas_call | solution.py:527
  63.9 0.0 collective-permute-done.8.rest.later_rest
  63.9 2.6 %shard_map.99 = f32[32,1,128]{2,1,0:T(1,128)S(1)} custom-call(bf16[192,8,3072]{2,1,0:T(8,128)(2,1)S(1)} %shard_map.98.held, f32[8,1536]{1,0:T(8,128)S(1)} %get-tuple-element.33.after.direction.direction_ref, f32[8,128]{1,0:T(8,128)S(1)} %get-tuple-element.39.scalars, f32[8,1536]{1,0:T(8,128)S(1)} %get-tuple-element.38.after.later, ...), custom_call_target="tpu_custom_call" | custom-call | tf_op jit(solution)/shard_map/pallas_call | solution.py:527
  66.5 10.8 %all_to_all.20.pieces = f32[32,1,128]{2,1,0:T(1,128)S(1)} all-to-all(f32[32,1,128]{2,1,0:T(1,128)S(1)} %shard_map.99), channel_id=1, replica_groups=mesh['gx'=4,'gy'=4,'gz'=2] {'gx','gy','gz'}, dimensions={0} | all-to-all | bytes 32768 | tf_op jit(solution)/shard_map/all_to_all | solution.py:567
  77.3 0.8 %shard_map.100 = f32[1,1,8,3072]{3,2,1,0:T(8,128)} custom-call(f32[32,1,128]{2,1,0:T(1,128)S(1)} %all_to_all.20.pieces, f32[8,128]{1,0:T(8,128)S(1)} %get-tuple-element.39.scalars, f32[8,3072]{1,0:T(8,128)S(1)} %get-tuple-element.40.estimate, f32[8,1536]{1,0:T(8,128)S(1)} %get-tuple-element.33.after.direction.direction_ref, ...), custom_call_target="tpu_custom_call" | custom-call | tf_op jit(solution)/shard_map/pallas_call | solution.py:527
Async XLA Ops:
  2.5 10.3 %collective-permute-start = (f32[8,768]{1,0:T(8,128)}, f32[8,768]{1,0:T(8,128)S(1)}, u32[]{:S(2)}, u32[]{:S(2)}) collective-permute-start(f32[8,768]{1,0:T(8,128)} %get-tuple-element.25), channel_id=1, source_target_pairs={{3,5},{5,3},{8,16},{10,18},{11,13},{12,20},{13,11},{14,22},{16,8},... | collective-permute-start | bytes 73736 | tf_op jit(solution)/shard_map/ppermute | solution.py:562
  3.2 9.6 %collective-permute-start.1 = (f32[8,768]{1,0:T(8,128)}, f32[8,768]{1,0:T(8,128)S(1)}, u32[]{:S(2)}, u32[]{:S(2)}) collective-permute-start(f32[8,768]{1,0:T(8,128)} %get-tuple-element.26), channel_id=1, source_target_pairs={{0,8},{1,3},{2,10},{3,1},{4,12},{5,7},{6,14},{7,5},{8,0},{9,11},{1... | collective-permute-start | bytes 73736 | tf_op jit(solution)/shard_map/ppermute | solution.py:562
  9.1 10.6 %all-to-all-start = ((f32[16,8,128]{2,1,0:T(8,128)}), f32[16,8,128]{2,1,0:T(8,128)S(1)}, u32[]{:S(2)}, u32[]{:S(2)}) async-start(f32[16,8,128]{2,1,0:T(8,128)} %get-tuple-element.23), calls=%async_computation | async-start | bytes 131072 | tf_op jit(solution)/shard_map/all_to_all | solution.py:567
  12.8 0.9 %copy-start = (f32[24,1536]{1,0:T(8,128)S(1)}, f32[24,1536]{1,0:T(8,128)}, u32[]{:S(2)}) copy-start(f32[24,1536]{1,0:T(8,128)} %get-tuple-element.24.base) | copy-start | bytes 442372
  14.1 5.6 %collective-permute-start.2 = (f32[16,1536]{1,0:T(8,128)S(1)}, f32[16,1536]{1,0:T(8,128)S(1)}, u32[]{:S(2)}, u32[]{:S(2)}) collective-permute-start(f32[16,1536]{1,0:T(8,128)S(1)} %get-tuple-element.29.modes_ref), channel_id=1, source_target_pairs={{0,1},{1,0},{2,3},{3,2},{4,5},{5,4},{6,7},{7,6},{8,9},{9,8},{10,11... | collective-permute-start | bytes 294920 | tf_op jit(solution)/shard_map/ppermute | solution.py:571
  25.5 12.6 %all-to-all-start.1 = ((f32[32,4,128]{2,1,0:T(4,128)}), f32[32,4,128]{2,1,0:T(4,128)S(1)}, u32[]{:S(2)}, u32[]{:S(2)}) async-start(f32[32,4,128]{2,1,0:T(4,128)} %get-tuple-element.30), calls=%async_computation.1 | async-start | bytes 131072 | tf_op jit(solution)/shard_map/all_to_all | solution.py:567
  30.5 5.2 %collective-permute-start.3 = (f32[8,768]{1,0:T(8,128)S(1)}, f32[8,768]{1,0:T(8,128)S(1)}, u32[]{:S(2)}, u32[]{:S(2)}) collective-permute-start(f32[8,768]{1,0:T(8,128)S(1)} %get-tuple-element.31.refs_0_), channel_id=1, source_target_pairs={{3,5},{5,3},{8,16},{10,18},{11,13},{12,20},{13,11},{14,22},{16,8},... | collective-permute-start | bytes 73736 | tf_op jit(solution)/shard_map/ppermute | solution.py:562
  31.2 6.4 %collective-permute-start.4 = (f32[8,768]{1,0:T(8,128)S(1)}, f32[8,768]{1,0:T(8,128)S(1)}, u32[]{:S(2)}, u32[]{:S(2)}) collective-permute-start(f32[8,768]{1,0:T(8,128)S(1)} %get-tuple-element.32.refs_1_), channel_id=1, source_target_pairs={{0,8},{1,3},{2,10},{3,1},{4,12},{5,7},{6,14},{7,5},{8,0},{9,11},{1... | collective-permute-start | bytes 73736 | tf_op jit(solution)/shard_map/ppermute | solution.py:562
  39.3 4.4 %collective-permute-start.5 = (f32[8,1536]{1,0:T(8,128)S(1)}, f32[8,1536]{1,0:T(8,128)S(1)}, u32[]{:S(2)}, u32[]{:S(2)}) collective-permute-start(f32[8,1536]{1,0:T(8,128)S(1)} %get-tuple-element.33.after.direction.direction_ref), channel_id=1, source_target_pairs={{0,1},{1,0},{2,3},{3,2},{4,5},{5,4},{6,7},{7,6},{8,9},{9,8},{10,11... | collective-permute-start | bytes 147464 | tf_op jit(solution)/shard_map/ppermute | solution.py:571
  47.0 11.4 %all-to-all-start.2 = ((f32[32,4,128]{2,1,0:T(4,128)}), f32[32,4,128]{2,1,0:T(4,128)S(1)}, u32[]{:S(2)}, u32[]{:S(2)}) async-start(f32[32,4,128]{2,1,0:T(4,128)} %get-tuple-element.35), calls=%async_computation.2 | async-start | bytes 131072 | tf_op jit(solution)/shard_map/all_to_all | solution.py:567
  50.8 5.2 %collective-permute-start.6 = (f32[8,768]{1,0:T(8,128)S(1)}, f32[8,768]{1,0:T(8,128)S(1)}, u32[]{:S(2)}, u32[]{:S(2)}) collective-permute-start(f32[8,768]{1,0:T(8,128)S(1)} %get-tuple-element.36.refs_0_), channel_id=1, source_target_pairs={{3,5},{5,3},{8,16},{10,18},{11,13},{12,20},{13,11},{14,22},{16,8},... | collective-permute-start | bytes 73736 | tf_op jit(solution)/shard_map/ppermute | solution.py:562
  51.4 6.4 %collective-permute-start.7 = (f32[8,768]{1,0:T(8,128)S(1)}, f32[8,768]{1,0:T(8,128)S(1)}, u32[]{:S(2)}, u32[]{:S(2)}) collective-permute-start(f32[8,768]{1,0:T(8,128)S(1)} %get-tuple-element.37.refs_1_), channel_id=1, source_target_pairs={{0,8},{1,3},{2,10},{3,1},{4,12},{5,7},{6,14},{7,5},{8,0},{9,11},{1... | collective-permute-start | bytes 73736 | tf_op jit(solution)/shard_map/ppermute | solution.py:562
  59.5 4.4 %collective-permute-start.8 = (f32[8,1536]{1,0:T(8,128)S(1)}, f32[8,1536]{1,0:T(8,128)S(1)}, u32[]{:S(2)}, u32[]{:S(2)}) collective-permute-start(f32[8,1536]{1,0:T(8,128)S(1)} %get-tuple-element.38.after.later), channel_id=1, source_target_pairs={{0,1},{1,0},{2,3},{3,2},{4,5},{5,4},{6,7},{7,6},{8,9},{9,8},{10,11... | collective-permute-start | bytes 147464 | tf_op jit(solution)/shard_map/ppermute | solution.py:571

commit v8 on v7

--- a/solution.py
+++ b/solution.py
@@ -99,11 +99,11 @@
 
 def put_slots(sz, outs, values):
     for out, value in zip(outs, by_slot(sz, values)):
-        out[...] = value
+        out[...] = value.astype(out.dtype)
 
 
 def get_slots(sz, refs):
-    return by_slot(sz, [ref[...] for ref in refs])
+    return by_slot(sz, [ref[...].astype(jnp.float32) for ref in refs])
 
 
 def permuted(sz, block, slots):
@@ -540,6 +540,7 @@
     coarse = pltpu.VMEM((8, sz.coarse_pad), jnp.float32)
     square = pltpu.VMEM((sz.coarse_pad, sz.coarse_pad), jnp.float32)
     half, full, face = f32(8, sz.rows), f32(8, sz.order), f32(8, sz.cap)
+    rounded_face = jax.ShapeDtypeStruct((8, sz.cap), jnp.bfloat16)
     blocks = operator.reshape(sz.rows // 8, 8, sz.order)
     one_step = sz.devices <= 64
     spread_tile = f32(sz.devices if one_step else 1, 4, TILE)
@@ -606,7 +607,7 @@
     )
     direction_rest = rest(direction)
     *own, pay = call(
-        second_apply_kernel, [face] * faces + [spread_tile], [vmem] * 5,
+        second_apply_kernel, [rounded_face] * faces + [spread_tile], [vmem] * 5,
         apply_scratch, hold(direction), modes, residual, direction, direction_rest,
     )
     after = share(pay, everywhere)

time: 78.5 us -> 78.4 us (level)
  no operation moved by 1% of the time
where the time goes in v8:
time: 78.4 us; the launch traced here: 78 us
  starting transfers between devices  31.8 us (41%)
  Pallas kernels  24.8 us (32%)
  blocking collectives  10.6 us (14%)
  waiting for transfers between devices  9.04 us (12%)
  local copies, waits for them, and re-layouts  0.9 us (1%)
  between operations  0.81 us (1%)
    pallas_call x10, Pallas kernels, call(): pl.pallas_call(functools.partial(kernel, sz), out_shape=out_shape, in_spe...  24.8 us
    ppermute x6, starting transfers between devices, swap(): lax.ppermute(own[j], everywhere, face_pairs(sz, j))  17 us
    all_to_all x3, starting transfers between devices, share(): return lax.all_to_all(chunk, axes, split_axis=0, concat_axis=0, tiled=True)  12.5 us
    all_to_all x1, blocking collectives, share(): return lax.all_to_all(chunk, axes, split_axis=0, concat_axis=0, tiled=True)  10.6 us
    all_to_all x3, waiting for transfers between devices, share(): return lax.all_to_all(chunk, axes, split_axis=0, concat_axis=0, tiled=True)  5.54 us
    ppermute x6, waiting for transfers between devices, swap(): lax.ppermute(own[j], everywhere, face_pairs(sz, j))  3.49 us
    ppermute x3, starting transfers between devices, rest(): return lax.ppermute(part, 'gz', [(0, 1), (1, 0)])  2.34 us
  transfers between devices with their start and end apart: 12, of which 5 were waited for; matrix products, arithmetic and copies ran while one was open for 0% of the time, Pallas kernels for 10%

profile of v8, /device:TPU:0, one launch (start us, length us, event | category | flops | bytes accessed | tf_op | source)
XLA Modules:
  0.0 78.0 jit_solution(10601423783611601523)
XLA Ops:
  0.7 1.9 %shard_map.91 = (f32[8,768]{1,0:T(8,128)}, f32[8,768]{1,0:T(8,128)}, f32[16,8,128]{2,1,0:T(8,128)}, f32[24,1536]{1,0:T(8,128)}) custom-call(f32[6,1,3072]{2,1,0:T(1,128)} %bitcast.7, f32[6,1,8]{2,1,0:T(1,128)} %bitcast.8, f32[6,1,96]{2,1,0:T(1,128)} %bitcast.9, f32[1,1,3072]{2,1,0:T(1,128)} %stiffness.1, s32[1,1,4,768]{3,2,1,0:T(4,128)} %orders.1, ...), custom_call_target="tpu_custom_call" | custom-call | tf_op jit(solution)/shard_map/pallas_call | solution.py:527
  2.5 0.7 collective-permute-start
  3.2 5.9 %collective-permute-start.1 = (f32[8,768]{1,0:T(8,128)}, f32[8,768]{1,0:T(8,128)S(1)}, u32[]{:S(2)}, u32[]{:S(2)}) collective-permute-start(f32[8,768]{1,0:T(8,128)} %get-tuple-element.26), channel_id=1, source_target_pairs={{0,8},{1,3},{2,10},{3,1},{4,12},{5,7},{6,14},{7,5},{8,0},{9,11},{1... | collective-permute-start | bytes 73736 | tf_op jit(solution)/shard_map/ppermute | solution.py:563
  9.1 3.7 %all-to-all-start = ((f32[16,8,128]{2,1,0:T(8,128)}), f32[16,8,128]{2,1,0:T(8,128)S(1)}, u32[]{:S(2)}, u32[]{:S(2)}) async-start(f32[16,8,128]{2,1,0:T(8,128)} %get-tuple-element.23), calls=%async_computation | async-start | bytes 131072 | tf_op jit(solution)/shard_map/all_to_all | solution.py:568
  12.8 0.0 collective-permute-done.refs_0_
  12.8 0.0 collective-permute-done.1.refs_1_
  12.8 0.0 copy-start
  12.8 0.9 %copy-done = f32[24,1536]{1,0:T(8,128)S(1)} copy-done((f32[24,1536]{1,0:T(8,128)S(1)}, f32[24,1536]{1,0:T(8,128)}, u32[]{:S(2)}) %copy-start) | copy-done | bytes 147480
  13.7 0.4 shard_map.92
  14.1 1.3 %collective-permute-start.2 = (f32[16,1536]{1,0:T(8,128)S(1)}, f32[16,1536]{1,0:T(8,128)S(1)}, u32[]{:S(2)}, u32[]{:S(2)}) collective-permute-start(f32[16,1536]{1,0:T(8,128)S(1)} %get-tuple-element.29.modes_ref), channel_id=1, source_target_pairs={{0,1},{1,0},{2,3},{3,2},{4,5},{5,4},{6,7},{7,6},{8,9},{9,8},{10,11... | collective-permute-start | bytes 294920 | tf_op jit(solution)/shard_map/ppermute | solution.py:572
  15.4 4.2 %all-to-all-done.shared = f32[16,8,128]{2,1,0:T(8,128)S(1)} async-done(((f32[16,8,128]{2,1,0:T(8,128)}), f32[16,8,128]{2,1,0:T(8,128)S(1)}, u32[]{:S(2)}, u32[]{:S(2)}) %all-to-all-start) | async-done | bytes 65568 | tf_op jit(solution)/shard_map/all_to_all | solution.py:568
  19.7 0.0 collective-permute-done.2.modes_rest
  19.7 5.8 %shard_map.93 = (f32[8,768]{1,0:T(8,128)S(1)}, f32[8,768]{1,0:T(8,128)S(1)}, f32[32,4,128]{2,1,0:T(4,128)}, f32[8,3072]{1,0:T(8,128)S(1)}) custom-call(bf16[192,8,3072]{2,1,0:T(8,128)(2,1)} %bitcast.4, f32[16,8,128]{2,1,0:T(8,128)S(1)} %all-to-all-done.shared, f32[8,1536]{1,0:T(8,128)S(1)} %get-tuple-element.27.right, ...), custom_call_target="tpu_custom_call" | custom-call | tf_op jit(solution)/shard_map/pallas_call | solution.py:527
  25.5 5.0 %all-to-all-start.1 = ((f32[32,4,128]{2,1,0:T(4,128)}), f32[32,4,128]{2,1,0:T(4,128)S(1)}, u32[]{:S(2)}, u32[]{:S(2)}) async-start(f32[32,4,128]{2,1,0:T(4,128)} %get-tuple-element.30), calls=%async_computation.1 | async-start | bytes 131072 | tf_op jit(solution)/shard_map/all_to_all | solution.py:568
  30.5 0.7 collective-permute-start.3
  31.2 4.5 %collective-permute-start.4 = (f32[8,768]{1,0:T(8,128)S(1)}, f32[8,768]{1,0:T(8,128)S(1)}, u32[]{:S(2)}, u32[]{:S(2)}) collective-permute-start(f32[8,768]{1,0:T(8,128)S(1)} %get-tuple-element.32.refs_1_), channel_id=1, source_target_pairs={{0,8},{1,3},{2,10},{3,1},{4,12},{5,7},{6,14},{7,5},{8,0},{9,11},{1... | collective-permute-start | bytes 73736 | tf_op jit(solution)/shard_map/ppermute | solution.py:563
  35.7 0.0 collective-permute-done.3.refs_2_
  35.8 1.8 %collective-permute-done.4.refs_3_ = f32[8,768]{1,0:T(8,128)S(1)} collective-permute-done((f32[8,768]{1,0:T(8,128)S(1)}, f32[8,768]{1,0:T(8,128)S(1)}, u32[]{:S(2)}, u32[]{:S(2)}) %collective-permute-start.4) | collective-permute-done | bytes 24608 | tf_op jit(solution)/shard_map/ppermute | solution.py:563
  37.6 0.6 all-to-all-done.1.pieces.before
  38.1 1.1 %shard_map.94 = (f32[8,1536]{1,0:T(8,128)S(1)}, f32[8,1536]{1,0:T(8,128)S(1)}) custom-call(f32[32,4,128]{2,1,0:T(4,128)S(1)} %all-to-all-done.1.pieces.before, f32[16,8,128]{2,1,0:T(8,128)S(1)} %all-to-all-done.shared, f32[16,1536]{1,0:T(8,128)S(1)} %get-tuple-element.29.modes_ref, f32[8,768]{1,0:T(8,128)S(1)} %get-tuple-element.31.refs_0_, ...), custom_call_target="tpu_custom_call" | custom-call | tf_op jit(solution)/shard_map/pallas_call | solution.py:527
  39.3 0.5 collective-permute-start.5
  39.8 3.8 %shard_map.95.held = bf16[192,8,3072]{2,1,0:T(8,128)(2,1)S(1)} custom-call(bf16[192,8,3072]{2,1,0:T(8,128)(2,1)} %bitcast.5, f32[8,1536]{1,0:T(8,128)S(1)} %get-tuple-element.33.after.direction.direction_ref), custom_call_target="tpu_custom_call" | custom-call | bytes 18874368 | tf_op jit(solution)/shard_map/pallas_call | solution.py:527
  43.6 0.0 collective-permute-done.5.rest.direction_rest
  43.6 3.4 %shard_map.96 = (bf16[8,768]{1,0:T(8,128)(2,1)S(1)}, bf16[8,768]{1,0:T(8,128)(2,1)S(1)}, f32[32,4,128]{2,1,0:T(4,128)}) custom-call(bf16[192,8,3072]{2,1,0:T(8,128)(2,1)S(1)} %shard_map.95.held, f32[16,1536]{1,0:T(8,128)S(1)} %get-tuple-element.29.modes_ref, f32[8,1536]{1,0:T(8,128)S(1)} %get-tuple-element.34.residual.residual_ref, ...), custom_call_target="tpu_custom_call" | custom-call | tf_op jit(solution)/shard_map/pallas_call | solution.py:527
  47.0 3.7 %all-to-all-start.2 = ((f32[32,4,128]{2,1,0:T(4,128)}), f32[32,4,128]{2,1,0:T(4,128)S(1)}, u32[]{:S(2)}, u32[]{:S(2)}) async-start(f32[32,4,128]{2,1,0:T(4,128)} %get-tuple-element.35), calls=%async_computation.2 | async-start | bytes 131072 | tf_op jit(solution)/shard_map/all_to_all | solution.py:568
  50.8 0.7 collective-permute-start.6
  51.4 4.5 %collective-permute-start.7 = (bf16[8,768]{1,0:T(8,128)(2,1)S(1)}, bf16[8,768]{1,0:T(8,128)(2,1)S(1)}, u32[]{:S(2)}, u32[]{:S(2)}) collective-permute-start(bf16[8,768]{1,0:T(8,128)(2,1)S(1)} %get-tuple-element.37.refs_1_), channel_id=1, source_target_pairs={{0,8},{1,3},{2,10},{3,1},{4,12},{5,7},{6,14},{7,5},{8,0},{9,11},{1... | collective-permute-start | bytes 36872 | tf_op jit(solution)/shard_map/ppermute | solution.py:563
  56.0 0.0 collective-permute-done.6.refs_2_
  56.0 1.7 %collective-permute-done.7.refs_3_ = bf16[8,768]{1,0:T(8,128)(2,1)S(1)} collective-permute-done((bf16[8,768]{1,0:T(8,128)(2,1)S(1)}, bf16[8,768]{1,0:T(8,128)(2,1)S(1)}, u32[]{:S(2)}, u32[]{:S(2)}) %collective-permute-start.7) | collective-permute-done | bytes 12320 | tf_op jit(solution)/shard_map/ppermute | solution.py:563
  57.7 0.7 all-to-all-done.2.pieces
  58.4 1.1 %shard_map.97 = (f32[8,1536]{1,0:T(8,128)S(1)}, f32[8,128]{1,0:T(8,128)S(1)}) custom-call(f32[32,4,128]{2,1,0:T(4,128)S(1)} %all-to-all-done.2.pieces, f32[16,8,128]{2,1,0:T(8,128)S(1)} %all-to-all-done.shared, f32[32,4,128]{2,1,0:T(4,128)S(1)} %all-to-all-done.1.pieces.before, f32[16,1536]{1,0:T(8,128)S(1)} %get-tuple-element.29.modes_ref, ...), custom_call_target="tpu_custom_call" | custom-call | tf_op jit(solution)/shard_map/pallas_call | solution.py:527
  59.5 0.5 collective-permute-start.8
  60.0 3.8 %shard_map.98.held = bf16[192,8,3072]{2,1,0:T(8,128)(2,1)S(1)} custom-call(bf16[192,8,3072]{2,1,0:T(8,128)(2,1)} %bitcast.6, f32[8,1536]{1,0:T(8,128)S(1)} %get-tuple-element.38.after.later), custom_call_target="tpu_custom_call" | custom-call | bytes 18874368 | tf_op jit(solution)/shard_map/pallas_call | solution.py:527
  63.9 0.0 collective-permute-done.8.rest.later_rest
  63.9 2.6 %shard_map.99 = f32[32,1,128]{2,1,0:T(1,128)S(1)} custom-call(bf16[192,8,3072]{2,1,0:T(8,128)(2,1)S(1)} %shard_map.98.held, f32[8,1536]{1,0:T(8,128)S(1)} %get-tuple-element.33.after.direction.direction_ref, f32[8,128]{1,0:T(8,128)S(1)} %get-tuple-element.39.scalars, f32[8,1536]{1,0:T(8,128)S(1)} %get-tuple-element.38.after.later, ...), custom_call_target="tpu_custom_call" | custom-call | tf_op jit(solution)/shard_map/pallas_call | solution.py:527
  66.5 10.6 %all_to_all.20.pieces = f32[32,1,128]{2,1,0:T(1,128)S(1)} all-to-all(f32[32,1,128]{2,1,0:T(1,128)S(1)} %shard_map.99), channel_id=1, replica_groups=mesh['gx'=4,'gy'=4,'gz'=2] {'gx','gy','gz'}, dimensions={0} | all-to-all | bytes 32768 | tf_op jit(solution)/shard_map/all_to_all | solution.py:568
  77.2 0.8 %shard_map.100 = f32[1,1,8,3072]{3,2,1,0:T(8,128)} custom-call(f32[32,1,128]{2,1,0:T(1,128)S(1)} %all_to_all.20.pieces, f32[8,128]{1,0:T(8,128)S(1)} %get-tuple-element.39.scalars, f32[8,3072]{1,0:T(8,128)S(1)} %get-tuple-element.40.estimate, f32[8,1536]{1,0:T(8,128)S(1)} %get-tuple-element.33.after.direction.direction_ref, ...), custom_call_target="tpu_custom_call" | custom-call | tf_op jit(solution)/shard_map/pallas_call | solution.py:527
Async XLA Ops:
  2.5 10.3 %collective-permute-start = (f32[8,768]{1,0:T(8,128)}, f32[8,768]{1,0:T(8,128)S(1)}, u32[]{:S(2)}, u32[]{:S(2)}) collective-permute-start(f32[8,768]{1,0:T(8,128)} %get-tuple-element.25), channel_id=1, source_target_pairs={{3,5},{5,3},{8,16},{10,18},{11,13},{12,20},{13,11},{14,22},{16,8},... | collective-permute-start | bytes 73736 | tf_op jit(solution)/shard_map/ppermute | solution.py:563
  3.2 9.6 %collective-permute-start.1 = (f32[8,768]{1,0:T(8,128)}, f32[8,768]{1,0:T(8,128)S(1)}, u32[]{:S(2)}, u32[]{:S(2)}) collective-permute-start(f32[8,768]{1,0:T(8,128)} %get-tuple-element.26), channel_id=1, source_target_pairs={{0,8},{1,3},{2,10},{3,1},{4,12},{5,7},{6,14},{7,5},{8,0},{9,11},{1... | collective-permute-start | bytes 73736 | tf_op jit(solution)/shard_map/ppermute | solution.py:563
  9.1 10.6 %all-to-all-start = ((f32[16,8,128]{2,1,0:T(8,128)}), f32[16,8,128]{2,1,0:T(8,128)S(1)}, u32[]{:S(2)}, u32[]{:S(2)}) async-start(f32[16,8,128]{2,1,0:T(8,128)} %get-tuple-element.23), calls=%async_computation | async-start | bytes 131072 | tf_op jit(solution)/shard_map/all_to_all | solution.py:568
  12.8 0.9 %copy-start = (f32[24,1536]{1,0:T(8,128)S(1)}, f32[24,1536]{1,0:T(8,128)}, u32[]{:S(2)}) copy-start(f32[24,1536]{1,0:T(8,128)} %get-tuple-element.24.base) | copy-start | bytes 442372
  14.1 5.6 %collective-permute-start.2 = (f32[16,1536]{1,0:T(8,128)S(1)}, f32[16,1536]{1,0:T(8,128)S(1)}, u32[]{:S(2)}, u32[]{:S(2)}) collective-permute-start(f32[16,1536]{1,0:T(8,128)S(1)} %get-tuple-element.29.modes_ref), channel_id=1, source_target_pairs={{0,1},{1,0},{2,3},{3,2},{4,5},{5,4},{6,7},{7,6},{8,9},{9,8},{10,11... | collective-permute-start | bytes 294920 | tf_op jit(solution)/shard_map/ppermute | solution.py:572
  25.5 12.6 %all-to-all-start.1 = ((f32[32,4,128]{2,1,0:T(4,128)}), f32[32,4,128]{2,1,0:T(4,128)S(1)}, u32[]{:S(2)}, u32[]{:S(2)}) async-start(f32[32,4,128]{2,1,0:T(4,128)} %get-tuple-element.30), calls=%async_computation.1 | async-start | bytes 131072 | tf_op jit(solution)/shard_map/all_to_all | solution.py:568
  30.5 5.2 %collective-permute-start.3 = (f32[8,768]{1,0:T(8,128)S(1)}, f32[8,768]{1,0:T(8,128)S(1)}, u32[]{:S(2)}, u32[]{:S(2)}) collective-permute-start(f32[8,768]{1,0:T(8,128)S(1)} %get-tuple-element.31.refs_0_), channel_id=1, source_target_pairs={{3,5},{5,3},{8,16},{10,18},{11,13},{12,20},{13,11},{14,22},{16,8},... | collective-permute-start | bytes 73736 | tf_op jit(solution)/shard_map/ppermute | solution.py:563
  31.2 6.4 %collective-permute-start.4 = (f32[8,768]{1,0:T(8,128)S(1)}, f32[8,768]{1,0:T(8,128)S(1)}, u32[]{:S(2)}, u32[]{:S(2)}) collective-permute-start(f32[8,768]{1,0:T(8,128)S(1)} %get-tuple-element.32.refs_1_), channel_id=1, source_target_pairs={{0,8},{1,3},{2,10},{3,1},{4,12},{5,7},{6,14},{7,5},{8,0},{9,11},{1... | collective-permute-start | bytes 73736 | tf_op jit(solution)/shard_map/ppermute | solution.py:563
  39.3 4.4 %collective-permute-start.5 = (f32[8,1536]{1,0:T(8,128)S(1)}, f32[8,1536]{1,0:T(8,128)S(1)}, u32[]{:S(2)}, u32[]{:S(2)}) collective-permute-start(f32[8,1536]{1,0:T(8,128)S(1)} %get-tuple-element.33.after.direction.direction_ref), channel_id=1, source_target_pairs={{0,1},{1,0},{2,3},{3,2},{4,5},{5,4},{6,7},{7,6},{8,9},{9,8},{10,11... | collective-permute-start | bytes 147464 | tf_op jit(solution)/shard_map/ppermute | solution.py:572
  47.0 11.4 %all-to-all-start.2 = ((f32[32,4,128]{2,1,0:T(4,128)}), f32[32,4,128]{2,1,0:T(4,128)S(1)}, u32[]{:S(2)}, u32[]{:S(2)}) async-start(f32[32,4,128]{2,1,0:T(4,128)} %get-tuple-element.35), calls=%async_computation.2 | async-start | bytes 131072 | tf_op jit(solution)/shard_map/all_to_all | solution.py:568
  50.8 5.2 %collective-permute-start.6 = (bf16[8,768]{1,0:T(8,128)(2,1)S(1)}, bf16[8,768]{1,0:T(8,128)(2,1)S(1)}, u32[]{:S(2)}, u32[]{:S(2)}) collective-permute-start(bf16[8,768]{1,0:T(8,128)(2,1)S(1)} %get-tuple-element.36.refs_0_), channel_id=1, source_target_pairs={{3,5},{5,3},{8,16},{10,18},{11,13},{12,20},{13,11},{14,22},{16,8},... | collective-permute-start | bytes 36872 | tf_op jit(solution)/shard_map/ppermute | solution.py:563
  51.4 6.2 %collective-permute-start.7 = (bf16[8,768]{1,0:T(8,128)(2,1)S(1)}, bf16[8,768]{1,0:T(8,128)(2,1)S(1)}, u32[]{:S(2)}, u32[]{:S(2)}) collective-permute-start(bf16[8,768]{1,0:T(8,128)(2,1)S(1)} %get-tuple-element.37.refs_1_), channel_id=1, source_target_pairs={{0,8},{1,3},{2,10},{3,1},{4,12},{5,7},{6,14},{7,5},{8,0},{9,11},{1... | collective-permute-start | bytes 36872 | tf_op jit(solution)/shard_map/ppermute | solution.py:563
  59.5 4.4 %collective-permute-start.8 = (f32[8,1536]{1,0:T(8,128)S(1)}, f32[8,1536]{1,0:T(8,128)S(1)}, u32[]{:S(2)}, u32[]{:S(2)}) collective-permute-start(f32[8,1536]{1,0:T(8,128)S(1)} %get-tuple-element.38.after.later), channel_id=1, source_target_pairs={{0,1},{1,0},{2,3},{3,2},{4,5},{5,4},{6,7},{7,6},{8,9},{9,8},{10,11... | collective-permute-start | bytes 147464 | tf_op jit(solution)/shard_map/ppermute | solution.py:572

commit v9 on v7

--- a/solution.py
+++ b/solution.py
@@ -9,6 +9,7 @@
 
 ROW_CHUNK = 256
 PIECE = 128
+HOLD_PIECE = 64
 LOAD_LANE = 6
 TILE = 128
 SLOT = 8
@@ -281,9 +282,9 @@
 
 def hold_kernel(sz, operator, after, held, sems):
     del after
-    blocks = ROW_CHUNK // 8
+    blocks = HOLD_PIECE // 8
     copies = []
-    for k in range(sz.rows // ROW_CHUNK):
+    for k in range(sz.rows // HOLD_PIECE):
         here = pl.ds(k * blocks, blocks)
         copies.append(pltpu.make_async_copy(operator.at[here], held.at[here], sems.at[k]))
         copies[-1].start()
@@ -554,7 +555,7 @@
     def hold(after):
         return call(
             hold_kernel, jax.ShapeDtypeStruct((sz.rows // 8, 8, sz.order), jnp.bfloat16),
-            [hbm, vmem], [pltpu.SemaphoreType.DMA((copies,))], blocks, after, limit=42,
+            [hbm, vmem], [pltpu.SemaphoreType.DMA((sz.rows // HOLD_PIECE,))], blocks, after, limit=42,
             cost=pl.CostEstimate(flops=0, bytes_accessed=4 * sz.rows * sz.order, transcendentals=0),
         )
 

time: 78.5 us -> 78.6 us (level)
  no operation moved by 1% of the time
where the time goes in v9:
time: 78.6 us; the launch traced here: 78.2 us
  starting transfers between devices  31.8 us (40%)
  Pallas kernels  24.9 us (32%)
  blocking collectives  10.8 us (14%)
  waiting for transfers between devices  9.04 us (12%)
  local copies, waits for them, and re-layouts  0.9 us (1%)
  between operations  0.81 us (1%)
    pallas_call x10, Pallas kernels, call(): pl.pallas_call(functools.partial(kernel, sz), out_shape=out_shape, in_spe...  24.9 us
    ppermute x6, starting transfers between devices, swap(): lax.ppermute(own[j], everywhere, face_pairs(sz, j))  17 us
    all_to_all x3, starting transfers between devices, share(): return lax.all_to_all(chunk, axes, split_axis=0, concat_axis=0, tiled=True)  12.5 us
    all_to_all x1, blocking collectives, share(): return lax.all_to_all(chunk, axes, split_axis=0, concat_axis=0, tiled=True)  10.8 us
    all_to_all x3, waiting for transfers between devices, share(): return lax.all_to_all(chunk, axes, split_axis=0, concat_axis=0, tiled=True)  5.41 us
    ppermute x6, waiting for transfers between devices, swap(): lax.ppermute(own[j], everywhere, face_pairs(sz, j))  3.62 us
    ppermute x3, starting transfers between devices, rest(): return lax.ppermute(part, 'gz', [(0, 1), (1, 0)])  2.34 us
  transfers between devices with their start and end apart: 12, of which 5 were waited for; matrix products, arithmetic and copies ran while one was open for 0% of the time, Pallas kernels for 10%

profile of v9, /device:TPU:0, one launch (start us, length us, event | category | flops | bytes accessed | tf_op | source)
XLA Modules:
  0.0 78.2 jit_solution(17745722138508698328)
XLA Ops:
  0.7 1.9 %shard_map.91 = (f32[8,768]{1,0:T(8,128)}, f32[8,768]{1,0:T(8,128)}, f32[16,8,128]{2,1,0:T(8,128)}, f32[24,1536]{1,0:T(8,128)}) custom-call(f32[6,1,3072]{2,1,0:T(1,128)} %bitcast.7, f32[6,1,8]{2,1,0:T(1,128)} %bitcast.8, f32[6,1,96]{2,1,0:T(1,128)} %bitcast.9, f32[1,1,3072]{2,1,0:T(1,128)} %stiffness.1, s32[1,1,4,768]{3,2,1,0:T(4,128)} %orders.1, ...), custom_call_target="tpu_custom_call" | custom-call | tf_op jit(solution)/shard_map/pallas_call | solution.py:528
  2.5 0.7 collective-permute-start
  3.2 5.9 %collective-permute-start.1 = (f32[8,768]{1,0:T(8,128)}, f32[8,768]{1,0:T(8,128)S(1)}, u32[]{:S(2)}, u32[]{:S(2)}) collective-permute-start(f32[8,768]{1,0:T(8,128)} %get-tuple-element.26), channel_id=1, source_target_pairs={{0,8},{1,3},{2,10},{3,1},{4,12},{5,7},{6,14},{7,5},{8,0},{9,11},{1... | collective-permute-start | bytes 73736 | tf_op jit(solution)/shard_map/ppermute | solution.py:563
  9.1 3.7 %all-to-all-start = ((f32[16,8,128]{2,1,0:T(8,128)}), f32[16,8,128]{2,1,0:T(8,128)S(1)}, u32[]{:S(2)}, u32[]{:S(2)}) async-start(f32[16,8,128]{2,1,0:T(8,128)} %get-tuple-element.23), calls=%async_computation | async-start | bytes 131072 | tf_op jit(solution)/shard_map/all_to_all | solution.py:568
  12.8 0.0 collective-permute-done.refs_0_
  12.8 0.0 collective-permute-done.1.refs_1_
  12.8 0.0 copy-start
  12.8 0.9 %copy-done = f32[24,1536]{1,0:T(8,128)S(1)} copy-done((f32[24,1536]{1,0:T(8,128)S(1)}, f32[24,1536]{1,0:T(8,128)}, u32[]{:S(2)}) %copy-start) | copy-done | bytes 147480
  13.7 0.4 shard_map.92
  14.1 1.3 %collective-permute-start.2 = (f32[16,1536]{1,0:T(8,128)S(1)}, f32[16,1536]{1,0:T(8,128)S(1)}, u32[]{:S(2)}, u32[]{:S(2)}) collective-permute-start(f32[16,1536]{1,0:T(8,128)S(1)} %get-tuple-element.29.modes_ref), channel_id=1, source_target_pairs={{0,1},{1,0},{2,3},{3,2},{4,5},{5,4},{6,7},{7,6},{8,9},{9,8},{10,11... | collective-permute-start | bytes 294920 | tf_op jit(solution)/shard_map/ppermute | solution.py:572
  15.4 4.2 %all-to-all-done.shared = f32[16,8,128]{2,1,0:T(8,128)S(1)} async-done(((f32[16,8,128]{2,1,0:T(8,128)}), f32[16,8,128]{2,1,0:T(8,128)S(1)}, u32[]{:S(2)}, u32[]{:S(2)}) %all-to-all-start) | async-done | bytes 65568 | tf_op jit(solution)/shard_map/all_to_all | solution.py:568
  19.7 0.0 collective-permute-done.2.modes_rest
  19.7 5.8 %shard_map.93 = (f32[8,768]{1,0:T(8,128)S(1)}, f32[8,768]{1,0:T(8,128)S(1)}, f32[32,4,128]{2,1,0:T(4,128)}, f32[8,3072]{1,0:T(8,128)S(1)}) custom-call(bf16[192,8,3072]{2,1,0:T(8,128)(2,1)} %bitcast.4, f32[16,8,128]{2,1,0:T(8,128)S(1)} %all-to-all-done.shared, f32[8,1536]{1,0:T(8,128)S(1)} %get-tuple-element.27.right, ...), custom_call_target="tpu_custom_call" | custom-call | tf_op jit(solution)/shard_map/pallas_call | solution.py:528
  25.5 5.0 %all-to-all-start.1 = ((f32[32,4,128]{2,1,0:T(4,128)}), f32[32,4,128]{2,1,0:T(4,128)S(1)}, u32[]{:S(2)}, u32[]{:S(2)}) async-start(f32[32,4,128]{2,1,0:T(4,128)} %get-tuple-element.30), calls=%async_computation.1 | async-start | bytes 131072 | tf_op jit(solution)/shard_map/all_to_all | solution.py:568
  30.5 0.7 collective-permute-start.3
  31.2 4.5 %collective-permute-start.4 = (f32[8,768]{1,0:T(8,128)S(1)}, f32[8,768]{1,0:T(8,128)S(1)}, u32[]{:S(2)}, u32[]{:S(2)}) collective-permute-start(f32[8,768]{1,0:T(8,128)S(1)} %get-tuple-element.32.refs_1_), channel_id=1, source_target_pairs={{0,8},{1,3},{2,10},{3,1},{4,12},{5,7},{6,14},{7,5},{8,0},{9,11},{1... | collective-permute-start | bytes 73736 | tf_op jit(solution)/shard_map/ppermute | solution.py:563
  35.7 0.0 collective-permute-done.3.refs_2_
  35.8 1.8 %collective-permute-done.4.refs_3_ = f32[8,768]{1,0:T(8,128)S(1)} collective-permute-done((f32[8,768]{1,0:T(8,128)S(1)}, f32[8,768]{1,0:T(8,128)S(1)}, u32[]{:S(2)}, u32[]{:S(2)}) %collective-permute-start.4) | collective-permute-done | bytes 24608 | tf_op jit(solution)/shard_map/ppermute | solution.py:563
  37.6 0.6 all-to-all-done.1.pieces.before
  38.1 1.1 %shard_map.94 = (f32[8,1536]{1,0:T(8,128)S(1)}, f32[8,1536]{1,0:T(8,128)S(1)}) custom-call(f32[32,4,128]{2,1,0:T(4,128)S(1)} %all-to-all-done.1.pieces.before, f32[16,8,128]{2,1,0:T(8,128)S(1)} %all-to-all-done.shared, f32[16,1536]{1,0:T(8,128)S(1)} %get-tuple-element.29.modes_ref, f32[8,768]{1,0:T(8,128)S(1)} %get-tuple-element.31.refs_0_, ...), custom_call_target="tpu_custom_call" | custom-call | tf_op jit(solution)/shard_map/pallas_call | solution.py:528
  39.3 0.5 collective-permute-start.5
  39.8 3.9 %shard_map.95.held = bf16[192,8,3072]{2,1,0:T(8,128)(2,1)S(1)} custom-call(bf16[192,8,3072]{2,1,0:T(8,128)(2,1)} %bitcast.5, f32[8,1536]{1,0:T(8,128)S(1)} %get-tuple-element.33.after.direction.direction_ref), custom_call_target="tpu_custom_call" | custom-call | bytes 18874368 | tf_op jit(solution)/shard_map/pallas_call | solution.py:528
  43.6 0.0 collective-permute-done.5.rest.direction_rest
  43.7 3.4 %shard_map.96 = (f32[8,768]{1,0:T(8,128)S(1)}, f32[8,768]{1,0:T(8,128)S(1)}, f32[32,4,128]{2,1,0:T(4,128)}) custom-call(bf16[192,8,3072]{2,1,0:T(8,128)(2,1)S(1)} %shard_map.95.held, f32[16,1536]{1,0:T(8,128)S(1)} %get-tuple-element.29.modes_ref, f32[8,1536]{1,0:T(8,128)S(1)} %get-tuple-element.34.residual.residual_ref, ...), custom_call_target="tpu_custom_call" | custom-call | tf_op jit(solution)/shard_map/pallas_call | solution.py:528
  47.1 3.7 %all-to-all-start.2 = ((f32[32,4,128]{2,1,0:T(4,128)}), f32[32,4,128]{2,1,0:T(4,128)S(1)}, u32[]{:S(2)}, u32[]{:S(2)}) async-start(f32[32,4,128]{2,1,0:T(4,128)} %get-tuple-element.35), calls=%async_computation.2 | async-start | bytes 131072 | tf_op jit(solution)/shard_map/all_to_all | solution.py:568
  50.8 0.7 collective-permute-start.6
  51.5 4.5 %collective-permute-start.7 = (f32[8,768]{1,0:T(8,128)S(1)}, f32[8,768]{1,0:T(8,128)S(1)}, u32[]{:S(2)}, u32[]{:S(2)}) collective-permute-start(f32[8,768]{1,0:T(8,128)S(1)} %get-tuple-element.37.refs_1_), channel_id=1, source_target_pairs={{0,8},{1,3},{2,10},{3,1},{4,12},{5,7},{6,14},{7,5},{8,0},{9,11},{1... | collective-permute-start | bytes 73736 | tf_op jit(solution)/shard_map/ppermute | solution.py:563
  56.0 0.0 collective-permute-done.6.refs_2_
  56.0 1.8 %collective-permute-done.7.refs_3_ = f32[8,768]{1,0:T(8,128)S(1)} collective-permute-done((f32[8,768]{1,0:T(8,128)S(1)}, f32[8,768]{1,0:T(8,128)S(1)}, u32[]{:S(2)}, u32[]{:S(2)}) %collective-permute-start.7) | collective-permute-done | bytes 24608 | tf_op jit(solution)/shard_map/ppermute | solution.py:563
  57.8 0.6 all-to-all-done.2.pieces
  58.4 1.1 %shard_map.97 = (f32[8,1536]{1,0:T(8,128)S(1)}, f32[8,128]{1,0:T(8,128)S(1)}) custom-call(f32[32,4,128]{2,1,0:T(4,128)S(1)} %all-to-all-done.2.pieces, f32[16,8,128]{2,1,0:T(8,128)S(1)} %all-to-all-done.shared, f32[32,4,128]{2,1,0:T(4,128)S(1)} %all-to-all-done.1.pieces.before, f32[16,1536]{1,0:T(8,128)S(1)} %get-tuple-element.29.modes_ref, ...), custom_call_target="tpu_custom_call" | custom-call | tf_op jit(solution)/shard_map/pallas_call | solution.py:528
  59.5 0.5 collective-permute-start.8
  60.0 3.9 %shard_map.98.held = bf16[192,8,3072]{2,1,0:T(8,128)(2,1)S(1)} custom-call(bf16[192,8,3072]{2,1,0:T(8,128)(2,1)} %bitcast.6, f32[8,1536]{1,0:T(8,128)S(1)} %get-tuple-element.38.after.later), custom_call_target="tpu_custom_call" | custom-call | bytes 18874368 | tf_op jit(solution)/shard_map/pallas_call | solution.py:528
  63.9 0.0 collective-permute-done.8.rest.later_rest
  63.9 2.6 %shard_map.99 = f32[32,1,128]{2,1,0:T(1,128)S(1)} custom-call(bf16[192,8,3072]{2,1,0:T(8,128)(2,1)S(1)} %shard_map.98.held, f32[8,1536]{1,0:T(8,128)S(1)} %get-tuple-element.33.after.direction.direction_ref, f32[8,128]{1,0:T(8,128)S(1)} %get-tuple-element.39.scalars, f32[8,1536]{1,0:T(8,128)S(1)} %get-tuple-element.38.after.later, ...), custom_call_target="tpu_custom_call" | custom-call | tf_op jit(solution)/shard_map/pallas_call | solution.py:528
  66.6 10.8 %all_to_all.20.pieces = f32[32,1,128]{2,1,0:T(1,128)S(1)} all-to-all(f32[32,1,128]{2,1,0:T(1,128)S(1)} %shard_map.99), channel_id=1, replica_groups=mesh['gx'=4,'gy'=4,'gz'=2] {'gx','gy','gz'}, dimensions={0} | all-to-all | bytes 32768 | tf_op jit(solution)/shard_map/all_to_all | solution.py:568
  77.3 0.8 %shard_map.100 = f32[1,1,8,3072]{3,2,1,0:T(8,128)} custom-call(f32[32,1,128]{2,1,0:T(1,128)S(1)} %all_to_all.20.pieces, f32[8,128]{1,0:T(8,128)S(1)} %get-tuple-element.39.scalars, f32[8,3072]{1,0:T(8,128)S(1)} %get-tuple-element.40.estimate, f32[8,1536]{1,0:T(8,128)S(1)} %get-tuple-element.33.after.direction.direction_ref, ...), custom_call_target="tpu_custom_call" | custom-call | tf_op jit(solution)/shard_map/pallas_call | solution.py:528
Async XLA Ops:
  2.5 10.3 %collective-permute-start = (f32[8,768]{1,0:T(8,128)}, f32[8,768]{1,0:T(8,128)S(1)}, u32[]{:S(2)}, u32[]{:S(2)}) collective-permute-start(f32[8,768]{1,0:T(8,128)} %get-tuple-element.25), channel_id=1, source_target_pairs={{3,5},{5,3},{8,16},{10,18},{11,13},{12,20},{13,11},{14,22},{16,8},... | collective-permute-start | bytes 73736 | tf_op jit(solution)/shard_map/ppermute | solution.py:563
  3.2 9.6 %collective-permute-start.1 = (f32[8,768]{1,0:T(8,128)}, f32[8,768]{1,0:T(8,128)S(1)}, u32[]{:S(2)}, u32[]{:S(2)}) collective-permute-start(f32[8,768]{1,0:T(8,128)} %get-tuple-element.26), channel_id=1, source_target_pairs={{0,8},{1,3},{2,10},{3,1},{4,12},{5,7},{6,14},{7,5},{8,0},{9,11},{1... | collective-permute-start | bytes 73736 | tf_op jit(solution)/shard_map/ppermute | solution.py:563
  9.1 10.6 %all-to-all-start = ((f32[16,8,128]{2,1,0:T(8,128)}), f32[16,8,128]{2,1,0:T(8,128)S(1)}, u32[]{:S(2)}, u32[]{:S(2)}) async-start(f32[16,8,128]{2,1,0:T(8,128)} %get-tuple-element.23), calls=%async_computation | async-start | bytes 131072 | tf_op jit(solution)/shard_map/all_to_all | solution.py:568
  12.8 0.9 %copy-start = (f32[24,1536]{1,0:T(8,128)S(1)}, f32[24,1536]{1,0:T(8,128)}, u32[]{:S(2)}) copy-start(f32[24,1536]{1,0:T(8,128)} %get-tuple-element.24.base) | copy-start | bytes 442372
  14.1 5.6 %collective-permute-start.2 = (f32[16,1536]{1,0:T(8,128)S(1)}, f32[16,1536]{1,0:T(8,128)S(1)}, u32[]{:S(2)}, u32[]{:S(2)}) collective-permute-start(f32[16,1536]{1,0:T(8,128)S(1)} %get-tuple-element.29.modes_ref), channel_id=1, source_target_pairs={{0,1},{1,0},{2,3},{3,2},{4,5},{5,4},{6,7},{7,6},{8,9},{9,8},{10,11... | collective-permute-start | bytes 294920 | tf_op jit(solution)/shard_map/ppermute | solution.py:572
  25.5 12.6 %all-to-all-start.1 = ((f32[32,4,128]{2,1,0:T(4,128)}), f32[32,4,128]{2,1,0:T(4,128)S(1)}, u32[]{:S(2)}, u32[]{:S(2)}) async-start(f32[32,4,128]{2,1,0:T(4,128)} %get-tuple-element.30), calls=%async_computation.1 | async-start | bytes 131072 | tf_op jit(solution)/shard_map/all_to_all | solution.py:568
  30.5 5.2 %collective-permute-start.3 = (f32[8,768]{1,0:T(8,128)S(1)}, f32[8,768]{1,0:T(8,128)S(1)}, u32[]{:S(2)}, u32[]{:S(2)}) collective-permute-start(f32[8,768]{1,0:T(8,128)S(1)} %get-tuple-element.31.refs_0_), channel_id=1, source_target_pairs={{3,5},{5,3},{8,16},{10,18},{11,13},{12,20},{13,11},{14,22},{16,8},... | collective-permute-start | bytes 73736 | tf_op jit(solution)/shard_map/ppermute | solution.py:563
  31.2 6.4 %collective-permute-start.4 = (f32[8,768]{1,0:T(8,128)S(1)}, f32[8,768]{1,0:T(8,128)S(1)}, u32[]{:S(2)}, u32[]{:S(2)}) collective-permute-start(f32[8,768]{1,0:T(8,128)S(1)} %get-tuple-element.32.refs_1_), channel_id=1, source_target_pairs={{0,8},{1,3},{2,10},{3,1},{4,12},{5,7},{6,14},{7,5},{8,0},{9,11},{1... | collective-permute-start | bytes 73736 | tf_op jit(solution)/shard_map/ppermute | solution.py:563
  39.3 4.4 %collective-permute-start.5 = (f32[8,1536]{1,0:T(8,128)S(1)}, f32[8,1536]{1,0:T(8,128)S(1)}, u32[]{:S(2)}, u32[]{:S(2)}) collective-permute-start(f32[8,1536]{1,0:T(8,128)S(1)} %get-tuple-element.33.after.direction.direction_ref), channel_id=1, source_target_pairs={{0,1},{1,0},{2,3},{3,2},{4,5},{5,4},{6,7},{7,6},{8,9},{9,8},{10,11... | collective-permute-start | bytes 147464 | tf_op jit(solution)/shard_map/ppermute | solution.py:572
  47.1 11.4 %all-to-all-start.2 = ((f32[32,4,128]{2,1,0:T(4,128)}), f32[32,4,128]{2,1,0:T(4,128)S(1)}, u32[]{:S(2)}, u32[]{:S(2)}) async-start(f32[32,4,128]{2,1,0:T(4,128)} %get-tuple-element.35), calls=%async_computation.2 | async-start | bytes 131072 | tf_op jit(solution)/shard_map/all_to_all | solution.py:568
  50.8 5.2 %collective-permute-start.6 = (f32[8,768]{1,0:T(8,128)S(1)}, f32[8,768]{1,0:T(8,128)S(1)}, u32[]{:S(2)}, u32[]{:S(2)}) collective-permute-start(f32[8,768]{1,0:T(8,128)S(1)} %get-tuple-element.36.refs_0_), channel_id=1, source_target_pairs={{3,5},{5,3},{8,16},{10,18},{11,13},{12,20},{13,11},{14,22},{16,8},... | collective-permute-start | bytes 73736 | tf_op jit(solution)/shard_map/ppermute | solution.py:563
  51.5 6.4 %collective-permute-start.7 = (f32[8,768]{1,0:T(8,128)S(1)}, f32[8,768]{1,0:T(8,128)S(1)}, u32[]{:S(2)}, u32[]{:S(2)}) collective-permute-start(f32[8,768]{1,0:T(8,128)S(1)} %get-tuple-element.37.refs_1_), channel_id=1, source_target_pairs={{0,8},{1,3},{2,10},{3,1},{4,12},{5,7},{6,14},{7,5},{8,0},{9,11},{1... | collective-permute-start | bytes 73736 | tf_op jit(solution)/shard_map/ppermute | solution.py:563
  59.5 4.4 %collective-permute-start.8 = (f32[8,1536]{1,0:T(8,128)S(1)}, f32[8,1536]{1,0:T(8,128)S(1)}, u32[]{:S(2)}, u32[]{:S(2)}) collective-permute-start(f32[8,1536]{1,0:T(8,128)S(1)} %get-tuple-element.38.after.later), channel_id=1, source_target_pairs={{0,1},{1,0},{2,3},{3,2},{4,5},{5,4},{6,7},{7,6},{8,9},{9,8},{10,11... | collective-permute-start | bytes 147464 | tf_op jit(solution)/shard_map/ppermute | solution.py:572

commit v10 on v7

--- a/solution.py
+++ b/solution.py
@@ -377,9 +377,27 @@
 
 
 def tile_products(sz, tile, vectors, modes_ref):
-    tile = mode_products(sz, tile, vectors, modes_ref, 0)
-    scaled = [v * w for v, w in zip(vectors, weights_of(sz, modes_ref))]
-    return mode_products(sz, tile, scaled, modes_ref, sz.group)
+    lane = lanes()
+
+    def put(tile, rows, source, target):
+        moved = pltpu.roll(rows, (target - source) % TILE, 1)
+        return jnp.where((lane >= target) & (lane < target + sz.modes), moved, tile)
+
+    own = None
+    for j, (vector, weight) in enumerate(zip(vectors, weights_of(sz, modes_ref))):
+        both = jnp.concatenate([vector, vector * weight], axis=0)
+        product = lax.dot_general(
+            both, modes_ref[0:16, own_face(sz, j)], (((1,), (1,)), ((), ())),
+            precision=lax.Precision.HIGHEST, preferred_element_type=jnp.float32,
+        )
+        product = jnp.concatenate([product, jnp.zeros((16, TILE - 16), jnp.float32)], axis=1)
+        own = product if own is None else own + product
+        for group in range(2):
+            rows = product[8 * group : 8 * group + 8]
+            tile = put(tile, rows, SLOT, group * sz.group + sz.modes * (1 + j))
+    for group in range(2):
+        tile = put(tile, own[8 * group : 8 * group + 8], 0, group * sz.group)
+    return tile
 
 
 def first_kernel(sz, operator, shared, right, coupling, modes_ref, modes_rest, *refs):

time: 78.5 us -> 78.8 us (level)
  no operation moved by 1% of the time
where the time goes in v10:
time: 78.8 us; the launch traced here: 78.4 us
  starting transfers between devices  31.8 us (40%)
  Pallas kernels  25.1 us (32%)
  blocking collectives  10.8 us (14%)
  waiting for transfers between devices  9.04 us (11%)
  local copies, waits for them, and re-layouts  0.9 us (1%)
  between operations  0.81 us (1%)
    pallas_call x10, Pallas kernels, call(): pl.pallas_call(functools.partial(kernel, sz), out_shape=out_shape, in_spe...  25.1 us
    ppermute x6, starting transfers between devices, swap(): lax.ppermute(own[j], everywhere, face_pairs(sz, j))  17 us
    all_to_all x3, starting transfers between devices, share(): return lax.all_to_all(chunk, axes, split_axis=0, concat_axis=0, tiled=True)  12.5 us
    all_to_all x1, blocking collectives, share(): return lax.all_to_all(chunk, axes, split_axis=0, concat_axis=0, tiled=True)  10.8 us
    all_to_all x3, waiting for transfers between devices, share(): return lax.all_to_all(chunk, axes, split_axis=0, concat_axis=0, tiled=True)  5.41 us
    ppermute x6, waiting for transfers between devices, swap(): lax.ppermute(own[j], everywhere, face_pairs(sz, j))  3.62 us
    ppermute x3, starting transfers between devices, rest(): return lax.ppermute(part, 'gz', [(0, 1), (1, 0)])  2.34 us
  transfers between devices with their start and end apart: 12, of which 5 were waited for; matrix products, arithmetic and copies ran while one was open for 0% of the time, Pallas kernels for 10%

profile of v10, /device:TPU:0, one launch (start us, length us, event | category | flops | bytes accessed | tf_op | source)
XLA Modules:
  0.0 78.4 jit_solution(3632165528901630898)
XLA Ops:
  0.7 1.9 %shard_map.91 = (f32[8,768]{1,0:T(8,128)}, f32[8,768]{1,0:T(8,128)}, f32[16,8,128]{2,1,0:T(8,128)}, f32[24,1536]{1,0:T(8,128)}) custom-call(f32[6,1,3072]{2,1,0:T(1,128)} %bitcast.7, f32[6,1,8]{2,1,0:T(1,128)} %bitcast.8, f32[6,1,96]{2,1,0:T(1,128)} %bitcast.9, f32[1,1,3072]{2,1,0:T(1,128)} %stiffness.1, s32[1,1,4,768]{3,2,1,0:T(4,128)} %orders.1, ...), custom_call_target="tpu_custom_call" | custom-call | tf_op jit(solution)/shard_map/pallas_call | solution.py:545
  2.5 0.7 collective-permute-start
  3.2 5.9 %collective-permute-start.1 = (f32[8,768]{1,0:T(8,128)}, f32[8,768]{1,0:T(8,128)S(1)}, u32[]{:S(2)}, u32[]{:S(2)}) collective-permute-start(f32[8,768]{1,0:T(8,128)} %get-tuple-element.26), channel_id=1, source_target_pairs={{0,8},{1,3},{2,10},{3,1},{4,12},{5,7},{6,14},{7,5},{8,0},{9,11},{1... | collective-permute-start | bytes 73736 | tf_op jit(solution)/shard_map/ppermute | solution.py:580
  9.1 3.7 %all-to-all-start = ((f32[16,8,128]{2,1,0:T(8,128)}), f32[16,8,128]{2,1,0:T(8,128)S(1)}, u32[]{:S(2)}, u32[]{:S(2)}) async-start(f32[16,8,128]{2,1,0:T(8,128)} %get-tuple-element.23), calls=%async_computation | async-start | bytes 131072 | tf_op jit(solution)/shard_map/all_to_all | solution.py:585
  12.8 0.0 collective-permute-done.refs_0_
  12.8 0.0 collective-permute-done.1.refs_1_
  12.8 0.0 copy-start
  12.8 0.9 %copy-done = f32[24,1536]{1,0:T(8,128)S(1)} copy-done((f32[24,1536]{1,0:T(8,128)S(1)}, f32[24,1536]{1,0:T(8,128)}, u32[]{:S(2)}) %copy-start) | copy-done | bytes 147480
  13.7 0.4 shard_map.92
  14.1 1.3 %collective-permute-start.2 = (f32[16,1536]{1,0:T(8,128)S(1)}, f32[16,1536]{1,0:T(8,128)S(1)}, u32[]{:S(2)}, u32[]{:S(2)}) collective-permute-start(f32[16,1536]{1,0:T(8,128)S(1)} %get-tuple-element.29.modes_ref), channel_id=1, source_target_pairs={{0,1},{1,0},{2,3},{3,2},{4,5},{5,4},{6,7},{7,6},{8,9},{9,8},{10,11... | collective-permute-start | bytes 294920 | tf_op jit(solution)/shard_map/ppermute | solution.py:589
  15.4 4.2 %all-to-all-done.shared = f32[16,8,128]{2,1,0:T(8,128)S(1)} async-done(((f32[16,8,128]{2,1,0:T(8,128)}), f32[16,8,128]{2,1,0:T(8,128)S(1)}, u32[]{:S(2)}, u32[]{:S(2)}) %all-to-all-start) | async-done | bytes 65568 | tf_op jit(solution)/shard_map/all_to_all | solution.py:585
  19.7 0.0 collective-permute-done.2.modes_rest
  19.7 5.9 %shard_map.93 = (f32[8,768]{1,0:T(8,128)S(1)}, f32[8,768]{1,0:T(8,128)S(1)}, f32[32,4,128]{2,1,0:T(4,128)}, f32[8,3072]{1,0:T(8,128)S(1)}) custom-call(bf16[192,8,3072]{2,1,0:T(8,128)(2,1)} %bitcast.4, f32[16,8,128]{2,1,0:T(8,128)S(1)} %all-to-all-done.shared, f32[8,1536]{1,0:T(8,128)S(1)} %get-tuple-element.27.right, ...), custom_call_target="tpu_custom_call" | custom-call | tf_op jit(solution)/shard_map/pallas_call | solution.py:545
  25.6 5.0 %all-to-all-start.1 = ((f32[32,4,128]{2,1,0:T(4,128)}), f32[32,4,128]{2,1,0:T(4,128)S(1)}, u32[]{:S(2)}, u32[]{:S(2)}) async-start(f32[32,4,128]{2,1,0:T(4,128)} %get-tuple-element.30), calls=%async_computation.1 | async-start | bytes 131072 | tf_op jit(solution)/shard_map/all_to_all | solution.py:585
  30.7 0.7 collective-permute-start.3
  31.3 4.5 %collective-permute-start.4 = (f32[8,768]{1,0:T(8,128)S(1)}, f32[8,768]{1,0:T(8,128)S(1)}, u32[]{:S(2)}, u32[]{:S(2)}) collective-permute-start(f32[8,768]{1,0:T(8,128)S(1)} %get-tuple-element.32.refs_1_), channel_id=1, source_target_pairs={{0,8},{1,3},{2,10},{3,1},{4,12},{5,7},{6,14},{7,5},{8,0},{9,11},{1... | collective-permute-start | bytes 73736 | tf_op jit(solution)/shard_map/ppermute | solution.py:580
  35.9 0.0 collective-permute-done.3.refs_2_
  35.9 1.8 %collective-permute-done.4.refs_3_ = f32[8,768]{1,0:T(8,128)S(1)} collective-permute-done((f32[8,768]{1,0:T(8,128)S(1)}, f32[8,768]{1,0:T(8,128)S(1)}, u32[]{:S(2)}, u32[]{:S(2)}) %collective-permute-start.4) | collective-permute-done | bytes 24608 | tf_op jit(solution)/shard_map/ppermute | solution.py:580
  37.7 0.6 all-to-all-done.1.pieces.before
  38.3 1.1 %shard_map.94 = (f32[8,1536]{1,0:T(8,128)S(1)}, f32[8,1536]{1,0:T(8,128)S(1)}) custom-call(f32[32,4,128]{2,1,0:T(4,128)S(1)} %all-to-all-done.1.pieces.before, f32[16,8,128]{2,1,0:T(8,128)S(1)} %all-to-all-done.shared, f32[16,1536]{1,0:T(8,128)S(1)} %get-tuple-element.29.modes_ref, f32[8,768]{1,0:T(8,128)S(1)} %get-tuple-element.31.refs_0_, ...), custom_call_target="tpu_custom_call" | custom-call | tf_op jit(solution)/shard_map/pallas_call | solution.py:545
  39.4 0.5 collective-permute-start.5
  39.9 3.8 %shard_map.95.held = bf16[192,8,3072]{2,1,0:T(8,128)(2,1)S(1)} custom-call(bf16[192,8,3072]{2,1,0:T(8,128)(2,1)} %bitcast.5, f32[8,1536]{1,0:T(8,128)S(1)} %get-tuple-element.33.after.direction.direction_ref), custom_call_target="tpu_custom_call" | custom-call | bytes 18874368 | tf_op jit(solution)/shard_map/pallas_call | solution.py:545
  43.7 0.0 collective-permute-done.5.rest.direction_rest
  43.8 3.6 %shard_map.96 = (f32[8,768]{1,0:T(8,128)S(1)}, f32[8,768]{1,0:T(8,128)S(1)}, f32[32,4,128]{2,1,0:T(4,128)}) custom-call(bf16[192,8,3072]{2,1,0:T(8,128)(2,1)S(1)} %shard_map.95.held, f32[16,1536]{1,0:T(8,128)S(1)} %get-tuple-element.29.modes_ref, f32[8,1536]{1,0:T(8,128)S(1)} %get-tuple-element.34.residual.residual_ref, ...), custom_call_target="tpu_custom_call" | custom-call | tf_op jit(solution)/shard_map/pallas_call | solution.py:545
  47.3 3.7 %all-to-all-start.2 = ((f32[32,4,128]{2,1,0:T(4,128)}), f32[32,4,128]{2,1,0:T(4,128)S(1)}, u32[]{:S(2)}, u32[]{:S(2)}) async-start(f32[32,4,128]{2,1,0:T(4,128)} %get-tuple-element.35), calls=%async_computation.2 | async-start | bytes 131072 | tf_op jit(solution)/shard_map/all_to_all | solution.py:585
  51.1 0.7 collective-permute-start.6
  51.7 4.5 %collective-permute-start.7 = (f32[8,768]{1,0:T(8,128)S(1)}, f32[8,768]{1,0:T(8,128)S(1)}, u32[]{:S(2)}, u32[]{:S(2)}) collective-permute-start(f32[8,768]{1,0:T(8,128)S(1)} %get-tuple-element.37.refs_1_), channel_id=1, source_target_pairs={{0,8},{1,3},{2,10},{3,1},{4,12},{5,7},{6,14},{7,5},{8,0},{9,11},{1... | collective-permute-start | bytes 73736 | tf_op jit(solution)/shard_map/ppermute | solution.py:580
  56.3 0.0 collective-permute-done.6.refs_2_
  56.3 1.8 %collective-permute-done.7.refs_3_ = f32[8,768]{1,0:T(8,128)S(1)} collective-permute-done((f32[8,768]{1,0:T(8,128)S(1)}, f32[8,768]{1,0:T(8,128)S(1)}, u32[]{:S(2)}, u32[]{:S(2)}) %collective-permute-start.7) | collective-permute-done | bytes 24608 | tf_op jit(solution)/shard_map/ppermute | solution.py:580
  58.1 0.6 all-to-all-done.2.pieces
  58.7 1.1 %shard_map.97 = (f32[8,1536]{1,0:T(8,128)S(1)}, f32[8,128]{1,0:T(8,128)S(1)}) custom-call(f32[32,4,128]{2,1,0:T(4,128)S(1)} %all-to-all-done.2.pieces, f32[16,8,128]{2,1,0:T(8,128)S(1)} %all-to-all-done.shared, f32[32,4,128]{2,1,0:T(4,128)S(1)} %all-to-all-done.1.pieces.before, f32[16,1536]{1,0:T(8,128)S(1)} %get-tuple-element.29.modes_ref, ...), custom_call_target="tpu_custom_call" | custom-call | tf_op jit(solution)/shard_map/pallas_call | solution.py:545
  59.8 0.5 collective-permute-start.8
  60.3 3.8 %shard_map.98.held = bf16[192,8,3072]{2,1,0:T(8,128)(2,1)S(1)} custom-call(bf16[192,8,3072]{2,1,0:T(8,128)(2,1)} %bitcast.6, f32[8,1536]{1,0:T(8,128)S(1)} %get-tuple-element.38.after.later), custom_call_target="tpu_custom_call" | custom-call | bytes 18874368 | tf_op jit(solution)/shard_map/pallas_call | solution.py:545
  64.2 0.0 collective-permute-done.8.rest.later_rest
  64.2 2.6 %shard_map.99 = f32[32,1,128]{2,1,0:T(1,128)S(1)} custom-call(bf16[192,8,3072]{2,1,0:T(8,128)(2,1)S(1)} %shard_map.98.held, f32[8,1536]{1,0:T(8,128)S(1)} %get-tuple-element.33.after.direction.direction_ref, f32[8,128]{1,0:T(8,128)S(1)} %get-tuple-element.39.scalars, f32[8,1536]{1,0:T(8,128)S(1)} %get-tuple-element.38.after.later, ...), custom_call_target="tpu_custom_call" | custom-call | tf_op jit(solution)/shard_map/pallas_call | solution.py:545
  66.8 10.8 %all_to_all.20.pieces = f32[32,1,128]{2,1,0:T(1,128)S(1)} all-to-all(f32[32,1,128]{2,1,0:T(1,128)S(1)} %shard_map.99), channel_id=1, replica_groups=mesh['gx'=4,'gy'=4,'gz'=2] {'gx','gy','gz'}, dimensions={0} | all-to-all | bytes 32768 | tf_op jit(solution)/shard_map/all_to_all | solution.py:585
  77.6 0.8 %shard_map.100 = f32[1,1,8,3072]{3,2,1,0:T(8,128)} custom-call(f32[32,1,128]{2,1,0:T(1,128)S(1)} %all_to_all.20.pieces, f32[8,128]{1,0:T(8,128)S(1)} %get-tuple-element.39.scalars, f32[8,3072]{1,0:T(8,128)S(1)} %get-tuple-element.40.estimate, f32[8,1536]{1,0:T(8,128)S(1)} %get-tuple-element.33.after.direction.direction_ref, ...), custom_call_target="tpu_custom_call" | custom-call | tf_op jit(solution)/shard_map/pallas_call | solution.py:545
Async XLA Ops:
  2.5 10.3 %collective-permute-start = (f32[8,768]{1,0:T(8,128)}, f32[8,768]{1,0:T(8,128)S(1)}, u32[]{:S(2)}, u32[]{:S(2)}) collective-permute-start(f32[8,768]{1,0:T(8,128)} %get-tuple-element.25), channel_id=1, source_target_pairs={{3,5},{5,3},{8,16},{10,18},{11,13},{12,20},{13,11},{14,22},{16,8},... | collective-permute-start | bytes 73736 | tf_op jit(solution)/shard_map/ppermute | solution.py:580
  3.2 9.6 %collective-permute-start.1 = (f32[8,768]{1,0:T(8,128)}, f32[8,768]{1,0:T(8,128)S(1)}, u32[]{:S(2)}, u32[]{:S(2)}) collective-permute-start(f32[8,768]{1,0:T(8,128)} %get-tuple-element.26), channel_id=1, source_target_pairs={{0,8},{1,3},{2,10},{3,1},{4,12},{5,7},{6,14},{7,5},{8,0},{9,11},{1... | collective-permute-start | bytes 73736 | tf_op jit(solution)/shard_map/ppermute | solution.py:580
  9.1 10.6 %all-to-all-start = ((f32[16,8,128]{2,1,0:T(8,128)}), f32[16,8,128]{2,1,0:T(8,128)S(1)}, u32[]{:S(2)}, u32[]{:S(2)}) async-start(f32[16,8,128]{2,1,0:T(8,128)} %get-tuple-element.23), calls=%async_computation | async-start | bytes 131072 | tf_op jit(solution)/shard_map/all_to_all | solution.py:585
  12.8 0.9 %copy-start = (f32[24,1536]{1,0:T(8,128)S(1)}, f32[24,1536]{1,0:T(8,128)}, u32[]{:S(2)}) copy-start(f32[24,1536]{1,0:T(8,128)} %get-tuple-element.24.base) | copy-start | bytes 442372
  14.1 5.6 %collective-permute-start.2 = (f32[16,1536]{1,0:T(8,128)S(1)}, f32[16,1536]{1,0:T(8,128)S(1)}, u32[]{:S(2)}, u32[]{:S(2)}) collective-permute-start(f32[16,1536]{1,0:T(8,128)S(1)} %get-tuple-element.29.modes_ref), channel_id=1, source_target_pairs={{0,1},{1,0},{2,3},{3,2},{4,5},{5,4},{6,7},{7,6},{8,9},{9,8},{10,11... | collective-permute-start | bytes 294920 | tf_op jit(solution)/shard_map/ppermute | solution.py:589
  25.6 12.6 %all-to-all-start.1 = ((f32[32,4,128]{2,1,0:T(4,128)}), f32[32,4,128]{2,1,0:T(4,128)S(1)}, u32[]{:S(2)}, u32[]{:S(2)}) async-start(f32[32,4,128]{2,1,0:T(4,128)} %get-tuple-element.30), calls=%async_computation.1 | async-start | bytes 131072 | tf_op jit(solution)/shard_map/all_to_all | solution.py:585
  30.7 5.2 %collective-permute-start.3 = (f32[8,768]{1,0:T(8,128)S(1)}, f32[8,768]{1,0:T(8,128)S(1)}, u32[]{:S(2)}, u32[]{:S(2)}) collective-permute-start(f32[8,768]{1,0:T(8,128)S(1)} %get-tuple-element.31.refs_0_), channel_id=1, source_target_pairs={{3,5},{5,3},{8,16},{10,18},{11,13},{12,20},{13,11},{14,22},{16,8},... | collective-permute-start | bytes 73736 | tf_op jit(solution)/shard_map/ppermute | solution.py:580
  31.3 6.4 %collective-permute-start.4 = (f32[8,768]{1,0:T(8,128)S(1)}, f32[8,768]{1,0:T(8,128)S(1)}, u32[]{:S(2)}, u32[]{:S(2)}) collective-permute-start(f32[8,768]{1,0:T(8,128)S(1)} %get-tuple-element.32.refs_1_), channel_id=1, source_target_pairs={{0,8},{1,3},{2,10},{3,1},{4,12},{5,7},{6,14},{7,5},{8,0},{9,11},{1... | collective-permute-start | bytes 73736 | tf_op jit(solution)/shard_map/ppermute | solution.py:580
  39.4 4.4 %collective-permute-start.5 = (f32[8,1536]{1,0:T(8,128)S(1)}, f32[8,1536]{1,0:T(8,128)S(1)}, u32[]{:S(2)}, u32[]{:S(2)}) collective-permute-start(f32[8,1536]{1,0:T(8,128)S(1)} %get-tuple-element.33.after.direction.direction_ref), channel_id=1, source_target_pairs={{0,1},{1,0},{2,3},{3,2},{4,5},{5,4},{6,7},{7,6},{8,9},{9,8},{10,11... | collective-permute-start | bytes 147464 | tf_op jit(solution)/shard_map/ppermute | solution.py:589
  47.3 11.4 %all-to-all-start.2 = ((f32[32,4,128]{2,1,0:T(4,128)}), f32[32,4,128]{2,1,0:T(4,128)S(1)}, u32[]{:S(2)}, u32[]{:S(2)}) async-start(f32[32,4,128]{2,1,0:T(4,128)} %get-tuple-element.35), calls=%async_computation.2 | async-start | bytes 131072 | tf_op jit(solution)/shard_map/all_to_all | solution.py:585
  51.1 5.2 %collective-permute-start.6 = (f32[8,768]{1,0:T(8,128)S(1)}, f32[8,768]{1,0:T(8,128)S(1)}, u32[]{:S(2)}, u32[]{:S(2)}) collective-permute-start(f32[8,768]{1,0:T(8,128)S(1)} %get-tuple-element.36.refs_0_), channel_id=1, source_target_pairs={{3,5},{5,3},{8,16},{10,18},{11,13},{12,20},{13,11},{14,22},{16,8},... | collective-permute-start | bytes 73736 | tf_op jit(solution)/shard_map/ppermute | solution.py:580
  51.7 6.4 %collective-permute-start.7 = (f32[8,768]{1,0:T(8,128)S(1)}, f32[8,768]{1,0:T(8,128)S(1)}, u32[]{:S(2)}, u32[]{:S(2)}) collective-permute-start(f32[8,768]{1,0:T(8,128)S(1)} %get-tuple-element.37.refs_1_), channel_id=1, source_target_pairs={{0,8},{1,3},{2,10},{3,1},{4,12},{5,7},{6,14},{7,5},{8,0},{9,11},{1... | collective-permute-start | bytes 73736 | tf_op jit(solution)/shard_map/ppermute | solution.py:580
  59.8 4.4 %collective-permute-start.8 = (f32[8,1536]{1,0:T(8,128)S(1)}, f32[8,1536]{1,0:T(8,128)S(1)}, u32[]{:S(2)}, u32[]{:S(2)}) collective-permute-start(f32[8,1536]{1,0:T(8,128)S(1)} %get-tuple-element.38.after.later), channel_id=1, source_target_pairs={{0,1},{1,0},{2,3},{3,2},{4,5},{5,4},{6,7},{7,6},{8,9},{9,8},{10,11... | collective-permute-start | bytes 147464 | tf_op jit(solution)/shard_map/ppermute | solution.py:589
